TPU v7x, 32 devices: a whole 2x2x4 slice. The times are simulated.
32 devices in a mesh: fsdp: 8 (over z, x), tensor: 4 (over y, core).
Axes of the slice: x: 2, y: 2, z: 4, core: 2. Of those that a mesh axis runs over, the one named last changes fastest.
Arguments:
- tokens: bfloat16 [6144, 5120], P('fsdp', 'tensor'), may hold values from -48 to 48
- live_rows: int32 [8], P('fsdp'), may hold values from 128 to 768, as said below
- first_row: int32 [6144], P('fsdp'), may hold values from 0 to 767, as said below
- w_query: bfloat16 [5120, 2560], P('fsdp', 'tensor'), may hold values from -1 to 1
- w_key: bfloat16 [5120, 512], P('fsdp', 'tensor'), may hold values from -1 to 1
- w_value: bfloat16 [5120, 512], P('fsdp', 'tensor'), may hold values from -0.078125 to 0.078125
- w_out: bfloat16 [2560, 5120], P('tensor', 'fsdp'), may hold values from -1 to 1
- query_gain: float32 [2560], P('tensor'), may hold values from 0.5 to 1.5
- key_gain: float32 [512], P('tensor'), may hold values from 0.5 to 1.5
- out_gain: float32 [5120], P('tensor'), may hold values from 0.5 to 1.5
Outputs:
- output: bfloat16 [6144, 5120], P('fsdp', 'tensor')
Inputs may be any that keep to these rules, and one draw needn't show every extreme that they name: `live_rows`: each entry is a multiple of 128; the largest value is reached on some index of every draw. `first_row`: each row's value is never above its own local index and never below the first local index of its pack (384 rows); the last row of each block begins a document of one row.
All inputs are finite; a program needn't handle non-finite values.
Results may differ from a plain program's by a relative error of at most 0.009.
Values may be sent and summed in bfloat16 or wider, within the bound.
No kernel may reach another device: no remote copies, remote signals or barrier semaphores. Data moves between devices by JAX's collectives and lax.ppermute only.
A program may use at most 128 MiB of HBM per device.

v0:
```python
import math

import jax
import jax.numpy as jnp
from jax import lax
from jax.sharding import PartitionSpec as P

D = 5120
HEADS = 20
KV_HEADS = 4
HEAD_DIM = 128
BLOCK = 128


EPS = 1e-06
ROPE_BASE = 500000.0


def rotate(field, positions):
    half_dim = field.shape[-1] // 2
    freqs = jnp.power(ROPE_BASE, -(jnp.arange(half_dim, dtype=jnp.float32) * 2.0 / field.shape[-1]))
    angle = positions[:, None] * freqs[None, :]
    cosine = jnp.cos(angle)[:, None, :]
    sine_part = jnp.sin(angle)[:, None, :]
    first = field[..., :half_dim]
    second = field[..., half_dim:]
    return jnp.concatenate(
        [first * cosine - second * sine_part, second * cosine + first * sine_part], axis=-1
    )


def attend(queries, keys, values, starts, offset):
    row_count = queries.shape[0]
    kv_count = keys.shape[1]
    group_size = queries.shape[1] // kv_count
    grouped = queries.reshape(row_count, kv_count, group_size, HEAD_DIM)
    scores = jnp.einsum(
        "qkgd,skd->kgqs", grouped, keys, preferred_element_type=jnp.float32
    ) / math.sqrt(HEAD_DIM)
    local = jnp.arange(row_count, dtype=jnp.int32)
    allowed = (local[None, :] >= (starts - offset)[:, None]) & (local[None, :] <= local[:, None])
    scores = jnp.where(allowed[None, None], scores, jnp.float32(-1e30))
    peak_value = jnp.max(scores, axis=-1, keepdims=True)
    expo = jnp.exp(scores - peak_value)
    totals = jnp.sum(expo, axis=-1, keepdims=True)
    probs = (expo / totals).astype(jnp.bfloat16)
    mixed = jnp.einsum("kgqs,skd->qkgd", probs, values, preferred_element_type=jnp.float32)
    return mixed.reshape(row_count, -1).astype(jnp.bfloat16)


def project(features, matrices, counts, half_rows):
    capacity = features.shape[0]
    results = tuple((jnp.zeros((capacity, matrix.shape[1]), jnp.float32) for matrix in matrices))
    for pack_index in range(2):

        def block_step(number, carried, pack_index=pack_index):
            row_start = pack_index * half_rows + number * BLOCK
            piece = lax.dynamic_slice_in_dim(features, row_start, BLOCK, 0)
            return tuple(
                (
                    lax.dynamic_update_slice_in_dim(
                        current,
                        jnp.dot(piece, matrix, preferred_element_type=jnp.float32),
                        row_start,
                        0,
                    )
                    for current, matrix in zip(carried, matrices)
                )
            )

        results = lax.fori_loop(0, counts[pack_index] // BLOCK, block_step, results)
    return results


def layer_rows(
    local_tokens, counts, starts, w_query, w_key, w_value, w_out, query_gain, key_gain, out_gain
):
    capacity = local_tokens.shape[0]
    half_rows = capacity // 2
    features = lax.all_gather(local_tokens, "tensor", axis=1, tiled=True)
    full_query, full_key, full_value = (
        lax.all_gather(w_query, "fsdp", axis=0, tiled=True),
        lax.all_gather(w_key, "fsdp", axis=0, tiled=True),
        lax.all_gather(w_value, "fsdp", axis=0, tiled=True),
    )
    query, key, value = project(features, (full_query, full_key, full_value), counts, half_rows)
    query_sq, key_sq = lax.psum(
        (jnp.sum(query * query, axis=1), jnp.sum(key * key, axis=1)), "tensor"
    )
    query_normed = query * lax.rsqrt(query_sq / (HEADS * HEAD_DIM) + EPS)[:, None] * query_gain
    key_normed = key * lax.rsqrt(key_sq / (KV_HEADS * HEAD_DIM) + EPS)[:, None] * key_gain
    row_ids = jnp.arange(capacity, dtype=jnp.int32)
    positions = (row_ids - starts).astype(jnp.float32)
    query_rot = rotate(query_normed.reshape(capacity, -1, HEAD_DIM), positions).astype(jnp.bfloat16)
    key_rot = rotate(key_normed.reshape(capacity, -1, HEAD_DIM), positions).astype(jnp.bfloat16)
    value_heads = value.astype(jnp.bfloat16).reshape(capacity, -1, HEAD_DIM)
    packs = []
    for pack_index in range(2):
        lower = pack_index * half_rows
        packs.append(
            attend(
                query_rot[lower : lower + half_rows],
                key_rot[lower : lower + half_rows],
                value_heads[lower : lower + half_rows],
                starts[lower : lower + half_rows],
                lower,
            )
        )
    attended = jnp.concatenate(packs, axis=0)
    full_out = lax.all_gather(w_out, "fsdp", axis=1, tiled=True)
    (partial_value,) = project(attended, (full_out,), counts, half_rows)
    attn_out = lax.psum_scatter(
        partial_value.astype(jnp.bfloat16), "tensor", scatter_dimension=1, tiled=True
    ).astype(jnp.float32)
    out_sq = lax.psum(jnp.sum(attn_out * attn_out, axis=1), "tensor")
    scale = lax.rsqrt(out_sq / D + EPS)[:, None]
    result = (local_tokens.astype(jnp.float32) + attn_out * scale * out_gain).astype(jnp.bfloat16)
    limit = jnp.where(row_ids < half_rows, counts[0], half_rows + counts[1])
    return jnp.where((row_ids < limit)[:, None], result, jnp.zeros_like(result))


def body(
    tokens, live_rows, first_row, w_query, w_key, w_value, w_out, query_gain, key_gain, out_gain
):
    capacity = tokens.shape[0]
    half_rows = capacity // 2
    live_count = live_rows[0]
    count_low = jnp.minimum(live_count, half_rows)
    count_high = jnp.maximum(live_count - half_rows, 0)
    return layer_rows(
        tokens,
        (count_low, count_high),
        first_row,
        w_query,
        w_key,
        w_value,
        w_out,
        query_gain,
        key_gain,
        out_gain,
    )


def solution(mesh):
    in_specs = (
        P("fsdp", "tensor"),
        P("fsdp"),
        P("fsdp"),
        P("fsdp", "tensor"),
        P("fsdp", "tensor"),
        P("fsdp", "tensor"),
        P("tensor", "fsdp"),
        P("tensor"),
        P("tensor"),
        P("tensor"),
    )
    out_specs = P("fsdp", "tensor")
    return jax.shard_map(body, mesh=mesh, in_specs=in_specs, out_specs=out_specs, check_vma=False)
```

profile of v0, /device:TPU:0, one launch (start us, length us, event | category | flops | bytes accessed | tf_op | source)
XLA Modules:
  0.0 479.3 jit_solution(1877972351221830055)
XLA Ops:
  6.5 0.7 all-gather.10.cloned.1.call-update
  7.3 0.7 all-gather.12.cloned.1.call-update
  8.1 0.7 all-gather.8.cloned.1.call-update
  8.8 0.5 all-gather.6.cloned.1.call-update
  9.4 0.5 all-gather.14.cloned.1.call-update
  10.7 1.4 multiply_cosine_fusion
  12.2 0.9 fusion.37
  13.1 41.3 %all-gather.10.cloned.1.call-done = bf16[5120,128]{1,0:T(8,128)(2,1)} async-done(((bf16[640,128]{1,0:T(8,128)(2,1)}), bf16[5120,128]{1,0:T(8,128)(2,1)}) %all-gather.10.cloned.1.call-update) | async-done | bytes 1310736 | tf_op jit(solution)/shard_map/all_gather | solution.py:83
  54.3 42.9 %all-gather.12.cloned.1.call-done = bf16[5120,128]{1,0:T(8,128)(2,1)} async-done(((bf16[640,128]{1,0:T(8,128)(2,1)}), bf16[5120,128]{1,0:T(8,128)(2,1)}) %all-gather.12.cloned.1.call-update) | async-done | bytes 1310736 | tf_op jit(solution)/shard_map/all_gather | solution.py:84
  97.3 103.1 %all-gather.8.cloned.1.call-done = bf16[5120,640]{1,0:T(8,128)(2,1)} async-done(((bf16[640,640]{1,0:T(8,128)(2,1)}), bf16[5120,640]{1,0:T(8,128)(2,1)}) %all-gather.8.cloned.1.call-update) | async-done | bytes 6553616 | tf_op jit(solution)/shard_map/all_gather | solution.py:82
  200.4 54.9 %all-gather.6.cloned.1.call-done = bf16[768,5120]{1,0:T(8,128)(2,1)} async-done(((bf16[768,1280]{1,0:T(8,128)(2,1)}), bf16[768,5120]{1,0:T(8,128)(2,1)}) %all-gather.6.cloned.1.call-update) | async-done | bytes 7864336 | tf_op jit(solution)/shard_map/all_gather | solution.py:80
  255.5 26.0 %while.52 = (s32[]{:T(128)}, f32[768,640]{1,0:T(8,128)S(1)}, f32[768,128]{1,0:T(8,128)S(1)}, bf16[768,128]{1,0:T(8,128)(2,1)S(1)}, s32[]{:T(128)}, /*index=5*/bf...) while((s32[]{:T(128)}, f32[768,640]{1,0:T(8,128)S(1)}, ...), condition=%wide.region_1.2_spmd, body=%wide.region_0.1_spmd.sunk | while | flops 1174405120 | bytes 24055012 | solution.py:71
  255.5 4.6 convolution_dynamic-update-slice_fusion.16
  260.1 1.9 convolution_dynamic-update-slice_fusion.17
  262.1 1.8 convolution_dynamic-update-slice_fusion.18
  263.9 5.3 %convolution_dynamic-update-slice_fusion.16 = f32[768,640]{1,0:T(8,128)S(1)} fusion(f32[768,640]{1,0:T(8,128)S(1)} %get-tuple-element.543, s32[]{:T(128)S(6)} %select_n.91, bf16[5120,640]{1,0:T(8,128)(2,1)} %get-tuple-element.561, bf16[768,5120]{1,0:T(8,128)(2,1)} %get-tuple-element.560), kind=kOutput, calls=%fused_computation.clone.1 | convolution fusion | flops 838860800 | bytes 8193024 | tf_op jit(solution)/shard_map/while/body/dot_general | solution.py:63
  269.2 1.9 convolution_dynamic-update-slice_fusion.17
  271.2 1.8 convolution_dynamic-update-slice_fusion.18
  273.0 4.6 convolution_dynamic-update-slice_fusion.16
  277.6 2.0 convolution_dynamic-update-slice_fusion.17
  279.6 1.8 convolution_dynamic-update-slice_fusion.18
  281.5 25.8 %while.53 = (s32[]{:T(128)}, f32[768,640]{1,0:T(8,128)S(1)}, f32[768,128]{1,0:T(8,128)S(1)}, bf16[768,128]{1,0:T(8,128)(2,1)S(1)}, s32[]{:T(128)}, /*index=5*/bf...) while((s32[]{:T(128)}, f32[768,640]{1,0:T(8,128)S(1)}, ...), condition=%wide.region_3.4_spmd, body=%wide.region_2.3_spmd.sunk | while | flops 1174405120 | bytes 24055032 | solution.py:71
  281.5 4.6 convolution_dynamic-update-slice_fusion.19
  286.1 1.9 convolution_dynamic-update-slice_fusion.20
  288.1 1.8 convolution_dynamic-update-slice_fusion.21
  290.0 4.6 convolution_dynamic-update-slice_fusion.19
  294.5 1.9 convolution_dynamic-update-slice_fusion.20
  296.5 1.8 convolution_dynamic-update-slice_fusion.21
  298.4 5.1 %convolution_dynamic-update-slice_fusion.19 = f32[768,640]{1,0:T(8,128)S(1)} fusion(f32[768,640]{1,0:T(8,128)S(1)} %get-tuple-element.583, s32[]{:T(128)S(6)} %select_n.92, bf16[5120,640]{1,0:T(8,128)(2,1)} %get-tuple-element.602, bf16[768,5120]{1,0:T(8,128)(2,1)} %get-tuple-element.601), kind=kOutput, calls=%fused_computation.9.clone.1 | convolution fusion | flops 838860800 | bytes 8193024 | tf_op jit(solution)/shard_map/while/body/dot_general | solution.py:63
  303.4 1.9 convolution_dynamic-update-slice_fusion.20
  305.4 1.8 convolution_dynamic-update-slice_fusion.21
  307.3 0.7 copy-done.7
  307.9 0.2 copy.25
  308.1 1.8 copy.26
  309.9 0.2 multiply_reduce_fusion.1
  310.1 0.2 multiply_reduce_fusion
  310.3 6.6 %all-reduce = (f32[768]{0:T(1024)S(1)}, f32[768]{0:T(1024)S(1)}) all-reduce(f32[768]{0:T(1024)S(1)} %multiply_reduce_fusion, f32[768]{0:T(1024)S(1)} %multiply_reduce_fusion.1), channel_id=1, replica_groups=mesh['fsdp'=8,'tensor'=4] {'tensor'}, use_global_device_ids=true, to_apply=%region_7.8 | all-reduce | flops 1536 | bytes 12288 | tf_op jit(solution)/shard_map/psum | solution.py:87
  316.9 1.8 multiply_multiply_fusion
  318.8 1.9 copy.41
  320.7 1.8 copy.42
  322.8 0.8 fusion.49
  323.7 2.7 subtract_convert_fusion
  326.4 0.9 fusion.22
  327.2 0.6 fusion.20
  327.9 1.1 fusion.31
  329.0 0.3 copy.33
  329.3 0.9 fusion.23
  330.2 0.6 fusion.21
  330.8 1.1 fusion.34
  331.9 0.3 copy.34
  332.2 27.5 %all-gather.14.cloned.1.call-done = bf16[640,5120]{1,0:T(8,128)(2,1)} async-done(((bf16[640,640]{1,0:T(8,128)(2,1)}), bf16[640,5120]{1,0:T(8,128)(2,1)}) %all-gather.14.cloned.1.call-update) | async-done | bytes 6553616 | tf_op jit(solution)/shard_map/all_gather | solution.py:110
  359.8 4.0 broadcast_in_dim.38
  363.8 15.4 %while.54 = (s32[]{:T(128)}, bf16[768,5120]{1,0:T(8,128)(2,1)}, s32[]{:T(128)}, bf16[768,640]{1,0:T(8,128)(2,1)S(1)}, bf16[640,5120]{1,0:T(8,128)(2,1)}, /*index=5*/s32[]{:T(128)}, s32[]{:T(128)}, s32[]{:T(128)}, s32[]{:T(128)}) while((s32[]{:T(128)}, bf16[768,5120]{1,0:T(8,128)(2,1)}, s32[]{:T(128)}, bf16[768,640]{1,0:T(8,128)(2,1)S(1)}, ...), condition=%wide.region_13.14_spmd, body=%wide.region_12.13_spmd.sunk | while | flops 838860800 | bytes 9340043 | solution.py:71
  363.8 5.1 %convolution_dynamic-update-slice_fusion.22 = bf16[768,5120]{1,0:T(8,128)(2,1)} fusion(bf16[768,5120]{1,0:T(8,128)(2,1)} %get-tuple-element.620, s32[]{:T(128)S(6)} %select_n.93, bf16[640,5120]{1,0:T(8,128)(2,1)} %get-tuple-element.632, bf16[768,640]{1,0:T(8,128)(2,1)S(1)} %get-tuple-element.631), kind=kOutput, calls=%fused_computation.18.clone.1 | convolution fusion | flops 838860800 | bytes 9339904 | tf_op jit(solution)/shard_map/while/body/dot_general | solution.py:63
  368.9 5.1 %convolution_dynamic-update-slice_fusion.22 = bf16[768,5120]{1,0:T(8,128)(2,1)} fusion(bf16[768,5120]{1,0:T(8,128)(2,1)} %get-tuple-element.620, s32[]{:T(128)S(6)} %select_n.93, bf16[640,5120]{1,0:T(8,128)(2,1)} %get-tuple-element.632, bf16[768,640]{1,0:T(8,128)(2,1)S(1)} %get-tuple-element.631), kind=kOutput, calls=%fused_computation.18.clone.1 | convolution fusion | flops 838860800 | bytes 9339904 | tf_op jit(solution)/shard_map/while/body/dot_general | solution.py:63
  374.1 5.1 %convolution_dynamic-update-slice_fusion.22 = bf16[768,5120]{1,0:T(8,128)(2,1)} fusion(bf16[768,5120]{1,0:T(8,128)(2,1)} %get-tuple-element.620, s32[]{:T(128)S(6)} %select_n.93, bf16[640,5120]{1,0:T(8,128)(2,1)} %get-tuple-element.632, bf16[768,640]{1,0:T(8,128)(2,1)S(1)} %get-tuple-element.631), kind=kOutput, calls=%fused_computation.18.clone.1 | convolution fusion | flops 838860800 | bytes 9339904 | tf_op jit(solution)/shard_map/while/body/dot_general | solution.py:63
  379.2 15.4 %while.55 = (s32[]{:T(128)}, bf16[768,5120]{1,0:T(8,128)(2,1)}, s32[]{:T(128)}, bf16[768,640]{1,0:T(8,128)(2,1)S(1)}, bf16[640,5120]{1,0:T(8,128)(2,1)}, /*index...) while((s32[]{:T(128)}, bf16[768,5120]{1,0:T(8,128)(2,1)}, s32[]{:T(128)}, ...), condition=%wide.region_15.16_spmd, body=%wide.region_14.15_spmd.sunk | while | flops 838860800 | bytes 9340063 | solution.py:71
  379.2 5.1 %convolution_dynamic-update-slice_fusion.23 = bf16[768,5120]{1,0:T(8,128)(2,1)} fusion(bf16[768,5120]{1,0:T(8,128)(2,1)} %get-tuple-element.648, s32[]{:T(128)S(6)} %select_n.94, bf16[640,5120]{1,0:T(8,128)(2,1)} %get-tuple-element.661, bf16[768,640]{1,0:T(8,128)(2,1)S(1)} %get-tuple-element.660), kind=kOutput, calls=%fused_computation.21.clone.1 | convolution fusion | flops 838860800 | bytes 9339904 | tf_op jit(solution)/shard_map/while/body/dot_general | solution.py:63
  384.3 5.2 %convolution_dynamic-update-slice_fusion.23 = bf16[768,5120]{1,0:T(8,128)(2,1)} fusion(bf16[768,5120]{1,0:T(8,128)(2,1)} %get-tuple-element.648, s32[]{:T(128)S(6)} %select_n.94, bf16[640,5120]{1,0:T(8,128)(2,1)} %get-tuple-element.661, bf16[768,640]{1,0:T(8,128)(2,1)S(1)} %get-tuple-element.660), kind=kOutput, calls=%fused_computation.21.clone.1 | convolution fusion | flops 838860800 | bytes 9339904 | tf_op jit(solution)/shard_map/while/body/dot_general | solution.py:63
  389.4 5.1 %convolution_dynamic-update-slice_fusion.23 = bf16[768,5120]{1,0:T(8,128)(2,1)} fusion(bf16[768,5120]{1,0:T(8,128)(2,1)} %get-tuple-element.648, s32[]{:T(128)S(6)} %select_n.94, bf16[640,5120]{1,0:T(8,128)(2,1)} %get-tuple-element.661, bf16[768,640]{1,0:T(8,128)(2,1)S(1)} %get-tuple-element.660), kind=kOutput, calls=%fused_computation.21.clone.1 | convolution fusion | flops 838860800 | bytes 9339904 | tf_op jit(solution)/shard_map/while/body/dot_general | solution.py:63
  394.6 66.4 %reduce-scatter.2.cloned.1.call-done = bf16[768,1280]{1,0:T(8,128)(2,1)} async-done(((bf16[768,5120]{1,0:T(8,128)(2,1)}), bf16[768,1280]{1,0:T(8,128)(2,1)}) %reduce-scatter.2.cloned.1.call-update) | async-done | bytes 1966096 | tf_op jit(solution)/shard_map/reduce_scatter | solution.py:112
  461.0 2.0 fusion.16
  463.0 5.8 %psum.23 = f32[768]{0:T(1024)S(1)} all-reduce(f32[768]{0:T(1024)S(1)} %fusion.16), channel_id=1, replica_groups=mesh['fsdp'=8,'tensor'=4] {'tensor'}, use_global_device_ids=true, to_apply=%region_18.19 | all-reduce | flops 768 | bytes 6144 | tf_op jit(solution)/shard_map/psum | solution.py:115
  468.8 3.7 fusion.24
  (65 shorter events, 1.0 us)
Async XLA Ops:
  6.5 4.1 copy-start.11
  6.5 47.8 %all-gather.10.cloned.1.call-start = ((), (), s32[]{:S(2)}) async-start(), calls=%async_computation.3 | async-start | bytes 1474560 | tf_op jit(solution)/shard_map/all_gather | solution.py:83
  7.3 90.0 %all-gather.12.cloned.1.call-start = ((), (), s32[]{:S(2)}) async-start(), calls=%async_computation.4 | async-start | bytes 1474560 | tf_op jit(solution)/shard_map/all_gather | solution.py:84
  8.0 192.4 %all-gather.8.cloned.1.call-start = ((), (), s32[]{:S(2)}) async-start(), calls=%async_computation.2 | async-start | bytes 7372800 | tf_op jit(solution)/shard_map/all_gather | solution.py:82
  8.7 246.6 %all-gather.6.cloned.1.call-start = ((), (), s32[]{:S(2)}) async-start(), calls=%async_computation.1 | async-start | bytes 9830400 | tf_op jit(solution)/shard_map/all_gather | solution.py:80
  9.3 350.5 %all-gather.14.cloned.1.call-start = ((), (), s32[]{:S(2)}) async-start(), calls=%async_computation.5 | async-start | bytes 7372800 | tf_op jit(solution)/shard_map/all_gather | solution.py:110
  9.9 451.1 %reduce-scatter.2.cloned.1.call-start = ((), (), s32[]{:S(2)}) async-start(), calls=%async_computation.6 | async-start | bytes 9830400 | tf_op jit(solution)/shard_map/reduce_scatter | solution.py:112
  255.5 4.6 copy-start
  260.1 2.0 copy-start.2
  263.9 5.3 %copy-start = (bf16[5120,128]{1,0:T(8,128)(2,1)S(1)}, bf16[5120,128]{1,0:T(8,128)(2,1)}, u32[]{:S(2)}) copy-start(bf16[5120,128]{1,0:T(8,128)(2,1)} %get-tuple-element.562) | copy-start | bytes 3932164 | tf_op jit(solution)/shard_map/while
  269.2 2.0 copy-start.2
  273.0 4.6 copy-start
  277.6 2.0 copy-start.2
  281.5 4.6 copy-start.1
  286.1 2.0 copy-start.3
  290.0 4.6 copy-start.1
  294.5 2.0 copy-start.3
  298.4 5.1 %copy-start.1 = (bf16[5120,128]{1,0:T(8,128)(2,1)S(1)}, bf16[5120,128]{1,0:T(8,128)(2,1)}, u32[]{:S(2)}) copy-start(bf16[5120,128]{1,0:T(8,128)(2,1)} %get-tuple-element.603) | copy-start | bytes 3932164 | tf_op jit(solution)/shard_map/while
  303.4 2.0 copy-start.3
  307.2 0.7 copy-start.7
  308.1 8.8 %copy-start.13 = (f32[640]{0:T(1024)S(1)}, f32[640]{0:T(1024)}, u32[]{:S(2)}) copy-start(f32[640]{0:T(1024)} %param.25) | copy-start | bytes 7684
  318.8 3.7 copy-start.8
  318.8 3.9 copy-start.14
  322.7 5.2 %copy-start.9 = (bf16[768,128]{0,1:T(8,128)(2,1)}, bf16[768,128]{0,1:T(8,128)(2,1)S(1)}, u32[]{:S(2)}) copy-start(bf16[768,128]{0,1:T(8,128)(2,1)S(1)} %copy.24) | copy-start | bytes 589828
  323.6 2.7 copy-start.6
  327.9 1.4 copy-start.5
  329.3 1.6 copy-start.10
  394.6 74.2 %copy-start.12 = (f32[1280]{0:T(1024)S(1)}, f32[1280]{0:T(1024)}, u32[]{:S(2)}) copy-start(f32[1280]{0:T(1024)} %param.27) | copy-start | bytes 15364
  394.6 74.2 %copy-start.4 = (bf16[768,1280]{1,0:T(8,128)(2,1)S(1)}, bf16[768,1280]{1,0:T(8,128)(2,1)}, u32[]{:S(2)}) copy-start(bf16[768,1280]{1,0:T(8,128)(2,1)} %param.18) | copy-start | bytes 5898244
Sparse Core Ops, SparseCore 0:
  9.5 44.7 all-gather.9
  56.5 40.7 all-gather.11
  99.4 100.9 all-gather.7
  201.8 53.4 all-gather.5
  257.4 102.3 all-gather.13
  394.7 66.2 reduce-scatter.1
where the time goes:
time: 480 us; the launch traced here: 479 us
  waiting for transfers between devices  339 us (71%)
  matrix products  86 us (18%)
  other arithmetic  15.3 us (3%)
  between operations  14.5 us (3%)
  blocking collectives  12.3 us (3%)
  local copies, waits for them, and re-layouts  11.4 us (2%)
    all_gather x1, waiting for transfers between devices, layer_rows(): lax.all_gather(w_query, 'fsdp', axis=0, tiled=True)  103 us
    dot_general x24, matrix products, block_step(): jnp.dot(piece, matrix, preferred_element_type=jnp.float32)  82.1 us
    reduce_scatter x1, waiting for transfers between devices, layer_rows(): lax.psum_scatter(partial_value.astype(jnp.bfloat16), 'tensor', scatter_di...  66.4 us
    all_gather x1, waiting for transfers between devices, layer_rows(): features = lax.all_gather(local_tokens, 'tensor', axis=1, tiled=True)  54.9 us
    all_gather x1, waiting for transfers between devices, layer_rows(): lax.all_gather(w_value, 'fsdp', axis=0, tiled=True)  42.9 us
    all_gather x1, waiting for transfers between devices, layer_rows(): lax.all_gather(w_key, 'fsdp', axis=0, tiled=True)  41.3 us
    all_gather x1, waiting for transfers between devices, layer_rows(): full_out = lax.all_gather(w_out, 'fsdp', axis=1, tiled=True)  27.5 us
  transfers between devices with their start and end apart: 6, of which 6 were waited for; matrix products, arithmetic and copies ran while one was open for 15% of the time, Pallas kernels for 0%

commit v1 on v0

v1 whole, which is shorter than its diff:
```python
import math

import jax
import jax.numpy as jnp
from jax import lax
from jax.sharding import PartitionSpec as P

HEAD_DIM = 128
EPS = 1e-06
ROPE_BASE = 500000.0
AXES = ("fsdp", "tensor")


def permute(array, mesh_sizes, target):
    n, tensor_size = mesh_sizes
    pairs = []
    for f in range(n):
        for t in range(tensor_size):
            to_f, to_t = target(f, t)
            pairs.append((f * tensor_size + t, to_f * tensor_size + to_t))
    return lax.ppermute(array, AXES, pairs)


def reverse_bits(value, size):
    result = 0
    while size > 1:
        result = result * 2 + value % 2
        value //= 2
        size //= 2
    return result


def snake(n):
    return list(range(0, n, 2)) + list(range(n - 1, 0, -2))


def gather_tensor(array, sizes):
    have = {0: array}
    bit = sizes[1] // 2
    while bit:
        for r in sorted(have):
            have[r ^ bit] = permute(have[r], sizes, lambda f, t, bit=bit: (f, t ^ bit))
        bit //= 2
    return [have[r] for r in range(sizes[1])]


def ring_gather(top, bottom, sizes):
    n = sizes[0]
    order = snake(n)
    place = {f: i for i, f in enumerate(order)}
    tops, bottoms = [top], [bottom]
    for _ in range(n - 1):
        tops.append(permute(tops[-1], sizes, lambda f, t: (order[(place[f] + 1) % n], t)))
        bottoms.append(permute(bottoms[-1], sizes, lambda f, t: (order[(place[f] - 1) % n], t)))
    return tops, bottoms


def rotate(field, cosine, sine):
    half_dim = field.shape[-1] // 2
    first = field[..., :half_dim]
    second = field[..., half_dim:]
    return jnp.concatenate([first * cosine - second * sine, second * cosine + first * sine], axis=-1)


def attend(queries, keys, values, starts, offset):
    row_count = queries.shape[0]
    kv_count = keys.shape[1]
    group_size = queries.shape[1] // kv_count
    grouped = queries.reshape(row_count, kv_count, group_size, HEAD_DIM)
    scores = jnp.einsum(
        "qkgd,skd->kgqs", grouped, keys, preferred_element_type=jnp.float32
    ) / math.sqrt(HEAD_DIM)
    local = jnp.arange(row_count, dtype=jnp.int32)
    allowed = (local[None, :] >= (starts - offset)[:, None]) & (local[None, :] <= local[:, None])
    scores = jnp.where(allowed[None, None], scores, jnp.float32(-1e30))
    peak_value = jnp.max(scores, axis=-1, keepdims=True)
    expo = jnp.exp(scores - peak_value)
    totals = jnp.sum(expo, axis=-1, keepdims=True)
    probs = (expo / totals).astype(jnp.bfloat16)
    mixed = jnp.einsum("kgqs,skd->qkgd", probs, values, preferred_element_type=jnp.float32)
    return mixed.reshape(row_count, -1).astype(jnp.bfloat16)


def body(
    sizes, tokens, live_rows, first_row, w_query, w_key, w_value, w_out, query_gain, key_gain, out_gain
):
    n, tensor_size = sizes
    capacity, width = tokens.shape
    half_rows = capacity // 2
    per_tensor = n // tensor_size
    f_index = lax.axis_index("fsdp")
    t_index = lax.axis_index("tensor")
    order = snake(n)
    place = [order.index(f) for f in range(n)]
    order_of = jnp.array(order, jnp.int32)
    position = jnp.array(place, jnp.int32)[f_index]

    weights = jnp.concatenate([w_query, w_key, w_value], axis=1)
    depth = weights.shape[0]
    half = depth // 2
    token_blocks = gather_tensor(tokens, sizes)
    tops, bottoms = ring_gather(weights[:half], weights[half:], sizes)

    moved = permute(
        w_out,
        sizes,
        lambda f, t: (
            ((f // per_tensor) ^ reverse_bits(t, tensor_size)) * per_tensor + f % per_tensor,
            t,
        ),
    )
    moved = permute(
        moved, sizes, lambda f, t: (f, (f // per_tensor) ^ reverse_bits(t, tensor_size))
    )

    token_stack = jnp.stack(token_blocks)
    total = None
    steps = [(0, n // 2)] + [(s, n - s) for s in range(n // 2 + 1, n)]
    for group in steps:
        for offset in group:
            block = order_of[lax.rem(position + offset, n)]
            relative = (block // per_tensor) ^ t_index
            piece = lax.dynamic_slice(
                token_stack, (relative, 0, lax.rem(block, per_tensor) * depth), (1, capacity, depth)
            )[0]
            matrix = jnp.concatenate([tops[(n - offset) % n], bottoms[offset]], axis=0)
            term = jnp.dot(piece, matrix, preferred_element_type=jnp.float32)
            total = term if total is None else total + term

    out_top, out_bottom, total = lax.optimization_barrier(
        (moved[: w_out.shape[0] // 2], moved[w_out.shape[0] // 2 :], total)
    )
    out_tops, out_bottoms = ring_gather(out_top, out_bottom, sizes)

    q_width, k_width = w_query.shape[1], w_key.shape[1]
    query = total[:, :q_width]
    key = total[:, q_width : q_width + k_width]
    value = total[:, q_width + k_width :]
    query_sq, key_sq = lax.psum(
        (jnp.sum(query * query, axis=1), jnp.sum(key * key, axis=1)), "tensor"
    )
    query_normed = (
        query * lax.rsqrt(query_sq / (q_width * tensor_size) + EPS)[:, None] * query_gain
    )
    key_normed = key * lax.rsqrt(key_sq / (k_width * tensor_size) + EPS)[:, None] * key_gain
    row_ids = jnp.arange(capacity, dtype=jnp.int32)
    positions = (row_ids - first_row).astype(jnp.float32)
    half_dim = HEAD_DIM // 2
    freqs = jnp.power(
        ROPE_BASE, -(jnp.arange(half_dim, dtype=jnp.float32) * 2.0 / HEAD_DIM)
    )
    angle = positions[:, None] * freqs[None, :]
    cosine = jnp.cos(angle)[:, None, :]
    sine = jnp.sin(angle)[:, None, :]
    query_rot = rotate(query_normed.reshape(capacity, -1, HEAD_DIM), cosine, sine).astype(jnp.bfloat16)
    key_rot = rotate(key_normed.reshape(capacity, -1, HEAD_DIM), cosine, sine).astype(jnp.bfloat16)
    value_heads = value.astype(jnp.bfloat16).reshape(capacity, -1, HEAD_DIM)
    packs = []
    for pack_index in range(2):
        lower = pack_index * half_rows
        packs.append(
            attend(
                query_rot[lower : lower + half_rows],
                key_rot[lower : lower + half_rows],
                value_heads[lower : lower + half_rows],
                first_row[lower : lower + half_rows],
                lower,
            )
        )
    attended = jnp.concatenate(packs, axis=0)
    attended_stack = jnp.stack(gather_tensor(attended, sizes))

    reversed_of = jnp.array(
        [reverse_bits(t, tensor_size) for t in range(tensor_size)], jnp.int32
    )
    result = jnp.zeros((per_tensor, capacity, w_out.shape[1]), jnp.float32)
    for group in steps:
        for offset in group:
            block = order_of[lax.rem(position + offset, n)]
            source = reversed_of[(block // per_tensor) ^ t_index]
            column = lax.rem(block, per_tensor)
            piece = lax.dynamic_index_in_dim(attended_stack, source ^ t_index, 0, False)
            matrix = jnp.concatenate([out_tops[(n - offset) % n], out_bottoms[offset]], axis=0)
            term = jnp.dot(piece, matrix, preferred_element_type=jnp.float32)
            current = lax.dynamic_index_in_dim(result, column, 0, False)
            result = lax.dynamic_update_index_in_dim(result, current + term, column, 0)
    attn_out = jnp.concatenate([result[q] for q in range(per_tensor)], axis=1)

    out_sq = lax.psum(jnp.sum(attn_out * attn_out, axis=1), "tensor")
    scale = lax.rsqrt(out_sq / (width * tensor_size) + EPS)[:, None]
    summed = (tokens.astype(jnp.float32) + attn_out * scale * out_gain).astype(jnp.bfloat16)
    return jnp.where((row_ids < live_rows[0])[:, None], summed, jnp.zeros_like(summed))


def solution(mesh):
    sizes = (mesh.shape["fsdp"], mesh.shape["tensor"])

    def run(*arrays):
        return body(sizes, *arrays)

    in_specs = (
        P("fsdp", "tensor"),
        P("fsdp"),
        P("fsdp"),
        P("fsdp", "tensor"),
        P("fsdp", "tensor"),
        P("fsdp", "tensor"),
        P("tensor", "fsdp"),
        P("tensor"),
        P("tensor"),
        P("tensor"),
    )
    return jax.shard_map(
        run, mesh=mesh, in_specs=in_specs, out_specs=P("fsdp", "tensor"), check_vma=False
    )
```

time: 480 us -> 339 us (0.71); the launches traced: 479 us -> 333 us
  waiting for transfers between devices: 339 us -> 86.7 us
  starting transfers between devices: 0.19 us -> 58.7 us
  local copies, waits for them, and re-layouts: 11.4 us -> 65.6 us
  matrix products: 86 us -> 56.6 us
  between operations: 14.5 us -> 32.8 us
    all_gather x5 -> x0, waiting for transfers between devices: 270 us -> none  [the longest x1 103 us: layer_rows(): lax.all_gather(w_query, 'fsdp', axis=0, tiled=True)]
    ppermute x0 -> x36, waiting for transfers between devices: none -> 86.7 us  [permute(): return lax.ppermute(array, AXES, pairs)]
    reduce_scatter x1 -> x0, waiting for transfers between devices: 66.4 us -> none  [layer_rows(): lax.psum_scatter(partial_value.astype(jnp.bfloat16), 'tensor', scatter_di...]
    ppermute x0 -> x36, starting transfers between devices: none -> 58.7 us  [permute(): return lax.ppermute(array, AXES, pairs)]
    dot_general x24 -> x16, matrix products: 82.1 us -> 50.9 us  [body(): term = jnp.dot(piece, matrix, preferred_element_type=jnp.float32)]
    dynamic_slice x0 -> x17, local copies, waits for them, and re-layouts: none -> 24.6 us  [the longest x14 22.6 us: body(): current = lax.dynamic_index_in_dim(result, column, 0, False)]
    dynamic_update_slice x0 -> x7, local copies, waits for them, and re-layouts: none -> 10.4 us  [body(): result = lax.dynamic_update_index_in_dim(result, current + term, column, 0)]
    broadcast_in_dim x2 -> x8, local copies, waits for them, and re-layouts: 4.14 us -> 13.4 us  [the longest x7 13.2 us: body(): result = lax.dynamic_update_index_in_dim(result, current + term, column, 0)]
  transfers between devices with their start and end apart: 6 -> 36, of which waited for: 6 -> 10; matrix products, arithmetic and copies ran while one was open for 15% -> 30% of each run, Pallas kernels for 0% -> 0%
where the time goes in v1:
time: 339 us; the launch traced here: 333 us
  waiting for transfers between devices  86.7 us (26%)
  local copies, waits for them, and re-layouts  65.6 us (19%)
  starting transfers between devices  58.7 us (17%)
  matrix products  56.6 us (17%)
  between operations  32.8 us (10%)
  other arithmetic  19.4 us (6%)
  blocking collectives  13.1 us (4%)
    ppermute x36, waiting for transfers between devices, permute(): return lax.ppermute(array, AXES, pairs)  86.7 us
    ppermute x36, starting transfers between devices, permute(): return lax.ppermute(array, AXES, pairs)  58.7 us
    dot_general x16, matrix products, body(): term = jnp.dot(piece, matrix, preferred_element_type=jnp.float32)  50.9 us
    dynamic_slice x14, local copies, waits for them, and re-layouts, body(): current = lax.dynamic_index_in_dim(result, column, 0, False)  22.6 us
    broadcast_in_dim x7, local copies, waits for them, and re-layouts, body(): result = lax.dynamic_update_index_in_dim(result, current + term, column, 0)  13.2 us
    unnamed x78, local copies, waits for them, and re-layouts  10.6 us
    dynamic_update_slice x7, local copies, waits for them, and re-layouts, body(): result = lax.dynamic_update_index_in_dim(result, current + term, column, 0)  10.4 us
    psum x1, blocking collectives, body(): lax.psum((jnp.sum(query * query, axis=1), jnp.sum(key * key, axis=1)), 't...  7.39 us
  transfers between devices with their start and end apart: 36, of which 10 were waited for; matrix products, arithmetic and copies ran while one was open for 30% of the time, Pallas kernels for 0%

profile of v1, /device:TPU:0, one launch (start us, length us, event | category | flops | bytes accessed | tf_op | source)
XLA Modules:
  0.0 332.9 jit_solution(18336044012270422301)
XLA Ops:
  0.0 3.0 collective-permute-start.3
  8.4 12.4 %collective-permute-done.9 = bf16[320,896]{1,0:T(8,128)(2,1)S(1)} collective-permute-done((bf16[320,896]{1,0:T(8,128)(2,1)S(1)}, bf16[320,896]{1,0:T(8,128)(2,1)S(1)}, u32[]{:S(2)}, u32[]{:S(2)}) %collective-permute-start.9) | collective-permute-done | bytes 573472 | tf_op jit(solution)/shard_map/ppermute | solution.py:21
  22.8 11.6 %collective-permute-done.10 = bf16[320,896]{1,0:T(8,128)(2,1)S(1)} collective-permute-done((bf16[320,896]{1,0:T(8,128)(2,1)S(1)}, bf16[320,896]{1,0:T(8,128)(2,1)S(1)}, u32[]{:S(2)}, u32[]{:S(2)}) %collective-permute-start.10) | collective-permute-done | bytes 573472 | tf_op jit(solution)/shard_map/ppermute | solution.py:21
  36.5 9.7 %collective-permute-done.3 = bf16[768,1280]{1,0:T(8,128)(2,1)} collective-permute-done((bf16[768,1280]{1,0:T(8,128)(2,1)}, bf16[768,1280]{1,0:T(8,128)(2,1)}, u32[]{:S(2)}, u32[]{:S(2)}) %collective-permute-start.3) | collective-permute-done | bytes 1966112 | tf_op jit(solution)/shard_map/ppermute | solution.py:21
  46.2 7.9 %collective-permute-start = (bf16[640,640]{1,0:T(8,128)(2,1)}, bf16[640,640]{1,0:T(8,128)(2,1)}, u32[]{:S(2)}, u32[]{:S(2)}) collective-permute-start(bf16[640,640]{1,0:T(8,128)(2,1)} %param.19), channel_id=1, source_target_pairs={{0,0},{1,17},{2,10},{3,27},{4,4},{5,21},{6,14},{7,31},{8,8},{9,25}... | collective-permute-start | bytes 2457608 | tf_op jit(solution)/shard_map/ppermute | solution.py:21
  54.1 1.7 collective-permute-start.12
  56.2 13.8 %collective-permute-done.12 = bf16[320,896]{1,0:T(8,128)(2,1)} collective-permute-done((bf16[320,896]{1,0:T(8,128)(2,1)S(1)}, bf16[320,896]{1,0:T(8,128)(2,1)}, u32[]{:S(2)}, u32[]{:S(2)}) %collective-permute-start.12) | collective-permute-done | bytes 573472 | tf_op jit(solution)/shard_map/ppermute | solution.py:21
  70.9 4.6 %collective-permute-start.14 = (bf16[320,896]{1,0:T(8,128)(2,1)}, bf16[320,896]{1,0:T(8,128)(2,1)}, u32[]{:S(2)}, u32[]{:S(2)}) collective-permute-start(bf16[320,896]{1,0:T(8,128)(2,1)} %collective-permute-done.8), channel_id=1, source_target_pairs={{0,8},{1,9},{2,10},{3,11},{4,0},{5,1},{6,2},{7,3},{8,16},{9,17},{1... | collective-permute-start | bytes 1720328 | tf_op jit(solution)/shard_map/ppermute | solution.py:21
  90.6 7.9 %collective-permute-start.1 = (bf16[640,640]{1,0:T(8,128)(2,1)}, bf16[640,640]{1,0:T(8,128)(2,1)}, u32[]{:S(2)}, u32[]{:S(2)}) collective-permute-start(bf16[640,640]{1,0:T(8,128)(2,1)} %collective-permute-done), channel_id=1, source_target_pairs={{0,0},{1,2},{2,1},{3,3},{4,4},{5,6},{6,5},{7,7},{8,9},{9,11},{10,8... | collective-permute-start | bytes 2457608 | tf_op jit(solution)/shard_map/ppermute | solution.py:21
  112.3 7.8 %collective-permute-start.16 = (bf16[320,896]{1,0:T(8,128)(2,1)}, bf16[320,896]{1,0:T(8,128)(2,1)S(1)}, u32[]{:S(2)}, u32[]{:S(2)}) collective-permute-start(bf16[320,896]{1,0:T(8,128)(2,1)} %collective-permute-done.14), channel_id=1, source_target_pairs={{0,8},{1,9},{2,10},{3,11},{4,0},{5,1},{6,2},{7,3},{8,16},{9,17},{1... | collective-permute-start | bytes 1720328 | tf_op jit(solution)/shard_map/ppermute | solution.py:21
  120.0 2.4 multiply_cosine_fusion
  122.4 2.1 fusion.172
  124.5 8.8 %collective-permute-done.15 = bf16[320,896]{1,0:T(8,128)(2,1)S(1)} collective-permute-done((bf16[320,896]{1,0:T(8,128)(2,1)}, bf16[320,896]{1,0:T(8,128)(2,1)S(1)}, u32[]{:S(2)}, u32[]{:S(2)}) %collective-permute-start.15) | collective-permute-done | bytes 573472 | tf_op jit(solution)/shard_map/ppermute | solution.py:21
  135.5 3.7 %pad_maximum_fusion = bf16[4,768,1280]{2,1,0:T(8,128)(2,1)S(1)} fusion(bf16[1,768,1280]{2,1,0:T(8,128)(2,1)} %bitcast.4, bf16[1,768,1280]{2,1,0:T(8,128)(2,1)} %bitcast.3, bf16[1,768,1280]{2,1,0:T(8,128)(2,1)} %bitcast.2, bf16[1,768,1280]{2,1,0:T(8,128)(2,1)S(1)} %bitcast.199), kind=kLoop, calls=%fused_computation | loop fusion | flops 11796480 | bytes 15728640 | tf_op jit(solution)/shard_map/stack | solution.py:116
  139.3 2.6 fusion.24
  141.9 2.4 fusion.28
  144.3 2.4 fusion.32
  149.4 2.8 fusion.69
  152.2 2.8 fusion.44
  155.1 4.4 %add_add_fusion = f32[768,896]{0,1:T(8,128)S(1)} fusion(f32[768,896]{0,1:T(8,128)} %fusion.44, f32[768,896]{0,1:T(8,128)S(1)} %fusion.40, f32[768,896]{0,1:T(8,128)S(1)} %fusion.36, f32[768,896]{0,1:T(8,128)S(1)} %fusion.32, f32[768,896]{0,1:T(8,128)S(1)} %fusion.28, f32[768,896]{0,1:T(8,128)} %fusion.69, f32[768,896]{0,1:T(8,128)S(1)} %fusion.24, ...), kind=kOutput, calls=%fused_computation.11 | convolution fusion | flops 887914496 | bytes 24150024 | tf_op jit(solution)/shard_map/dot_general | solution.py:127
  161.0 7.4 %all-reduce = (f32[768]{0:T(1024)S(1)}, f32[768]{0:T(1024)S(1)}) all-reduce(f32[768]{0:T(1024)S(1)} %multiply_reduce_fusion.1, f32[768]{0:T(1024)S(1)} %multiply_reduce_fusion.2), channel_id=1, replica_groups=mesh['fsdp'=8,'tensor'=4] {'tensor'}, use_global_device_ids=true, to_apply=%region_3.4 | all-reduce | flops 1536 | bytes 12288 | tf_op jit(solution)/shard_map/psum | solution.py:139
  171.3 1.8 copy.100
  173.1 1.9 copy.101
  174.9 2.1 subtract_convert_fusion
  179.5 2.0 fusion.18
  182.1 2.0 fusion.21
  185.1 2.1 collective-permute-start.26
  187.2 8.4 %collective-permute-done.26 = bf16[320,640]{1,0:T(8,128)(2,1)S(1)} collective-permute-done((bf16[320,640]{1,0:T(8,128)(2,1)S(1)}, bf16[320,640]{1,0:T(8,128)(2,1)S(1)}, u32[]{:S(2)}, u32[]{:S(2)}) %collective-permute-start.26) | collective-permute-done | bytes 409632 | tf_op jit(solution)/shard_map/ppermute | solution.py:21
  195.6 2.1 collective-permute-start.27
  197.7 8.8 %collective-permute-done.20 = bf16[768,640]{0,1:T(8,128)(2,1)S(1)} collective-permute-done((bf16[768,640]{0,1:T(8,128)(2,1)S(1)}, bf16[768,640]{0,1:T(8,128)(2,1)S(1)}, u32[]{:S(2)}, u32[]{:S(2)}) %collective-permute-start.20) | collective-permute-done | bytes 983072 | tf_op jit(solution)/shard_map/ppermute | solution.py:21
  206.5 2.0 collective-permute-start.28
  208.9 9.6 %collective-permute-done.28 = bf16[320,640]{1,0:T(8,128)(2,1)} collective-permute-done((bf16[320,640]{1,0:T(8,128)(2,1)S(1)}, bf16[320,640]{1,0:T(8,128)(2,1)}, u32[]{:S(2)}, u32[]{:S(2)}) %collective-permute-start.28) | collective-permute-done | bytes 409632 | tf_op jit(solution)/shard_map/ppermute | solution.py:21
  218.5 2.0 collective-permute-start.29
  227.4 3.2 collective-permute-done.29
  233.0 1.7 pad_maximum_fusion.1
  237.2 1.9 copy-done
  239.3 1.8 copy.72
  241.1 4.4 %fusion.11 = f32[1,768,640]{1,2,0:T(8,128)} fusion(f32[1,768,640]{1,2,0:T(8,128)} %copy.72, bf16[4,768,640]{1,2,0:T(8,128)(2,1)} %copy-done.3, s32[]{:T(128)S(6)} %select_n.233, bf16[320,640]{1,0:T(8,128)(2,1)} %collective-permute-done.29, bf16[320,640]{1,0:T(8,128)(2,1)} %collective-permute-done.25), kind=kOutput, calls=%fused_computation.33 | convolution fusion | flops 631275520 | bytes 5734404 | tf_op jit(solution)/shard_map/dot_general | solution.py:184
  245.4 1.9 copy.73
  248.8 1.7 constant_dynamic-slice_fusion.5
  250.5 1.8 copy.74
  252.2 4.4 %fusion.10 = f32[1,768,640]{1,2,0:T(8,128)} fusion(f32[1,768,640]{1,2,0:T(8,128)} %copy.74, bf16[4,768,640]{1,2,0:T(8,128)(2,1)} %copy-done.3, s32[]{:T(128)S(6)} %select_n.235, bf16[320,640]{1,0:T(8,128)(2,1)} %collective-permute-done.30, bf16[320,640]{1,0:T(8,128)(2,1)} %collective-permute-done.24), kind=kOutput, calls=%fused_computation.31 | convolution fusion | flops 631275520 | bytes 5734404 | tf_op jit(solution)/shard_map/dot_general | solution.py:184
  256.6 1.9 copy.75
  261.7 1.8 copy.76
  264.7 4.4 %fusion.9 = f32[1,768,640]{1,2,0:T(8,128)} fusion(f32[1,768,640]{1,2,0:T(8,128)} %copy.76, bf16[4,768,640]{1,2,0:T(8,128)(2,1)} %copy-done.3, s32[]{:T(128)S(6)} %select_n.237, bf16[320,640]{1,0:T(8,128)(2,1)} %collective-permute-done.28, bf16[320,640]{1,0:T(8,128)(2,1)} %collective-permute-done.31), kind=kOutput, calls=%fused_computation.29 | convolution fusion | flops 631275520 | bytes 5734404 | tf_op jit(solution)/shard_map/dot_general | solution.py:184
  269.1 1.9 copy.77
  272.4 1.7 constant_dynamic-slice_fusion.3
  274.1 1.8 copy.78
  276.7 4.1 %fusion.8 = f32[1,768,640]{1,2,0:T(8,128)} fusion(f32[1,768,640]{1,2,0:T(8,128)} %copy.78, bf16[4,768,640]{1,2,0:T(8,128)(2,1)} %copy-done.3, s32[]{:T(128)S(6)} %select_n.239, bf16[320,640]{1,0:T(8,128)(2,1)S(1)} %collective-permute-done.32, bf16[320,640]{1,0:T(8,128)(2,1)S(1)} %copy-done.35), kind=kOutput, calls=%fused_computation.27 | convolution fusion | flops 631275520 | bytes 5734404 | tf_op jit(solution)/shard_map/dot_general | solution.py:184
  280.8 1.9 copy.79
  284.2 1.7 constant_dynamic-slice_fusion.2
  285.8 1.8 copy.80
  288.9 4.1 %fusion.7 = f32[1,768,640]{1,2,0:T(8,128)} fusion(f32[1,768,640]{1,2,0:T(8,128)} %copy.80, bf16[4,768,640]{1,2,0:T(8,128)(2,1)} %copy-done.3, s32[]{:T(128)S(6)} %select_n.241, bf16[320,640]{1,0:T(8,128)(2,1)S(1)} %copy-done.33, bf16[320,640]{1,0:T(8,128)(2,1)S(1)} %collective-permute-done.33), kind=kOutput, calls=%fused_computation.25 | convolution fusion | flops 631275520 | bytes 5734404 | tf_op jit(solution)/shard_map/dot_general | solution.py:184
  293.0 1.9 copy.81
  296.3 1.7 constant_dynamic-slice_fusion.1
  298.0 1.8 copy.82
  300.7 4.2 %fusion.6 = f32[1,768,640]{1,2,0:T(8,128)} fusion(f32[1,768,640]{1,2,0:T(8,128)} %copy.82, bf16[4,768,640]{1,2,0:T(8,128)(2,1)} %copy-done.3, s32[]{:T(128)S(6)} %select_n.243, bf16[320,640]{1,0:T(8,128)(2,1)} %collective-permute-done.34, bf16[320,640]{1,0:T(8,128)(2,1)S(1)} %copy-done.31), kind=kOutput, calls=%fused_computation.23 | convolution fusion | flops 631275520 | bytes 5734404 | tf_op jit(solution)/shard_map/dot_general | solution.py:184
  305.0 1.9 copy.83
  310.0 1.8 copy.84
  311.8 4.2 %fusion.5 = f32[1,768,640]{1,2,0:T(8,128)} fusion(f32[1,768,640]{1,2,0:T(8,128)} %copy.84, bf16[4,768,640]{1,2,0:T(8,128)(2,1)} %copy-done.3, s32[]{:T(128)S(6)} %select_n.245, bf16[320,640]{1,0:T(8,128)(2,1)S(1)} %copy-done.29, bf16[320,640]{1,0:T(8,128)(2,1)} %collective-permute-done.35), kind=kOutput, calls=%fused_computation.21 | convolution fusion | flops 631275520 | bytes 5734404 | tf_op jit(solution)/shard_map/dot_general | solution.py:184
  316.1 1.9 copy.85
  319.4 2.4 slice_bitcast_fusion.1
  323.4 5.7 %psum.23 = f32[768]{0:T(1024)S(1)} all-reduce(f32[768]{0:T(1024)S(1)} %multiply_reduce_fusion), channel_id=1, replica_groups=mesh['fsdp'=8,'tensor'=4] {'tensor'}, use_global_device_ids=true, to_apply=%region_9.10 | all-reduce | flops 768 | bytes 6144 | tf_op jit(solution)/shard_map/psum | solution.py:189
  329.1 3.6 %fusion.4 = bf16[768,1280]{1,0:T(8,128)(2,1)} fusion(f32[768,640]{1,0:T(8,128)} %copy-done.1, f32[768,640]{1,0:T(8,128)S(1)} %get-tuple-element.15, bf16[768,1280]{1,0:T(8,128)(2,1)} %param.13, f32[1280]{0:T(1024)S(1)} %copy-done.15, f32[768]{0:T(1024)S(1)} %add_rsqrt_fusion, pred[768]{0:T(1024)(128)(4,1)S(1)} %iota_compare_fusion.3), kind=kLoop, calls=%fused_computation.16 | loop fusion | flops 6881280 | bytes 7873280 | tf_op jit(solution)/shard_map/jit(_where)/select_n | solution.py:192
  (167 shorter events, 52.5 us)
Async XLA Ops:
  0.0 75.5 %copy-start.36 = (s32[8]{0:T(128)S(1)}, s32[8]{0:T(128)}, u32[]{:S(2)}) copy-start(s32[8]{0:T(128)} %constant.218.clone) | copy-start | bytes 100
  0.0 82.3 %copy-start.13 = (s32[8]{0:T(128)S(1)}, s32[8]{0:T(128)}, u32[]{:S(2)}) copy-start(s32[8]{0:T(128)} %constant.217.clone) | copy-start | bytes 100
  0.0 36.5 %copy-start.2 = (bf16[768,1280]{1,0:T(8,128)(2,1)S(1)}, bf16[768,1280]{1,0:T(8,128)(2,1)}, u32[]{:S(2)}) copy-start(bf16[768,1280]{1,0:T(8,128)(2,1)} %param.13) | copy-start | bytes 5898244
  0.0 75.5 %copy-start.14 = (s32[768]{0:T(1024)S(1)}, s32[768]{0:T(1024)}, u32[]{:S(2)}) copy-start(s32[768]{0:T(1024)} %param.15) | copy-start | bytes 9220
  0.0 46.2 %collective-permute-start.3 = (bf16[768,1280]{1,0:T(8,128)(2,1)}, bf16[768,1280]{1,0:T(8,128)(2,1)}, u32[]{:S(2)}, u32[]{:S(2)}) collective-permute-start(bf16[768,1280]{1,0:T(8,128)(2,1)} %param.13), channel_id=1, source_target_pairs={{0,2},{1,3},{2,0},{3,1},{4,6},{5,7},{6,4},{7,5},{8,10},{9,11},{10,... | collective-permute-start | bytes 5898248 | tf_op jit(solution)/shard_map/ppermute | solution.py:21
  6.3 14.5 %collective-permute-start.9 = (bf16[320,896]{1,0:T(8,128)(2,1)S(1)}, bf16[320,896]{1,0:T(8,128)(2,1)S(1)}, u32[]{:S(2)}, u32[]{:S(2)}) collective-permute-start(bf16[320,896]{1,0:T(8,128)(2,1)S(1)} %get-tuple-element.20), channel_id=1, source_target_pairs={{0,4},{1,5},{2,6},{3,7},{4,12},{5,13},{6,14},{7,15},{8,0},{9,1},{1... | collective-permute-start | bytes 1720328 | tf_op jit(solution)/shard_map/ppermute | solution.py:21
  7.8 14.4 %collective-permute-start.5 = (bf16[320,896]{1,0:T(8,128)(2,1)S(1)}, bf16[320,896]{1,0:T(8,128)(2,1)S(1)}, u32[]{:S(2)}, u32[]{:S(2)}) collective-permute-start(bf16[320,896]{1,0:T(8,128)(2,1)S(1)} %get-tuple-element.19), channel_id=1, source_target_pairs={{0,8},{1,9},{2,10},{3,11},{4,0},{5,1},{6,2},{7,3},{8,16},{9,17},{1... | collective-permute-start | bytes 1720328 | tf_op jit(solution)/shard_map/ppermute | solution.py:21
  20.8 15.1 %copy-start.7 = (bf16[320,896]{1,0:T(8,128)(2,1)}, bf16[320,896]{1,0:T(8,128)(2,1)S(1)}, u32[]{:S(2)}) copy-start(bf16[320,896]{1,0:T(8,128)(2,1)S(1)} %collective-permute-done.9) | copy-start | bytes 1720324
  20.8 13.6 %collective-permute-start.10 = (bf16[320,896]{1,0:T(8,128)(2,1)S(1)}, bf16[320,896]{1,0:T(8,128)(2,1)S(1)}, u32[]{:S(2)}, u32[]{:S(2)}) collective-permute-start(bf16[320,896]{1,0:T(8,128)(2,1)S(1)} %collective-permute-done.9), channel_id=1, source_target_pairs={{0,4},{1,5},{2,6},{3,7},{4,12},{5,13},{6,14},{7,15},{8,0},{9,1},{1... | collective-permute-start | bytes 1720328 | tf_op jit(solution)/shard_map/ppermute | solution.py:21
  22.3 48.6 %copy-start.18 = (bf16[320,896]{1,0:T(8,128)(2,1)}, bf16[320,896]{1,0:T(8,128)(2,1)S(1)}, u32[]{:S(2)}) copy-start(bf16[320,896]{1,0:T(8,128)(2,1)S(1)} %collective-permute-done.5) | copy-start | bytes 1720324
  22.3 13.6 %collective-permute-start.6 = (bf16[320,896]{1,0:T(8,128)(2,1)S(1)}, bf16[320,896]{1,0:T(8,128)(2,1)S(1)}, u32[]{:S(2)}, u32[]{:S(2)}) collective-permute-start(bf16[320,896]{1,0:T(8,128)(2,1)S(1)} %collective-permute-done.5), channel_id=1, source_target_pairs={{0,8},{1,9},{2,10},{3,11},{4,0},{5,1},{6,2},{7,3},{8,16},{9,17},{1... | collective-permute-start | bytes 1720328 | tf_op jit(solution)/shard_map/ppermute | solution.py:21
  34.4 36.4 %copy-start.20 = (bf16[320,896]{1,0:T(8,128)(2,1)}, bf16[320,896]{1,0:T(8,128)(2,1)S(1)}, u32[]{:S(2)}) copy-start(bf16[320,896]{1,0:T(8,128)(2,1)S(1)} %collective-permute-done.10) | copy-start | bytes 1720324
  34.4 19.7 %collective-permute-start.11 = (bf16[320,896]{1,0:T(8,128)(2,1)S(1)}, bf16[320,896]{1,0:T(8,128)(2,1)S(1)}, u32[]{:S(2)}, u32[]{:S(2)}) collective-permute-start(bf16[320,896]{1,0:T(8,128)(2,1)S(1)} %collective-permute-done.10), channel_id=1, source_target_pairs={{0,4},{1,5},{2,6},{3,7},{4,12},{5,13},{6,14},{7,15},{8,0},{9,1},{1... | collective-permute-start | bytes 1720328 | tf_op jit(solution)/shard_map/ppermute | solution.py:21
  35.9 34.9 %copy-start.22 = (bf16[320,896]{1,0:T(8,128)(2,1)}, bf16[320,896]{1,0:T(8,128)(2,1)S(1)}, u32[]{:S(2)}) copy-start(bf16[320,896]{1,0:T(8,128)(2,1)S(1)} %collective-permute-done.6) | copy-start | bytes 1720324
  35.9 19.9 %collective-permute-start.7 = (bf16[320,896]{1,0:T(8,128)(2,1)S(1)}, bf16[320,896]{1,0:T(8,128)(2,1)S(1)}, u32[]{:S(2)}, u32[]{:S(2)}) collective-permute-start(bf16[320,896]{1,0:T(8,128)(2,1)S(1)} %collective-permute-done.6), channel_id=1, source_target_pairs={{0,8},{1,9},{2,10},{3,11},{4,0},{5,1},{6,2},{7,3},{8,16},{9,17},{1... | collective-permute-start | bytes 1720328 | tf_op jit(solution)/shard_map/ppermute | solution.py:21
  36.5 99.0 %collective-permute-start.2 = (bf16[768,1280]{1,0:T(8,128)(2,1)S(1)}, bf16[768,1280]{1,0:T(8,128)(2,1)}, u32[]{:S(2)}, u32[]{:S(2)}) collective-permute-start(bf16[768,1280]{1,0:T(8,128)(2,1)S(1)} %copy-done.2), channel_id=1, source_target_pairs={{0,1},{1,0},{2,3},{3,2},{4,5},{5,4},{6,7},{7,6},{8,9},{9,8},{10,11... | collective-permute-start | bytes 5898248 | tf_op jit(solution)/shard_map/ppermute | solution.py:21
  46.2 89.3 %collective-permute-start.4 = (bf16[768,1280]{1,0:T(8,128)(2,1)}, bf16[768,1280]{1,0:T(8,128)(2,1)}, u32[]{:S(2)}, u32[]{:S(2)}) collective-permute-start(bf16[768,1280]{1,0:T(8,128)(2,1)} %collective-permute-done.3), channel_id=1, source_target_pairs={{0,1},{1,0},{2,3},{3,2},{4,5},{5,4},{6,7},{7,6},{8,9},{9,8},{10,11... | collective-permute-start | bytes 5898248 | tf_op jit(solution)/shard_map/ppermute | solution.py:21
  46.2 44.4 %collective-permute-start = (bf16[640,640]{1,0:T(8,128)(2,1)}, bf16[640,640]{1,0:T(8,128)(2,1)}, u32[]{:S(2)}, u32[]{:S(2)}) collective-permute-start(bf16[640,640]{1,0:T(8,128)(2,1)} %param.19), channel_id=1, source_target_pairs={{0,0},{1,17},{2,10},{3,27},{4,4},{5,21},{6,14},{7,31},{8,8},{9,25}... | collective-permute-start | bytes 2457608 | tf_op jit(solution)/shard_map/ppermute | solution.py:21
  54.1 16.7 %copy-start.24 = (bf16[320,896]{1,0:T(8,128)(2,1)}, bf16[320,896]{1,0:T(8,128)(2,1)S(1)}, u32[]{:S(2)}) copy-start(bf16[320,896]{1,0:T(8,128)(2,1)S(1)} %collective-permute-done.11) | copy-start | bytes 1720324
  54.1 15.8 %collective-permute-start.12 = (bf16[320,896]{1,0:T(8,128)(2,1)S(1)}, bf16[320,896]{1,0:T(8,128)(2,1)}, u32[]{:S(2)}, u32[]{:S(2)}) collective-permute-start(bf16[320,896]{1,0:T(8,128)(2,1)S(1)} %collective-permute-done.11), channel_id=1, source_target_pairs={{0,4},{1,5},{2,6},{3,7},{4,12},{5,13},{6,14},{7,15},{8,0},{9,1},{1... | collective-permute-start | bytes 1720328 | tf_op jit(solution)/shard_map/ppermute | solution.py:21
  55.8 15.0 %copy-start.26 = (bf16[320,896]{1,0:T(8,128)(2,1)}, bf16[320,896]{1,0:T(8,128)(2,1)S(1)}, u32[]{:S(2)}) copy-start(bf16[320,896]{1,0:T(8,128)(2,1)S(1)} %collective-permute-done.7) | copy-start | bytes 1720324
  55.8 15.0 %collective-permute-start.8 = (bf16[320,896]{1,0:T(8,128)(2,1)S(1)}, bf16[320,896]{1,0:T(8,128)(2,1)}, u32[]{:S(2)}, u32[]{:S(2)}) collective-permute-start(bf16[320,896]{1,0:T(8,128)(2,1)S(1)} %collective-permute-done.7), channel_id=1, source_target_pairs={{0,8},{1,9},{2,10},{3,11},{4,0},{5,1},{6,2},{7,3},{8,16},{9,17},{1... | collective-permute-start | bytes 1720328 | tf_op jit(solution)/shard_map/ppermute | solution.py:21
  69.9 41.9 %collective-permute-start.13 = (bf16[320,896]{1,0:T(8,128)(2,1)}, bf16[320,896]{1,0:T(8,128)(2,1)}, u32[]{:S(2)}, u32[]{:S(2)}) collective-permute-start(bf16[320,896]{1,0:T(8,128)(2,1)} %collective-permute-done.12), channel_id=1, source_target_pairs={{0,4},{1,5},{2,6},{3,7},{4,12},{5,13},{6,14},{7,15},{8,0},{9,1},{1... | collective-permute-start | bytes 1720328 | tf_op jit(solution)/shard_map/ppermute | solution.py:21
  70.9 41.4 %collective-permute-start.14 = (bf16[320,896]{1,0:T(8,128)(2,1)}, bf16[320,896]{1,0:T(8,128)(2,1)}, u32[]{:S(2)}, u32[]{:S(2)}) collective-permute-start(bf16[320,896]{1,0:T(8,128)(2,1)} %collective-permute-done.8), channel_id=1, source_target_pairs={{0,8},{1,9},{2,10},{3,11},{4,0},{5,1},{6,2},{7,3},{8,16},{9,17},{1... | collective-permute-start | bytes 1720328 | tf_op jit(solution)/shard_map/ppermute | solution.py:21
  90.6 31.9 %collective-permute-start.1 = (bf16[640,640]{1,0:T(8,128)(2,1)}, bf16[640,640]{1,0:T(8,128)(2,1)}, u32[]{:S(2)}, u32[]{:S(2)}) collective-permute-start(bf16[640,640]{1,0:T(8,128)(2,1)} %collective-permute-done), channel_id=1, source_target_pairs={{0,0},{1,2},{2,1},{3,3},{4,4},{5,6},{6,5},{7,7},{8,9},{9,11},{10,8... | collective-permute-start | bytes 2457608 | tf_op jit(solution)/shard_map/ppermute | solution.py:21
  111.8 21.5 %collective-permute-start.15 = (bf16[320,896]{1,0:T(8,128)(2,1)}, bf16[320,896]{1,0:T(8,128)(2,1)S(1)}, u32[]{:S(2)}, u32[]{:S(2)}) collective-permute-start(bf16[320,896]{1,0:T(8,128)(2,1)} %collective-permute-done.13), channel_id=1, source_target_pairs={{0,4},{1,5},{2,6},{3,7},{4,12},{5,13},{6,14},{7,15},{8,0},{9,1},{1... | collective-permute-start | bytes 1720328 | tf_op jit(solution)/shard_map/ppermute | solution.py:21
  112.3 22.9 %collective-permute-start.16 = (bf16[320,896]{1,0:T(8,128)(2,1)}, bf16[320,896]{1,0:T(8,128)(2,1)S(1)}, u32[]{:S(2)}, u32[]{:S(2)}) collective-permute-start(bf16[320,896]{1,0:T(8,128)(2,1)} %collective-permute-done.14), channel_id=1, source_target_pairs={{0,8},{1,9},{2,10},{3,11},{4,0},{5,1},{6,2},{7,3},{8,16},{9,17},{1... | collective-permute-start | bytes 1720328 | tf_op jit(solution)/shard_map/ppermute | solution.py:21
  133.3 18.9 %collective-permute-start.17 = (bf16[320,896]{1,0:T(8,128)(2,1)S(1)}, bf16[320,896]{1,0:T(8,128)(2,1)S(1)}, u32[]{:S(2)}, u32[]{:S(2)}) collective-permute-start(bf16[320,896]{1,0:T(8,128)(2,1)S(1)} %collective-permute-done.15), channel_id=1, source_target_pairs={{0,4},{1,5},{2,6},{3,7},{4,12},{5,13},{6,14},{7,15},{8,0},{9,1},{1... | collective-permute-start | bytes 1720328 | tf_op jit(solution)/shard_map/ppermute | solution.py:21
  135.2 19.9 %collective-permute-start.18 = (bf16[320,896]{1,0:T(8,128)(2,1)S(1)}, bf16[320,896]{1,0:T(8,128)(2,1)S(1)}, u32[]{:S(2)}, u32[]{:S(2)}) collective-permute-start(bf16[320,896]{1,0:T(8,128)(2,1)S(1)} %collective-permute-done.16), channel_id=1, source_target_pairs={{0,8},{1,9},{2,10},{3,11},{4,0},{5,1},{6,2},{7,3},{8,16},{9,17},{1... | collective-permute-start | bytes 1720328 | tf_op jit(solution)/shard_map/ppermute | solution.py:21
  139.2 2.6 copy-start.27
  141.9 2.4 copy-start.25
  144.3 2.4 copy-start.23
  149.4 2.8 copy-start.19
  152.2 2.8 copy-start.8
  159.7 8.7 %copy-start.17 = (f32[128]{0:T(128)S(1)}, f32[128]{0:T(128)}, u32[]{:S(2)}) copy-start(f32[128]{0:T(128)} %param.21) | copy-start | bytes 1540
  159.7 10.2 %copy-start.16 = (f32[640]{0:T(1024)S(1)}, f32[640]{0:T(1024)}, u32[]{:S(2)}) copy-start(f32[640]{0:T(1024)} %param.20) | copy-start | bytes 7684
  174.9 2.2 copy-start.6
  184.1 3.1 copy-start.10
  184.1 36.8 %copy-start.12 = (s32[4]{0:T(128)S(1)}, s32[4]{0:T(128)}, u32[]{:S(2)}) copy-start(s32[4]{0:T(128)} %constant.219.clone) | copy-start | bytes 52
  184.3 22.2 %collective-permute-start.20 = (bf16[768,640]{0,1:T(8,128)(2,1)S(1)}, bf16[768,640]{0,1:T(8,128)(2,1)S(1)}, u32[]{:S(2)}, u32[]{:S(2)}) collective-permute-start(bf16[768,640]{0,1:T(8,128)(2,1)S(1)} %get-tuple-element.22), channel_id=1, source_target_pairs={{0,2},{1,3},{2,0},{3,1},{4,6},{5,7},{6,4},{7,5},{8,10},{9,11},{10,... | collective-permute-start | bytes 2949128 | tf_op jit(solution)/shard_map/ppermute | solution.py:21
  185.1 10.5 %collective-permute-start.26 = (bf16[320,640]{1,0:T(8,128)(2,1)S(1)}, bf16[320,640]{1,0:T(8,128)(2,1)S(1)}, u32[]{:S(2)}, u32[]{:S(2)}) collective-permute-start(bf16[320,640]{1,0:T(8,128)(2,1)S(1)} %copy-done.9), channel_id=1, source_target_pairs={{0,4},{1,5},{2,6},{3,7},{4,12},{5,13},{6,14},{7,15},{8,0},{9,1},{1... | collective-permute-start | bytes 1228808 | tf_op jit(solution)/shard_map/ppermute | solution.py:21
  187.2 10.4 %collective-permute-start.22 = (bf16[320,640]{1,0:T(8,128)(2,1)S(1)}, bf16[320,640]{1,0:T(8,128)(2,1)S(1)}, u32[]{:S(2)}, u32[]{:S(2)}) collective-permute-start(bf16[320,640]{1,0:T(8,128)(2,1)S(1)} %copy-done.10), channel_id=1, source_target_pairs={{0,8},{1,9},{2,10},{3,11},{4,0},{5,1},{6,2},{7,3},{8,16},{9,17},{1... | collective-permute-start | bytes 1228808 | tf_op jit(solution)/shard_map/ppermute | solution.py:21
  195.6 10.9 %copy-start.28 = (bf16[320,640]{1,0:T(8,128)(2,1)}, bf16[320,640]{1,0:T(8,128)(2,1)S(1)}, u32[]{:S(2)}) copy-start(bf16[320,640]{1,0:T(8,128)(2,1)S(1)} %collective-permute-done.26) | copy-start | bytes 1228804
  195.6 10.9 %collective-permute-start.27 = (bf16[320,640]{1,0:T(8,128)(2,1)S(1)}, bf16[320,640]{1,0:T(8,128)(2,1)S(1)}, u32[]{:S(2)}, u32[]{:S(2)}) collective-permute-start(bf16[320,640]{1,0:T(8,128)(2,1)S(1)} %collective-permute-done.26), channel_id=1, source_target_pairs={{0,4},{1,5},{2,6},{3,7},{4,12},{5,13},{6,14},{7,15},{8,0},{9,1},{1... | collective-permute-start | bytes 1228808 | tf_op jit(solution)/shard_map/ppermute | solution.py:21
  197.6 8.9 %copy-start.30 = (bf16[320,640]{1,0:T(8,128)(2,1)}, bf16[320,640]{1,0:T(8,128)(2,1)S(1)}, u32[]{:S(2)}) copy-start(bf16[320,640]{1,0:T(8,128)(2,1)S(1)} %collective-permute-done.22) | copy-start | bytes 1228804
  197.6 10.9 %collective-permute-start.23 = (bf16[320,640]{1,0:T(8,128)(2,1)S(1)}, bf16[320,640]{1,0:T(8,128)(2,1)S(1)}, u32[]{:S(2)}, u32[]{:S(2)}) collective-permute-start(bf16[320,640]{1,0:T(8,128)(2,1)S(1)} %collective-permute-done.22), channel_id=1, source_target_pairs={{0,8},{1,9},{2,10},{3,11},{4,0},{5,1},{6,2},{7,3},{8,16},{9,17},{1... | collective-permute-start | bytes 1228808 | tf_op jit(solution)/shard_map/ppermute | solution.py:21
  197.6 35.4 %collective-permute-start.19 = (bf16[768,640]{0,1:T(8,128)(2,1)S(1)}, bf16[768,640]{0,1:T(8,128)(2,1)}, u32[]{:S(2)}, u32[]{:S(2)}) collective-permute-start(bf16[768,640]{0,1:T(8,128)(2,1)S(1)} %get-tuple-element.22), channel_id=1, source_target_pairs={{0,1},{1,0},{2,3},{3,2},{4,5},{5,4},{6,7},{7,6},{8,9},{9,8},{10,11... | collective-permute-start | bytes 2949128 | tf_op jit(solution)/shard_map/ppermute | solution.py:21
  206.5 26.6 %collective-permute-start.21 = (bf16[768,640]{0,1:T(8,128)(2,1)S(1)}, bf16[768,640]{0,1:T(8,128)(2,1)}, u32[]{:S(2)}, u32[]{:S(2)}) collective-permute-start(bf16[768,640]{0,1:T(8,128)(2,1)S(1)} %collective-permute-done.20), channel_id=1, source_target_pairs={{0,1},{1,0},{2,3},{3,2},{4,5},{5,4},{6,7},{7,6},{8,9},{9,8},{10,11... | collective-permute-start | bytes 2949128 | tf_op jit(solution)/shard_map/ppermute | solution.py:21
  206.5 12.0 %collective-permute-start.28 = (bf16[320,640]{1,0:T(8,128)(2,1)S(1)}, bf16[320,640]{1,0:T(8,128)(2,1)}, u32[]{:S(2)}, u32[]{:S(2)}) collective-permute-start(bf16[320,640]{1,0:T(8,128)(2,1)S(1)} %collective-permute-done.27), channel_id=1, source_target_pairs={{0,4},{1,5},{2,6},{3,7},{4,12},{5,13},{6,14},{7,15},{8,0},{9,1},{1... | collective-permute-start | bytes 1228808 | tf_op jit(solution)/shard_map/ppermute | solution.py:21
  208.6 10.0 %copy-start.34 = (bf16[320,640]{1,0:T(8,128)(2,1)}, bf16[320,640]{1,0:T(8,128)(2,1)S(1)}, u32[]{:S(2)}) copy-start(bf16[320,640]{1,0:T(8,128)(2,1)S(1)} %collective-permute-done.23) | copy-start | bytes 1228804
  208.6 12.0 %collective-permute-start.24 = (bf16[320,640]{1,0:T(8,128)(2,1)S(1)}, bf16[320,640]{1,0:T(8,128)(2,1)}, u32[]{:S(2)}, u32[]{:S(2)}) collective-permute-start(bf16[320,640]{1,0:T(8,128)(2,1)S(1)} %collective-permute-done.23), channel_id=1, source_target_pairs={{0,8},{1,9},{2,10},{3,11},{4,0},{5,1},{6,2},{7,3},{8,16},{9,17},{1... | collective-permute-start | bytes 1228808 | tf_op jit(solution)/shard_map/ppermute | solution.py:21
  218.5 12.1 %collective-permute-start.29 = (bf16[320,640]{1,0:T(8,128)(2,1)}, bf16[320,640]{1,0:T(8,128)(2,1)}, u32[]{:S(2)}, u32[]{:S(2)}) collective-permute-start(bf16[320,640]{1,0:T(8,128)(2,1)} %collective-permute-done.28), channel_id=1, source_target_pairs={{0,4},{1,5},{2,6},{3,7},{4,12},{5,13},{6,14},{7,15},{8,0},{9,1},{1... | collective-permute-start | bytes 1228808 | tf_op jit(solution)/shard_map/ppermute | solution.py:21
  220.5 11.4 %collective-permute-start.25 = (bf16[320,640]{1,0:T(8,128)(2,1)}, bf16[320,640]{1,0:T(8,128)(2,1)}, u32[]{:S(2)}, u32[]{:S(2)}) collective-permute-start(bf16[320,640]{1,0:T(8,128)(2,1)} %collective-permute-done.24), channel_id=1, source_target_pairs={{0,8},{1,9},{2,10},{3,11},{4,0},{5,1},{6,2},{7,3},{8,16},{9,17},{1... | collective-permute-start | bytes 1228808 | tf_op jit(solution)/shard_map/ppermute | solution.py:21
  230.6 21.6 %collective-permute-start.30 = (bf16[320,640]{1,0:T(8,128)(2,1)}, bf16[320,640]{1,0:T(8,128)(2,1)}, u32[]{:S(2)}, u32[]{:S(2)}) collective-permute-start(bf16[320,640]{1,0:T(8,128)(2,1)} %collective-permute-done.29), channel_id=1, source_target_pairs={{0,4},{1,5},{2,6},{3,7},{4,12},{5,13},{6,14},{7,15},{8,0},{9,1},{1... | collective-permute-start | bytes 1228808 | tf_op jit(solution)/shard_map/ppermute | solution.py:21
  231.9 32.8 %collective-permute-start.31 = (bf16[320,640]{1,0:T(8,128)(2,1)}, bf16[320,640]{1,0:T(8,128)(2,1)}, u32[]{:S(2)}, u32[]{:S(2)}) collective-permute-start(bf16[320,640]{1,0:T(8,128)(2,1)} %collective-permute-done.25), channel_id=1, source_target_pairs={{0,8},{1,9},{2,10},{3,11},{4,0},{5,1},{6,2},{7,3},{8,16},{9,17},{1... | collective-permute-start | bytes 1228808 | tf_op jit(solution)/shard_map/ppermute | solution.py:21
  234.8 2.4 copy-start.3
  263.4 13.2 %collective-permute-start.32 = (bf16[320,640]{1,0:T(8,128)(2,1)}, bf16[320,640]{1,0:T(8,128)(2,1)S(1)}, u32[]{:S(2)}, u32[]{:S(2)}) collective-permute-start(bf16[320,640]{1,0:T(8,128)(2,1)} %collective-permute-done.30), channel_id=1, source_target_pairs={{0,4},{1,5},{2,6},{3,7},{4,12},{5,13},{6,14},{7,15},{8,0},{9,1},{1... | collective-permute-start | bytes 1228808 | tf_op jit(solution)/shard_map/ppermute | solution.py:21
  274.1 2.6 copy-start.35
  275.9 13.0 %collective-permute-start.33 = (bf16[320,640]{1,0:T(8,128)(2,1)}, bf16[320,640]{1,0:T(8,128)(2,1)S(1)}, u32[]{:S(2)}, u32[]{:S(2)}) collective-permute-start(bf16[320,640]{1,0:T(8,128)(2,1)} %collective-permute-done.31), channel_id=1, source_target_pairs={{0,8},{1,9},{2,10},{3,11},{4,0},{5,1},{6,2},{7,3},{8,16},{9,17},{1... | collective-permute-start | bytes 1228808 | tf_op jit(solution)/shard_map/ppermute | solution.py:21
  285.8 3.0 copy-start.33
  287.6 13.1 %collective-permute-start.34 = (bf16[320,640]{1,0:T(8,128)(2,1)S(1)}, bf16[320,640]{1,0:T(8,128)(2,1)}, u32[]{:S(2)}, u32[]{:S(2)}) collective-permute-start(bf16[320,640]{1,0:T(8,128)(2,1)S(1)} %collective-permute-done.32), channel_id=1, source_target_pairs={{0,4},{1,5},{2,6},{3,7},{4,12},{5,13},{6,14},{7,15},{8,0},{9,1},{1... | collective-permute-start | bytes 1228808 | tf_op jit(solution)/shard_map/ppermute | solution.py:21
  298.0 2.7 copy-start.31
  299.8 12.0 %collective-permute-start.35 = (bf16[320,640]{1,0:T(8,128)(2,1)S(1)}, bf16[320,640]{1,0:T(8,128)(2,1)}, u32[]{:S(2)}, u32[]{:S(2)}) collective-permute-start(bf16[320,640]{1,0:T(8,128)(2,1)S(1)} %collective-permute-done.33), channel_id=1, source_target_pairs={{0,8},{1,9},{2,10},{3,11},{4,0},{5,1},{6,2},{7,3},{8,16},{9,17},{1... | collective-permute-start | bytes 1228808 | tf_op jit(solution)/shard_map/ppermute | solution.py:21
  321.8 7.3 %copy-start.15 = (f32[1280]{0:T(1024)S(1)}, f32[1280]{0:T(1024)}, u32[]{:S(2)}) copy-start(f32[1280]{0:T(1024)} %param.22) | copy-start | bytes 15364
  (9 other events, 13.8 us)

commit v2 on v1

v2 whole, which is shorter than its diff:
```python
import math

import jax
import jax.numpy as jnp
from jax import lax
from jax.experimental import pallas as pl
from jax.experimental.pallas import tpu as pltpu
from jax.sharding import PartitionSpec as P

HEAD_DIM = 128
EPS = 1e-06
ROPE_BASE = 500000.0
AXES = ("fsdp", "tensor")


def permute(array, mesh_sizes, target):
    n, tensor_size = mesh_sizes
    pairs = []
    for f in range(n):
        for t in range(tensor_size):
            to_f, to_t = target(f, t)
            pairs.append((f * tensor_size + t, to_f * tensor_size + to_t))
    return lax.ppermute(array, AXES, pairs)


def reverse_bits(value, size):
    result = 0
    while size > 1:
        result = result * 2 + value % 2
        value //= 2
        size //= 2
    return result


def snake(n):
    return list(range(0, n, 2)) + list(range(n - 1, 0, -2))


def gather_tensor(array, sizes):
    have = {0: array}
    bit = sizes[1] // 2
    while bit:
        for r in sorted(have):
            have[r ^ bit] = permute(have[r], sizes, lambda f, t, bit=bit: (f, t ^ bit))
        bit //= 2
    return [have[r] for r in range(sizes[1])]


def ring_gather(top, bottom, sizes):
    n = sizes[0]
    order = snake(n)
    place = {f: i for i, f in enumerate(order)}
    tops, bottoms = [top], [bottom]
    for _ in range(n - 1):
        tops.append(permute(tops[-1], sizes, lambda f, t: (order[(place[f] + 1) % n], t)))
        bottoms.append(permute(bottoms[-1], sizes, lambda f, t: (order[(place[f] - 1) % n], t)))
    return tops, bottoms


def block_product(sizes, sources, choices, tops, bottoms, accumulated, columns, with_squares):
    rows, source_width = sources[0].shape
    half, width = tops[0].shape
    depth = 2 * half
    count = len(tops)
    if depth % 128 or width % 128:
        stack = jnp.stack(sources)
        total = jnp.zeros((rows, columns), jnp.float32) if accumulated is None else accumulated
        for j in range(count):
            piece = lax.dynamic_slice(
                stack, (choices[3 * j], 0, choices[3 * j + 1]), (1, rows, depth)
            )[0]
            matrix = jnp.concatenate([tops[j], bottoms[j]], axis=0)
            term = jnp.dot(piece, matrix, preferred_element_type=jnp.float32)
            current = lax.dynamic_slice(total, (0, choices[3 * j + 2]), (rows, width))
            total = lax.dynamic_update_slice(total, current + term, (0, choices[3 * j + 2]))
        if not with_squares:
            return total
        squares = jnp.sum(total * total, axis=1)
        return total, jnp.broadcast_to(squares[None, :], (8, rows))

    tile = 256 if rows % 256 == 0 else rows
    extra = 0 if accumulated is None else 1
    whole = width == columns

    def kernel(*refs):
        choice = refs[0]
        source = refs[1 : 1 + len(sources)]
        top = refs[1 + len(sources) : 1 + len(sources) + count]
        bottom = refs[1 + len(sources) + count : 1 + len(sources) + 2 * count]
        rest = refs[1 + len(sources) + 2 * count :]
        start = rest[0] if extra else None
        out = rest[extra]
        squares = rest[extra + 1] if with_squares else None
        piece, matrix, sems = rest[-3:]

        def piece_copy(j, which):
            first = pl.multiple_of(choice[3 * j + 1], 128)
            return pltpu.make_async_copy(
                source[which].at[:, pl.ds(first, depth)],
                piece.at[:, pl.ds(j * depth, depth)],
                sems.at[j, 0],
            )

        def matrix_copies(j):
            return (
                pltpu.make_async_copy(top[j], matrix.at[pl.ds(j * depth, half)], sems.at[j, 1]),
                pltpu.make_async_copy(
                    bottom[j], matrix.at[pl.ds(j * depth + half, half)], sems.at[j, 2]
                ),
            )

        for j in range(count):
            for which in range(len(sources)):

                @pl.when(choice[3 * j] == which)
                def _(j=j, which=which):
                    piece_copy(j, which).start()

            for copy in matrix_copies(j):
                copy.start()
        for j in range(count):
            piece_copy(j, 0).wait()
            for copy in matrix_copies(j):
                copy.wait()
        if not whole:
            out[...] = start[...] if extra else jnp.zeros_like(out)
        for lower in range(0, rows, tile):
            part = pl.ds(lower, tile)
            if whole:
                term = jnp.dot(piece[part, :], matrix[...], preferred_element_type=jnp.float32)
                out[part, :] = start[part, :] + term if extra else term
            else:
                for j in range(count):
                    term = jnp.dot(
                        piece[part, pl.ds(j * depth, depth)],
                        matrix[pl.ds(j * depth, depth), :],
                        preferred_element_type=jnp.float32,
                    )
                    span = pl.ds(pl.multiple_of(choice[3 * j + 2], 128), width)
                    out[part, span] += term
            if with_squares:
                total = out[part, :]
                sums = jnp.sum(total * total, axis=1, keepdims=True)
                squares[:, part] = jnp.broadcast_to(sums, (tile, 128)).T[:8]

    any_space = pl.BlockSpec(memory_space=pl.ANY)
    in_vmem = pl.BlockSpec(memory_space=pltpu.VMEM)
    out_shape = [jax.ShapeDtypeStruct((rows, columns), jnp.float32)]
    if with_squares:
        out_shape.append(jax.ShapeDtypeStruct((8, rows), jnp.float32))
    operands = [jnp.stack(choices).astype(jnp.int32), *sources, *tops, *bottoms]
    specs = [pl.BlockSpec(memory_space=pltpu.SMEM)] + [any_space] * (len(operands) - 1)
    if extra:
        operands.append(accumulated)
        specs.append(in_vmem)
    results = pl.pallas_call(
        kernel,
        out_shape=out_shape,
        in_specs=specs,
        out_specs=[in_vmem] * len(out_shape),
        scratch_shapes=[
            pltpu.VMEM((rows, count * depth), sources[0].dtype),
            pltpu.VMEM((count * depth, width), tops[0].dtype),
            pltpu.SemaphoreType.DMA((count, 3)),
        ],
        compiler_params=pltpu.CompilerParams(vmem_limit_bytes=40 * 2**20),
        cost_estimate=pl.CostEstimate(
            flops=2 * rows * count * depth * width,
            bytes_accessed=2 * count * depth * (rows + width) + 8 * rows * columns,
            transcendentals=0,
        ),
    )(*operands)
    return tuple(results) if with_squares else results[0]


def attention(total, sums, cosine, sine, starts, query_gain, key_gain, tensor_size, half_rows):
    capacity = total.shape[0]
    q_width, k_width = query_gain.shape[1], key_gain.shape[1]
    heads, kv_heads = q_width // HEAD_DIM, k_width // HEAD_DIM
    group = heads // kv_heads
    block = 128

    def kernel(*refs):
        total_ref, sum_refs = refs[0], refs[1 : 1 + len(sums)]
        cosine_ref, sine_ref, starts_ref, q_gain_ref, k_gain_ref, out_ref = refs[1 + len(sums) :]
        offset = pl.program_id(0) * half_rows
        squares = sum_refs[0][...]
        for other in sum_refs[1:]:
            squares = squares + other[...]
        q_scale = lax.rsqrt(squares[0:1] / (q_width * tensor_size) + EPS)
        k_scale = lax.rsqrt(squares[1:2] / (k_width * tensor_size) + EPS)
        q_scale = jnp.broadcast_to(q_scale, (HEAD_DIM, half_rows)).T
        k_scale = jnp.broadcast_to(k_scale, (HEAD_DIM, half_rows)).T
        cosines, sines = cosine_ref[...], sine_ref[...]

        def rotated(lower, scale, gain):
            field = total_ref[:, lower : lower + HEAD_DIM] * scale * gain
            return (
                field * cosines + pltpu.roll(field, HEAD_DIM // 2, 1) * sines
            ).astype(jnp.bfloat16)

        for g in range(kv_heads):
            low = g * HEAD_DIM
            keys = rotated(q_width + low, k_scale, k_gain_ref[:, low : low + HEAD_DIM])
            values = total_ref[:, q_width + k_width + low : q_width + k_width + low + HEAD_DIM]
            values = values.astype(jnp.bfloat16)
            queries = []
            for h in range(g * group, (g + 1) * group):
                span = slice(h * HEAD_DIM, (h + 1) * HEAD_DIM)
                queries.append(rotated(h * HEAD_DIM, q_scale, q_gain_ref[:, span]))
            for i in range(half_rows // block):
                lower, reach = i * block, (i + 1) * block
                stacked = jnp.concatenate([q[lower:reach] for q in queries], axis=0)
                scores = lax.dot_general(
                    stacked,
                    keys[:reach],
                    (((1,), (1,)), ((), ())),
                    preferred_element_type=jnp.float32,
                ) * (1.0 / math.sqrt(HEAD_DIM))
                first = starts_ref[lower:reach, :] - offset
                lanes = lax.broadcasted_iota(jnp.int32, (block, block), 1)
                row = lax.broadcasted_iota(jnp.int32, (block, block), 0)
                allowed = jnp.concatenate(
                    [lanes + c * block >= first for c in range(i)]
                    + [(lanes + lower >= first) & (lanes <= row)],
                    axis=1,
                )
                scores = scores.reshape(group, block, reach)
                scores = jnp.where(allowed[None], scores, jnp.float32(-1e30))
                peak = jnp.max(scores, axis=-1, keepdims=True)
                expo = jnp.exp(scores - peak)
                probs = expo / jnp.sum(expo, axis=-1, keepdims=True)
                probs = probs.astype(jnp.bfloat16).reshape(group * block, reach)
                mixed = jnp.dot(probs, values[:reach], preferred_element_type=jnp.float32)
                mixed = mixed.astype(jnp.bfloat16)
                for h in range(group):
                    column = (g * group + h) * HEAD_DIM
                    out_ref[lower:reach, column : column + HEAD_DIM] = mixed[
                        h * block : (h + 1) * block
                    ]

    def by_rows(width):
        return pl.BlockSpec((half_rows, width), lambda i: (i, 0))

    def constant(width):
        return pl.BlockSpec((1, width), lambda i: (0, 0))

    return pl.pallas_call(
        kernel,
        grid=(capacity // half_rows,),
        out_shape=jax.ShapeDtypeStruct((capacity, q_width), jnp.bfloat16),
        in_specs=[by_rows(total.shape[1])]
        + [pl.BlockSpec((8, half_rows), lambda i: (0, i))] * len(sums)
        + [by_rows(HEAD_DIM)] * 3
        + [constant(q_width), constant(k_width)],
        out_specs=by_rows(q_width),
        compiler_params=pltpu.CompilerParams(vmem_limit_bytes=40 * 2**20),
        cost_estimate=pl.CostEstimate(
            flops=4 * capacity * half_rows * q_width,
            bytes_accessed=8 * capacity * total.shape[1],
            transcendentals=capacity * half_rows * heads,
        ),
    )(total, *sums, cosine, sine, starts, query_gain, key_gain)


def finish(attn_out, sums, tokens, out_gain, live_rows, features):
    rows, width = tokens.shape
    tile = 256 if rows % 256 == 0 else rows

    def kernel(*refs):
        live_ref, attn_ref, sum_refs = refs[0], refs[1], refs[2 : 2 + len(sums)]
        tokens_ref, gain_ref, out_ref = refs[2 + len(sums) :]
        squares = sum_refs[0][...]
        for other in sum_refs[1:]:
            squares = squares + other[...]
        scale = lax.rsqrt(squares[0:1] / features + EPS)
        scale = jnp.broadcast_to(scale, (128, tile)).T
        row = pl.program_id(0) * tile + lax.broadcasted_iota(jnp.int32, (tile, 128), 0)
        live = row < live_ref[0]
        for lower in range(0, width, 128):
            span = slice(lower, lower + 128)
            value = tokens_ref[:, span].astype(jnp.float32) + attn_ref[:, span] * scale * gain_ref[:, span]
            out_ref[:, span] = jnp.where(live, value, 0.0).astype(jnp.bfloat16)

    return pl.pallas_call(
        kernel,
        grid=(rows // tile,),
        out_shape=jax.ShapeDtypeStruct((rows, width), jnp.bfloat16),
        in_specs=[
            pl.BlockSpec(memory_space=pltpu.SMEM),
            pl.BlockSpec((tile, width), lambda i: (i, 0)),
        ]
        + [pl.BlockSpec((8, tile), lambda i: (0, i))] * len(sums)
        + [
            pl.BlockSpec((tile, width), lambda i: (i, 0)),
            pl.BlockSpec((1, width), lambda i: (0, 0)),
        ],
        out_specs=pl.BlockSpec((tile, width), lambda i: (i, 0)),
        compiler_params=pltpu.CompilerParams(vmem_limit_bytes=32 * 2**20),
    )(live_rows, attn_out, *sums, tokens, out_gain)


def body(
    sizes, tokens, live_rows, first_row, w_query, w_key, w_value, w_out, query_gain, key_gain, out_gain
):
    n, tensor_size = sizes
    capacity, width = tokens.shape
    half_rows = capacity // 2
    per_tensor = n // tensor_size
    f_index = lax.axis_index("fsdp")
    t_index = lax.axis_index("tensor")
    order = snake(n)
    place = [order.index(f) for f in range(n)]
    order_of = jnp.array(order, jnp.int32)
    position = jnp.array(place, jnp.int32)[f_index]

    weights = jnp.concatenate([w_query, w_key, w_value], axis=1)
    depth = weights.shape[0]
    half = depth // 2
    token_blocks = gather_tensor(tokens, sizes)
    tops, bottoms = ring_gather(weights[:half], weights[half:], sizes)

    moved = permute(
        w_out,
        sizes,
        lambda f, t: (
            ((f // per_tensor) ^ reverse_bits(t, tensor_size)) * per_tensor + f % per_tensor,
            t,
        ),
    )
    moved = permute(
        moved, sizes, lambda f, t: (f, (f // per_tensor) ^ reverse_bits(t, tensor_size))
    )

    q_width, k_width = w_query.shape[1], w_key.shape[1]
    columns = weights.shape[1]
    steps = [[0, n // 2]] + [[s, n - s] for s in range(n // 2 + 1, n)]
    early = [offset for group in steps[: len(steps) // 2] for offset in group]
    late = [offset for group in steps[len(steps) // 2 :] for offset in group]

    def source_blocks(offsets):
        return [order_of[lax.rem(position + offset, n)] for offset in offsets]

    total = None
    for offsets in (early, late):
        choices = []
        for block in source_blocks(offsets):
            choices += [
                (block // per_tensor) ^ t_index,
                lax.rem(block, per_tensor) * depth,
                jnp.int32(0),
            ]
        total = block_product(
            sizes,
            token_blocks,
            choices,
            [tops[(n - offset) % n] for offset in offsets],
            [bottoms[offset] for offset in offsets],
            total,
            columns,
            False,
        )

    out_half = w_out.shape[0] // 2
    out_top, out_bottom, _ = lax.optimization_barrier(
        (moved[:out_half], moved[out_half:], (tops[-1], bottoms[-1]))
    )
    out_tops, out_bottoms = ring_gather(out_top, out_bottom, sizes)

    query = total[:, :q_width]
    key = total[:, q_width : q_width + k_width]
    squares = jnp.stack([jnp.sum(query * query, axis=1), jnp.sum(key * key, axis=1)])
    squares = jnp.concatenate([squares, jnp.zeros((6, capacity), jnp.float32)])
    square_blocks = gather_tensor(squares, sizes)
    row_ids = jnp.arange(capacity, dtype=jnp.int32)
    positions = (row_ids - first_row).astype(jnp.float32)
    half_dim = HEAD_DIM // 2
    freqs = jnp.power(
        ROPE_BASE, -(jnp.arange(half_dim, dtype=jnp.float32) * 2.0 / HEAD_DIM)
    )
    angle = positions[:, None] * freqs[None, :]
    cosine, sine = jnp.cos(angle), jnp.sin(angle)
    attended = attention(
        total,
        square_blocks,
        jnp.concatenate([cosine, cosine], axis=1),
        jnp.concatenate([-sine, sine], axis=1),
        jnp.broadcast_to(first_row[:, None], (capacity, HEAD_DIM)),
        query_gain[None, :],
        key_gain[None, :],
        tensor_size,
        half_rows,
    )
    attended_blocks = gather_tensor(attended, sizes)

    reversed_of = jnp.array(
        [reverse_bits(t, tensor_size) for t in range(tensor_size)], jnp.int32
    )
    attn_out = None
    for offsets in (early, late):
        choices = []
        for block in source_blocks(offsets):
            choices += [
                reversed_of[(block // per_tensor) ^ t_index] ^ t_index,
                jnp.int32(0),
                lax.rem(block, per_tensor) * w_out.shape[1],
            ]
        attn_out = block_product(
            sizes,
            attended_blocks,
            choices,
            [out_tops[(n - offset) % n] for offset in offsets],
            [out_bottoms[offset] for offset in offsets],
            attn_out,
            width,
            offsets is late,
        )
    attn_out, out_squares = attn_out
    return finish(
        attn_out,
        gather_tensor(out_squares, sizes),
        tokens,
        out_gain[None, :],
        live_rows,
        width * tensor_size,
    )


def solution(mesh):
    sizes = (mesh.shape["fsdp"], mesh.shape["tensor"])

    def run(*arrays):
        return body(sizes, *arrays)

    in_specs = (
        P("fsdp", "tensor"),
        P("fsdp"),
        P("fsdp"),
        P("fsdp", "tensor"),
        P("fsdp", "tensor"),
        P("fsdp", "tensor"),
        P("tensor", "fsdp"),
        P("tensor"),
        P("tensor"),
        P("tensor"),
    )
    return jax.shard_map(
        run, mesh=mesh, in_specs=in_specs, out_specs=P("fsdp", "tensor"), check_vma=False
    )
```

time: 339 us -> 248 us (0.73); the launches traced: 333 us -> 246 us
  matrix products: 56.6 us -> 0 us
  Pallas kernels: 0 us -> 42 us
  local copies, waits for them, and re-layouts: 65.6 us -> 31 us
  other arithmetic: 19.4 us -> 4.87 us
  blocking collectives: 13.1 us -> 0 us
  waiting for transfers between devices: 86.7 us -> 76.8 us
    dot_general x20 -> x0, matrix products: 56.6 us -> none  [the longest x16 50.9 us: body(): term = jnp.dot(piece, matrix, preferred_element_type=jnp.float32)]
    pallas_call x0 -> x6, Pallas kernels: none -> 42 us  [the longest x4 35.2 us: block_product(): pl.pallas_call(kernel, out_shape=out_shape, in_specs=specs, out_specs=[in...]
    dynamic_slice x16 -> x2, local copies, waits for them, and re-layouts: 24 us -> 1.37 us  [the longest x1 0.7 us: source_blocks(): return [order_of[lax.rem(position + offset, n)] for offset in offsets]]
    unnamed x78 -> x100, local copies, waits for them, and re-layouts: 10.6 us -> 26.1 us
    broadcast_in_dim x8 -> x4, local copies, waits for them, and re-layouts: 13.4 us -> 0.16 us  [the longest x1 0.15 us: body(): jnp.broadcast_to(first_row[:, None], (capacity, HEAD_DIM))]
    psum x2 -> x0, blocking collectives: 13.1 us -> none  [the longest x1 7.39 us: body(): lax.psum((jnp.sum(query * query, axis=1), jnp.sum(key * key, axis=1)), 't...]
    another operation x6 -> x0, other arithmetic: 10.4 us -> none
    dynamic_update_slice x7 -> x0, local copies, waits for them, and re-layouts: 10.4 us -> none  [body(): result = lax.dynamic_update_index_in_dim(result, current + term, column, 0)]
  transfers between devices with their start and end apart: 36 -> 42, of which waited for: 10 -> 16; matrix products, arithmetic and copies ran while one was open for 30% -> 5% of each run, Pallas kernels for 0% -> 13%
where the time goes in v2:
time: 248 us; the launch traced here: 246 us
  waiting for transfers between devices  76.8 us (31%)
  starting transfers between devices  58.1 us (23%)
  Pallas kernels  42 us (17%)
  between operations  33 us (13%)
  local copies, waits for them, and re-layouts  31 us (12%)
  other arithmetic  4.87 us (2%)
    ppermute x42, waiting for transfers between devices, permute(): return lax.ppermute(array, AXES, pairs)  76.8 us
    ppermute x42, starting transfers between devices, permute(): return lax.ppermute(array, AXES, pairs)  58.1 us
    pallas_call x4, Pallas kernels, block_product(): pl.pallas_call(kernel, out_shape=out_shape, in_specs=specs, out_specs=[in...  35.2 us
    unnamed x100, local copies, waits for them, and re-layouts  26.1 us
  transfers between devices with their start and end apart: 42, of which 16 were waited for; matrix products, arithmetic and copies ran while one was open for 5% of the time, Pallas kernels for 13%

profile of v2, /device:TPU:0, one launch (start us, length us, event | category | flops | bytes accessed | tf_op | source)
XLA Modules:
  0.0 245.8 jit_solution(17098424554091111298)
XLA Ops:
  0.0 3.0 %collective-permute-start.1 = (bf16[768,1280]{1,0:T(8,128)(2,1)}, bf16[768,1280]{1,0:T(8,128)(2,1)}, u32[]{:S(2)}, u32[]{:S(2)}) collective-permute-start(bf16[768,1280]{1,0:T(8,128)(2,1)} %refs_6_.1), channel_id=1, source_target_pairs={{0,2},{1,3},{2,0},{3,1},{4,6},{5,7},{6,4},{7,5},{8,10},{9,11},{10,... | collective-permute-start | bytes 5898248 | tf_op jit(solution)/shard_map/ppermute | solution.py:23
  3.0 1.2 constant_dynamic-update-slice_fusion.2
  4.3 1.0 constant_dynamic-update-slice_fusion.1
  5.3 1.0 constant_dynamic-update-slice_fusion
  6.3 1.5 collective-permute-start.10
  8.4 12.4 %collective-permute-done.10.refs_12_ = bf16[320,896]{1,0:T(8,128)(2,1)S(1)} collective-permute-done((bf16[320,896]{1,0:T(8,128)(2,1)S(1)}, bf16[320,896]{1,0:T(8,128)(2,1)S(1)}, u32[]{:S(2)}, u32[]{:S(2)}) %collective-permute-start.10) | collective-permute-done | bytes 573472 | tf_op jit(solution)/shard_map/ppermute | solution.py:23
  20.8 1.5 collective-permute-start.11
  22.3 0.9 copy-done.5
  23.7 0.8 copy-done.7
  24.5 9.9 %collective-permute-done.11.refs_10_ = bf16[320,896]{1,0:T(8,128)(2,1)S(1)} collective-permute-done((bf16[320,896]{1,0:T(8,128)(2,1)S(1)}, bf16[320,896]{1,0:T(8,128)(2,1)S(1)}, u32[]{:S(2)}, u32[]{:S(2)}) %collective-permute-start.11) | collective-permute-done | bytes 573472 | tf_op jit(solution)/shard_map/ppermute | solution.py:23
  34.4 1.5 collective-permute-start.12
  35.9 0.8 copy-done.9
  37.3 0.8 copy-done.11
  38.1 9.4 %collective-permute-done.12.refs_12_ = bf16[320,896]{1,0:T(8,128)(2,1)S(1)} collective-permute-done((bf16[320,896]{1,0:T(8,128)(2,1)S(1)}, bf16[320,896]{1,0:T(8,128)(2,1)S(1)}, u32[]{:S(2)}, u32[]{:S(2)}) %collective-permute-start.12) | collective-permute-done | bytes 573472 | tf_op jit(solution)/shard_map/ppermute | solution.py:23
  47.5 1.5 collective-permute-start.13
  49.0 0.8 copy-done.13
  50.3 0.8 copy-done.15
  51.7 1.5 collective-permute-start.23
  53.2 9.5 %collective-permute-done.13.refs_10_ = bf16[320,896]{1,0:T(8,128)(2,1)S(1)} collective-permute-done((bf16[320,896]{1,0:T(8,128)(2,1)S(1)}, bf16[320,896]{1,0:T(8,128)(2,1)S(1)}, u32[]{:S(2)}, u32[]{:S(2)}) %collective-permute-start.13) | collective-permute-done | bytes 573472 | tf_op jit(solution)/shard_map/ppermute | solution.py:23
  62.7 0.8 copy-done.17
  63.5 10.6 %collective-permute-start.7 = (bf16[320,896]{1,0:T(8,128)(2,1)S(1)}, bf16[320,896]{1,0:T(8,128)(2,1)}, u32[]{:S(2)}, u32[]{:S(2)}) collective-permute-start(bf16[320,896]{1,0:T(8,128)(2,1)S(1)} %collective-permute-done.6.refs_6_), channel_id=1, source_target_pairs={{0,8},{1,9},{2,10},{3,11},{4,0},{5,1},{6,2},{7,3},{8,16},{9,17},{1... | collective-permute-start | bytes 1720328 | tf_op jit(solution)/shard_map/ppermute | solution.py:23
  74.1 0.8 copy-done.19
  75.0 7.9 %collective-permute-start.24 = (bf16[640,640]{1,0:T(8,128)(2,1)}, bf16[640,640]{1,0:T(8,128)(2,1)}, u32[]{:S(2)}, u32[]{:S(2)}) collective-permute-start(bf16[640,640]{1,0:T(8,128)(2,1)} %collective-permute-done.23), channel_id=1, source_target_pairs={{0,0},{1,2},{2,1},{3,3},{4,4},{5,6},{6,5},{7,7},{8,9},{9,11},{10,8... | collective-permute-start | bytes 2457608 | tf_op jit(solution)/shard_map/ppermute | solution.py:23
  82.9 1.5 collective-permute-done.14.refs_11_
  84.4 5.2 %collective-permute-start.8 = (bf16[320,896]{1,0:T(8,128)(2,1)}, bf16[320,896]{1,0:T(8,128)(2,1)}, u32[]{:S(2)}, u32[]{:S(2)}) collective-permute-start(bf16[320,896]{1,0:T(8,128)(2,1)} %collective-permute-done.7.refs_8_), channel_id=1, source_target_pairs={{0,8},{1,9},{2,10},{3,11},{4,0},{5,1},{6,2},{7,3},{8,16},{9,17},{1... | collective-permute-start | bytes 1720328 | tf_op jit(solution)/shard_map/ppermute | solution.py:23
  118.1 2.6 %collective-permute-start.9 = (bf16[320,896]{1,0:T(8,128)(2,1)}, bf16[320,896]{1,0:T(8,128)(2,1)S(1)}, u32[]{:S(2)}, u32[]{:S(2)}) collective-permute-start(bf16[320,896]{1,0:T(8,128)(2,1)} %collective-permute-done.8.refs_6_), channel_id=1, source_target_pairs={{0,8},{1,9},{2,10},{3,11},{4,0},{5,1},{6,2},{7,3},{8,16},{9,17},{1... | collective-permute-start | bytes 1720328 | tf_op jit(solution)/shard_map/ppermute | solution.py:23
  120.8 1.2 fusion.4
  122.1 1.2 copy-done.18
  123.3 1.1 copy-done.20
  124.4 8.9 %shard_map.127.refs_13_ = f32[768,896]{1,0:T(8,128)} custom-call(s32[12]{0:T(128)S(1)} %stack.120.refs_0_, bf16[768,1280]{1,0:T(8,128)(2,1)S(1)} %copy-done.1, bf16[768,1280]{1,0:T(8,128)(2,1)} %collective-permute-done.refs_2_, bf16[768,1280]{1,0:T(8,128)(2,1)} %collective-permute-done.1.refs_3_, bf16[768,1280]{1,0:T(8,128)(2,1)} %collective-permute-done.2.refs_4_, ...), custom_call_target="tpu_custom_call" | custom-call | flops 3523215360 | bytes 14024704 | tf_op jit(solution)/shard_map/pallas_call | solution.py:156
  133.3 0.9 collective-permute-done.16.refs_11_
  134.2 1.9 collective-permute-done.9.refs_8_
  136.5 1.6 collective-permute-start.32
  138.2 10.0 %shard_map.128.refs_0_ = f32[768,896]{1,0:T(8,128)} custom-call(s32[12]{0:T(128)S(1)} %stack.111.refs_0_, bf16[768,1280]{1,0:T(8,128)(2,1)S(1)} %copy-done.1, bf16[768,1280]{1,0:T(8,128)(2,1)} %collective-permute-done.refs_2_, bf16[768,1280]{1,0:T(8,128)(2,1)} %collective-permute-done.1.refs_3_, bf16[768,1280]{1,0:T(8,128)(2,1)} %collective-permute-done.2.refs_4_, ...), custom_call_target="tpu_custom_call" | custom-call | flops 3523215360 | bytes 14024704 | tf_op jit(solution)/shard_map/pallas_call | solution.py:156
  148.2 1.7 fusion
  150.0 1.3 fusion.1
  151.9 1.9 collective-permute-start.26
  153.9 1.4 fusion.2
  157.0 4.4 %shard_map.129.refs_1_ = bf16[768,640]{1,0:T(8,128)(2,1)S(1)} custom-call(f32[768,896]{1,0:T(8,128)S(1)} %copy-done, f32[8,768]{1,0:T(8,128)S(1)} %maximum_maximum_fusion.refs_1_, f32[8,768]{1,0:T(8,128)S(1)} %collective-permute-done.17.refs_2_, f32[8,768]{1,0:T(8,128)S(1)} %collective-permute-done.18.refs_3_, f32[8,768]{1,0:T(8,128)S(1)} %collective-permute-done.19.refs_4_, ...), custom_call_target="tpu_custom_call" | custom-call | flops 754974720 | bytes 5505024 | tf_op jit(solution)/shard_map/pallas_call | solution.py:248
  161.5 1.8 collective-permute-start.21
  164.6 1.4 collective-permute-start.34
  166.8 7.9 %collective-permute-done.27.refs_7_ = bf16[320,640]{1,0:T(8,128)(2,1)S(1)} collective-permute-done((bf16[320,640]{1,0:T(8,128)(2,1)S(1)}, bf16[320,640]{1,0:T(8,128)(2,1)S(1)}, u32[]{:S(2)}, u32[]{:S(2)}) %collective-permute-start.27) | collective-permute-done | bytes 409632 | tf_op jit(solution)/shard_map/ppermute | solution.py:23
  174.7 0.9 collective-permute-start.28
  176.3 1.2 collective-permute-start.35
  178.3 7.2 %collective-permute-done.28.refs_6_ = bf16[320,640]{1,0:T(8,128)(2,1)S(1)} collective-permute-done((bf16[320,640]{1,0:T(8,128)(2,1)S(1)}, bf16[320,640]{1,0:T(8,128)(2,1)S(1)}, u32[]{:S(2)}, u32[]{:S(2)}) %collective-permute-start.28) | collective-permute-done | bytes 409632 | tf_op jit(solution)/shard_map/ppermute | solution.py:23
  185.4 1.1 collective-permute-start.29
  187.3 0.9 collective-permute-start.36
  189.5 5.9 %collective-permute-done.29.refs_8_ = bf16[320,640]{1,0:T(8,128)(2,1)S(1)} collective-permute-done((bf16[320,640]{1,0:T(8,128)(2,1)S(1)}, bf16[320,640]{1,0:T(8,128)(2,1)S(1)}, u32[]{:S(2)}, u32[]{:S(2)}) %collective-permute-start.29) | collective-permute-done | bytes 409632 | tf_op jit(solution)/shard_map/ppermute | solution.py:23
  195.4 1.4 collective-permute-start.30
  198.9 5.9 %collective-permute-done.30.refs_6_ = bf16[320,640]{1,0:T(8,128)(2,1)} collective-permute-done((bf16[320,640]{1,0:T(8,128)(2,1)S(1)}, bf16[320,640]{1,0:T(8,128)(2,1)}, u32[]{:S(2)}, u32[]{:S(2)}) %collective-permute-start.30) | collective-permute-done | bytes 409632 | tf_op jit(solution)/shard_map/ppermute | solution.py:23
  204.8 1.4 collective-permute-start.31
  213.1 1.0 copy-done.4
  214.1 1.0 copy-done.30
  215.1 1.0 copy-done.32
  216.1 1.0 copy-done.34
  217.1 1.0 copy-done.36
  218.1 1.0 copy-done.38
  219.1 1.0 copy-done.40
  220.1 7.4 %shard_map.130.refs_13_ = f32[768,1280]{1,0:T(8,128)S(1)} custom-call(s32[12]{0:T(128)S(1)} %stack.127.refs_0_, bf16[768,640]{1,0:T(8,128)(2,1)S(1)} %shard_map.129.refs_1_, bf16[768,640]{1,0:T(8,128)(2,1)} %collective-permute-done.20.refs_2_, bf16[768,640]{1,0:T(8,128)(2,1)} %collective-permute-done.21.refs_3_, ...), custom_call_target="tpu_custom_call" | custom-call | flops 2516582400 | bytes 15073280 | tf_op jit(solution)/shard_map/pallas_call | solution.py:156
  227.5 1.9 copy-done.2
  229.5 8.9 %shard_map.131 = (f32[768,1280]{1,0:T(8,128)S(1)}, f32[8,768]{1,0:T(8,128)S(1)}) custom-call(s32[12]{0:T(128)S(1)} %stack.106.refs_0_, bf16[768,640]{1,0:T(8,128)(2,1)S(1)} %shard_map.129.refs_1_, bf16[768,640]{1,0:T(8,128)(2,1)} %collective-permute-done.20.refs_2_, bf16[768,640]{1,0:T(8,128)(2,1)} %collective-permute-done.21.refs_3_, ...), custom_call_target="tpu_custom_call" | custom-call | flops 2516582400 | bytes 15073280 | tf_op jit(solution)/shard_map/pallas_call | solution.py:156
  238.4 1.2 collective-permute-start.40
  239.6 2.6 %collective-permute-done.40.refs_4_ = f32[8,768]{1,0:T(8,128)S(1)} collective-permute-done((f32[8,768]{1,0:T(8,128)S(1)}, f32[8,768]{1,0:T(8,128)S(1)}, u32[]{:S(2)}, u32[]{:S(2)}) %collective-permute-start.40) | collective-permute-done | bytes 24608 | tf_op jit(solution)/shard_map/ppermute | solution.py:23
  243.5 2.4 shard_map.132
  (150 shorter events, 17.4 us)
Async XLA Ops:
  0.0 89.6 %copy-start.48 = (s32[8]{0:T(128)S(1)}, s32[8]{0:T(128)}, u32[]{:S(2)}) copy-start(s32[8]{0:T(128)} %constant.140.clone) | copy-start | bytes 100
  0.0 51.1 %copy-start.1 = (bf16[768,1280]{1,0:T(8,128)(2,1)S(1)}, bf16[768,1280]{1,0:T(8,128)(2,1)}, u32[]{:S(2)}) copy-start(bf16[768,1280]{1,0:T(8,128)(2,1)} %refs_6_.1) | copy-start | bytes 5898244
  0.0 51.6 %copy-start.47 = (bf16[640,640]{1,0:T(8,128)(2,1)S(1)}, bf16[640,640]{1,0:T(8,128)(2,1)}, u32[]{:S(2)}) copy-start(bf16[640,640]{1,0:T(8,128)(2,1)} %param.19) | copy-start | bytes 2457604
  0.0 51.1 %collective-permute-start.1 = (bf16[768,1280]{1,0:T(8,128)(2,1)}, bf16[768,1280]{1,0:T(8,128)(2,1)}, u32[]{:S(2)}, u32[]{:S(2)}) collective-permute-start(bf16[768,1280]{1,0:T(8,128)(2,1)} %refs_6_.1), channel_id=1, source_target_pairs={{0,2},{1,3},{2,0},{3,1},{4,6},{5,7},{6,4},{7,5},{8,10},{9,11},{10,... | collective-permute-start | bytes 5898248 | tf_op jit(solution)/shard_map/ppermute | solution.py:23
  4.3 92.3 %copy-start.43 = (s32[8]{0:T(128)S(1)}, s32[8]{0:T(128)}, u32[]{:S(2)}) copy-start(s32[8]{0:T(128)} %constant.139.clone) | copy-start | bytes 100
  4.3 113.8 %copy-start.44 = (s32[768]{0:T(1024)S(1)}, s32[768]{0:T(1024)}, u32[]{:S(2)}) copy-start(s32[768]{0:T(1024)} %param.15) | copy-start | bytes 9220
  6.3 14.5 %collective-permute-start.10 = (bf16[320,896]{1,0:T(8,128)(2,1)S(1)}, bf16[320,896]{1,0:T(8,128)(2,1)S(1)}, u32[]{:S(2)}, u32[]{:S(2)}) collective-permute-start(bf16[320,896]{1,0:T(8,128)(2,1)S(1)} %get-tuple-element.13.refs_9_), channel_id=1, source_target_pairs={{0,4},{1,5},{2,6},{3,7},{4,12},{5,13},{6,14},{7,15},{8,0},{9,1},{1... | collective-permute-start | bytes 1720328 | tf_op jit(solution)/shard_map/ppermute | solution.py:23
  7.9 15.3 %collective-permute-start.3 = (bf16[320,896]{1,0:T(8,128)(2,1)S(1)}, bf16[320,896]{1,0:T(8,128)(2,1)S(1)}, u32[]{:S(2)}, u32[]{:S(2)}) collective-permute-start(bf16[320,896]{1,0:T(8,128)(2,1)S(1)} %get-tuple-element.14.refs_5_), channel_id=1, source_target_pairs={{0,8},{1,9},{2,10},{3,11},{4,0},{5,1},{6,2},{7,3},{8,16},{9,17},{1... | collective-permute-start | bytes 1720328 | tf_op jit(solution)/shard_map/ppermute | solution.py:23
  20.8 13.6 %collective-permute-start.11 = (bf16[320,896]{1,0:T(8,128)(2,1)S(1)}, bf16[320,896]{1,0:T(8,128)(2,1)S(1)}, u32[]{:S(2)}, u32[]{:S(2)}) collective-permute-start(bf16[320,896]{1,0:T(8,128)(2,1)S(1)} %collective-permute-done.10.refs_12_), channel_id=1, source_target_pairs={{0,4},{1,5},{2,6},{3,7},{4,12},{5,13},{6,14},{7,15},{8,0},{9,1},{1... | collective-permute-start | bytes 1720328 | tf_op jit(solution)/shard_map/ppermute | solution.py:23
  23.2 13.6 %collective-permute-start.4 = (bf16[320,896]{1,0:T(8,128)(2,1)S(1)}, bf16[320,896]{1,0:T(8,128)(2,1)S(1)}, u32[]{:S(2)}, u32[]{:S(2)}) collective-permute-start(bf16[320,896]{1,0:T(8,128)(2,1)S(1)} %collective-permute-done.3.refs_7_), channel_id=1, source_target_pairs={{0,8},{1,9},{2,10},{3,11},{4,0},{5,1},{6,2},{7,3},{8,16},{9,17},{1... | collective-permute-start | bytes 1720328 | tf_op jit(solution)/shard_map/ppermute | solution.py:23
  34.4 13.0 %collective-permute-start.12 = (bf16[320,896]{1,0:T(8,128)(2,1)S(1)}, bf16[320,896]{1,0:T(8,128)(2,1)S(1)}, u32[]{:S(2)}, u32[]{:S(2)}) collective-permute-start(bf16[320,896]{1,0:T(8,128)(2,1)S(1)} %collective-permute-done.11.refs_10_), channel_id=1, source_target_pairs={{0,4},{1,5},{2,6},{3,7},{4,12},{5,13},{6,14},{7,15},{8,0},{9,1},{1... | collective-permute-start | bytes 1720328 | tf_op jit(solution)/shard_map/ppermute | solution.py:23
  36.7 13.0 %collective-permute-start.5 = (bf16[320,896]{1,0:T(8,128)(2,1)S(1)}, bf16[320,896]{1,0:T(8,128)(2,1)S(1)}, u32[]{:S(2)}, u32[]{:S(2)}) collective-permute-start(bf16[320,896]{1,0:T(8,128)(2,1)S(1)} %collective-permute-done.4.refs_5_), channel_id=1, source_target_pairs={{0,8},{1,9},{2,10},{3,11},{4,0},{5,1},{6,2},{7,3},{8,16},{9,17},{1... | collective-permute-start | bytes 1720328 | tf_op jit(solution)/shard_map/ppermute | solution.py:23
  47.5 15.2 %collective-permute-start.13 = (bf16[320,896]{1,0:T(8,128)(2,1)S(1)}, bf16[320,896]{1,0:T(8,128)(2,1)S(1)}, u32[]{:S(2)}, u32[]{:S(2)}) collective-permute-start(bf16[320,896]{1,0:T(8,128)(2,1)S(1)} %collective-permute-done.12.refs_12_), channel_id=1, source_target_pairs={{0,4},{1,5},{2,6},{3,7},{4,12},{5,13},{6,14},{7,15},{8,0},{9,1},{1... | collective-permute-start | bytes 1720328 | tf_op jit(solution)/shard_map/ppermute | solution.py:23
  49.8 13.7 %collective-permute-start.6 = (bf16[320,896]{1,0:T(8,128)(2,1)S(1)}, bf16[320,896]{1,0:T(8,128)(2,1)S(1)}, u32[]{:S(2)}, u32[]{:S(2)}) collective-permute-start(bf16[320,896]{1,0:T(8,128)(2,1)S(1)} %collective-permute-done.5.refs_7_), channel_id=1, source_target_pairs={{0,8},{1,9},{2,10},{3,11},{4,0},{5,1},{6,2},{7,3},{8,16},{9,17},{1... | collective-permute-start | bytes 1720328 | tf_op jit(solution)/shard_map/ppermute | solution.py:23
  51.1 70.9 %collective-permute-start = (bf16[768,1280]{1,0:T(8,128)(2,1)S(1)}, bf16[768,1280]{1,0:T(8,128)(2,1)}, u32[]{:S(2)}, u32[]{:S(2)}) collective-permute-start(bf16[768,1280]{1,0:T(8,128)(2,1)S(1)} %copy-done.1), channel_id=1, source_target_pairs={{0,1},{1,0},{2,3},{3,2},{4,5},{5,4},{6,7},{7,6},{8,9},{9,8},{10,11... | collective-permute-start | bytes 5898248 | tf_op jit(solution)/shard_map/ppermute | solution.py:23
  51.1 70.9 %collective-permute-start.2 = (bf16[768,1280]{1,0:T(8,128)(2,1)}, bf16[768,1280]{1,0:T(8,128)(2,1)}, u32[]{:S(2)}, u32[]{:S(2)}) collective-permute-start(bf16[768,1280]{1,0:T(8,128)(2,1)} %collective-permute-done.1.refs_3_), channel_id=1, source_target_pairs={{0,1},{1,0},{2,3},{3,2},{4,5},{5,4},{6,7},{7,6},{8,9},{9,8},{10,11... | collective-permute-start | bytes 5898248 | tf_op jit(solution)/shard_map/ppermute | solution.py:23
  51.7 23.3 %collective-permute-start.23 = (bf16[640,640]{1,0:T(8,128)(2,1)S(1)}, bf16[640,640]{1,0:T(8,128)(2,1)}, u32[]{:S(2)}, u32[]{:S(2)}) collective-permute-start(bf16[640,640]{1,0:T(8,128)(2,1)S(1)} %copy-done.47), channel_id=1, source_target_pairs={{0,0},{1,17},{2,10},{3,27},{4,4},{5,21},{6,14},{7,31},{8,8},{9,25}... | collective-permute-start | bytes 2457608 | tf_op jit(solution)/shard_map/ppermute | solution.py:23
  62.7 21.7 %collective-permute-start.14 = (bf16[320,896]{1,0:T(8,128)(2,1)S(1)}, bf16[320,896]{1,0:T(8,128)(2,1)}, u32[]{:S(2)}, u32[]{:S(2)}) collective-permute-start(bf16[320,896]{1,0:T(8,128)(2,1)S(1)} %collective-permute-done.13.refs_10_), channel_id=1, source_target_pairs={{0,4},{1,5},{2,6},{3,7},{4,12},{5,13},{6,14},{7,15},{8,0},{9,1},{1... | collective-permute-start | bytes 1720328 | tf_op jit(solution)/shard_map/ppermute | solution.py:23
  63.5 20.9 %collective-permute-start.7 = (bf16[320,896]{1,0:T(8,128)(2,1)S(1)}, bf16[320,896]{1,0:T(8,128)(2,1)}, u32[]{:S(2)}, u32[]{:S(2)}) collective-permute-start(bf16[320,896]{1,0:T(8,128)(2,1)S(1)} %collective-permute-done.6.refs_6_), channel_id=1, source_target_pairs={{0,8},{1,9},{2,10},{3,11},{4,0},{5,1},{6,2},{7,3},{8,16},{9,17},{1... | collective-permute-start | bytes 1720328 | tf_op jit(solution)/shard_map/ppermute | solution.py:23
  75.0 45.8 %collective-permute-start.24 = (bf16[640,640]{1,0:T(8,128)(2,1)}, bf16[640,640]{1,0:T(8,128)(2,1)}, u32[]{:S(2)}, u32[]{:S(2)}) collective-permute-start(bf16[640,640]{1,0:T(8,128)(2,1)} %collective-permute-done.23), channel_id=1, source_target_pairs={{0,0},{1,2},{2,1},{3,3},{4,4},{5,6},{6,5},{7,7},{8,9},{9,11},{10,8... | collective-permute-start | bytes 2457608 | tf_op jit(solution)/shard_map/ppermute | solution.py:23
  84.4 33.7 %collective-permute-start.15 = (bf16[320,896]{1,0:T(8,128)(2,1)}, bf16[320,896]{1,0:T(8,128)(2,1)}, u32[]{:S(2)}, u32[]{:S(2)}) collective-permute-start(bf16[320,896]{1,0:T(8,128)(2,1)} %collective-permute-done.14.refs_11_), channel_id=1, source_target_pairs={{0,4},{1,5},{2,6},{3,7},{4,12},{5,13},{6,14},{7,15},{8,0},{9,1},{1... | collective-permute-start | bytes 1720328 | tf_op jit(solution)/shard_map/ppermute | solution.py:23
  84.4 33.8 %collective-permute-start.8 = (bf16[320,896]{1,0:T(8,128)(2,1)}, bf16[320,896]{1,0:T(8,128)(2,1)}, u32[]{:S(2)}, u32[]{:S(2)}) collective-permute-start(bf16[320,896]{1,0:T(8,128)(2,1)} %collective-permute-done.7.refs_8_), channel_id=1, source_target_pairs={{0,8},{1,9},{2,10},{3,11},{4,0},{5,1},{6,2},{7,3},{8,16},{9,17},{1... | collective-permute-start | bytes 1720328 | tf_op jit(solution)/shard_map/ppermute | solution.py:23
  118.0 4.1 %copy-start.14 = (bf16[320,896]{1,0:T(8,128)(2,1)S(1)}, bf16[320,896]{1,0:T(8,128)(2,1)}, u32[]{:S(2)}) copy-start(bf16[320,896]{1,0:T(8,128)(2,1)} %copy-done.13) | copy-start | bytes 1720324
  118.1 16.1 %collective-permute-start.16 = (bf16[320,896]{1,0:T(8,128)(2,1)}, bf16[320,896]{1,0:T(8,128)(2,1)S(1)}, u32[]{:S(2)}, u32[]{:S(2)}) collective-permute-start(bf16[320,896]{1,0:T(8,128)(2,1)} %collective-permute-done.15.refs_9_), channel_id=1, source_target_pairs={{0,4},{1,5},{2,6},{3,7},{4,12},{5,13},{6,14},{7,15},{8,0},{9,1},{1... | collective-permute-start | bytes 1720328 | tf_op jit(solution)/shard_map/ppermute | solution.py:23
  118.1 17.9 %collective-permute-start.9 = (bf16[320,896]{1,0:T(8,128)(2,1)}, bf16[320,896]{1,0:T(8,128)(2,1)S(1)}, u32[]{:S(2)}, u32[]{:S(2)}) collective-permute-start(bf16[320,896]{1,0:T(8,128)(2,1)} %collective-permute-done.8.refs_6_), channel_id=1, source_target_pairs={{0,8},{1,9},{2,10},{3,11},{4,0},{5,1},{6,2},{7,3},{8,16},{9,17},{1... | collective-permute-start | bytes 1720328 | tf_op jit(solution)/shard_map/ppermute | solution.py:23
  122.0 14.1 %copy-start.3 = (bf16[320,640]{1,0:T(8,128)(2,1)}, bf16[320,640]{1,0:T(8,128)(2,1)S(1)}, u32[]{:S(2)}) copy-start(bf16[320,640]{1,0:T(8,128)(2,1)S(1)} %get-tuple-element.9.refs_5_) | copy-start | bytes 1228804
  122.0 16.2 %copy-start.6 = (bf16[320,896]{1,0:T(8,128)(2,1)S(1)}, bf16[320,896]{1,0:T(8,128)(2,1)}, u32[]{:S(2)}) copy-start(bf16[320,896]{1,0:T(8,128)(2,1)} %copy-done.5) | copy-start | bytes 1720324
  122.0 16.1 %copy-start.8 = (bf16[320,896]{1,0:T(8,128)(2,1)S(1)}, bf16[320,896]{1,0:T(8,128)(2,1)}, u32[]{:S(2)}) copy-start(bf16[320,896]{1,0:T(8,128)(2,1)} %copy-done.7) | copy-start | bytes 1720324
  122.0 16.1 %copy-start.10 = (bf16[320,896]{1,0:T(8,128)(2,1)S(1)}, bf16[320,896]{1,0:T(8,128)(2,1)}, u32[]{:S(2)}) copy-start(bf16[320,896]{1,0:T(8,128)(2,1)} %copy-done.9) | copy-start | bytes 1720324
  122.0 16.1 %copy-start.12 = (bf16[320,896]{1,0:T(8,128)(2,1)S(1)}, bf16[320,896]{1,0:T(8,128)(2,1)}, u32[]{:S(2)}) copy-start(bf16[320,896]{1,0:T(8,128)(2,1)} %copy-done.11) | copy-start | bytes 1720324
  136.1 15.8 %collective-permute-start.25 = (bf16[320,640]{1,0:T(8,128)(2,1)S(1)}, bf16[320,640]{1,0:T(8,128)(2,1)S(1)}, u32[]{:S(2)}, u32[]{:S(2)}) collective-permute-start(bf16[320,640]{1,0:T(8,128)(2,1)S(1)} %get-tuple-element.9.refs_5_), channel_id=1, source_target_pairs={{0,8},{1,9},{2,10},{3,11},{4,0},{5,1},{6,2},{7,3},{8,16},{9,17},{1... | collective-permute-start | bytes 1228808 | tf_op jit(solution)/shard_map/ppermute | solution.py:23
  136.5 17.3 %collective-permute-start.32 = (bf16[320,640]{1,0:T(8,128)(2,1)S(1)}, bf16[320,640]{1,0:T(8,128)(2,1)S(1)}, u32[]{:S(2)}, u32[]{:S(2)}) collective-permute-start(bf16[320,640]{1,0:T(8,128)(2,1)S(1)} %get-tuple-element.10.refs_9_), channel_id=1, source_target_pairs={{0,4},{1,5},{2,6},{3,7},{4,12},{5,13},{6,14},{7,15},{8,0},{9,1},{1... | collective-permute-start | bytes 1228808 | tf_op jit(solution)/shard_map/ppermute | solution.py:23
  149.9 6.3 %copy-start.46 = (f32[640]{0:T(1024)S(1)}, f32[640]{0:T(1024)}, u32[]{:S(2)}) copy-start(f32[640]{0:T(1024)} %param.20) | copy-start | bytes 7684
  149.9 7.0 %copy-start = (f32[768,896]{1,0:T(8,128)S(1)}, f32[768,896]{1,0:T(8,128)}, u32[]{:S(2)}) copy-start(f32[768,896]{1,0:T(8,128)} %shard_map.128.refs_0_) | copy-start | bytes 8257540
  149.9 7.0 %copy-start.41 = (f32[128]{0:T(128)S(1)}, f32[128]{0:T(128)}, u32[]{:S(2)}) copy-start(f32[128]{0:T(128)} %param.21) | copy-start | bytes 1540
  151.4 4.1 %collective-permute-start.18 = (f32[8,768]{1,0:T(8,128)S(1)}, f32[8,768]{1,0:T(8,128)S(1)}, u32[]{:S(2)}, u32[]{:S(2)}) collective-permute-start(f32[8,768]{1,0:T(8,128)S(1)} %maximum_maximum_fusion.refs_1_), channel_id=1, source_target_pairs={{0,2},{1,3},{2,0},{3,1},{4,6},{5,7},{6,4},{7,5},{8,10},{9,11},{10,... | collective-permute-start | bytes 73736 | tf_op jit(solution)/shard_map/ppermute | solution.py:23
  151.8 9.6 %copy-start.21 = (bf16[320,640]{1,0:T(8,128)(2,1)}, bf16[320,640]{1,0:T(8,128)(2,1)S(1)}, u32[]{:S(2)}) copy-start(bf16[320,640]{1,0:T(8,128)(2,1)S(1)} %collective-permute-done.25.refs_7_) | copy-start | bytes 1228804
  151.9 11.4 %collective-permute-start.26 = (bf16[320,640]{1,0:T(8,128)(2,1)S(1)}, bf16[320,640]{1,0:T(8,128)(2,1)S(1)}, u32[]{:S(2)}, u32[]{:S(2)}) collective-permute-start(bf16[320,640]{1,0:T(8,128)(2,1)S(1)} %collective-permute-done.25.refs_7_), channel_id=1, source_target_pairs={{0,8},{1,9},{2,10},{3,11},{4,0},{5,1},{6,2},{7,3},{8,16},{9,17},{1... | collective-permute-start | bytes 1228808 | tf_op jit(solution)/shard_map/ppermute | solution.py:23
  153.8 7.6 %copy-start.23 = (bf16[320,640]{1,0:T(8,128)(2,1)}, bf16[320,640]{1,0:T(8,128)(2,1)S(1)}, u32[]{:S(2)}) copy-start(bf16[320,640]{1,0:T(8,128)(2,1)S(1)} %collective-permute-done.32.refs_12_) | copy-start | bytes 1228804
  153.8 10.8 %collective-permute-start.33 = (bf16[320,640]{1,0:T(8,128)(2,1)S(1)}, bf16[320,640]{1,0:T(8,128)(2,1)S(1)}, u32[]{:S(2)}, u32[]{:S(2)}) collective-permute-start(bf16[320,640]{1,0:T(8,128)(2,1)S(1)} %collective-permute-done.32.refs_12_), channel_id=1, source_target_pairs={{0,4},{1,5},{2,6},{3,7},{4,12},{5,13},{6,14},{7,15},{8,0},{9,1},{1... | collective-permute-start | bytes 1228808 | tf_op jit(solution)/shard_map/ppermute | solution.py:23
  155.4 1.3 collective-permute-start.17
  155.5 1.3 collective-permute-start.19
  157.0 50.2 %copy-start.42 = (s32[4]{0:T(128)S(1)}, s32[4]{0:T(128)}, u32[]{:S(2)}) copy-start(s32[4]{0:T(128)} %constant.141.clone) | copy-start | bytes 52
  161.5 27.5 %collective-permute-start.21 = (bf16[768,640]{1,0:T(8,128)(2,1)S(1)}, bf16[768,640]{1,0:T(8,128)(2,1)}, u32[]{:S(2)}, u32[]{:S(2)}) collective-permute-start(bf16[768,640]{1,0:T(8,128)(2,1)S(1)} %shard_map.129.refs_1_), channel_id=1, source_target_pairs={{0,2},{1,3},{2,0},{3,1},{4,6},{5,7},{6,4},{7,5},{8,10},{9,11},{10,... | collective-permute-start | bytes 2949128 | tf_op jit(solution)/shard_map/ppermute | solution.py:23
  163.2 11.5 %collective-permute-start.27 = (bf16[320,640]{1,0:T(8,128)(2,1)S(1)}, bf16[320,640]{1,0:T(8,128)(2,1)S(1)}, u32[]{:S(2)}, u32[]{:S(2)}) collective-permute-start(bf16[320,640]{1,0:T(8,128)(2,1)S(1)} %collective-permute-done.26.refs_5_), channel_id=1, source_target_pairs={{0,8},{1,9},{2,10},{3,11},{4,0},{5,1},{6,2},{7,3},{8,16},{9,17},{1... | collective-permute-start | bytes 1228808 | tf_op jit(solution)/shard_map/ppermute | solution.py:23
  164.6 11.7 %collective-permute-start.34 = (bf16[320,640]{1,0:T(8,128)(2,1)S(1)}, bf16[320,640]{1,0:T(8,128)(2,1)S(1)}, u32[]{:S(2)}, u32[]{:S(2)}) collective-permute-start(bf16[320,640]{1,0:T(8,128)(2,1)S(1)} %collective-permute-done.33.refs_10_), channel_id=1, source_target_pairs={{0,4},{1,5},{2,6},{3,7},{4,12},{5,13},{6,14},{7,15},{8,0},{9,1},{1... | collective-permute-start | bytes 1228808 | tf_op jit(solution)/shard_map/ppermute | solution.py:23
  174.7 10.7 %collective-permute-start.28 = (bf16[320,640]{1,0:T(8,128)(2,1)S(1)}, bf16[320,640]{1,0:T(8,128)(2,1)S(1)}, u32[]{:S(2)}, u32[]{:S(2)}) collective-permute-start(bf16[320,640]{1,0:T(8,128)(2,1)S(1)} %collective-permute-done.27.refs_7_), channel_id=1, source_target_pairs={{0,8},{1,9},{2,10},{3,11},{4,0},{5,1},{6,2},{7,3},{8,16},{9,17},{1... | collective-permute-start | bytes 1228808 | tf_op jit(solution)/shard_map/ppermute | solution.py:23
  176.3 11.0 %collective-permute-start.35 = (bf16[320,640]{1,0:T(8,128)(2,1)S(1)}, bf16[320,640]{1,0:T(8,128)(2,1)S(1)}, u32[]{:S(2)}, u32[]{:S(2)}) collective-permute-start(bf16[320,640]{1,0:T(8,128)(2,1)S(1)} %collective-permute-done.34.refs_12_), channel_id=1, source_target_pairs={{0,4},{1,5},{2,6},{3,7},{4,12},{5,13},{6,14},{7,15},{8,0},{9,1},{1... | collective-permute-start | bytes 1228808 | tf_op jit(solution)/shard_map/ppermute | solution.py:23
  185.4 9.9 %collective-permute-start.29 = (bf16[320,640]{1,0:T(8,128)(2,1)S(1)}, bf16[320,640]{1,0:T(8,128)(2,1)S(1)}, u32[]{:S(2)}, u32[]{:S(2)}) collective-permute-start(bf16[320,640]{1,0:T(8,128)(2,1)S(1)} %collective-permute-done.28.refs_6_), channel_id=1, source_target_pairs={{0,8},{1,9},{2,10},{3,11},{4,0},{5,1},{6,2},{7,3},{8,16},{9,17},{1... | collective-permute-start | bytes 1228808 | tf_op jit(solution)/shard_map/ppermute | solution.py:23
  187.3 10.2 %collective-permute-start.36 = (bf16[320,640]{1,0:T(8,128)(2,1)S(1)}, bf16[320,640]{1,0:T(8,128)(2,1)S(1)}, u32[]{:S(2)}, u32[]{:S(2)}) collective-permute-start(bf16[320,640]{1,0:T(8,128)(2,1)S(1)} %collective-permute-done.35.refs_10_), channel_id=1, source_target_pairs={{0,4},{1,5},{2,6},{3,7},{4,12},{5,13},{6,14},{7,15},{8,0},{9,1},{1... | collective-permute-start | bytes 1228808 | tf_op jit(solution)/shard_map/ppermute | solution.py:23
  188.9 24.1 %collective-permute-start.20 = (bf16[768,640]{1,0:T(8,128)(2,1)S(1)}, bf16[768,640]{1,0:T(8,128)(2,1)}, u32[]{:S(2)}, u32[]{:S(2)}) collective-permute-start(bf16[768,640]{1,0:T(8,128)(2,1)S(1)} %shard_map.129.refs_1_), channel_id=1, source_target_pairs={{0,1},{1,0},{2,3},{3,2},{4,5},{5,4},{6,7},{7,6},{8,9},{9,8},{10,11... | collective-permute-start | bytes 2949128 | tf_op jit(solution)/shard_map/ppermute | solution.py:23
  189.0 24.1 %collective-permute-start.22 = (bf16[768,640]{1,0:T(8,128)(2,1)}, bf16[768,640]{1,0:T(8,128)(2,1)}, u32[]{:S(2)}, u32[]{:S(2)}) collective-permute-start(bf16[768,640]{1,0:T(8,128)(2,1)} %collective-permute-done.21.refs_3_), channel_id=1, source_target_pairs={{0,1},{1,0},{2,3},{3,2},{4,5},{5,4},{6,7},{7,6},{8,9},{9,8},{10,11... | collective-permute-start | bytes 2949128 | tf_op jit(solution)/shard_map/ppermute | solution.py:23
  195.4 9.4 %collective-permute-start.30 = (bf16[320,640]{1,0:T(8,128)(2,1)S(1)}, bf16[320,640]{1,0:T(8,128)(2,1)}, u32[]{:S(2)}, u32[]{:S(2)}) collective-permute-start(bf16[320,640]{1,0:T(8,128)(2,1)S(1)} %collective-permute-done.29.refs_8_), channel_id=1, source_target_pairs={{0,8},{1,9},{2,10},{3,11},{4,0},{5,1},{6,2},{7,3},{8,16},{9,17},{1... | collective-permute-start | bytes 1228808 | tf_op jit(solution)/shard_map/ppermute | solution.py:23
  197.6 9.4 %collective-permute-start.37 = (bf16[320,640]{1,0:T(8,128)(2,1)S(1)}, bf16[320,640]{1,0:T(8,128)(2,1)}, u32[]{:S(2)}, u32[]{:S(2)}) collective-permute-start(bf16[320,640]{1,0:T(8,128)(2,1)S(1)} %collective-permute-done.36.refs_11_), channel_id=1, source_target_pairs={{0,4},{1,5},{2,6},{3,7},{4,12},{5,13},{6,14},{7,15},{8,0},{9,1},{1... | collective-permute-start | bytes 1228808 | tf_op jit(solution)/shard_map/ppermute | solution.py:23
  204.8 24.6 %collective-permute-start.31 = (bf16[320,640]{1,0:T(8,128)(2,1)}, bf16[320,640]{1,0:T(8,128)(2,1)}, u32[]{:S(2)}, u32[]{:S(2)}) collective-permute-start(bf16[320,640]{1,0:T(8,128)(2,1)} %collective-permute-done.30.refs_6_), channel_id=1, source_target_pairs={{0,8},{1,9},{2,10},{3,11},{4,0},{5,1},{6,2},{7,3},{8,16},{9,17},{1... | collective-permute-start | bytes 1228808 | tf_op jit(solution)/shard_map/ppermute | solution.py:23
  207.0 22.4 %collective-permute-start.38 = (bf16[320,640]{1,0:T(8,128)(2,1)}, bf16[320,640]{1,0:T(8,128)(2,1)}, u32[]{:S(2)}, u32[]{:S(2)}) collective-permute-start(bf16[320,640]{1,0:T(8,128)(2,1)} %collective-permute-done.37.refs_9_), channel_id=1, source_target_pairs={{0,4},{1,5},{2,6},{3,7},{4,12},{5,13},{6,14},{7,15},{8,0},{9,1},{1... | collective-permute-start | bytes 1228808 | tf_op jit(solution)/shard_map/ppermute | solution.py:23
  220.1 9.4 %copy-start.22 = (bf16[320,640]{1,0:T(8,128)(2,1)S(1)}, bf16[320,640]{1,0:T(8,128)(2,1)}, u32[]{:S(2)}) copy-start(bf16[320,640]{1,0:T(8,128)(2,1)} %copy-done.21) | copy-start | bytes 1228804
  220.1 9.4 %copy-start.24 = (bf16[320,640]{1,0:T(8,128)(2,1)S(1)}, bf16[320,640]{1,0:T(8,128)(2,1)}, u32[]{:S(2)}) copy-start(bf16[320,640]{1,0:T(8,128)(2,1)} %copy-done.23) | copy-start | bytes 1228804
  220.1 9.4 %copy-start.26 = (bf16[320,640]{1,0:T(8,128)(2,1)S(1)}, bf16[320,640]{1,0:T(8,128)(2,1)}, u32[]{:S(2)}) copy-start(bf16[320,640]{1,0:T(8,128)(2,1)} %copy-done.25) | copy-start | bytes 1228804
  220.1 9.4 %copy-start.28 = (bf16[320,640]{1,0:T(8,128)(2,1)S(1)}, bf16[320,640]{1,0:T(8,128)(2,1)}, u32[]{:S(2)}) copy-start(bf16[320,640]{1,0:T(8,128)(2,1)} %copy-done.27) | copy-start | bytes 1228804
  229.4 12.9 %copy-start.45 = (f32[1280]{0:T(1024)S(1)}, f32[1280]{0:T(1024)}, u32[]{:S(2)}) copy-start(f32[1280]{0:T(1024)} %param.22) | copy-start | bytes 15364
  238.4 3.9 %collective-permute-start.40 = (f32[8,768]{1,0:T(8,128)S(1)}, f32[8,768]{1,0:T(8,128)S(1)}, u32[]{:S(2)}, u32[]{:S(2)}) collective-permute-start(f32[8,768]{1,0:T(8,128)S(1)} %get-tuple-element.12.refs_2_), channel_id=1, source_target_pairs={{0,2},{1,3},{2,0},{3,1},{4,6},{5,7},{6,4},{7,5},{8,10},{9,11},{10,... | collective-permute-start | bytes 73736 | tf_op jit(solution)/shard_map/ppermute | solution.py:23
  239.6 3.3 %collective-permute-start.39 = (f32[8,768]{1,0:T(8,128)S(1)}, f32[8,768]{1,0:T(8,128)S(1)}, u32[]{:S(2)}, u32[]{:S(2)}) collective-permute-start(f32[8,768]{1,0:T(8,128)S(1)} %get-tuple-element.12.refs_2_), channel_id=1, source_target_pairs={{0,1},{1,0},{2,3},{3,2},{4,5},{5,4},{6,7},{7,6},{8,9},{9,8},{10,11... | collective-permute-start | bytes 73736 | tf_op jit(solution)/shard_map/ppermute | solution.py:23
  242.3 1.2 collective-permute-start.41
  (27 other events, 27.9 us)

commit v3 on v2

--- a/solution.py
+++ b/solution.py
@@ -57,8 +57,27 @@
     return tops, bottoms
 
 
-def block_product(sizes, sources, choices, tops, bottoms, accumulated, columns, with_squares):
+def snake_block(sizes, f_index, offset):
+    n = sizes[0]
+    ahead = lax.rem(f_index, 2) == 0
+    position = jnp.where(ahead, f_index // 2, n - 1 - f_index // 2)
+    place = lax.rem(position + offset, n)
+    return jnp.where(place < (n + 1) // 2, 2 * place, 2 * (n - place) - 1)
+
+
+def traced_reverse(value, size):
+    result = value * 0
+    while size > 1:
+        result = result * 2 + lax.rem(value, 2)
+        value = value // 2
+        size //= 2
+    return result
+
+
+def block_product(sizes, sources, choose, offsets, tops, bottoms, accumulated, columns, spans):
     rows, source_width = sources[0].shape
+    tops = [tops[(sizes[0] - offset) % sizes[0]] for offset in offsets]
+    bottoms = [bottoms[offset] for offset in offsets]
     half, width = tops[0].shape
     depth = 2 * half
     count = len(tops)
@@ -66,35 +85,37 @@
         stack = jnp.stack(sources)
         total = jnp.zeros((rows, columns), jnp.float32) if accumulated is None else accumulated
         for j in range(count):
-            piece = lax.dynamic_slice(
-                stack, (choices[3 * j], 0, choices[3 * j + 1]), (1, rows, depth)
-            )[0]
+            which, first, column = choose(offsets[j])
+            piece = lax.dynamic_slice(stack, (which, 0, first), (1, rows, depth))[0]
             matrix = jnp.concatenate([tops[j], bottoms[j]], axis=0)
             term = jnp.dot(piece, matrix, preferred_element_type=jnp.float32)
-            current = lax.dynamic_slice(total, (0, choices[3 * j + 2]), (rows, width))
-            total = lax.dynamic_update_slice(total, current + term, (0, choices[3 * j + 2]))
-        if not with_squares:
+            current = lax.dynamic_slice(total, (0, column), (rows, width))
+            total = lax.dynamic_update_slice(total, current + term, (0, column))
+        if spans is None:
             return total
-        squares = jnp.sum(total * total, axis=1)
-        return total, jnp.broadcast_to(squares[None, :], (8, rows))
+        squares = [jnp.sum(total[:, low:high] ** 2, axis=1) for low, high in spans]
+        squares += [jnp.zeros_like(squares[0])] * (8 - len(squares))
+        return total, jnp.stack(squares)
 
     tile = 256 if rows % 256 == 0 else rows
+    tiles = rows // tile
     extra = 0 if accumulated is None else 1
     whole = width == columns
 
     def kernel(*refs):
-        choice = refs[0]
-        source = refs[1 : 1 + len(sources)]
-        top = refs[1 + len(sources) : 1 + len(sources) + count]
-        bottom = refs[1 + len(sources) + count : 1 + len(sources) + 2 * count]
-        rest = refs[1 + len(sources) + 2 * count :]
-        start = rest[0] if extra else None
-        out = rest[extra]
-        squares = rest[extra + 1] if with_squares else None
-        piece, matrix, sems = rest[-3:]
+        source, refs = refs[: len(sources)], refs[len(sources) :]
+        top, refs = refs[:count], refs[count:]
+        bottom, refs = refs[:count], refs[count:]
+        start, refs = refs[:extra], refs[extra:]
+        out, refs = refs[0], refs[1:]
+        squares, refs = refs[: spans is not None], refs[spans is not None :]
+        piece, matrix, total, sems, tile_sems = refs
+        choices = [choose(offset) for offset in offsets]
 
         def piece_copy(j, which):
-            first = pl.multiple_of(choice[3 * j + 1], 128)
+            first = choices[j][1]
+            if not isinstance(first, int):
+                first = pl.multiple_of(first, 128)
             return pltpu.make_async_copy(
                 source[which].at[:, pl.ds(first, depth)],
                 piece.at[:, pl.ds(j * depth, depth)],
@@ -109,68 +130,89 @@
                 ),
             )
 
+        def in_copy(i):
+            part = pl.ds(i * tile, tile)
+            return pltpu.make_async_copy(start[0].at[part], total.at[part], tile_sems.at[i, 0])
+
+        def out_copy(i):
+            part = pl.ds(i * tile, tile)
+            return pltpu.make_async_copy(total.at[part], out.at[part], tile_sems.at[i, 1])
+
         for j in range(count):
             for which in range(len(sources)):
 
-                @pl.when(choice[3 * j] == which)
+                @pl.when(choices[j][0] == which)
                 def _(j=j, which=which):
                     piece_copy(j, which).start()
 
             for copy in matrix_copies(j):
                 copy.start()
+        for i in range(tiles * extra):
+            in_copy(i).start()
         for j in range(count):
             piece_copy(j, 0).wait()
             for copy in matrix_copies(j):
                 copy.wait()
-        if not whole:
-            out[...] = start[...] if extra else jnp.zeros_like(out)
-        for lower in range(0, rows, tile):
-            part = pl.ds(lower, tile)
+        for i in range(tiles):
+            part = pl.ds(i * tile, tile)
+            if extra:
+                in_copy(i).wait()
             if whole:
                 term = jnp.dot(piece[part, :], matrix[...], preferred_element_type=jnp.float32)
-                out[part, :] = start[part, :] + term if extra else term
+                total[part, :] = total[part, :] + term if extra else term
             else:
+                if not extra:
+                    total[part, :] = jnp.zeros((tile, columns), jnp.float32)
                 for j in range(count):
                     term = jnp.dot(
                         piece[part, pl.ds(j * depth, depth)],
                         matrix[pl.ds(j * depth, depth), :],
                         preferred_element_type=jnp.float32,
                     )
-                    span = pl.ds(pl.multiple_of(choice[3 * j + 2], 128), width)
-                    out[part, span] += term
-            if with_squares:
-                total = out[part, :]
-                sums = jnp.sum(total * total, axis=1, keepdims=True)
-                squares[:, part] = jnp.broadcast_to(sums, (tile, 128)).T[:8]
+                    total[part, pl.ds(pl.multiple_of(choices[j][2], 128), width)] += term
+            out_copy(i).start()
+            if spans is not None:
+                sums = []
+                for low, high in spans:
+                    chosen = total[part, low:high]
+                    chosen = jnp.sum(chosen * chosen, axis=1, keepdims=True)
+                    sums.append(jnp.broadcast_to(chosen, (tile, 128)).T[:8])
+                lines = lax.broadcasted_iota(jnp.int32, (8, tile), 0)
+                line = sums[0]
+                for index in range(1, len(sums)):
+                    line = jnp.where(lines == index, sums[index], line)
+                squares[0][:, part] = line
+        for i in range(tiles):
+            out_copy(i).wait()
 
     any_space = pl.BlockSpec(memory_space=pl.ANY)
-    in_vmem = pl.BlockSpec(memory_space=pltpu.VMEM)
     out_shape = [jax.ShapeDtypeStruct((rows, columns), jnp.float32)]
-    if with_squares:
+    out_specs = [any_space]
+    if spans is not None:
         out_shape.append(jax.ShapeDtypeStruct((8, rows), jnp.float32))
-    operands = [jnp.stack(choices).astype(jnp.int32), *sources, *tops, *bottoms]
-    specs = [pl.BlockSpec(memory_space=pltpu.SMEM)] + [any_space] * (len(operands) - 1)
-    if extra:
-        operands.append(accumulated)
-        specs.append(in_vmem)
+        out_specs.append(pl.BlockSpec(memory_space=pltpu.VMEM))
+    operands = [*sources, *tops, *bottoms] + [accumulated] * extra
+    needed = 2 * count * depth * (rows + width) + 4 * rows * columns
     results = pl.pallas_call(
         kernel,
         out_shape=out_shape,
-        in_specs=specs,
-        out_specs=[in_vmem] * len(out_shape),
+        in_specs=[any_space] * len(operands),
+        out_specs=out_specs,
         scratch_shapes=[
             pltpu.VMEM((rows, count * depth), sources[0].dtype),
             pltpu.VMEM((count * depth, width), tops[0].dtype),
+            pltpu.VMEM((rows, columns), jnp.float32),
             pltpu.SemaphoreType.DMA((count, 3)),
+            pltpu.SemaphoreType.DMA((tiles, 2)),
         ],
-        compiler_params=pltpu.CompilerParams(vmem_limit_bytes=40 * 2**20),
+        compiler_params=pltpu.CompilerParams(vmem_limit_bytes=needed + 6 * 2**20),
         cost_estimate=pl.CostEstimate(
             flops=2 * rows * count * depth * width,
             bytes_accessed=2 * count * depth * (rows + width) + 8 * rows * columns,
             transcendentals=0,
         ),
     )(*operands)
-    return tuple(results) if with_squares else results[0]
+    return tuple(results) if spans is not None else results[0]
 
 
 def attention(total, sums, cosine, sine, starts, query_gain, key_gain, tensor_size, half_rows):
@@ -254,7 +296,7 @@
         + [by_rows(HEAD_DIM)] * 3
         + [constant(q_width), constant(k_width)],
         out_specs=by_rows(q_width),
-        compiler_params=pltpu.CompilerParams(vmem_limit_bytes=40 * 2**20),
+        compiler_params=pltpu.CompilerParams(vmem_limit_bytes=24 * 2**20),
         cost_estimate=pl.CostEstimate(
             flops=4 * capacity * half_rows * q_width,
             bytes_accessed=8 * capacity * total.shape[1],
@@ -296,7 +338,7 @@
             pl.BlockSpec((1, width), lambda i: (0, 0)),
         ],
         out_specs=pl.BlockSpec((tile, width), lambda i: (i, 0)),
-        compiler_params=pltpu.CompilerParams(vmem_limit_bytes=32 * 2**20),
+        compiler_params=pltpu.CompilerParams(vmem_limit_bytes=16 * 2**20),
     )(live_rows, attn_out, *sums, tokens, out_gain)
 
 
@@ -307,12 +349,6 @@
     capacity, width = tokens.shape
     half_rows = capacity // 2
     per_tensor = n // tensor_size
-    f_index = lax.axis_index("fsdp")
-    t_index = lax.axis_index("tensor")
-    order = snake(n)
-    place = [order.index(f) for f in range(n)]
-    order_of = jnp.array(order, jnp.int32)
-    position = jnp.array(place, jnp.int32)[f_index]
 
     weights = jnp.concatenate([w_query, w_key, w_value], axis=1)
     depth = weights.shape[0]
@@ -335,31 +371,28 @@
     q_width, k_width = w_query.shape[1], w_key.shape[1]
     columns = weights.shape[1]
     steps = [[0, n // 2]] + [[s, n - s] for s in range(n // 2 + 1, n)]
-    early = [offset for group in steps[: len(steps) // 2] for offset in group]
-    late = [offset for group in steps[len(steps) // 2 :] for offset in group]
-
-    def source_blocks(offsets):
-        return [order_of[lax.rem(position + offset, n)] for offset in offsets]
+    middle = (len(steps) + 1) // 2
+    groups = [[offset for group in steps[:middle] for offset in group]] + steps[middle:]
+
+    def choose_tokens(offset):
+        block = snake_block(sizes, lax.axis_index("fsdp"), offset)
+        which = (block // per_tensor) ^ lax.axis_index("tensor")
+        return which, lax.rem(block, per_tensor) * depth, 0
 
     total = None
-    for offsets in (early, late):
-        choices = []
-        for block in source_blocks(offsets):
-            choices += [
-                (block // per_tensor) ^ t_index,
-                lax.rem(block, per_tensor) * depth,
-                jnp.int32(0),
-            ]
+    for number, offsets in enumerate(groups):
         total = block_product(
             sizes,
             token_blocks,
-            choices,
-            [tops[(n - offset) % n] for offset in offsets],
-            [bottoms[offset] for offset in offsets],
+            choose_tokens,
+            offsets,
+            tops,
+            bottoms,
             total,
             columns,
-            False,
+            [(0, q_width), (q_width, q_width + k_width)] if number == len(groups) - 1 else None,
         )
+    total, squares = total
 
     out_half = w_out.shape[0] // 2
     out_top, out_bottom, _ = lax.optimization_barrier(
@@ -367,10 +400,6 @@
     )
     out_tops, out_bottoms = ring_gather(out_top, out_bottom, sizes)
 
-    query = total[:, :q_width]
-    key = total[:, q_width : q_width + k_width]
-    squares = jnp.stack([jnp.sum(query * query, axis=1), jnp.sum(key * key, axis=1)])
-    squares = jnp.concatenate([squares, jnp.zeros((6, capacity), jnp.float32)])
     square_blocks = gather_tensor(squares, sizes)
     row_ids = jnp.arange(capacity, dtype=jnp.int32)
     positions = (row_ids - first_row).astype(jnp.float32)
@@ -393,27 +422,24 @@
     )
     attended_blocks = gather_tensor(attended, sizes)
 
-    reversed_of = jnp.array(
-        [reverse_bits(t, tensor_size) for t in range(tensor_size)], jnp.int32
-    )
+    def choose_attended(offset):
+        block = snake_block(sizes, lax.axis_index("fsdp"), offset)
+        t_index = lax.axis_index("tensor")
+        source = traced_reverse((block // per_tensor) ^ t_index, tensor_size)
+        return source ^ t_index, 0, lax.rem(block, per_tensor) * w_out.shape[1]
+
     attn_out = None
-    for offsets in (early, late):
-        choices = []
-        for block in source_blocks(offsets):
-            choices += [
-                reversed_of[(block // per_tensor) ^ t_index] ^ t_index,
-                jnp.int32(0),
-                lax.rem(block, per_tensor) * w_out.shape[1],
-            ]
+    for number, offsets in enumerate(groups):
         attn_out = block_product(
             sizes,
             attended_blocks,
-            choices,
-            [out_tops[(n - offset) % n] for offset in offsets],
-            [out_bottoms[offset] for offset in offsets],
+            choose_attended,
+            offsets,
+            out_tops,
+            out_bottoms,
             attn_out,
             width,
-            offsets is late,
+            [(0, width)] if number == len(groups) - 1 else None,
         )
     attn_out, out_squares = attn_out
     return finish(

time: 248 us -> 209 us (0.84)
  waiting for transfers between devices: 76.8 us -> 116 us
  between operations: 33 us -> 0.93 us
  local copies, waits for them, and re-layouts: 31 us -> 3.49 us
  starting transfers between devices: 58.1 us -> 47.1 us
  other arithmetic: 4.87 us -> 1.73 us
  Pallas kernels: 42 us -> 39.4 us
    ppermute x42, waiting for transfers between devices: 76.8 us -> 116 us  [permute(): return lax.ppermute(array, AXES, pairs)]
    unnamed x100 -> x14, local copies, waits for them, and re-layouts: 26.1 us -> 2.2 us
    ppermute x42, starting transfers between devices: 58.1 us -> 47.1 us  [permute(): return lax.ppermute(array, AXES, pairs)]
    reduce_sum x2 -> x0, other arithmetic: 3.06 us -> none  [the longest x1 1.74 us: body(): jnp.sum(query * query, axis=1)]
    pallas_call x4 -> x6, Pallas kernels: 35.2 us -> 32.6 us  [block_product(): pl.pallas_call(kernel, out_shape=out_shape, in_specs=[any_space] * len(op...]
  transfers between devices with their start and end apart: 42 -> 42, of which waited for: 16 -> 17; matrix products, arithmetic and copies ran while one was open for 5% -> 2% of each run, Pallas kernels for 13% -> 15%
where the time goes in v3:
time: 209 us
  waiting for transfers between devices  116 us (56%)
  starting transfers between devices  47.1 us (23%)
  Pallas kernels  39.4 us (19%)
  local copies, waits for them, and re-layouts  3.49 us (2%)
    ppermute x42, waiting for transfers between devices, permute(): return lax.ppermute(array, AXES, pairs)  116 us
    ppermute x42, starting transfers between devices, permute(): return lax.ppermute(array, AXES, pairs)  47.1 us
    pallas_call x6, Pallas kernels, block_product(): pl.pallas_call(kernel, out_shape=out_shape, in_specs=[any_space] * len(op...  32.6 us
    pallas_call x1, Pallas kernels, attention(): pl.pallas_call(kernel, grid=(capacity // half_rows,), out_shape=jax.Shape...  4.42 us
  transfers between devices with their start and end apart: 42, of which 17 were waited for; matrix products, arithmetic and copies ran while one was open for 2% of the time, Pallas kernels for 15%

profile of v3, /device:TPU:0, one launch (start us, length us, event | category | flops | bytes accessed | tf_op | source)
XLA Modules:
  0.0 209.2 jit_solution(2617822845927565284)
XLA Ops:
  0.0 3.0 %collective-permute-start.1 = (bf16[768,1280]{1,0:T(8,128)(2,1)}, bf16[768,1280]{1,0:T(8,128)(2,1)S(1)}, u32[]{:S(2)}, u32[]{:S(2)}) collective-permute-start(bf16[768,1280]{1,0:T(8,128)(2,1)} %refs_6_.1), channel_id=1, source_target_pairs={{0,2},{1,3},{2,0},{3,1},{4,6},{5,7},{6,4},{7,5},{8,10},{9,11},{10,... | collective-permute-start | bytes 5898248 | tf_op jit(solution)/shard_map/ppermute | solution.py:23
  3.0 1.2 constant_dynamic-update-slice_fusion.2
  4.3 1.0 constant_dynamic-update-slice_fusion.1
  5.2 1.0 constant_dynamic-update-slice_fusion
  6.2 0.1 fusion.1
  6.3 1.5 collective-permute-start.10
  7.8 0.5 collective-permute-start.3
  8.4 12.4 %collective-permute-done.10.refs_7_ = bf16[320,896]{1,0:T(8,128)(2,1)S(1)} collective-permute-done((bf16[320,896]{1,0:T(8,128)(2,1)S(1)}, bf16[320,896]{1,0:T(8,128)(2,1)S(1)}, u32[]{:S(2)}, u32[]{:S(2)}) %collective-permute-start.10) | collective-permute-done | bytes 573472 | tf_op jit(solution)/shard_map/ppermute | solution.py:23
  20.8 1.5 collective-permute-start.11
  22.3 0.5 collective-permute-start.4
  22.8 11.5 %collective-permute-done.11.refs_7_ = bf16[320,896]{1,0:T(8,128)(2,1)S(1)} collective-permute-done((bf16[320,896]{1,0:T(8,128)(2,1)S(1)}, bf16[320,896]{1,0:T(8,128)(2,1)S(1)}, u32[]{:S(2)}, u32[]{:S(2)}) %collective-permute-start.11) | collective-permute-done | bytes 573472 | tf_op jit(solution)/shard_map/ppermute | solution.py:23
  34.3 1.5 collective-permute-start.12
  35.8 0.5 collective-permute-start.5
  36.3 11.1 %collective-permute-done.12.refs_11_ = bf16[320,896]{1,0:T(8,128)(2,1)S(1)} collective-permute-done((bf16[320,896]{1,0:T(8,128)(2,1)S(1)}, bf16[320,896]{1,0:T(8,128)(2,1)S(1)}, u32[]{:S(2)}, u32[]{:S(2)}) %collective-permute-start.12) | collective-permute-done | bytes 573472 | tf_op jit(solution)/shard_map/ppermute | solution.py:23
  47.4 1.5 collective-permute-start.13
  48.9 0.5 collective-permute-start.6
  49.5 0.5 collective-permute-start.2
  50.0 0.7 collective-permute-start.23
  50.7 12.6 %collective-permute-done.13.refs_9_ = bf16[320,896]{1,0:T(8,128)(2,1)S(1)} collective-permute-done((bf16[320,896]{1,0:T(8,128)(2,1)S(1)}, bf16[320,896]{1,0:T(8,128)(2,1)S(1)}, u32[]{:S(2)}, u32[]{:S(2)}) %collective-permute-start.13) | collective-permute-done | bytes 573472 | tf_op jit(solution)/shard_map/ppermute | solution.py:23
  63.4 10.4 %collective-permute-start.7 = (bf16[320,896]{1,0:T(8,128)(2,1)S(1)}, bf16[320,896]{1,0:T(8,128)(2,1)S(1)}, u32[]{:S(2)}, u32[]{:S(2)}) collective-permute-start(bf16[320,896]{1,0:T(8,128)(2,1)S(1)} %collective-permute-done.6.refs_5_), channel_id=1, source_target_pairs={{0,8},{1,9},{2,10},{3,11},{4,0},{5,1},{6,2},{7,3},{8,16},{9,17},{1... | collective-permute-start | bytes 1720328 | tf_op jit(solution)/shard_map/ppermute | solution.py:23
  73.7 0.7 collective-permute-start.24
  74.4 9.5 %collective-permute-done.14.refs_10_ = bf16[320,896]{1,0:T(8,128)(2,1)S(1)} collective-permute-done((bf16[320,896]{1,0:T(8,128)(2,1)S(1)}, bf16[320,896]{1,0:T(8,128)(2,1)S(1)}, u32[]{:S(2)}, u32[]{:S(2)}) %collective-permute-start.14) | collective-permute-done | bytes 573472 | tf_op jit(solution)/shard_map/ppermute | solution.py:23
  83.9 5.7 %collective-permute-start.8 = (bf16[320,896]{1,0:T(8,128)(2,1)S(1)}, bf16[320,896]{1,0:T(8,128)(2,1)S(1)}, u32[]{:S(2)}, u32[]{:S(2)}) collective-permute-start(bf16[320,896]{1,0:T(8,128)(2,1)S(1)} %collective-permute-done.7.refs_7_), channel_id=1, source_target_pairs={{0,8},{1,9},{2,10},{3,11},{4,0},{5,1},{6,2},{7,3},{8,16},{9,17},{1... | collective-permute-start | bytes 1720328 | tf_op jit(solution)/shard_map/ppermute | solution.py:23
  89.7 13.5 %collective-permute-done.15.refs_6_ = bf16[320,896]{1,0:T(8,128)(2,1)S(1)} collective-permute-done((bf16[320,896]{1,0:T(8,128)(2,1)S(1)}, bf16[320,896]{1,0:T(8,128)(2,1)S(1)}, u32[]{:S(2)}, u32[]{:S(2)}) %collective-permute-start.15) | collective-permute-done | bytes 573472 | tf_op jit(solution)/shard_map/ppermute | solution.py:23
  103.1 2.2 %collective-permute-start.9 = (bf16[320,896]{1,0:T(8,128)(2,1)S(1)}, bf16[320,896]{1,0:T(8,128)(2,1)S(1)}, u32[]{:S(2)}, u32[]{:S(2)}) collective-permute-start(bf16[320,896]{1,0:T(8,128)(2,1)S(1)} %collective-permute-done.8.refs_5_), channel_id=1, source_target_pairs={{0,8},{1,9},{2,10},{3,11},{4,0},{5,1},{6,2},{7,3},{8,16},{9,17},{1... | collective-permute-start | bytes 1720328 | tf_op jit(solution)/shard_map/ppermute | solution.py:23
  105.5 6.8 %shard_map.100.refs_8_ = f32[768,896]{1,0:T(8,128)S(1)} custom-call(bf16[768,1280]{1,0:T(8,128)(2,1)S(1)} %copy-done, bf16[768,1280]{1,0:T(8,128)(2,1)S(1)} %collective-permute-done.refs_1_, bf16[768,1280]{1,0:T(8,128)(2,1)S(1)} %collective-permute-done.1.refs_2_, bf16[768,1280]{1,0:T(8,128)(2,1)S(1)} %collective-permute-done.2.refs_3_, ...), custom_call_target="tpu_custom_call" | custom-call | flops 3523215360 | bytes 14024704 | tf_op jit(solution)/shard_map/pallas_call | solution.py:196
  112.3 4.7 %shard_map.101.refs_8_ = f32[768,896]{1,0:T(8,128)S(1)} custom-call(bf16[768,1280]{1,0:T(8,128)(2,1)S(1)} %copy-done, bf16[768,1280]{1,0:T(8,128)(2,1)S(1)} %collective-permute-done.refs_1_, bf16[768,1280]{1,0:T(8,128)(2,1)S(1)} %collective-permute-done.1.refs_2_, bf16[768,1280]{1,0:T(8,128)(2,1)S(1)} %collective-permute-done.2.refs_3_, ...), custom_call_target="tpu_custom_call" | custom-call | flops 1761607680 | bytes 9764864 | tf_op jit(solution)/shard_map/pallas_call | solution.py:196
  116.9 1.7 collective-permute-done.16.refs_6_
  118.6 1.0 collective-permute-done.9.refs_5_
  119.7 0.7 collective-permute-start.25
  120.4 1.3 collective-permute-start.32
  121.7 5.4 %shard_map.102 = (f32[768,896]{1,0:T(8,128)S(1)}, f32[8,768]{1,0:T(8,128)S(1)}) custom-call(bf16[768,1280]{1,0:T(8,128)(2,1)S(1)} %copy-done, bf16[768,1280]{1,0:T(8,128)(2,1)S(1)} %collective-permute-done.refs_1_, bf16[768,1280]{1,0:T(8,128)(2,1)S(1)} %collective-permute-done.1.refs_2_, bf16[768,1280]{1,0:T(8,128)(2,1)S(1)} %collective-permute-done.2.refs_3_, ...), custom_call_target="tpu_custom_call" | custom-call | flops 1761607680 | bytes 9764864 | tf_op jit(solution)/shard_map/pallas_call | solution.py:196
  127.1 0.4 collective-permute-start.18
  127.5 1.4 fusion
  129.0 2.0 collective-permute-done.18.refs_3_
  131.0 0.7 collective-permute-start.26
  131.7 1.3 collective-permute-start.33
  133.0 0.3 pad_maximum_fusion
  133.3 0.2 broadcast_in_dim.8.refs_7_
  133.5 4.4 %shard_map.103.refs_0_ = bf16[768,640]{1,0:T(8,128)(2,1)S(1)} custom-call(f32[768,896]{1,0:T(8,128)S(1)} %get-tuple-element.11.refs_0_, f32[8,768]{1,0:T(8,128)S(1)} %get-tuple-element.12.refs_1_, f32[8,768]{1,0:T(8,128)S(1)} %collective-permute-done.17.refs_2_, f32[8,768]{1,0:T(8,128)S(1)} %collective-permute-done.18.refs_3_, ...), custom_call_target="tpu_custom_call" | custom-call | flops 754974720 | bytes 5505024 | tf_op jit(solution)/shard_map/pallas_call | solution.py:290
  138.0 0.4 collective-permute-start.21
  138.4 4.6 %collective-permute-done.26.refs_4_ = bf16[320,640]{1,0:T(8,128)(2,1)S(1)} collective-permute-done((bf16[320,640]{1,0:T(8,128)(2,1)S(1)}, bf16[320,640]{1,0:T(8,128)(2,1)S(1)}, u32[]{:S(2)}, u32[]{:S(2)}) %collective-permute-start.26) | collective-permute-done | bytes 409632 | tf_op jit(solution)/shard_map/ppermute | solution.py:23
  143.0 0.6 collective-permute-start.27
  143.6 1.4 collective-permute-start.34
  145.0 9.2 %collective-permute-done.27.refs_6_ = bf16[320,640]{1,0:T(8,128)(2,1)S(1)} collective-permute-done((bf16[320,640]{1,0:T(8,128)(2,1)S(1)}, bf16[320,640]{1,0:T(8,128)(2,1)S(1)}, u32[]{:S(2)}, u32[]{:S(2)}) %collective-permute-start.27) | collective-permute-done | bytes 409632 | tf_op jit(solution)/shard_map/ppermute | solution.py:23
  154.2 0.5 collective-permute-start.28
  154.7 1.6 collective-permute-start.35
  156.3 5.6 %collective-permute-done.21.refs_2_ = bf16[768,640]{1,0:T(8,128)(2,1)S(1)} collective-permute-done((bf16[768,640]{1,0:T(8,128)(2,1)S(1)}, bf16[768,640]{1,0:T(8,128)(2,1)S(1)}, u32[]{:S(2)}, u32[]{:S(2)}) %collective-permute-start.21) | collective-permute-done | bytes 983072 | tf_op jit(solution)/shard_map/ppermute | solution.py:23
  161.8 2.8 %collective-permute-done.28.refs_5_ = bf16[320,640]{1,0:T(8,128)(2,1)S(1)} collective-permute-done((bf16[320,640]{1,0:T(8,128)(2,1)S(1)}, bf16[320,640]{1,0:T(8,128)(2,1)S(1)}, u32[]{:S(2)}, u32[]{:S(2)}) %collective-permute-start.28) | collective-permute-done | bytes 409632 | tf_op jit(solution)/shard_map/ppermute | solution.py:23
  164.6 0.3 collective-permute-start.29
  164.9 1.7 collective-permute-start.36
  166.6 7.6 %collective-permute-done.29.refs_7_ = bf16[320,640]{1,0:T(8,128)(2,1)S(1)} collective-permute-done((bf16[320,640]{1,0:T(8,128)(2,1)S(1)}, bf16[320,640]{1,0:T(8,128)(2,1)S(1)}, u32[]{:S(2)}, u32[]{:S(2)}) %collective-permute-start.29) | collective-permute-done | bytes 409632 | tf_op jit(solution)/shard_map/ppermute | solution.py:23
  174.2 0.3 collective-permute-start.30
  174.5 1.7 collective-permute-start.37
  176.3 7.6 %collective-permute-done.30.refs_5_ = bf16[320,640]{1,0:T(8,128)(2,1)S(1)} collective-permute-done((bf16[320,640]{1,0:T(8,128)(2,1)S(1)}, bf16[320,640]{1,0:T(8,128)(2,1)S(1)}, u32[]{:S(2)}, u32[]{:S(2)}) %collective-permute-start.30) | collective-permute-done | bytes 409632 | tf_op jit(solution)/shard_map/ppermute | solution.py:23
  183.9 0.3 collective-permute-start.31
  184.2 1.7 collective-permute-start.38
  185.9 7.1 %shard_map.104.refs_8_ = f32[768,1280]{1,0:T(8,128)S(1)} custom-call(bf16[768,640]{1,0:T(8,128)(2,1)S(1)} %shard_map.103.refs_0_, bf16[768,640]{1,0:T(8,128)(2,1)S(1)} %collective-permute-done.20.refs_1_, bf16[768,640]{1,0:T(8,128)(2,1)S(1)} %collective-permute-done.21.refs_2_, bf16[768,640]{1,0:T(8,128)(2,1)S(1)} %collective-permute-done.22.refs_3_, ...), custom_call_target="tpu_custom_call" | custom-call | flops 2516582400 | bytes 15073280 | tf_op jit(solution)/shard_map/pallas_call | solution.py:196
  193.0 4.0 %shard_map.105.refs_8_ = f32[768,1280]{1,0:T(8,128)S(1)} custom-call(bf16[768,640]{1,0:T(8,128)(2,1)S(1)} %shard_map.103.refs_0_, bf16[768,640]{1,0:T(8,128)(2,1)S(1)} %collective-permute-done.20.refs_1_, bf16[768,640]{1,0:T(8,128)(2,1)S(1)} %collective-permute-done.21.refs_2_, bf16[768,640]{1,0:T(8,128)(2,1)S(1)} %collective-permute-done.22.refs_3_, ...), custom_call_target="tpu_custom_call" | custom-call | flops 1258291200 | bytes 11468800 | tf_op jit(solution)/shard_map/pallas_call | solution.py:196
  197.1 4.6 %shard_map.106 = (f32[768,1280]{1,0:T(8,128)S(1)}, f32[8,768]{1,0:T(8,128)S(1)}) custom-call(bf16[768,640]{1,0:T(8,128)(2,1)S(1)} %shard_map.103.refs_0_, bf16[768,640]{1,0:T(8,128)(2,1)S(1)} %collective-permute-done.20.refs_1_, bf16[768,640]{1,0:T(8,128)(2,1)S(1)} %collective-permute-done.21.refs_2_, bf16[768,640]{1,0:T(8,128)(2,1)S(1)} %collective-permute-done.22.refs_3_, ...), custom_call_target="tpu_custom_call" | custom-call | flops 1258291200 | bytes 11468800 | tf_op jit(solution)/shard_map/pallas_call | solution.py:196
  201.7 0.6 collective-permute-start.40
  202.4 3.2 %collective-permute-done.40.refs_4_ = f32[8,768]{1,0:T(8,128)S(1)} collective-permute-done((f32[8,768]{1,0:T(8,128)S(1)}, f32[8,768]{1,0:T(8,128)S(1)}, u32[]{:S(2)}, u32[]{:S(2)}) %collective-permute-start.40) | collective-permute-done | bytes 24608 | tf_op jit(solution)/shard_map/ppermute | solution.py:23
  206.3 0.5 collective-permute-done.41.refs_5_
  206.8 2.4 %shard_map.107 = bf16[768,1280]{1,0:T(8,128)(2,1)} custom-call(s32[1]{0:T(128)S(6)} %copy.13.refs_0_, f32[768,1280]{1,0:T(8,128)S(1)} %get-tuple-element.15.refs_1_, f32[8,768]{1,0:T(8,128)S(1)} %get-tuple-element.16.refs_2_, f32[8,768]{1,0:T(8,128)S(1)} %collective-permute-done.39.refs_3_, f32[8,768]{1,0:T(8,128)S(1)} %collective-permute-done.40.refs_4_, ...), custom_call_target="tpu_custom_call" | custom-call | tf_op jit(solution)/shard_map/pallas_call | solution.py:327
  (52 shorter events, 0.3 us)
Async XLA Ops:
  0.0 49.5 %copy-start = (bf16[768,1280]{1,0:T(8,128)(2,1)S(1)}, bf16[768,1280]{1,0:T(8,128)(2,1)}, u32[]{:S(2)}) copy-start(bf16[768,1280]{1,0:T(8,128)(2,1)} %refs_6_.1) | copy-start | bytes 5898244
  0.0 50.0 %copy-start.5 = (bf16[640,640]{1,0:T(8,128)(2,1)S(1)}, bf16[640,640]{1,0:T(8,128)(2,1)}, u32[]{:S(2)}) copy-start(bf16[640,640]{1,0:T(8,128)(2,1)} %param.16) | copy-start | bytes 2457604
  0.0 89.6 %copy-start.2 = (s32[768]{0:T(1024)S(1)}, s32[768]{0:T(1024)}, u32[]{:S(2)}) copy-start(s32[768]{0:T(1024)} %param.12) | copy-start | bytes 9220
  0.0 49.5 %collective-permute-start.1 = (bf16[768,1280]{1,0:T(8,128)(2,1)}, bf16[768,1280]{1,0:T(8,128)(2,1)S(1)}, u32[]{:S(2)}, u32[]{:S(2)}) collective-permute-start(bf16[768,1280]{1,0:T(8,128)(2,1)} %refs_6_.1), channel_id=1, source_target_pairs={{0,2},{1,3},{2,0},{3,1},{4,6},{5,7},{6,4},{7,5},{8,10},{9,11},{10,... | collective-permute-start | bytes 5898248 | tf_op jit(solution)/shard_map/ppermute | solution.py:23
  6.3 14.5 %collective-permute-start.10 = (bf16[320,896]{1,0:T(8,128)(2,1)S(1)}, bf16[320,896]{1,0:T(8,128)(2,1)S(1)}, u32[]{:S(2)}, u32[]{:S(2)}) collective-permute-start(bf16[320,896]{1,0:T(8,128)(2,1)S(1)} %get-tuple-element.17.refs_8_), channel_id=1, source_target_pairs={{0,4},{1,5},{2,6},{3,7},{4,12},{5,13},{6,14},{7,15},{8,0},{9,1},{1... | collective-permute-start | bytes 1720328 | tf_op jit(solution)/shard_map/ppermute | solution.py:23
  7.8 14.4 %collective-permute-start.3 = (bf16[320,896]{1,0:T(8,128)(2,1)S(1)}, bf16[320,896]{1,0:T(8,128)(2,1)S(1)}, u32[]{:S(2)}, u32[]{:S(2)}) collective-permute-start(bf16[320,896]{1,0:T(8,128)(2,1)S(1)} %get-tuple-element.18.refs_4_), channel_id=1, source_target_pairs={{0,8},{1,9},{2,10},{3,11},{4,0},{5,1},{6,2},{7,3},{8,16},{9,17},{1... | collective-permute-start | bytes 1720328 | tf_op jit(solution)/shard_map/ppermute | solution.py:23
  20.8 13.5 %collective-permute-start.11 = (bf16[320,896]{1,0:T(8,128)(2,1)S(1)}, bf16[320,896]{1,0:T(8,128)(2,1)S(1)}, u32[]{:S(2)}, u32[]{:S(2)}) collective-permute-start(bf16[320,896]{1,0:T(8,128)(2,1)S(1)} %collective-permute-done.10.refs_7_), channel_id=1, source_target_pairs={{0,4},{1,5},{2,6},{3,7},{4,12},{5,13},{6,14},{7,15},{8,0},{9,1},{1... | collective-permute-start | bytes 1720328 | tf_op jit(solution)/shard_map/ppermute | solution.py:23
  22.3 13.5 %collective-permute-start.4 = (bf16[320,896]{1,0:T(8,128)(2,1)S(1)}, bf16[320,896]{1,0:T(8,128)(2,1)S(1)}, u32[]{:S(2)}, u32[]{:S(2)}) collective-permute-start(bf16[320,896]{1,0:T(8,128)(2,1)S(1)} %collective-permute-done.3.refs_4_), channel_id=1, source_target_pairs={{0,8},{1,9},{2,10},{3,11},{4,0},{5,1},{6,2},{7,3},{8,16},{9,17},{1... | collective-permute-start | bytes 1720328 | tf_op jit(solution)/shard_map/ppermute | solution.py:23
  34.3 13.1 %collective-permute-start.12 = (bf16[320,896]{1,0:T(8,128)(2,1)S(1)}, bf16[320,896]{1,0:T(8,128)(2,1)S(1)}, u32[]{:S(2)}, u32[]{:S(2)}) collective-permute-start(bf16[320,896]{1,0:T(8,128)(2,1)S(1)} %collective-permute-done.11.refs_7_), channel_id=1, source_target_pairs={{0,4},{1,5},{2,6},{3,7},{4,12},{5,13},{6,14},{7,15},{8,0},{9,1},{1... | collective-permute-start | bytes 1720328 | tf_op jit(solution)/shard_map/ppermute | solution.py:23
  35.8 13.1 %collective-permute-start.5 = (bf16[320,896]{1,0:T(8,128)(2,1)S(1)}, bf16[320,896]{1,0:T(8,128)(2,1)S(1)}, u32[]{:S(2)}, u32[]{:S(2)}) collective-permute-start(bf16[320,896]{1,0:T(8,128)(2,1)S(1)} %collective-permute-done.4.refs_4_), channel_id=1, source_target_pairs={{0,8},{1,9},{2,10},{3,11},{4,0},{5,1},{6,2},{7,3},{8,16},{9,17},{1... | collective-permute-start | bytes 1720328 | tf_op jit(solution)/shard_map/ppermute | solution.py:23
  47.4 15.9 %collective-permute-start.13 = (bf16[320,896]{1,0:T(8,128)(2,1)S(1)}, bf16[320,896]{1,0:T(8,128)(2,1)S(1)}, u32[]{:S(2)}, u32[]{:S(2)}) collective-permute-start(bf16[320,896]{1,0:T(8,128)(2,1)S(1)} %collective-permute-done.12.refs_11_), channel_id=1, source_target_pairs={{0,4},{1,5},{2,6},{3,7},{4,12},{5,13},{6,14},{7,15},{8,0},{9,1},{1... | collective-permute-start | bytes 1720328 | tf_op jit(solution)/shard_map/ppermute | solution.py:23
  48.9 14.4 %collective-permute-start.6 = (bf16[320,896]{1,0:T(8,128)(2,1)S(1)}, bf16[320,896]{1,0:T(8,128)(2,1)S(1)}, u32[]{:S(2)}, u32[]{:S(2)}) collective-permute-start(bf16[320,896]{1,0:T(8,128)(2,1)S(1)} %collective-permute-done.5.refs_6_), channel_id=1, source_target_pairs={{0,8},{1,9},{2,10},{3,11},{4,0},{5,1},{6,2},{7,3},{8,16},{9,17},{1... | collective-permute-start | bytes 1720328 | tf_op jit(solution)/shard_map/ppermute | solution.py:23
  49.5 56.0 %collective-permute-start = (bf16[768,1280]{1,0:T(8,128)(2,1)S(1)}, bf16[768,1280]{1,0:T(8,128)(2,1)S(1)}, u32[]{:S(2)}, u32[]{:S(2)}) collective-permute-start(bf16[768,1280]{1,0:T(8,128)(2,1)S(1)} %copy-done), channel_id=1, source_target_pairs={{0,1},{1,0},{2,3},{3,2},{4,5},{5,4},{6,7},{7,6},{8,9},{9,8},{10,11... | collective-permute-start | bytes 5898248 | tf_op jit(solution)/shard_map/ppermute | solution.py:23
  49.5 56.0 %collective-permute-start.2 = (bf16[768,1280]{1,0:T(8,128)(2,1)S(1)}, bf16[768,1280]{1,0:T(8,128)(2,1)S(1)}, u32[]{:S(2)}, u32[]{:S(2)}) collective-permute-start(bf16[768,1280]{1,0:T(8,128)(2,1)S(1)} %collective-permute-done.1.refs_2_), channel_id=1, source_target_pairs={{0,1},{1,0},{2,3},{3,2},{4,5},{5,4},{6,7},{7,6},{8,9},{9,8},{10,11... | collective-permute-start | bytes 5898248 | tf_op jit(solution)/shard_map/ppermute | solution.py:23
  50.0 23.7 %collective-permute-start.23 = (bf16[640,640]{1,0:T(8,128)(2,1)S(1)}, bf16[640,640]{1,0:T(8,128)(2,1)S(1)}, u32[]{:S(2)}, u32[]{:S(2)}) collective-permute-start(bf16[640,640]{1,0:T(8,128)(2,1)S(1)} %copy-done.5), channel_id=1, source_target_pairs={{0,0},{1,17},{2,10},{3,27},{4,4},{5,21},{6,14},{7,31},{8,8},{9,25}... | collective-permute-start | bytes 2457608 | tf_op jit(solution)/shard_map/ppermute | solution.py:23
  63.3 20.6 %collective-permute-start.14 = (bf16[320,896]{1,0:T(8,128)(2,1)S(1)}, bf16[320,896]{1,0:T(8,128)(2,1)S(1)}, u32[]{:S(2)}, u32[]{:S(2)}) collective-permute-start(bf16[320,896]{1,0:T(8,128)(2,1)S(1)} %collective-permute-done.13.refs_9_), channel_id=1, source_target_pairs={{0,4},{1,5},{2,6},{3,7},{4,12},{5,13},{6,14},{7,15},{8,0},{9,1},{1... | collective-permute-start | bytes 1720328 | tf_op jit(solution)/shard_map/ppermute | solution.py:23
  63.4 20.6 %collective-permute-start.7 = (bf16[320,896]{1,0:T(8,128)(2,1)S(1)}, bf16[320,896]{1,0:T(8,128)(2,1)S(1)}, u32[]{:S(2)}, u32[]{:S(2)}) collective-permute-start(bf16[320,896]{1,0:T(8,128)(2,1)S(1)} %collective-permute-done.6.refs_5_), channel_id=1, source_target_pairs={{0,8},{1,9},{2,10},{3,11},{4,0},{5,1},{6,2},{7,3},{8,16},{9,17},{1... | collective-permute-start | bytes 1720328 | tf_op jit(solution)/shard_map/ppermute | solution.py:23
  73.7 31.6 %collective-permute-start.24 = (bf16[640,640]{1,0:T(8,128)(2,1)S(1)}, bf16[640,640]{1,0:T(8,128)(2,1)S(1)}, u32[]{:S(2)}, u32[]{:S(2)}) collective-permute-start(bf16[640,640]{1,0:T(8,128)(2,1)S(1)} %collective-permute-done.23), channel_id=1, source_target_pairs={{0,0},{1,2},{2,1},{3,3},{4,4},{5,6},{6,5},{7,7},{8,9},{9,11},{10,8... | collective-permute-start | bytes 2457608 | tf_op jit(solution)/shard_map/ppermute | solution.py:23
  83.9 19.2 %collective-permute-start.15 = (bf16[320,896]{1,0:T(8,128)(2,1)S(1)}, bf16[320,896]{1,0:T(8,128)(2,1)S(1)}, u32[]{:S(2)}, u32[]{:S(2)}) collective-permute-start(bf16[320,896]{1,0:T(8,128)(2,1)S(1)} %collective-permute-done.14.refs_10_), channel_id=1, source_target_pairs={{0,4},{1,5},{2,6},{3,7},{4,12},{5,13},{6,14},{7,15},{8,0},{9,1},{1... | collective-permute-start | bytes 1720328 | tf_op jit(solution)/shard_map/ppermute | solution.py:23
  83.9 19.2 %collective-permute-start.8 = (bf16[320,896]{1,0:T(8,128)(2,1)S(1)}, bf16[320,896]{1,0:T(8,128)(2,1)S(1)}, u32[]{:S(2)}, u32[]{:S(2)}) collective-permute-start(bf16[320,896]{1,0:T(8,128)(2,1)S(1)} %collective-permute-done.7.refs_7_), channel_id=1, source_target_pairs={{0,8},{1,9},{2,10},{3,11},{4,0},{5,1},{6,2},{7,3},{8,16},{9,17},{1... | collective-permute-start | bytes 1720328 | tf_op jit(solution)/shard_map/ppermute | solution.py:23
  103.1 15.5 %collective-permute-start.16 = (bf16[320,896]{1,0:T(8,128)(2,1)S(1)}, bf16[320,896]{1,0:T(8,128)(2,1)S(1)}, u32[]{:S(2)}, u32[]{:S(2)}) collective-permute-start(bf16[320,896]{1,0:T(8,128)(2,1)S(1)} %collective-permute-done.15.refs_6_), channel_id=1, source_target_pairs={{0,4},{1,5},{2,6},{3,7},{4,12},{5,13},{6,14},{7,15},{8,0},{9,1},{1... | collective-permute-start | bytes 1720328 | tf_op jit(solution)/shard_map/ppermute | solution.py:23
  103.1 16.5 %collective-permute-start.9 = (bf16[320,896]{1,0:T(8,128)(2,1)S(1)}, bf16[320,896]{1,0:T(8,128)(2,1)S(1)}, u32[]{:S(2)}, u32[]{:S(2)}) collective-permute-start(bf16[320,896]{1,0:T(8,128)(2,1)S(1)} %collective-permute-done.8.refs_5_), channel_id=1, source_target_pairs={{0,8},{1,9},{2,10},{3,11},{4,0},{5,1},{6,2},{7,3},{8,16},{9,17},{1... | collective-permute-start | bytes 1720328 | tf_op jit(solution)/shard_map/ppermute | solution.py:23
  119.7 11.3 %collective-permute-start.25 = (bf16[320,640]{1,0:T(8,128)(2,1)S(1)}, bf16[320,640]{1,0:T(8,128)(2,1)S(1)}, u32[]{:S(2)}, u32[]{:S(2)}) collective-permute-start(bf16[320,640]{1,0:T(8,128)(2,1)S(1)} %get-tuple-element.13.refs_4_), channel_id=1, source_target_pairs={{0,8},{1,9},{2,10},{3,11},{4,0},{5,1},{6,2},{7,3},{8,16},{9,17},{1... | collective-permute-start | bytes 1228808 | tf_op jit(solution)/shard_map/ppermute | solution.py:23
  120.4 11.4 %collective-permute-start.32 = (bf16[320,640]{1,0:T(8,128)(2,1)S(1)}, bf16[320,640]{1,0:T(8,128)(2,1)S(1)}, u32[]{:S(2)}, u32[]{:S(2)}) collective-permute-start(bf16[320,640]{1,0:T(8,128)(2,1)S(1)} %get-tuple-element.14.refs_8_), channel_id=1, source_target_pairs={{0,4},{1,5},{2,6},{3,7},{4,12},{5,13},{6,14},{7,15},{8,0},{9,1},{1... | collective-permute-start | bytes 1228808 | tf_op jit(solution)/shard_map/ppermute | solution.py:23
  127.1 6.2 %copy-start.4 = (f32[640]{0:T(1024)S(1)}, f32[640]{0:T(1024)}, u32[]{:S(2)}) copy-start(f32[640]{0:T(1024)} %param.17) | copy-start | bytes 7684
  127.1 6.4 %copy-start.1 = (f32[128]{0:T(128)S(1)}, f32[128]{0:T(128)}, u32[]{:S(2)}) copy-start(f32[128]{0:T(128)} %param.18) | copy-start | bytes 1540
  127.1 3.9 %collective-permute-start.18 = (f32[8,768]{1,0:T(8,128)S(1)}, f32[8,768]{1,0:T(8,128)S(1)}, u32[]{:S(2)}, u32[]{:S(2)}) collective-permute-start(f32[8,768]{1,0:T(8,128)S(1)} %get-tuple-element.12.refs_1_), channel_id=1, source_target_pairs={{0,2},{1,3},{2,0},{3,1},{4,6},{5,7},{6,4},{7,5},{8,10},{9,11},{10,... | collective-permute-start | bytes 73736 | tf_op jit(solution)/shard_map/ppermute | solution.py:23
  128.9 4.4 %collective-permute-start.17 = (f32[8,768]{1,0:T(8,128)S(1)}, f32[8,768]{1,0:T(8,128)S(1)}, u32[]{:S(2)}, u32[]{:S(2)}) collective-permute-start(f32[8,768]{1,0:T(8,128)S(1)} %get-tuple-element.12.refs_1_), channel_id=1, source_target_pairs={{0,1},{1,0},{2,3},{3,2},{4,5},{5,4},{6,7},{7,6},{8,9},{9,8},{10,11... | collective-permute-start | bytes 73736 | tf_op jit(solution)/shard_map/ppermute | solution.py:23
  131.0 2.3 %collective-permute-start.19 = (f32[8,768]{1,0:T(8,128)S(1)}, f32[8,768]{1,0:T(8,128)S(1)}, u32[]{:S(2)}, u32[]{:S(2)}) collective-permute-start(f32[8,768]{1,0:T(8,128)S(1)} %collective-permute-done.18.refs_3_), channel_id=1, source_target_pairs={{0,1},{1,0},{2,3},{3,2},{4,5},{5,4},{6,7},{7,6},{8,9},{9,8},{10,11... | collective-permute-start | bytes 73736 | tf_op jit(solution)/shard_map/ppermute | solution.py:23
  131.0 12.0 %collective-permute-start.26 = (bf16[320,640]{1,0:T(8,128)(2,1)S(1)}, bf16[320,640]{1,0:T(8,128)(2,1)S(1)}, u32[]{:S(2)}, u32[]{:S(2)}) collective-permute-start(bf16[320,640]{1,0:T(8,128)(2,1)S(1)} %collective-permute-done.25.refs_4_), channel_id=1, source_target_pairs={{0,8},{1,9},{2,10},{3,11},{4,0},{5,1},{6,2},{7,3},{8,16},{9,17},{1... | collective-permute-start | bytes 1228808 | tf_op jit(solution)/shard_map/ppermute | solution.py:23
  131.7 11.9 %collective-permute-start.33 = (bf16[320,640]{1,0:T(8,128)(2,1)S(1)}, bf16[320,640]{1,0:T(8,128)(2,1)S(1)}, u32[]{:S(2)}, u32[]{:S(2)}) collective-permute-start(bf16[320,640]{1,0:T(8,128)(2,1)S(1)} %collective-permute-done.32.refs_7_), channel_id=1, source_target_pairs={{0,4},{1,5},{2,6},{3,7},{4,12},{5,13},{6,14},{7,15},{8,0},{9,1},{1... | collective-permute-start | bytes 1228808 | tf_op jit(solution)/shard_map/ppermute | solution.py:23
  138.0 23.9 %collective-permute-start.21 = (bf16[768,640]{1,0:T(8,128)(2,1)S(1)}, bf16[768,640]{1,0:T(8,128)(2,1)S(1)}, u32[]{:S(2)}, u32[]{:S(2)}) collective-permute-start(bf16[768,640]{1,0:T(8,128)(2,1)S(1)} %shard_map.103.refs_0_), channel_id=1, source_target_pairs={{0,2},{1,3},{2,0},{3,1},{4,6},{5,7},{6,4},{7,5},{8,10},{9,11},{10,... | collective-permute-start | bytes 2949128 | tf_op jit(solution)/shard_map/ppermute | solution.py:23
  143.0 11.2 %collective-permute-start.27 = (bf16[320,640]{1,0:T(8,128)(2,1)S(1)}, bf16[320,640]{1,0:T(8,128)(2,1)S(1)}, u32[]{:S(2)}, u32[]{:S(2)}) collective-permute-start(bf16[320,640]{1,0:T(8,128)(2,1)S(1)} %collective-permute-done.26.refs_4_), channel_id=1, source_target_pairs={{0,8},{1,9},{2,10},{3,11},{4,0},{5,1},{6,2},{7,3},{8,16},{9,17},{1... | collective-permute-start | bytes 1228808 | tf_op jit(solution)/shard_map/ppermute | solution.py:23
  143.6 11.1 %collective-permute-start.34 = (bf16[320,640]{1,0:T(8,128)(2,1)S(1)}, bf16[320,640]{1,0:T(8,128)(2,1)S(1)}, u32[]{:S(2)}, u32[]{:S(2)}) collective-permute-start(bf16[320,640]{1,0:T(8,128)(2,1)S(1)} %collective-permute-done.33.refs_7_), channel_id=1, source_target_pairs={{0,4},{1,5},{2,6},{3,7},{4,12},{5,13},{6,14},{7,15},{8,0},{9,1},{1... | collective-permute-start | bytes 1228808 | tf_op jit(solution)/shard_map/ppermute | solution.py:23
  154.2 10.4 %collective-permute-start.28 = (bf16[320,640]{1,0:T(8,128)(2,1)S(1)}, bf16[320,640]{1,0:T(8,128)(2,1)S(1)}, u32[]{:S(2)}, u32[]{:S(2)}) collective-permute-start(bf16[320,640]{1,0:T(8,128)(2,1)S(1)} %collective-permute-done.27.refs_6_), channel_id=1, source_target_pairs={{0,8},{1,9},{2,10},{3,11},{4,0},{5,1},{6,2},{7,3},{8,16},{9,17},{1... | collective-permute-start | bytes 1228808 | tf_op jit(solution)/shard_map/ppermute | solution.py:23
  154.7 10.2 %collective-permute-start.35 = (bf16[320,640]{1,0:T(8,128)(2,1)S(1)}, bf16[320,640]{1,0:T(8,128)(2,1)S(1)}, u32[]{:S(2)}, u32[]{:S(2)}) collective-permute-start(bf16[320,640]{1,0:T(8,128)(2,1)S(1)} %collective-permute-done.34.refs_11_), channel_id=1, source_target_pairs={{0,4},{1,5},{2,6},{3,7},{4,12},{5,13},{6,14},{7,15},{8,0},{9,1},{1... | collective-permute-start | bytes 1228808 | tf_op jit(solution)/shard_map/ppermute | solution.py:23
  156.3 29.6 %collective-permute-start.20 = (bf16[768,640]{1,0:T(8,128)(2,1)S(1)}, bf16[768,640]{1,0:T(8,128)(2,1)S(1)}, u32[]{:S(2)}, u32[]{:S(2)}) collective-permute-start(bf16[768,640]{1,0:T(8,128)(2,1)S(1)} %shard_map.103.refs_0_), channel_id=1, source_target_pairs={{0,1},{1,0},{2,3},{3,2},{4,5},{5,4},{6,7},{7,6},{8,9},{9,8},{10,11... | collective-permute-start | bytes 2949128 | tf_op jit(solution)/shard_map/ppermute | solution.py:23
  161.8 24.1 %collective-permute-start.22 = (bf16[768,640]{1,0:T(8,128)(2,1)S(1)}, bf16[768,640]{1,0:T(8,128)(2,1)S(1)}, u32[]{:S(2)}, u32[]{:S(2)}) collective-permute-start(bf16[768,640]{1,0:T(8,128)(2,1)S(1)} %collective-permute-done.21.refs_2_), channel_id=1, source_target_pairs={{0,1},{1,0},{2,3},{3,2},{4,5},{5,4},{6,7},{7,6},{8,9},{9,8},{10,11... | collective-permute-start | bytes 2949128 | tf_op jit(solution)/shard_map/ppermute | solution.py:23
  164.6 9.6 %collective-permute-start.29 = (bf16[320,640]{1,0:T(8,128)(2,1)S(1)}, bf16[320,640]{1,0:T(8,128)(2,1)S(1)}, u32[]{:S(2)}, u32[]{:S(2)}) collective-permute-start(bf16[320,640]{1,0:T(8,128)(2,1)S(1)} %collective-permute-done.28.refs_5_), channel_id=1, source_target_pairs={{0,8},{1,9},{2,10},{3,11},{4,0},{5,1},{6,2},{7,3},{8,16},{9,17},{1... | collective-permute-start | bytes 1228808 | tf_op jit(solution)/shard_map/ppermute | solution.py:23
  164.9 9.6 %collective-permute-start.36 = (bf16[320,640]{1,0:T(8,128)(2,1)S(1)}, bf16[320,640]{1,0:T(8,128)(2,1)S(1)}, u32[]{:S(2)}, u32[]{:S(2)}) collective-permute-start(bf16[320,640]{1,0:T(8,128)(2,1)S(1)} %collective-permute-done.35.refs_9_), channel_id=1, source_target_pairs={{0,4},{1,5},{2,6},{3,7},{4,12},{5,13},{6,14},{7,15},{8,0},{9,1},{1... | collective-permute-start | bytes 1228808 | tf_op jit(solution)/shard_map/ppermute | solution.py:23
  174.2 9.6 %collective-permute-start.30 = (bf16[320,640]{1,0:T(8,128)(2,1)S(1)}, bf16[320,640]{1,0:T(8,128)(2,1)S(1)}, u32[]{:S(2)}, u32[]{:S(2)}) collective-permute-start(bf16[320,640]{1,0:T(8,128)(2,1)S(1)} %collective-permute-done.29.refs_7_), channel_id=1, source_target_pairs={{0,8},{1,9},{2,10},{3,11},{4,0},{5,1},{6,2},{7,3},{8,16},{9,17},{1... | collective-permute-start | bytes 1228808 | tf_op jit(solution)/shard_map/ppermute | solution.py:23
  174.5 9.6 %collective-permute-start.37 = (bf16[320,640]{1,0:T(8,128)(2,1)S(1)}, bf16[320,640]{1,0:T(8,128)(2,1)S(1)}, u32[]{:S(2)}, u32[]{:S(2)}) collective-permute-start(bf16[320,640]{1,0:T(8,128)(2,1)S(1)} %collective-permute-done.36.refs_10_), channel_id=1, source_target_pairs={{0,4},{1,5},{2,6},{3,7},{4,12},{5,13},{6,14},{7,15},{8,0},{9,1},{1... | collective-permute-start | bytes 1228808 | tf_op jit(solution)/shard_map/ppermute | solution.py:23
  183.9 13.2 %collective-permute-start.31 = (bf16[320,640]{1,0:T(8,128)(2,1)S(1)}, bf16[320,640]{1,0:T(8,128)(2,1)S(1)}, u32[]{:S(2)}, u32[]{:S(2)}) collective-permute-start(bf16[320,640]{1,0:T(8,128)(2,1)S(1)} %collective-permute-done.30.refs_5_), channel_id=1, source_target_pairs={{0,8},{1,9},{2,10},{3,11},{4,0},{5,1},{6,2},{7,3},{8,16},{9,17},{1... | collective-permute-start | bytes 1228808 | tf_op jit(solution)/shard_map/ppermute | solution.py:23
  184.2 12.9 %collective-permute-start.38 = (bf16[320,640]{1,0:T(8,128)(2,1)S(1)}, bf16[320,640]{1,0:T(8,128)(2,1)S(1)}, u32[]{:S(2)}, u32[]{:S(2)}) collective-permute-start(bf16[320,640]{1,0:T(8,128)(2,1)S(1)} %collective-permute-done.37.refs_6_), channel_id=1, source_target_pairs={{0,4},{1,5},{2,6},{3,7},{4,12},{5,13},{6,14},{7,15},{8,0},{9,1},{1... | collective-permute-start | bytes 1228808 | tf_op jit(solution)/shard_map/ppermute | solution.py:23
  197.0 8.6 %copy-start.3 = (f32[1280]{0:T(1024)S(1)}, f32[1280]{0:T(1024)}, u32[]{:S(2)}) copy-start(f32[1280]{0:T(1024)} %param.19) | copy-start | bytes 15364
  201.7 3.9 %collective-permute-start.40 = (f32[8,768]{1,0:T(8,128)S(1)}, f32[8,768]{1,0:T(8,128)S(1)}, u32[]{:S(2)}, u32[]{:S(2)}) collective-permute-start(f32[8,768]{1,0:T(8,128)S(1)} %get-tuple-element.16.refs_2_), channel_id=1, source_target_pairs={{0,2},{1,3},{2,0},{3,1},{4,6},{5,7},{6,4},{7,5},{8,10},{9,11},{10,... | collective-permute-start | bytes 73736 | tf_op jit(solution)/shard_map/ppermute | solution.py:23
  202.3 3.9 %collective-permute-start.39 = (f32[8,768]{1,0:T(8,128)S(1)}, f32[8,768]{1,0:T(8,128)S(1)}, u32[]{:S(2)}, u32[]{:S(2)}) collective-permute-start(f32[8,768]{1,0:T(8,128)S(1)} %get-tuple-element.16.refs_2_), channel_id=1, source_target_pairs={{0,1},{1,0},{2,3},{3,2},{4,5},{5,4},{6,7},{7,6},{8,9},{9,8},{10,11... | collective-permute-start | bytes 73736 | tf_op jit(solution)/shard_map/ppermute | solution.py:23
  205.6 1.2 collective-permute-start.41

commit v4 on v3

--- a/solution.py
+++ b/solution.py
@@ -46,14 +46,63 @@
     return [have[r] for r in range(sizes[1])]
 
 
-def ring_gather(top, bottom, sizes):
+def swap_small(array, sizes):
+    return [array] + [
+        permute(array, sizes, lambda f, t, r=r: (f, t ^ r)) for r in range(1, sizes[1])
+    ]
+
+
+def pack_weights(parts):
+    rows = parts[0].shape[0]
+    half = rows // 2
+    widths = [part.shape[1] for part in parts]
+    if any(width % 128 for width in widths) or half % 16:
+        packed = jnp.concatenate(parts, axis=1)
+        return packed[:half], packed[half:]
+
+    def kernel(*refs):
+        sources, outs, sems = refs[: len(parts)], refs[len(parts) : -1], refs[-1]
+        copies = []
+        first = 0
+        for number, (source, width) in enumerate(zip(sources, widths)):
+            for side in range(2):
+                copies.append(
+                    pltpu.make_async_copy(
+                        source.at[pl.ds(side * half, half)],
+                        outs[side].at[:, pl.ds(first, width)],
+                        sems.at[number, side],
+                    )
+                )
+            first += width
+        for copy in copies:
+            copy.start()
+        for copy in copies:
+            copy.wait()
+
+    shape = jax.ShapeDtypeStruct((half, sum(widths)), parts[0].dtype)
+    any_space = pl.BlockSpec(memory_space=pl.ANY)
+    return pl.pallas_call(
+        kernel,
+        out_shape=[shape, shape],
+        in_specs=[any_space] * len(parts),
+        out_specs=[any_space] * 2,
+        scratch_shapes=[pltpu.SemaphoreType.DMA((len(parts), 2))],
+    )(*parts)
+
+
+def ring_gather(top, bottom, sizes, ties):
     n = sizes[0]
     order = snake(n)
     place = {f: i for i, f in enumerate(order)}
     tops, bottoms = [top], [bottom]
-    for _ in range(n - 1):
+    for step in range(1, n):
         tops.append(permute(tops[-1], sizes, lambda f, t: (order[(place[f] + 1) % n], t)))
         bottoms.append(permute(bottoms[-1], sizes, lambda f, t: (order[(place[f] - 1) % n], t)))
+        if step in ties:
+            tied = ties[step](tops, bottoms)
+            tops[-1], bottoms[-1], ties[step] = lax.optimization_barrier(
+                (tops[-1], bottoms[-1], tied)
+            )
     return tops, bottoms
 
 
@@ -149,39 +198,39 @@
                 copy.start()
         for i in range(tiles * extra):
             in_copy(i).start()
-        for j in range(count):
-            piece_copy(j, 0).wait()
-            for copy in matrix_copies(j):
-                copy.wait()
-        for i in range(tiles):
-            part = pl.ds(i * tile, tile)
-            if extra:
-                in_copy(i).wait()
-            if whole:
-                term = jnp.dot(piece[part, :], matrix[...], preferred_element_type=jnp.float32)
-                total[part, :] = total[part, :] + term if extra else term
-            else:
-                if not extra:
+        together = 2 if whole else 1
+        for low in range(0, count, together):
+            blocks = range(low, min(low + together, count))
+            for j in blocks:
+                piece_copy(j, 0).wait()
+                for copy in matrix_copies(j):
+                    copy.wait()
+            span = pl.ds(low * depth, len(blocks) * depth)
+            for i in range(tiles):
+                part = pl.ds(i * tile, tile)
+                if low == 0 and extra:
+                    in_copy(i).wait()
+                if low == 0 and not extra and not whole:
                     total[part, :] = jnp.zeros((tile, columns), jnp.float32)
-                for j in range(count):
-                    term = jnp.dot(
-                        piece[part, pl.ds(j * depth, depth)],
-                        matrix[pl.ds(j * depth, depth), :],
-                        preferred_element_type=jnp.float32,
-                    )
-                    total[part, pl.ds(pl.multiple_of(choices[j][2], 128), width)] += term
-            out_copy(i).start()
-            if spans is not None:
-                sums = []
-                for low, high in spans:
-                    chosen = total[part, low:high]
-                    chosen = jnp.sum(chosen * chosen, axis=1, keepdims=True)
-                    sums.append(jnp.broadcast_to(chosen, (tile, 128)).T[:8])
-                lines = lax.broadcasted_iota(jnp.int32, (8, tile), 0)
-                line = sums[0]
-                for index in range(1, len(sums)):
-                    line = jnp.where(lines == index, sums[index], line)
-                squares[0][:, part] = line
+                term = jnp.dot(piece[part, span], matrix[span, :], preferred_element_type=jnp.float32)
+                if whole:
+                    total[part, :] = total[part, :] + term if extra or low else term
+                else:
+                    total[part, pl.ds(pl.multiple_of(choices[low][2], 128), width)] += term
+                if blocks[-1] < count - 1:
+                    continue
+                out_copy(i).start()
+                if spans is not None:
+                    sums = []
+                    for first, last in spans:
+                        chosen = total[part, first:last]
+                        chosen = jnp.sum(chosen * chosen, axis=1, keepdims=True)
+                        sums.append(jnp.broadcast_to(chosen, (tile, 128)).T[:8])
+                    lines = lax.broadcasted_iota(jnp.int32, (8, tile), 0)
+                    line = sums[0]
+                    for index in range(1, len(sums)):
+                        line = jnp.where(lines == index, sums[index], line)
+                    squares[0][:, part] = line
         for i in range(tiles):
             out_copy(i).wait()
 
@@ -350,12 +399,9 @@
     half_rows = capacity // 2
     per_tensor = n // tensor_size
 
-    weights = jnp.concatenate([w_query, w_key, w_value], axis=1)
-    depth = weights.shape[0]
-    half = depth // 2
-    token_blocks = gather_tensor(tokens, sizes)
-    tops, bottoms = ring_gather(weights[:half], weights[half:], sizes)
-
+    depth = w_query.shape[0]
+    columns = w_query.shape[1] + w_key.shape[1] + w_value.shape[1]
+    top, bottom = pack_weights([w_query, w_key, w_value])
     moved = permute(
         w_out,
         sizes,
@@ -364,12 +410,16 @@
             t,
         ),
     )
+    local_tokens, top, bottom = lax.optimization_barrier((tokens, top, bottom))
+    token_blocks = gather_tensor(local_tokens, sizes)
+    ties = {2: lambda *_: moved}
+    tops, bottoms = ring_gather(top, bottom, sizes, ties)
+    moved = ties[2]
     moved = permute(
         moved, sizes, lambda f, t: (f, (f // per_tensor) ^ reverse_bits(t, tensor_size))
     )
 
     q_width, k_width = w_query.shape[1], w_key.shape[1]
-    columns = weights.shape[1]
     steps = [[0, n // 2]] + [[s, n - s] for s in range(n // 2 + 1, n)]
     middle = (len(steps) + 1) // 2
     groups = [[offset for group in steps[:middle] for offset in group]] + steps[middle:]
@@ -398,9 +448,7 @@
     out_top, out_bottom, _ = lax.optimization_barrier(
         (moved[:out_half], moved[out_half:], (tops[-1], bottoms[-1]))
     )
-    out_tops, out_bottoms = ring_gather(out_top, out_bottom, sizes)
-
-    square_blocks = gather_tensor(squares, sizes)
+    square_blocks = swap_small(squares, sizes)
     row_ids = jnp.arange(capacity, dtype=jnp.int32)
     positions = (row_ids - first_row).astype(jnp.float32)
     half_dim = HEAD_DIM // 2
@@ -428,23 +476,29 @@
         source = traced_reverse((block // per_tensor) ^ t_index, tensor_size)
         return source ^ t_index, 0, lax.rem(block, per_tensor) * w_out.shape[1]
 
-    attn_out = None
-    for number, offsets in enumerate(groups):
-        attn_out = block_product(
+    def out_product(number, out_tops, out_bottoms, attn_out):
+        return block_product(
             sizes,
             attended_blocks,
             choose_attended,
-            offsets,
+            groups[number],
             out_tops,
             out_bottoms,
             attn_out,
             width,
             [(0, width)] if number == len(groups) - 1 else None,
         )
+
+    ready = max(groups[0])
+    ties = {ready + 1: lambda now_tops, now_bottoms: out_product(0, now_tops, now_bottoms, None)}
+    out_tops, out_bottoms = ring_gather(out_top, out_bottom, sizes, ties)
+    attn_out = ties[ready + 1]
+    for number in range(1, len(groups)):
+        attn_out = out_product(number, out_tops, out_bottoms, attn_out)
     attn_out, out_squares = attn_out
     return finish(
         attn_out,
-        gather_tensor(out_squares, sizes),
+        swap_small(out_squares, sizes),
         tokens,
         out_gain[None, :],
         live_rows,

time: 209 us -> 245 us (1.17)
  Pallas kernels: 39.4 us -> 76.6 us
  starting transfers between devices: 47.1 us -> 53.7 us
  waiting for transfers between devices: 116 us -> 111 us
  local copies, waits for them, and re-layouts: 3.49 us -> 0.27 us
    pallas_call x0 -> x1, Pallas kernels: none -> 35.9 us  [pack_weights(): pl.pallas_call(kernel, out_shape=[shape, shape], in_specs=[any_space] * l...]
    ppermute x42, starting transfers between devices: 47.1 us -> 53.7 us  [permute(): return lax.ppermute(array, AXES, pairs)]
    ppermute x42, waiting for transfers between devices: 116 us -> 111 us  [permute(): return lax.ppermute(array, AXES, pairs)]
  transfers between devices with their start and end apart: 42 -> 42, of which waited for: 17 -> 20; matrix products, arithmetic and copies ran while one was open for 2% -> 1% of each run, Pallas kernels for 15% -> 14%
where the time goes in v4:
time: 245 us
  waiting for transfers between devices  111 us (45%)
  Pallas kernels  76.6 us (31%)
  starting transfers between devices  53.7 us (22%)
    ppermute x42, waiting for transfers between devices, permute(): return lax.ppermute(array, AXES, pairs)  111 us
    ppermute x42, starting transfers between devices, permute(): return lax.ppermute(array, AXES, pairs)  53.7 us
    pallas_call x1, Pallas kernels, pack_weights(): pl.pallas_call(kernel, out_shape=[shape, shape], in_specs=[any_space] * l...  35.9 us
    pallas_call x6, Pallas kernels, block_product(): pl.pallas_call(kernel, out_shape=out_shape, in_specs=[any_space] * len(op...  33.9 us
  transfers between devices with their start and end apart: 42, of which 20 were waited for; matrix products, arithmetic and copies ran while one was open for 1% of the time, Pallas kernels for 14%

profile of v4, /device:TPU:0, one launch (start us, length us, event | category | flops | bytes accessed | tf_op | source)
XLA Modules:
  0.0 244.7 jit_solution(2484300789195429286)
XLA Ops:
  0.0 35.9 %shard_map.100 = (bf16[320,896]{1,0:T(8,128)(2,1)}, bf16[320,896]{1,0:T(8,128)(2,1)}) custom-call(bf16[640,640]{1,0:T(8,128)(2,1)} %refs_0_.2, bf16[640,128]{1,0:T(8,128)(2,1)} %refs_1_.1, bf16[640,128]{1,0:T(8,128)(2,1)} %refs_2_.1), custom_call_target="tpu_custom_call" | custom-call | tf_op jit(solution)/shard_map/pallas_call | solution.py:84
  35.9 3.0 %collective-permute-start.1 = (bf16[768,1280]{1,0:T(8,128)(2,1)}, bf16[768,1280]{1,0:T(8,128)(2,1)S(1)}, u32[]{:S(2)}, u32[]{:S(2)}) collective-permute-start(bf16[768,1280]{1,0:T(8,128)(2,1)} %refs_6_.1), channel_id=1, source_target_pairs={{0,2},{1,3},{2,0},{3,1},{4,6},{5,7},{6,4},{7,5},{8,10},{9,11},{10,... | collective-permute-start | bytes 5898248 | tf_op jit(solution)/shard_map/ppermute | solution.py:23
  39.0 1.6 collective-permute-start.3
  40.5 0.4 collective-permute-start.5
  41.0 1.8 collective-permute-start.7
  42.8 11.5 %collective-permute-done.3.refs_4_ = bf16[320,896]{1,0:T(8,128)(2,1)S(1)} collective-permute-done((bf16[320,896]{1,0:T(8,128)(2,1)}, bf16[320,896]{1,0:T(8,128)(2,1)S(1)}, u32[]{:S(2)}, u32[]{:S(2)}) %collective-permute-start.3) | collective-permute-done | bytes 573472 | tf_op jit(solution)/shard_map/ppermute | solution.py:23
  54.3 10.4 %collective-permute-start.4 = (bf16[320,896]{1,0:T(8,128)(2,1)S(1)}, bf16[320,896]{1,0:T(8,128)(2,1)S(1)}, u32[]{:S(2)}, u32[]{:S(2)}) collective-permute-start(bf16[320,896]{1,0:T(8,128)(2,1)S(1)} %collective-permute-done.3.refs_4_), channel_id=1, source_target_pairs={{0,8},{1,9},{2,10},{3,11},{4,0},{5,1},{6,2},{7,3},{8,16},{9,17},{1... | collective-permute-start | bytes 1720328 | tf_op jit(solution)/shard_map/ppermute | solution.py:23
  64.6 9.2 %collective-permute-done.4.refs_4_ = bf16[320,896]{1,0:T(8,128)(2,1)S(1)} collective-permute-done((bf16[320,896]{1,0:T(8,128)(2,1)S(1)}, bf16[320,896]{1,0:T(8,128)(2,1)S(1)}, u32[]{:S(2)}, u32[]{:S(2)}) %collective-permute-start.4) | collective-permute-done | bytes 573472 | tf_op jit(solution)/shard_map/ppermute | solution.py:23
  73.8 5.8 %collective-permute-done.6.refs_7_ = bf16[320,896]{1,0:T(8,128)(2,1)S(1)} collective-permute-done((bf16[320,896]{1,0:T(8,128)(2,1)S(1)}, bf16[320,896]{1,0:T(8,128)(2,1)S(1)}, u32[]{:S(2)}, u32[]{:S(2)}) %collective-permute-start.6) | collective-permute-done | bytes 573472 | tf_op jit(solution)/shard_map/ppermute | solution.py:23
  79.6 3.3 %collective-permute-start.8 = (bf16[320,896]{1,0:T(8,128)(2,1)S(1)}, bf16[320,896]{1,0:T(8,128)(2,1)S(1)}, u32[]{:S(2)}, u32[]{:S(2)}) collective-permute-start(bf16[320,896]{1,0:T(8,128)(2,1)S(1)} %collective-permute-done.4.refs_4_), channel_id=1, source_target_pairs={{0,8},{1,9},{2,10},{3,11},{4,0},{5,1},{6,2},{7,3},{8,16},{9,17},{1... | collective-permute-start | bytes 1720328 | tf_op jit(solution)/shard_map/ppermute | solution.py:23
  82.9 11.1 %collective-permute-done.8.refs_6_ = bf16[320,896]{1,0:T(8,128)(2,1)S(1)} collective-permute-done((bf16[320,896]{1,0:T(8,128)(2,1)S(1)}, bf16[320,896]{1,0:T(8,128)(2,1)S(1)}, u32[]{:S(2)}, u32[]{:S(2)}) %collective-permute-start.8) | collective-permute-done | bytes 573472 | tf_op jit(solution)/shard_map/ppermute | solution.py:23
  94.0 2.5 %collective-permute-start.9 = (bf16[320,896]{1,0:T(8,128)(2,1)S(1)}, bf16[320,896]{1,0:T(8,128)(2,1)S(1)}, u32[]{:S(2)}, u32[]{:S(2)}) collective-permute-start(bf16[320,896]{1,0:T(8,128)(2,1)S(1)} %collective-permute-done.8.refs_6_), channel_id=1, source_target_pairs={{0,8},{1,9},{2,10},{3,11},{4,0},{5,1},{6,2},{7,3},{8,16},{9,17},{1... | collective-permute-start | bytes 1720328 | tf_op jit(solution)/shard_map/ppermute | solution.py:23
  96.5 0.3 collective-permute-done.13.refs_11_
  96.8 2.1 collective-permute-start
  99.0 9.7 %collective-permute-done.9.refs_5_ = bf16[320,896]{1,0:T(8,128)(2,1)S(1)} collective-permute-done((bf16[320,896]{1,0:T(8,128)(2,1)S(1)}, bf16[320,896]{1,0:T(8,128)(2,1)S(1)}, u32[]{:S(2)}, u32[]{:S(2)}) %collective-permute-start.9) | collective-permute-done | bytes 573472 | tf_op jit(solution)/shard_map/ppermute | solution.py:23
  108.7 2.5 %collective-permute-start.10 = (bf16[320,896]{1,0:T(8,128)(2,1)S(1)}, bf16[320,896]{1,0:T(8,128)(2,1)S(1)}, u32[]{:S(2)}, u32[]{:S(2)}) collective-permute-start(bf16[320,896]{1,0:T(8,128)(2,1)S(1)} %collective-permute-done.9.refs_5_), channel_id=1, source_target_pairs={{0,8},{1,9},{2,10},{3,11},{4,0},{5,1},{6,2},{7,3},{8,16},{9,17},{1... | collective-permute-start | bytes 1720328 | tf_op jit(solution)/shard_map/ppermute | solution.py:23
  111.2 0.3 collective-permute-done.14.refs_9_
  111.4 0.7 collective-permute-start.24
  112.1 12.4 %collective-permute-done.10.refs_7_ = bf16[320,896]{1,0:T(8,128)(2,1)S(1)} collective-permute-done((bf16[320,896]{1,0:T(8,128)(2,1)S(1)}, bf16[320,896]{1,0:T(8,128)(2,1)S(1)}, u32[]{:S(2)}, u32[]{:S(2)}) %collective-permute-start.10) | collective-permute-done | bytes 573472 | tf_op jit(solution)/shard_map/ppermute | solution.py:23
  124.5 2.5 %collective-permute-start.11 = (bf16[320,896]{1,0:T(8,128)(2,1)S(1)}, bf16[320,896]{1,0:T(8,128)(2,1)S(1)}, u32[]{:S(2)}, u32[]{:S(2)}) collective-permute-start(bf16[320,896]{1,0:T(8,128)(2,1)S(1)} %collective-permute-done.10.refs_7_), channel_id=1, source_target_pairs={{0,8},{1,9},{2,10},{3,11},{4,0},{5,1},{6,2},{7,3},{8,16},{9,17},{1... | collective-permute-start | bytes 1720328 | tf_op jit(solution)/shard_map/ppermute | solution.py:23
  127.0 0.7 subtract_convert_fusion
  127.7 1.4 fusion
  129.2 10.4 %collective-permute-done.11.refs_5_ = bf16[320,896]{1,0:T(8,128)(2,1)S(1)} collective-permute-done((bf16[320,896]{1,0:T(8,128)(2,1)S(1)}, bf16[320,896]{1,0:T(8,128)(2,1)S(1)}, u32[]{:S(2)}, u32[]{:S(2)}) %collective-permute-start.11) | collective-permute-done | bytes 573472 | tf_op jit(solution)/shard_map/ppermute | solution.py:23
  139.6 2.4 %collective-permute-start.12 = (bf16[320,896]{1,0:T(8,128)(2,1)S(1)}, bf16[320,896]{1,0:T(8,128)(2,1)S(1)}, u32[]{:S(2)}, u32[]{:S(2)}) collective-permute-start(bf16[320,896]{1,0:T(8,128)(2,1)S(1)} %collective-permute-done.11.refs_5_), channel_id=1, source_target_pairs={{0,8},{1,9},{2,10},{3,11},{4,0},{5,1},{6,2},{7,3},{8,16},{9,17},{1... | collective-permute-start | bytes 1720328 | tf_op jit(solution)/shard_map/ppermute | solution.py:23
  142.0 0.3 collective-permute-start.17
  142.4 7.0 %shard_map.101.refs_8_ = f32[768,896]{1,0:T(8,128)S(1)} custom-call(bf16[768,1280]{1,0:T(8,128)(2,1)S(1)} %copy-done, bf16[768,1280]{1,0:T(8,128)(2,1)S(1)} %collective-permute-done.refs_1_, bf16[768,1280]{1,0:T(8,128)(2,1)S(1)} %collective-permute-done.1.refs_2_, bf16[768,1280]{1,0:T(8,128)(2,1)S(1)} %collective-permute-done.2.refs_3_, ...), custom_call_target="tpu_custom_call" | custom-call | flops 3523215360 | bytes 14024704 | tf_op jit(solution)/shard_map/pallas_call | solution.py:245
  149.4 4.7 %shard_map.102.refs_8_ = f32[768,896]{1,0:T(8,128)S(1)} custom-call(bf16[768,1280]{1,0:T(8,128)(2,1)S(1)} %copy-done, bf16[768,1280]{1,0:T(8,128)(2,1)S(1)} %collective-permute-done.refs_1_, bf16[768,1280]{1,0:T(8,128)(2,1)S(1)} %collective-permute-done.1.refs_2_, bf16[768,1280]{1,0:T(8,128)(2,1)S(1)} %collective-permute-done.2.refs_3_, ...), custom_call_target="tpu_custom_call" | custom-call | flops 1761607680 | bytes 9764864 | tf_op jit(solution)/shard_map/pallas_call | solution.py:245
  154.1 2.1 collective-permute-done.17.refs_6_
  156.2 0.4 collective-permute-start.25
  156.5 1.7 collective-permute-start.31
  158.2 5.4 %shard_map.103 = (f32[768,896]{1,0:T(8,128)S(1)}, f32[8,768]{1,0:T(8,128)S(1)}) custom-call(bf16[768,1280]{1,0:T(8,128)(2,1)S(1)} %copy-done, bf16[768,1280]{1,0:T(8,128)(2,1)S(1)} %collective-permute-done.refs_1_, bf16[768,1280]{1,0:T(8,128)(2,1)S(1)} %collective-permute-done.1.refs_2_, bf16[768,1280]{1,0:T(8,128)(2,1)S(1)} %collective-permute-done.2.refs_3_, ...), custom_call_target="tpu_custom_call" | custom-call | flops 1761607680 | bytes 9764864 | tf_op jit(solution)/shard_map/pallas_call | solution.py:245
  163.7 0.2 collective-permute-start.19
  163.9 1.6 collective-permute-start.20
  165.5 0.3 pad_maximum_fusion
  165.9 1.7 collective-permute-done.19.refs_3_
  167.6 0.2 broadcast_in_dim.8.refs_7_
  167.8 4.4 %shard_map.104.refs_0_ = bf16[768,640]{1,0:T(8,128)(2,1)S(1)} custom-call(f32[768,896]{1,0:T(8,128)S(1)} %get-tuple-element.29.refs_0_, f32[8,768]{1,0:T(8,128)S(1)} %get-tuple-element.30.refs_1_, f32[8,768]{1,0:T(8,128)S(1)} %collective-permute-done.18.refs_2_, f32[8,768]{1,0:T(8,128)S(1)} %collective-permute-done.19.refs_3_, ...), custom_call_target="tpu_custom_call" | custom-call | flops 754974720 | bytes 5505024 | tf_op jit(solution)/shard_map/pallas_call | solution.py:339
  172.2 1.5 collective-permute-start.22
  173.7 0.6 collective-permute-start.26
  174.3 1.4 collective-permute-start.32
  175.7 9.2 %collective-permute-done.26.refs_4_ = bf16[320,640]{1,0:T(8,128)(2,1)S(1)} collective-permute-done((bf16[320,640]{1,0:T(8,128)(2,1)S(1)}, bf16[320,640]{1,0:T(8,128)(2,1)S(1)}, u32[]{:S(2)}, u32[]{:S(2)}) %collective-permute-start.26) | collective-permute-done | bytes 409632 | tf_op jit(solution)/shard_map/ppermute | solution.py:23
  185.0 0.6 collective-permute-start.27
  185.5 1.5 collective-permute-start.33
  187.0 8.4 %collective-permute-done.27.refs_6_ = bf16[320,640]{1,0:T(8,128)(2,1)S(1)} collective-permute-done((bf16[320,640]{1,0:T(8,128)(2,1)S(1)}, bf16[320,640]{1,0:T(8,128)(2,1)S(1)}, u32[]{:S(2)}, u32[]{:S(2)}) %collective-permute-start.27) | collective-permute-done | bytes 409632 | tf_op jit(solution)/shard_map/ppermute | solution.py:23
  195.3 0.5 collective-permute-start.28
  195.9 1.5 collective-permute-start.34
  197.4 0.5 collective-permute-start.23
  197.9 7.1 %collective-permute-done.28.refs_5_ = bf16[320,640]{1,0:T(8,128)(2,1)S(1)} collective-permute-done((bf16[320,640]{1,0:T(8,128)(2,1)S(1)}, bf16[320,640]{1,0:T(8,128)(2,1)S(1)}, u32[]{:S(2)}, u32[]{:S(2)}) %collective-permute-start.28) | collective-permute-done | bytes 409632 | tf_op jit(solution)/shard_map/ppermute | solution.py:23
  205.0 0.5 collective-permute-start.29
  205.5 1.5 collective-permute-start.35
  207.0 7.6 %collective-permute-done.29.refs_7_ = bf16[320,640]{1,0:T(8,128)(2,1)S(1)} collective-permute-done((bf16[320,640]{1,0:T(8,128)(2,1)S(1)}, bf16[320,640]{1,0:T(8,128)(2,1)S(1)}, u32[]{:S(2)}, u32[]{:S(2)}) %collective-permute-start.29) | collective-permute-done | bytes 409632 | tf_op jit(solution)/shard_map/ppermute | solution.py:23
  214.6 0.5 collective-permute-start.30
  215.1 1.5 collective-permute-start.36
  216.6 7.4 %shard_map.105.refs_8_ = f32[768,1280]{1,0:T(8,128)S(1)} custom-call(bf16[768,640]{1,0:T(8,128)(2,1)S(1)} %shard_map.104.refs_0_, bf16[768,640]{1,0:T(8,128)(2,1)S(1)} %collective-permute-done.21.refs_1_, bf16[768,640]{1,0:T(8,128)(2,1)S(1)} %collective-permute-done.22.refs_2_, bf16[768,640]{1,0:T(8,128)(2,1)S(1)} %collective-permute-done.23.refs_3_, ...), custom_call_target="tpu_custom_call" | custom-call | flops 2516582400 | bytes 15073280 | tf_op jit(solution)/shard_map/pallas_call | solution.py:245
  224.1 0.4 collective-permute-done.36.refs_6_
  224.6 1.9 collective-permute-start.38
  226.5 4.6 %shard_map.106.refs_8_ = f32[768,1280]{1,0:T(8,128)S(1)} custom-call(bf16[768,640]{1,0:T(8,128)(2,1)S(1)} %shard_map.104.refs_0_, bf16[768,640]{1,0:T(8,128)(2,1)S(1)} %collective-permute-done.21.refs_1_, bf16[768,640]{1,0:T(8,128)(2,1)S(1)} %collective-permute-done.22.refs_2_, bf16[768,640]{1,0:T(8,128)(2,1)S(1)} %collective-permute-done.23.refs_3_, ...), custom_call_target="tpu_custom_call" | custom-call | flops 1258291200 | bytes 11468800 | tf_op jit(solution)/shard_map/pallas_call | solution.py:245
  231.1 1.4 collective-permute-done.37.refs_5_
  232.6 4.9 %shard_map.107 = (f32[768,1280]{1,0:T(8,128)S(1)}, f32[8,768]{1,0:T(8,128)S(1)}) custom-call(bf16[768,640]{1,0:T(8,128)(2,1)S(1)} %shard_map.104.refs_0_, bf16[768,640]{1,0:T(8,128)(2,1)S(1)} %collective-permute-done.21.refs_1_, bf16[768,640]{1,0:T(8,128)(2,1)S(1)} %collective-permute-done.22.refs_2_, bf16[768,640]{1,0:T(8,128)(2,1)S(1)} %collective-permute-done.23.refs_3_, ...), custom_call_target="tpu_custom_call" | custom-call | flops 1258291200 | bytes 11468800 | tf_op jit(solution)/shard_map/pallas_call | solution.py:245
  237.6 1.4 collective-permute-start.40
  239.0 0.4 collective-permute-start.41
  240.1 1.4 collective-permute-done.40.refs_4_
  241.5 0.8 collective-permute-done.41.refs_5_
  242.3 2.4 shard_map.108
  (51 shorter events, 0.7 us)
Async XLA Ops:
  0.0 142.4 %copy-start = (bf16[768,1280]{1,0:T(8,128)(2,1)S(1)}, bf16[768,1280]{1,0:T(8,128)(2,1)}, u32[]{:S(2)}) copy-start(bf16[768,1280]{1,0:T(8,128)(2,1)} %refs_6_.1) | copy-start | bytes 5898244
  35.9 106.5 %copy-start.1 = (bf16[320,896]{1,0:T(8,128)(2,1)S(1)}, bf16[320,896]{1,0:T(8,128)(2,1)}, u32[]{:S(2)}) copy-start(bf16[320,896]{1,0:T(8,128)(2,1)} %get-tuple-element.25.refs_4_) | copy-start | bytes 1720324
  35.9 106.5 %copy-start.2 = (bf16[320,896]{1,0:T(8,128)(2,1)S(1)}, bf16[320,896]{1,0:T(8,128)(2,1)}, u32[]{:S(2)}) copy-start(bf16[320,896]{1,0:T(8,128)(2,1)} %get-tuple-element.26.refs_8_) | copy-start | bytes 1720324
  35.9 63.0 %collective-permute-start.1 = (bf16[768,1280]{1,0:T(8,128)(2,1)}, bf16[768,1280]{1,0:T(8,128)(2,1)S(1)}, u32[]{:S(2)}, u32[]{:S(2)}) collective-permute-start(bf16[768,1280]{1,0:T(8,128)(2,1)} %refs_6_.1), channel_id=1, source_target_pairs={{0,2},{1,3},{2,0},{3,1},{4,6},{5,7},{6,4},{7,5},{8,10},{9,11},{10,... | collective-permute-start | bytes 5898248 | tf_op jit(solution)/shard_map/ppermute | solution.py:23
  39.0 15.3 %collective-permute-start.3 = (bf16[320,896]{1,0:T(8,128)(2,1)}, bf16[320,896]{1,0:T(8,128)(2,1)S(1)}, u32[]{:S(2)}, u32[]{:S(2)}) collective-permute-start(bf16[320,896]{1,0:T(8,128)(2,1)} %get-tuple-element.25.refs_4_), channel_id=1, source_target_pairs={{0,8},{1,9},{2,10},{3,11},{4,0},{5,1},{6,2},{7,3},{8,16},{9,17},{1... | collective-permute-start | bytes 1720328 | tf_op jit(solution)/shard_map/ppermute | solution.py:23
  40.5 24.1 %collective-permute-start.5 = (bf16[320,896]{1,0:T(8,128)(2,1)}, bf16[320,896]{1,0:T(8,128)(2,1)S(1)}, u32[]{:S(2)}, u32[]{:S(2)}) collective-permute-start(bf16[320,896]{1,0:T(8,128)(2,1)} %get-tuple-element.26.refs_8_), channel_id=1, source_target_pairs={{0,4},{1,5},{2,6},{3,7},{4,12},{5,13},{6,14},{7,15},{8,0},{9,1},{1... | collective-permute-start | bytes 1720328 | tf_op jit(solution)/shard_map/ppermute | solution.py:23
  41.0 23.6 %collective-permute-start.7 = (bf16[640,640]{1,0:T(8,128)(2,1)}, bf16[640,640]{1,0:T(8,128)(2,1)S(1)}, u32[]{:S(2)}, u32[]{:S(2)}) collective-permute-start(bf16[640,640]{1,0:T(8,128)(2,1)} %param.16), channel_id=1, source_target_pairs={{0,0},{1,17},{2,10},{3,27},{4,4},{5,21},{6,14},{7,31},{8,8},{9,25}... | collective-permute-start | bytes 2457608 | tf_op jit(solution)/shard_map/ppermute | solution.py:23
  54.3 19.5 %collective-permute-start.4 = (bf16[320,896]{1,0:T(8,128)(2,1)S(1)}, bf16[320,896]{1,0:T(8,128)(2,1)S(1)}, u32[]{:S(2)}, u32[]{:S(2)}) collective-permute-start(bf16[320,896]{1,0:T(8,128)(2,1)S(1)} %collective-permute-done.3.refs_4_), channel_id=1, source_target_pairs={{0,8},{1,9},{2,10},{3,11},{4,0},{5,1},{6,2},{7,3},{8,16},{9,17},{1... | collective-permute-start | bytes 1720328 | tf_op jit(solution)/shard_map/ppermute | solution.py:23
  64.6 15.0 %collective-permute-start.6 = (bf16[320,896]{1,0:T(8,128)(2,1)S(1)}, bf16[320,896]{1,0:T(8,128)(2,1)S(1)}, u32[]{:S(2)}, u32[]{:S(2)}) collective-permute-start(bf16[320,896]{1,0:T(8,128)(2,1)S(1)} %collective-permute-done.5.refs_7_), channel_id=1, source_target_pairs={{0,4},{1,5},{2,6},{3,7},{4,12},{5,13},{6,14},{7,15},{8,0},{9,1},{1... | collective-permute-start | bytes 1720328 | tf_op jit(solution)/shard_map/ppermute | solution.py:23
  79.6 14.4 %collective-permute-start.8 = (bf16[320,896]{1,0:T(8,128)(2,1)S(1)}, bf16[320,896]{1,0:T(8,128)(2,1)S(1)}, u32[]{:S(2)}, u32[]{:S(2)}) collective-permute-start(bf16[320,896]{1,0:T(8,128)(2,1)S(1)} %collective-permute-done.4.refs_4_), channel_id=1, source_target_pairs={{0,8},{1,9},{2,10},{3,11},{4,0},{5,1},{6,2},{7,3},{8,16},{9,17},{1... | collective-permute-start | bytes 1720328 | tf_op jit(solution)/shard_map/ppermute | solution.py:23
  82.9 13.8 %collective-permute-start.13 = (bf16[320,896]{1,0:T(8,128)(2,1)S(1)}, bf16[320,896]{1,0:T(8,128)(2,1)S(1)}, u32[]{:S(2)}, u32[]{:S(2)}) collective-permute-start(bf16[320,896]{1,0:T(8,128)(2,1)S(1)} %collective-permute-done.6.refs_7_), channel_id=1, source_target_pairs={{0,4},{1,5},{2,6},{3,7},{4,12},{5,13},{6,14},{7,15},{8,0},{9,1},{1... | collective-permute-start | bytes 1720328 | tf_op jit(solution)/shard_map/ppermute | solution.py:23
  94.0 14.7 %collective-permute-start.9 = (bf16[320,896]{1,0:T(8,128)(2,1)S(1)}, bf16[320,896]{1,0:T(8,128)(2,1)S(1)}, u32[]{:S(2)}, u32[]{:S(2)}) collective-permute-start(bf16[320,896]{1,0:T(8,128)(2,1)S(1)} %collective-permute-done.8.refs_6_), channel_id=1, source_target_pairs={{0,8},{1,9},{2,10},{3,11},{4,0},{5,1},{6,2},{7,3},{8,16},{9,17},{1... | collective-permute-start | bytes 1720328 | tf_op jit(solution)/shard_map/ppermute | solution.py:23
  96.8 14.7 %collective-permute-start.14 = (bf16[320,896]{1,0:T(8,128)(2,1)S(1)}, bf16[320,896]{1,0:T(8,128)(2,1)S(1)}, u32[]{:S(2)}, u32[]{:S(2)}) collective-permute-start(bf16[320,896]{1,0:T(8,128)(2,1)S(1)} %collective-permute-done.13.refs_11_), channel_id=1, source_target_pairs={{0,4},{1,5},{2,6},{3,7},{4,12},{5,13},{6,14},{7,15},{8,0},{9,1},{1... | collective-permute-start | bytes 1720328 | tf_op jit(solution)/shard_map/ppermute | solution.py:23
  96.8 45.6 %collective-permute-start = (bf16[768,1280]{1,0:T(8,128)(2,1)}, bf16[768,1280]{1,0:T(8,128)(2,1)S(1)}, u32[]{:S(2)}, u32[]{:S(2)}) collective-permute-start(bf16[768,1280]{1,0:T(8,128)(2,1)} %refs_6_.1), channel_id=1, source_target_pairs={{0,1},{1,0},{2,3},{3,2},{4,5},{5,4},{6,7},{7,6},{8,9},{9,8},{10,11... | collective-permute-start | bytes 5898248 | tf_op jit(solution)/shard_map/ppermute | solution.py:23
  98.9 43.5 %collective-permute-start.2 = (bf16[768,1280]{1,0:T(8,128)(2,1)S(1)}, bf16[768,1280]{1,0:T(8,128)(2,1)S(1)}, u32[]{:S(2)}, u32[]{:S(2)}) collective-permute-start(bf16[768,1280]{1,0:T(8,128)(2,1)S(1)} %collective-permute-done.1.refs_2_), channel_id=1, source_target_pairs={{0,1},{1,0},{2,3},{3,2},{4,5},{5,4},{6,7},{7,6},{8,9},{9,8},{10,11... | collective-permute-start | bytes 5898248 | tf_op jit(solution)/shard_map/ppermute | solution.py:23
  108.7 15.8 %collective-permute-start.10 = (bf16[320,896]{1,0:T(8,128)(2,1)S(1)}, bf16[320,896]{1,0:T(8,128)(2,1)S(1)}, u32[]{:S(2)}, u32[]{:S(2)}) collective-permute-start(bf16[320,896]{1,0:T(8,128)(2,1)S(1)} %collective-permute-done.9.refs_5_), channel_id=1, source_target_pairs={{0,8},{1,9},{2,10},{3,11},{4,0},{5,1},{6,2},{7,3},{8,16},{9,17},{1... | collective-permute-start | bytes 1720328 | tf_op jit(solution)/shard_map/ppermute | solution.py:23
  111.4 15.6 %collective-permute-start.15 = (bf16[320,896]{1,0:T(8,128)(2,1)S(1)}, bf16[320,896]{1,0:T(8,128)(2,1)S(1)}, u32[]{:S(2)}, u32[]{:S(2)}) collective-permute-start(bf16[320,896]{1,0:T(8,128)(2,1)S(1)} %collective-permute-done.14.refs_9_), channel_id=1, source_target_pairs={{0,4},{1,5},{2,6},{3,7},{4,12},{5,13},{6,14},{7,15},{8,0},{9,1},{1... | collective-permute-start | bytes 1720328 | tf_op jit(solution)/shard_map/ppermute | solution.py:23
  111.4 30.9 %collective-permute-start.24 = (bf16[640,640]{1,0:T(8,128)(2,1)S(1)}, bf16[640,640]{1,0:T(8,128)(2,1)S(1)}, u32[]{:S(2)}, u32[]{:S(2)}) collective-permute-start(bf16[640,640]{1,0:T(8,128)(2,1)S(1)} %collective-permute-done.7), channel_id=1, source_target_pairs={{0,0},{1,2},{2,1},{3,3},{4,4},{5,6},{6,5},{7,7},{8,9},{9,11},{10,8... | collective-permute-start | bytes 2457608 | tf_op jit(solution)/shard_map/ppermute | solution.py:23
  124.5 15.1 %collective-permute-start.11 = (bf16[320,896]{1,0:T(8,128)(2,1)S(1)}, bf16[320,896]{1,0:T(8,128)(2,1)S(1)}, u32[]{:S(2)}, u32[]{:S(2)}) collective-permute-start(bf16[320,896]{1,0:T(8,128)(2,1)S(1)} %collective-permute-done.10.refs_7_), channel_id=1, source_target_pairs={{0,8},{1,9},{2,10},{3,11},{4,0},{5,1},{6,2},{7,3},{8,16},{9,17},{1... | collective-permute-start | bytes 1720328 | tf_op jit(solution)/shard_map/ppermute | solution.py:23
  127.0 15.0 %collective-permute-start.16 = (bf16[320,896]{1,0:T(8,128)(2,1)S(1)}, bf16[320,896]{1,0:T(8,128)(2,1)S(1)}, u32[]{:S(2)}, u32[]{:S(2)}) collective-permute-start(bf16[320,896]{1,0:T(8,128)(2,1)S(1)} %collective-permute-done.15.refs_10_), channel_id=1, source_target_pairs={{0,4},{1,5},{2,6},{3,7},{4,12},{5,13},{6,14},{7,15},{8,0},{9,1},{1... | collective-permute-start | bytes 1720328 | tf_op jit(solution)/shard_map/ppermute | solution.py:23
  139.6 14.5 %collective-permute-start.12 = (bf16[320,896]{1,0:T(8,128)(2,1)S(1)}, bf16[320,896]{1,0:T(8,128)(2,1)S(1)}, u32[]{:S(2)}, u32[]{:S(2)}) collective-permute-start(bf16[320,896]{1,0:T(8,128)(2,1)S(1)} %collective-permute-done.11.refs_5_), channel_id=1, source_target_pairs={{0,8},{1,9},{2,10},{3,11},{4,0},{5,1},{6,2},{7,3},{8,16},{9,17},{1... | collective-permute-start | bytes 1720328 | tf_op jit(solution)/shard_map/ppermute | solution.py:23
  142.0 14.2 %collective-permute-start.17 = (bf16[320,896]{1,0:T(8,128)(2,1)S(1)}, bf16[320,896]{1,0:T(8,128)(2,1)S(1)}, u32[]{:S(2)}, u32[]{:S(2)}) collective-permute-start(bf16[320,896]{1,0:T(8,128)(2,1)S(1)} %collective-permute-done.16.refs_6_), channel_id=1, source_target_pairs={{0,4},{1,5},{2,6},{3,7},{4,12},{5,13},{6,14},{7,15},{8,0},{9,1},{1... | collective-permute-start | bytes 1720328 | tf_op jit(solution)/shard_map/ppermute | solution.py:23
  156.2 9.7 %copy-start.6 = (f32[640]{0:T(1024)S(1)}, f32[640]{0:T(1024)}, u32[]{:S(2)}) copy-start(f32[640]{0:T(1024)} %param.17) | copy-start | bytes 7684
  156.2 11.4 %copy-start.4 = (s32[768]{0:T(1024)S(1)}, s32[768]{0:T(1024)}, u32[]{:S(2)}) copy-start(s32[768]{0:T(1024)} %param.12) | copy-start | bytes 9220
  156.2 11.6 %copy-start.3 = (f32[128]{0:T(128)S(1)}, f32[128]{0:T(128)}, u32[]{:S(2)}) copy-start(f32[128]{0:T(128)} %param.18) | copy-start | bytes 1540
  156.2 17.5 %collective-permute-start.25 = (bf16[320,640]{1,0:T(8,128)(2,1)S(1)}, bf16[320,640]{1,0:T(8,128)(2,1)S(1)}, u32[]{:S(2)}, u32[]{:S(2)}) collective-permute-start(bf16[320,640]{1,0:T(8,128)(2,1)S(1)} %get-tuple-element.32.refs_4_), channel_id=1, source_target_pairs={{0,8},{1,9},{2,10},{3,11},{4,0},{5,1},{6,2},{7,3},{8,16},{9,17},{1... | collective-permute-start | bytes 1228808 | tf_op jit(solution)/shard_map/ppermute | solution.py:23
  156.5 17.8 %collective-permute-start.31 = (bf16[320,640]{1,0:T(8,128)(2,1)S(1)}, bf16[320,640]{1,0:T(8,128)(2,1)S(1)}, u32[]{:S(2)}, u32[]{:S(2)}) collective-permute-start(bf16[320,640]{1,0:T(8,128)(2,1)S(1)} %get-tuple-element.33.refs_8_), channel_id=1, source_target_pairs={{0,4},{1,5},{2,6},{3,7},{4,12},{5,13},{6,14},{7,15},{8,0},{9,1},{1... | collective-permute-start | bytes 1228808 | tf_op jit(solution)/shard_map/ppermute | solution.py:23
  163.6 2.2 collective-permute-start.18
  163.7 3.9 %collective-permute-start.19 = (f32[8,768]{1,0:T(8,128)S(1)}, f32[8,768]{1,0:T(8,128)S(1)}, u32[]{:S(2)}, u32[]{:S(2)}) collective-permute-start(f32[8,768]{1,0:T(8,128)S(1)} %get-tuple-element.30.refs_1_), channel_id=1, source_target_pairs={{0,2},{1,3},{2,0},{3,1},{4,6},{5,7},{6,4},{7,5},{8,10},{9,11},{10,... | collective-permute-start | bytes 73736 | tf_op jit(solution)/shard_map/ppermute | solution.py:23
  163.9 3.7 %collective-permute-start.20 = (f32[8,768]{1,0:T(8,128)S(1)}, f32[8,768]{1,0:T(8,128)S(1)}, u32[]{:S(2)}, u32[]{:S(2)}) collective-permute-start(f32[8,768]{1,0:T(8,128)S(1)} %get-tuple-element.30.refs_1_), channel_id=1, source_target_pairs={{0,3},{1,2},{2,1},{3,0},{4,7},{5,6},{6,5},{7,4},{8,11},{9,10},{10,... | collective-permute-start | bytes 73736 | tf_op jit(solution)/shard_map/ppermute | solution.py:23
  172.2 25.2 %collective-permute-start.22 = (bf16[768,640]{1,0:T(8,128)(2,1)S(1)}, bf16[768,640]{1,0:T(8,128)(2,1)S(1)}, u32[]{:S(2)}, u32[]{:S(2)}) collective-permute-start(bf16[768,640]{1,0:T(8,128)(2,1)S(1)} %shard_map.104.refs_0_), channel_id=1, source_target_pairs={{0,2},{1,3},{2,0},{3,1},{4,6},{5,7},{6,4},{7,5},{8,10},{9,11},{10,... | collective-permute-start | bytes 2949128 | tf_op jit(solution)/shard_map/ppermute | solution.py:23
  173.7 11.3 %collective-permute-start.26 = (bf16[320,640]{1,0:T(8,128)(2,1)S(1)}, bf16[320,640]{1,0:T(8,128)(2,1)S(1)}, u32[]{:S(2)}, u32[]{:S(2)}) collective-permute-start(bf16[320,640]{1,0:T(8,128)(2,1)S(1)} %collective-permute-done.25.refs_4_), channel_id=1, source_target_pairs={{0,8},{1,9},{2,10},{3,11},{4,0},{5,1},{6,2},{7,3},{8,16},{9,17},{1... | collective-permute-start | bytes 1228808 | tf_op jit(solution)/shard_map/ppermute | solution.py:23
  174.3 11.2 %collective-permute-start.32 = (bf16[320,640]{1,0:T(8,128)(2,1)S(1)}, bf16[320,640]{1,0:T(8,128)(2,1)S(1)}, u32[]{:S(2)}, u32[]{:S(2)}) collective-permute-start(bf16[320,640]{1,0:T(8,128)(2,1)S(1)} %collective-permute-done.31.refs_7_), channel_id=1, source_target_pairs={{0,4},{1,5},{2,6},{3,7},{4,12},{5,13},{6,14},{7,15},{8,0},{9,1},{1... | collective-permute-start | bytes 1228808 | tf_op jit(solution)/shard_map/ppermute | solution.py:23
  185.0 10.4 %collective-permute-start.27 = (bf16[320,640]{1,0:T(8,128)(2,1)S(1)}, bf16[320,640]{1,0:T(8,128)(2,1)S(1)}, u32[]{:S(2)}, u32[]{:S(2)}) collective-permute-start(bf16[320,640]{1,0:T(8,128)(2,1)S(1)} %collective-permute-done.26.refs_4_), channel_id=1, source_target_pairs={{0,8},{1,9},{2,10},{3,11},{4,0},{5,1},{6,2},{7,3},{8,16},{9,17},{1... | collective-permute-start | bytes 1228808 | tf_op jit(solution)/shard_map/ppermute | solution.py:23
  185.5 10.3 %collective-permute-start.33 = (bf16[320,640]{1,0:T(8,128)(2,1)S(1)}, bf16[320,640]{1,0:T(8,128)(2,1)S(1)}, u32[]{:S(2)}, u32[]{:S(2)}) collective-permute-start(bf16[320,640]{1,0:T(8,128)(2,1)S(1)} %collective-permute-done.32.refs_7_), channel_id=1, source_target_pairs={{0,4},{1,5},{2,6},{3,7},{4,12},{5,13},{6,14},{7,15},{8,0},{9,1},{1... | collective-permute-start | bytes 1228808 | tf_op jit(solution)/shard_map/ppermute | solution.py:23
  195.3 9.6 %collective-permute-start.28 = (bf16[320,640]{1,0:T(8,128)(2,1)S(1)}, bf16[320,640]{1,0:T(8,128)(2,1)S(1)}, u32[]{:S(2)}, u32[]{:S(2)}) collective-permute-start(bf16[320,640]{1,0:T(8,128)(2,1)S(1)} %collective-permute-done.27.refs_6_), channel_id=1, source_target_pairs={{0,8},{1,9},{2,10},{3,11},{4,0},{5,1},{6,2},{7,3},{8,16},{9,17},{1... | collective-permute-start | bytes 1228808 | tf_op jit(solution)/shard_map/ppermute | solution.py:23
  195.9 9.6 %collective-permute-start.34 = (bf16[320,640]{1,0:T(8,128)(2,1)S(1)}, bf16[320,640]{1,0:T(8,128)(2,1)S(1)}, u32[]{:S(2)}, u32[]{:S(2)}) collective-permute-start(bf16[320,640]{1,0:T(8,128)(2,1)S(1)} %collective-permute-done.33.refs_11_), channel_id=1, source_target_pairs={{0,4},{1,5},{2,6},{3,7},{4,12},{5,13},{6,14},{7,15},{8,0},{9,1},{1... | collective-permute-start | bytes 1228808 | tf_op jit(solution)/shard_map/ppermute | solution.py:23
  197.4 19.3 %collective-permute-start.21 = (bf16[768,640]{1,0:T(8,128)(2,1)S(1)}, bf16[768,640]{1,0:T(8,128)(2,1)S(1)}, u32[]{:S(2)}, u32[]{:S(2)}) collective-permute-start(bf16[768,640]{1,0:T(8,128)(2,1)S(1)} %shard_map.104.refs_0_), channel_id=1, source_target_pairs={{0,1},{1,0},{2,3},{3,2},{4,5},{5,4},{6,7},{7,6},{8,9},{9,8},{10,11... | collective-permute-start | bytes 2949128 | tf_op jit(solution)/shard_map/ppermute | solution.py:23
  197.4 19.3 %collective-permute-start.23 = (bf16[768,640]{1,0:T(8,128)(2,1)S(1)}, bf16[768,640]{1,0:T(8,128)(2,1)S(1)}, u32[]{:S(2)}, u32[]{:S(2)}) collective-permute-start(bf16[768,640]{1,0:T(8,128)(2,1)S(1)} %collective-permute-done.22.refs_2_), channel_id=1, source_target_pairs={{0,1},{1,0},{2,3},{3,2},{4,5},{5,4},{6,7},{7,6},{8,9},{9,8},{10,11... | collective-permute-start | bytes 2949128 | tf_op jit(solution)/shard_map/ppermute | solution.py:23
  205.0 9.6 %collective-permute-start.29 = (bf16[320,640]{1,0:T(8,128)(2,1)S(1)}, bf16[320,640]{1,0:T(8,128)(2,1)S(1)}, u32[]{:S(2)}, u32[]{:S(2)}) collective-permute-start(bf16[320,640]{1,0:T(8,128)(2,1)S(1)} %collective-permute-done.28.refs_5_), channel_id=1, source_target_pairs={{0,8},{1,9},{2,10},{3,11},{4,0},{5,1},{6,2},{7,3},{8,16},{9,17},{1... | collective-permute-start | bytes 1228808 | tf_op jit(solution)/shard_map/ppermute | solution.py:23
  205.5 9.6 %collective-permute-start.35 = (bf16[320,640]{1,0:T(8,128)(2,1)S(1)}, bf16[320,640]{1,0:T(8,128)(2,1)S(1)}, u32[]{:S(2)}, u32[]{:S(2)}) collective-permute-start(bf16[320,640]{1,0:T(8,128)(2,1)S(1)} %collective-permute-done.34.refs_9_), channel_id=1, source_target_pairs={{0,4},{1,5},{2,6},{3,7},{4,12},{5,13},{6,14},{7,15},{8,0},{9,1},{1... | collective-permute-start | bytes 1228808 | tf_op jit(solution)/shard_map/ppermute | solution.py:23
  214.6 9.4 %collective-permute-start.30 = (bf16[320,640]{1,0:T(8,128)(2,1)S(1)}, bf16[320,640]{1,0:T(8,128)(2,1)S(1)}, u32[]{:S(2)}, u32[]{:S(2)}) collective-permute-start(bf16[320,640]{1,0:T(8,128)(2,1)S(1)} %collective-permute-done.29.refs_7_), channel_id=1, source_target_pairs={{0,8},{1,9},{2,10},{3,11},{4,0},{5,1},{6,2},{7,3},{8,16},{9,17},{1... | collective-permute-start | bytes 1228808 | tf_op jit(solution)/shard_map/ppermute | solution.py:23
  215.1 9.4 %collective-permute-start.36 = (bf16[320,640]{1,0:T(8,128)(2,1)S(1)}, bf16[320,640]{1,0:T(8,128)(2,1)S(1)}, u32[]{:S(2)}, u32[]{:S(2)}) collective-permute-start(bf16[320,640]{1,0:T(8,128)(2,1)S(1)} %collective-permute-done.35.refs_10_), channel_id=1, source_target_pairs={{0,4},{1,5},{2,6},{3,7},{4,12},{5,13},{6,14},{7,15},{8,0},{9,1},{1... | collective-permute-start | bytes 1228808 | tf_op jit(solution)/shard_map/ppermute | solution.py:23
  224.5 8.0 %collective-permute-start.37 = (bf16[320,640]{1,0:T(8,128)(2,1)S(1)}, bf16[320,640]{1,0:T(8,128)(2,1)S(1)}, u32[]{:S(2)}, u32[]{:S(2)}) collective-permute-start(bf16[320,640]{1,0:T(8,128)(2,1)S(1)} %collective-permute-done.30.refs_5_), channel_id=1, source_target_pairs={{0,8},{1,9},{2,10},{3,11},{4,0},{5,1},{6,2},{7,3},{8,16},{9,17},{1... | collective-permute-start | bytes 1228808 | tf_op jit(solution)/shard_map/ppermute | solution.py:23
  224.6 8.0 %collective-permute-start.38 = (bf16[320,640]{1,0:T(8,128)(2,1)S(1)}, bf16[320,640]{1,0:T(8,128)(2,1)S(1)}, u32[]{:S(2)}, u32[]{:S(2)}) collective-permute-start(bf16[320,640]{1,0:T(8,128)(2,1)S(1)} %collective-permute-done.36.refs_6_), channel_id=1, source_target_pairs={{0,4},{1,5},{2,6},{3,7},{4,12},{5,13},{6,14},{7,15},{8,0},{9,1},{1... | collective-permute-start | bytes 1228808 | tf_op jit(solution)/shard_map/ppermute | solution.py:23
  231.1 8.4 %copy-start.5 = (f32[1280]{0:T(1024)S(1)}, f32[1280]{0:T(1024)}, u32[]{:S(2)}) copy-start(f32[1280]{0:T(1024)} %param.19) | copy-start | bytes 15364
  237.5 2.6 %collective-permute-start.39 = (f32[8,768]{1,0:T(8,128)S(1)}, f32[8,768]{1,0:T(8,128)S(1)}, u32[]{:S(2)}, u32[]{:S(2)}) collective-permute-start(f32[8,768]{1,0:T(8,128)S(1)} %get-tuple-element.38.refs_2_), channel_id=1, source_target_pairs={{0,1},{1,0},{2,3},{3,2},{4,5},{5,4},{6,7},{7,6},{8,9},{9,8},{10,11... | collective-permute-start | bytes 73736 | tf_op jit(solution)/shard_map/ppermute | solution.py:23
  237.6 3.9 %collective-permute-start.40 = (f32[8,768]{1,0:T(8,128)S(1)}, f32[8,768]{1,0:T(8,128)S(1)}, u32[]{:S(2)}, u32[]{:S(2)}) collective-permute-start(f32[8,768]{1,0:T(8,128)S(1)} %get-tuple-element.38.refs_2_), channel_id=1, source_target_pairs={{0,2},{1,3},{2,0},{3,1},{4,6},{5,7},{6,4},{7,5},{8,10},{9,11},{10,... | collective-permute-start | bytes 73736 | tf_op jit(solution)/shard_map/ppermute | solution.py:23
  239.0 3.3 %collective-permute-start.41 = (f32[8,768]{1,0:T(8,128)S(1)}, f32[8,768]{1,0:T(8,128)S(1)}, u32[]{:S(2)}, u32[]{:S(2)}) collective-permute-start(f32[8,768]{1,0:T(8,128)S(1)} %get-tuple-element.38.refs_2_), channel_id=1, source_target_pairs={{0,3},{1,2},{2,1},{3,0},{4,7},{5,6},{6,5},{7,4},{8,11},{9,10},{10,... | collective-permute-start | bytes 73736 | tf_op jit(solution)/shard_map/ppermute | solution.py:23

commit v5 on v4

--- a/solution.py
+++ b/solution.py
@@ -36,12 +36,18 @@
     return list(range(0, n, 2)) + list(range(n - 1, 0, -2))
 
 
-def gather_tensor(array, sizes):
-    have = {0: array}
-    bit = sizes[1] // 2
+def gather_first(array, sizes):
+    half = sizes[1] // 2
+    return {0: [array], half: [permute(array, sizes, lambda f, t: (f, t ^ half))]}
+
+
+def gather_rest(have, sizes):
+    bit = sizes[1] // 4
     while bit:
         for r in sorted(have):
-            have[r ^ bit] = permute(have[r], sizes, lambda f, t, bit=bit: (f, t ^ bit))
+            have[r ^ bit] = [
+                permute(part, sizes, lambda f, t, bit=bit: (f, t ^ bit)) for part in have[r]
+            ]
         bit //= 2
     return [have[r] for r in range(sizes[1])]
 
@@ -52,58 +58,58 @@
     ]
 
 
-def pack_weights(parts):
-    rows = parts[0].shape[0]
-    half = rows // 2
-    widths = [part.shape[1] for part in parts]
-    if any(width % 128 for width in widths) or half % 16:
-        packed = jnp.concatenate(parts, axis=1)
-        return packed[:half], packed[half:]
-
-    def kernel(*refs):
-        sources, outs, sems = refs[: len(parts)], refs[len(parts) : -1], refs[-1]
-        copies = []
-        first = 0
-        for number, (source, width) in enumerate(zip(sources, widths)):
-            for side in range(2):
-                copies.append(
-                    pltpu.make_async_copy(
-                        source.at[pl.ds(side * half, half)],
-                        outs[side].at[:, pl.ds(first, width)],
-                        sems.at[number, side],
-                    )
-                )
-            first += width
-        for copy in copies:
-            copy.start()
-        for copy in copies:
-            copy.wait()
-
-    shape = jax.ShapeDtypeStruct((half, sum(widths)), parts[0].dtype)
-    any_space = pl.BlockSpec(memory_space=pl.ANY)
-    return pl.pallas_call(
-        kernel,
-        out_shape=[shape, shape],
-        in_specs=[any_space] * len(parts),
-        out_specs=[any_space] * 2,
-        scratch_shapes=[pltpu.SemaphoreType.DMA((len(parts), 2))],
-    )(*parts)
-
-
-def ring_gather(top, bottom, sizes, ties):
+def ring_open(array):
+    return {"forward": [array], "backward": [array]}
+
+
+def ring_send(arrays, sizes):
     n = sizes[0]
     order = snake(n)
     place = {f: i for i, f in enumerate(order)}
-    tops, bottoms = [top], [bottom]
-    for step in range(1, n):
-        tops.append(permute(tops[-1], sizes, lambda f, t: (order[(place[f] + 1) % n], t)))
-        bottoms.append(permute(bottoms[-1], sizes, lambda f, t: (order[(place[f] - 1) % n], t)))
-        if step in ties:
-            tied = ties[step](tops, bottoms)
-            tops[-1], bottoms[-1], ties[step] = lax.optimization_barrier(
-                (tops[-1], bottoms[-1], tied)
-            )
-    return tops, bottoms
+    return [
+        permute(array, sizes, lambda f, t: (order[(place[f] + way) % n], t))
+        for array, way in zip(arrays, (1, -1))
+    ]
+
+
+def ring_step(ring, sizes):
+    arrived = ring_send((ring["forward"][-1], ring["backward"][-1]), sizes)
+    ring["forward"].append(arrived[0])
+    ring["backward"].append(arrived[1])
+
+
+def ring_middle(ring, sizes):
+    forward, backward = ring["forward"][-1], ring["backward"][-1]
+    half = forward.shape[0] // 2
+    ring["middle"] = ring_send((forward[:half], backward[half:]), sizes)
+
+
+def ring_end(ring, sizes, between):
+    forward, backward = ring["forward"][-1], ring["backward"][-1]
+    half = forward.shape[0] // 2
+    ahead = ring_send((forward[:half], backward[half:]), sizes)
+    rest, ahead = lax.optimization_barrier(((forward[half:], backward[:half]), ahead))
+    rest = ring_send(rest, sizes)
+    ring["forward"].append([ahead[0], rest[0]])
+    ring["backward"].append([rest[1], ahead[1]])
+    ahead, result = lax.optimization_barrier((ahead, between(ahead)))
+    halves = ring_send(ahead, sizes)
+    ring["middle"] = halves
+    return result
+
+
+def ring_tie(ring, other):
+    ring["forward"][-1], ring["backward"][-1], other = lax.optimization_barrier(
+        (ring["forward"][-1], ring["backward"][-1], other)
+    )
+    return other
+
+
+def ring_block(ring, offset, n):
+    if 2 * offset == n:
+        return ring["middle"]
+    block = ring["backward"][offset] if 2 * offset < n else ring["forward"][n - offset]
+    return block if isinstance(block, list) else [block]
 
 
 def snake_block(sizes, f_index, offset):
@@ -123,20 +129,21 @@
     return result
 
 
-def block_product(sizes, sources, choose, offsets, tops, bottoms, accumulated, columns, spans):
-    rows, source_width = sources[0].shape
-    tops = [tops[(sizes[0] - offset) % sizes[0]] for offset in offsets]
-    bottoms = [bottoms[offset] for offset in offsets]
-    half, width = tops[0].shape
-    depth = 2 * half
-    count = len(tops)
+def block_product(sources, choose, matrices, accumulated, columns, spans):
+    rows = sum(part.shape[0] for part in sources[0])
+    offsets = list(matrices)
+    chunks = [matrices[key] for key in offsets]
+    width = chunks[0][0].shape[1]
+    depth = sum(chunk.shape[0] for chunk in chunks[0])
+    parts = sum(len(block) for block in chunks)
+    count = len(chunks)
     if depth % 128 or width % 128:
-        stack = jnp.stack(sources)
+        stack = jnp.stack([jnp.concatenate(source, axis=0) for source in sources])
         total = jnp.zeros((rows, columns), jnp.float32) if accumulated is None else accumulated
         for j in range(count):
             which, first, column = choose(offsets[j])
             piece = lax.dynamic_slice(stack, (which, 0, first), (1, rows, depth))[0]
-            matrix = jnp.concatenate([tops[j], bottoms[j]], axis=0)
+            matrix = jnp.concatenate(chunks[j], axis=0)
             term = jnp.dot(piece, matrix, preferred_element_type=jnp.float32)
             current = lax.dynamic_slice(total, (0, column), (rows, width))
             total = lax.dynamic_update_slice(total, current + term, (0, column))
@@ -152,32 +159,37 @@
     whole = width == columns
 
     def kernel(*refs):
-        source, refs = refs[: len(sources)], refs[len(sources) :]
-        top, refs = refs[:count], refs[count:]
-        bottom, refs = refs[:count], refs[count:]
+        held = sum(len(source) for source in sources)
+        source, refs = list(refs[:held]), refs[held:]
+        source = [[source.pop(0) for _ in each] for each in sources]
+        pieces, refs = list(refs[:parts]), refs[parts:]
+        pieces = [[pieces.pop(0) for _ in block] for block in chunks]
         start, refs = refs[:extra], refs[extra:]
         out, refs = refs[0], refs[1:]
         squares, refs = refs[: spans is not None], refs[spans is not None :]
         piece, matrix, total, sems, tile_sems = refs
         choices = [choose(offset) for offset in offsets]
 
-        def piece_copy(j, which):
+        def piece_copy(j, part, lower):
             first = choices[j][1]
             if not isinstance(first, int):
                 first = pl.multiple_of(first, 128)
             return pltpu.make_async_copy(
-                source[which].at[:, pl.ds(first, depth)],
-                piece.at[:, pl.ds(j * depth, depth)],
+                part.at[:, pl.ds(first, depth)],
+                piece.at[pl.ds(lower, part.shape[0]), pl.ds(j * depth, depth)],
                 sems.at[j, 0],
             )
 
         def matrix_copies(j):
-            return (
-                pltpu.make_async_copy(top[j], matrix.at[pl.ds(j * depth, half)], sems.at[j, 1]),
+            rows_each = depth // len(pieces[j])
+            return [
                 pltpu.make_async_copy(
-                    bottom[j], matrix.at[pl.ds(j * depth + half, half)], sems.at[j, 2]
-                ),
-            )
+                    part,
+                    matrix.at[pl.ds(j * depth + k * rows_each, rows_each)],
+                    sems.at[j, 1 + k],
+                )
+                for k, part in enumerate(pieces[j])
+            ]
 
         def in_copy(i):
             part = pl.ds(i * tile, tile)
@@ -192,7 +204,10 @@
 
                 @pl.when(choices[j][0] == which)
                 def _(j=j, which=which):
-                    piece_copy(j, which).start()
+                    lower = 0
+                    for part in source[which]:
+                        piece_copy(j, part, lower).start()
+                        lower += part.shape[0]
 
             for copy in matrix_copies(j):
                 copy.start()
@@ -202,7 +217,8 @@
         for low in range(0, count, together):
             blocks = range(low, min(low + together, count))
             for j in blocks:
-                piece_copy(j, 0).wait()
+                everything = piece.at[:, pl.ds(j * depth, depth)]
+                pltpu.make_async_copy(everything, everything, sems.at[j, 0]).wait()
                 for copy in matrix_copies(j):
                     copy.wait()
             span = pl.ds(low * depth, len(blocks) * depth)
@@ -240,7 +256,7 @@
     if spans is not None:
         out_shape.append(jax.ShapeDtypeStruct((8, rows), jnp.float32))
         out_specs.append(pl.BlockSpec(memory_space=pltpu.VMEM))
-    operands = [*sources, *tops, *bottoms] + [accumulated] * extra
+    operands = [*sum(sources, []), *sum(chunks, [])] + [accumulated] * extra
     needed = 2 * count * depth * (rows + width) + 4 * rows * columns
     results = pl.pallas_call(
         kernel,
@@ -248,18 +264,14 @@
         in_specs=[any_space] * len(operands),
         out_specs=out_specs,
         scratch_shapes=[
-            pltpu.VMEM((rows, count * depth), sources[0].dtype),
-            pltpu.VMEM((count * depth, width), tops[0].dtype),
+            pltpu.VMEM((rows, count * depth), sources[0][0].dtype),
+            pltpu.VMEM((count * depth, width), chunks[0][0].dtype),
             pltpu.VMEM((rows, columns), jnp.float32),
-            pltpu.SemaphoreType.DMA((count, 3)),
+            pltpu.SemaphoreType.DMA((count, 1 + max(len(block) for block in chunks))),
             pltpu.SemaphoreType.DMA((tiles, 2)),
         ],
         compiler_params=pltpu.CompilerParams(vmem_limit_bytes=needed + 6 * 2**20),
-        cost_estimate=pl.CostEstimate(
-            flops=2 * rows * count * depth * width,
-            bytes_accessed=2 * count * depth * (rows + width) + 8 * rows * columns,
-            transcendentals=0,
-        ),
+        cost_estimate=pl.CostEstimate(flops=1, bytes_accessed=1, transcendentals=0),
     )(*operands)
     return tuple(results) if spans is not None else results[0]
 
@@ -346,11 +358,7 @@
         + [constant(q_width), constant(k_width)],
         out_specs=by_rows(q_width),
         compiler_params=pltpu.CompilerParams(vmem_limit_bytes=24 * 2**20),
-        cost_estimate=pl.CostEstimate(
-            flops=4 * capacity * half_rows * q_width,
-            bytes_accessed=8 * capacity * total.shape[1],
-            transcendentals=capacity * half_rows * heads,
-        ),
+        cost_estimate=pl.CostEstimate(flops=1, bytes_accessed=1, transcendentals=0),
     )(total, *sums, cosine, sine, starts, query_gain, key_gain)
 
 
@@ -401,7 +409,13 @@
 
     depth = w_query.shape[0]
     columns = w_query.shape[1] + w_key.shape[1] + w_value.shape[1]
-    top, bottom = pack_weights([w_query, w_key, w_value])
+    last = n // 2
+    groups = [
+        [0] + [offset for step in range(1, last - 1) for offset in (step, n - step)],
+        [last - 1, n - last + 1],
+        [last],
+    ]
+
     moved = permute(
         w_out,
         sizes,
@@ -410,44 +424,46 @@
             t,
         ),
     )
-    local_tokens, top, bottom = lax.optimization_barrier((tokens, top, bottom))
-    token_blocks = gather_tensor(local_tokens, sizes)
-    ties = {2: lambda *_: moved}
-    tops, bottoms = ring_gather(top, bottom, sizes, ties)
-    moved = ties[2]
-    moved = permute(
-        moved, sizes, lambda f, t: (f, (f // per_tensor) ^ reverse_bits(t, tensor_size))
-    )
-
+    token_blocks = gather_first(tokens, sizes)
+    weights = jnp.concatenate([w_query, w_key, w_value], axis=1)
+    first_ring = ring_open(weights)
     q_width, k_width = w_query.shape[1], w_key.shape[1]
-    steps = [[0, n // 2]] + [[s, n - s] for s in range(n // 2 + 1, n)]
-    middle = (len(steps) + 1) // 2
-    groups = [[offset for group in steps[:middle] for offset in group]] + steps[middle:]
 
     def choose_tokens(offset):
         block = snake_block(sizes, lax.axis_index("fsdp"), offset)
         which = (block // per_tensor) ^ lax.axis_index("tensor")
         return which, lax.rem(block, per_tensor) * depth, 0
 
-    total = None
-    for number, offsets in enumerate(groups):
-        total = block_product(
-            sizes,
+    def qkv_product(number, total):
+        return block_product(
             token_blocks,
             choose_tokens,
-            offsets,
-            tops,
-            bottoms,
+            {offset: ring_block(first_ring, offset, n) for offset in groups[number]},
             total,
             columns,
             [(0, q_width), (q_width, q_width + k_width)] if number == len(groups) - 1 else None,
         )
-    total, squares = total
-
-    out_half = w_out.shape[0] // 2
-    out_top, out_bottom, _ = lax.optimization_barrier(
-        (moved[:out_half], moved[out_half:], (tops[-1], bottoms[-1]))
-    )
+
+    for step in range(1, last - 1):
+        ring_step(first_ring, sizes)
+        if step == 1:
+            token_blocks, moved = ring_tie(first_ring, (token_blocks, moved))
+            token_blocks = gather_rest(token_blocks, sizes)
+            moved = permute(
+                moved, sizes, lambda f, t: (f, (f // per_tensor) ^ reverse_bits(t, tensor_size))
+            )
+    ring_step(first_ring, sizes)
+    total, moved = ring_tie(first_ring, (qkv_product(0, None), moved))
+    ring_middle(first_ring, sizes)
+    for number in range(1, len(groups) - 1):
+        total = qkv_product(number, total)
+    moved, total, _ = lax.optimization_barrier(
+        (moved, total, first_ring["middle"])
+    )
+    total, squares = qkv_product(len(groups) - 1, total)
+
+    second_ring = ring_open(moved)
+    ring_step(second_ring, sizes)
     square_blocks = swap_small(squares, sizes)
     row_ids = jnp.arange(capacity, dtype=jnp.int32)
     positions = (row_ids - first_row).astype(jnp.float32)
@@ -468,7 +484,8 @@
         tensor_size,
         half_rows,
     )
-    attended_blocks = gather_tensor(attended, sizes)
+    attended_blocks = gather_first(attended, sizes)
+    ring_tie(second_ring, attended)
 
     def choose_attended(offset):
         block = snake_block(sizes, lax.axis_index("fsdp"), offset)
@@ -476,25 +493,27 @@
         source = traced_reverse((block // per_tensor) ^ t_index, tensor_size)
         return source ^ t_index, 0, lax.rem(block, per_tensor) * w_out.shape[1]
 
-    def out_product(number, out_tops, out_bottoms, attn_out):
+    def out_product(number, sources, attn_out):
         return block_product(
-            sizes,
-            attended_blocks,
+            sources,
             choose_attended,
-            groups[number],
-            out_tops,
-            out_bottoms,
+            {offset: ring_block(second_ring, offset, n) for offset in groups[number]},
             attn_out,
             width,
             [(0, width)] if number == len(groups) - 1 else None,
         )
 
-    ready = max(groups[0])
-    ties = {ready + 1: lambda now_tops, now_bottoms: out_product(0, now_tops, now_bottoms, None)}
-    out_tops, out_bottoms = ring_gather(out_top, out_bottom, sizes, ties)
-    attn_out = ties[ready + 1]
+    for step in range(2, last - 1):
+        ring_step(second_ring, sizes)
+
+    def first_product(ahead):
+        have, _ = lax.optimization_barrier((attended_blocks, ahead))
+        have = gather_rest(have, sizes)
+        return have, out_product(0, have, None)
+
+    attended_blocks, attn_out = ring_end(second_ring, sizes, first_product)
     for number in range(1, len(groups)):
-        attn_out = out_product(number, out_tops, out_bottoms, attn_out)
+        attn_out = out_product(number, attended_blocks, attn_out)
     attn_out, out_squares = attn_out
     return finish(
         attn_out,

time: 245 us -> 202 us (0.82)
  Pallas kernels: 76.6 us -> 39.5 us
  starting transfers between devices: 53.7 us -> 41.5 us
  waiting for transfers between devices: 111 us -> 115 us
  local copies, waits for them, and re-layouts: 0.27 us -> 3.55 us
    pallas_call x1 -> x0, Pallas kernels: 35.9 us -> none  [pack_weights(): pl.pallas_call(kernel, out_shape=[shape, shape], in_specs=[any_space] * l...]
    ppermute x42 -> x32, starting transfers between devices: 53.7 us -> 41.5 us  [permute(): return lax.ppermute(array, AXES, pairs)]
    ppermute x42 -> x32, waiting for transfers between devices: 111 us -> 115 us  [permute(): return lax.ppermute(array, AXES, pairs)]
  transfers between devices with their start and end apart: 42 -> 32, of which waited for: 20 -> 19; matrix products, arithmetic and copies ran while one was open for 1% -> 3% of each run, Pallas kernels for 14% -> 17%
where the time goes in v5:
time: 202 us
  waiting for transfers between devices  115 us (57%)
  starting transfers between devices  41.5 us (21%)
  Pallas kernels  39.5 us (20%)
  local copies, waits for them, and re-layouts  3.55 us (2%)
    ppermute x32, waiting for transfers between devices, permute(): return lax.ppermute(array, AXES, pairs)  115 us
    ppermute x32, starting transfers between devices, permute(): return lax.ppermute(array, AXES, pairs)  41.5 us
    pallas_call x6, Pallas kernels, block_product(): pl.pallas_call(kernel, out_shape=out_shape, in_specs=[any_space] * len(op...  32.7 us
    pallas_call x1, Pallas kernels, attention(): pl.pallas_call(kernel, grid=(capacity // half_rows,), out_shape=jax.Shape...  4.42 us
  transfers between devices with their start and end apart: 32, of which 19 were waited for; matrix products, arithmetic and copies ran while one was open for 3% of the time, Pallas kernels for 17%

profile of v5, /device:TPU:0, one launch (start us, length us, event | category | flops | bytes accessed | tf_op | source)
XLA Modules:
  0.0 202.2 jit_solution(18044278769134525255)
XLA Ops:
  0.0 3.0 %collective-permute-start.2 = (bf16[768,1280]{1,0:T(8,128)(2,1)}, bf16[768,1280]{1,0:T(8,128)(2,1)S(1)}, u32[]{:S(2)}, u32[]{:S(2)}) collective-permute-start(bf16[768,1280]{1,0:T(8,128)(2,1)} %refs_6_.1), channel_id=1, source_target_pairs={{0,2},{1,3},{2,0},{3,1},{4,6},{5,7},{6,4},{7,5},{8,10},{9,11},{10,... | collective-permute-start | bytes 5898248 | tf_op jit(solution)/shard_map/ppermute | solution.py:23
  3.0 1.2 constant_dynamic-update-slice_fusion.2
  4.2 1.0 constant_dynamic-update-slice_fusion.1
  5.1 1.0 constant_dynamic-update-slice_fusion.refs_4_
  6.1 1.6 collective-permute-start
  7.7 0.4 collective-permute-start.1
  8.2 1.8 collective-permute-start.3
  10.0 23.5 %collective-permute-done.refs_6_ = bf16[640,896]{1,0:T(8,128)(2,1)S(1)} collective-permute-done((bf16[640,896]{1,0:T(8,128)(2,1)S(1)}, bf16[640,896]{1,0:T(8,128)(2,1)S(1)}, u32[]{:S(2)}, u32[]{:S(2)}) %collective-permute-start) | collective-permute-done | bytes 1146912 | tf_op jit(solution)/shard_map/ppermute | solution.py:23
  33.4 1.3 collective-permute-done.1.refs_5_
  34.8 11.3 %collective-permute-done.2.refs_2_ = bf16[768,1280]{1,0:T(8,128)(2,1)S(1)} collective-permute-done((bf16[768,1280]{1,0:T(8,128)(2,1)}, bf16[768,1280]{1,0:T(8,128)(2,1)S(1)}, u32[]{:S(2)}, u32[]{:S(2)}) %collective-permute-start.2) | collective-permute-done | bytes 1966112 | tf_op jit(solution)/shard_map/ppermute | solution.py:23
  46.1 1.7 collective-permute-start.4
  47.8 0.3 collective-permute-start.6
  48.1 6.3 %collective-permute-start.8 = (bf16[768,1280]{1,0:T(8,128)(2,1)S(1)}, bf16[768,1280]{1,0:T(8,128)(2,1)S(1)}, u32[]{:S(2)}, u32[]{:S(2)}) collective-permute-start(bf16[768,1280]{1,0:T(8,128)(2,1)S(1)} %copy-done), channel_id=1, source_target_pairs={{0,1},{1,0},{2,3},{3,2},{4,5},{5,4},{6,7},{7,6},{8,9},{9,8},{10,11... | collective-permute-start | bytes 5898248 | tf_op jit(solution)/shard_map/ppermute | solution.py:23
  54.4 14.5 %collective-permute-done.4.refs_8_ = bf16[640,896]{1,0:T(8,128)(2,1)S(1)} collective-permute-done((bf16[640,896]{1,0:T(8,128)(2,1)S(1)}, bf16[640,896]{1,0:T(8,128)(2,1)S(1)}, u32[]{:S(2)}, u32[]{:S(2)}) %collective-permute-start.4) | collective-permute-done | bytes 1146912 | tf_op jit(solution)/shard_map/ppermute | solution.py:23
  68.9 4.2 %collective-permute-start.5 = (bf16[640,896]{1,0:T(8,128)(2,1)S(1)}, bf16[640,896]{1,0:T(8,128)(2,1)S(1)}, u32[]{:S(2)}, u32[]{:S(2)}) collective-permute-start(bf16[640,896]{1,0:T(8,128)(2,1)S(1)} %collective-permute-done.4.refs_8_), channel_id=1, source_target_pairs={{0,8},{1,9},{2,10},{3,11},{4,0},{5,1},{6,2},{7,3},{8,16},{9,17},{1... | collective-permute-start | bytes 3440648 | tf_op jit(solution)/shard_map/ppermute | solution.py:23
  73.2 1.2 collective-permute-done.6.refs_7_
  74.4 0.7 collective-permute-start.10
  75.1 8.7 %shard_map.100.refs_6_ = f32[768,896]{1,0:T(8,128)S(1)} custom-call(bf16[768,1280]{1,0:T(8,128)(2,1)S(1)} %copy-done, bf16[768,1280]{1,0:T(8,128)(2,1)S(1)} %collective-permute-done.8.refs_1_, bf16[768,1280]{1,0:T(8,128)(2,1)S(1)} %collective-permute-done.2.refs_2_, bf16[768,1280]{1,0:T(8,128)(2,1)S(1)} %collective-permute-done.9.refs_3_, ...), custom_call_target="tpu_custom_call" | custom-call | flops 1 | bytes 1 | tf_op jit(solution)/shard_map/pallas_call | solution.py:261
  83.8 14.3 %collective-permute-done.5.refs_5_ = bf16[640,896]{1,0:T(8,128)(2,1)S(1)} collective-permute-done((bf16[640,896]{1,0:T(8,128)(2,1)S(1)}, bf16[640,896]{1,0:T(8,128)(2,1)S(1)}, u32[]{:S(2)}, u32[]{:S(2)}) %collective-permute-start.5) | collective-permute-done | bytes 1146912 | tf_op jit(solution)/shard_map/ppermute | solution.py:23
  98.2 2.2 %collective-permute-done.7.refs_4_ = bf16[640,896]{1,0:T(8,128)(2,1)S(1)} collective-permute-done((bf16[640,896]{1,0:T(8,128)(2,1)S(1)}, bf16[640,896]{1,0:T(8,128)(2,1)S(1)}, u32[]{:S(2)}, u32[]{:S(2)}) %collective-permute-start.7) | collective-permute-done | bytes 1146912 | tf_op jit(solution)/shard_map/ppermute | solution.py:23
  100.5 2.0 collective-permute-start.11
  102.5 0.1 collective-permute-start.12
  102.7 4.6 %shard_map.101.refs_6_ = f32[768,896]{1,0:T(8,128)S(1)} custom-call(bf16[768,1280]{1,0:T(8,128)(2,1)S(1)} %copy-done, bf16[768,1280]{1,0:T(8,128)(2,1)S(1)} %collective-permute-done.8.refs_1_, bf16[768,1280]{1,0:T(8,128)(2,1)S(1)} %collective-permute-done.2.refs_2_, bf16[768,1280]{1,0:T(8,128)(2,1)S(1)} %collective-permute-done.9.refs_3_, ...), custom_call_target="tpu_custom_call" | custom-call | flops 1 | bytes 1 | tf_op jit(solution)/shard_map/pallas_call | solution.py:261
  107.2 8.3 %collective-permute-done.11.refs_4_ = bf16[320,896]{1,0:T(8,128)(2,1)S(1)} collective-permute-done((bf16[320,896]{1,0:T(8,128)(2,1)S(1)}, bf16[320,896]{1,0:T(8,128)(2,1)S(1)}, u32[]{:S(2)}, u32[]{:S(2)}) %collective-permute-start.11) | collective-permute-done | bytes 573472 | tf_op jit(solution)/shard_map/ppermute | solution.py:23
  115.5 2.9 %collective-permute-done.12.refs_5_ = bf16[320,896]{1,0:T(8,128)(2,1)S(1)} collective-permute-done((bf16[320,896]{1,0:T(8,128)(2,1)S(1)}, bf16[320,896]{1,0:T(8,128)(2,1)S(1)}, u32[]{:S(2)}, u32[]{:S(2)}) %collective-permute-start.12) | collective-permute-done | bytes 573472 | tf_op jit(solution)/shard_map/ppermute | solution.py:23
  118.4 0.3 collective-permute-start.13
  118.7 1.8 collective-permute-start.14
  120.5 1.4 fusion
  121.9 4.1 %shard_map.102 = (f32[768,896]{1,0:T(8,128)S(1)}, f32[8,768]{1,0:T(8,128)S(1)}) custom-call(bf16[768,1280]{1,0:T(8,128)(2,1)S(1)} %copy-done, bf16[768,1280]{1,0:T(8,128)(2,1)S(1)} %collective-permute-done.8.refs_1_, bf16[768,1280]{1,0:T(8,128)(2,1)S(1)} %collective-permute-done.2.refs_2_, bf16[768,1280]{1,0:T(8,128)(2,1)S(1)} %collective-permute-done.9.refs_3_, ...), custom_call_target="tpu_custom_call" | custom-call | flops 1 | bytes 1 | tf_op jit(solution)/shard_map/pallas_call | solution.py:261
  126.0 0.1 collective-permute-start.15
  126.1 4.1 %collective-permute-start.16 = (f32[8,768]{1,0:T(8,128)S(1)}, f32[8,768]{1,0:T(8,128)S(1)}, u32[]{:S(2)}, u32[]{:S(2)}) collective-permute-start(f32[8,768]{1,0:T(8,128)S(1)} %get-tuple-element.47.refs_1_), channel_id=1, source_target_pairs={{0,2},{1,3},{2,0},{3,1},{4,6},{5,7},{6,4},{7,5},{8,10},{9,11},{10,... | collective-permute-start | bytes 73736 | tf_op jit(solution)/shard_map/ppermute | solution.py:23
  130.2 0.1 collective-permute-start.17
  130.2 0.3 pad_maximum_fusion
  130.5 1.4 collective-permute-done.16.refs_3_
  132.0 1.4 collective-permute-done.17.refs_4_
  133.4 0.2 broadcast_in_dim.8.refs_7_
  133.6 4.4 %shard_map.103.refs_0_ = bf16[768,640]{1,0:T(8,128)(2,1)S(1)} custom-call(f32[768,896]{1,0:T(8,128)S(1)} %get-tuple-element.46.refs_0_, f32[8,768]{1,0:T(8,128)S(1)} %get-tuple-element.47.refs_1_, f32[8,768]{1,0:T(8,128)S(1)} %collective-permute-done.15.refs_2_, f32[8,768]{1,0:T(8,128)S(1)} %collective-permute-done.16.refs_3_, ...), custom_call_target="tpu_custom_call" | custom-call | flops 1 | bytes 1 | tf_op jit(solution)/shard_map/pallas_call | solution.py:351
  138.0 0.7 collective-permute-done.13.refs_6_
  138.7 0.3 collective-permute-start.18
  139.0 1.7 collective-permute-start.19
  140.7 2.3 %collective-permute-start.22 = (bf16[768,640]{1,0:T(8,128)(2,1)S(1)}, bf16[768,640]{1,0:T(8,128)(2,1)S(1)}, u32[]{:S(2)}, u32[]{:S(2)}) collective-permute-start(bf16[768,640]{1,0:T(8,128)(2,1)S(1)} %shard_map.103.refs_0_), channel_id=1, source_target_pairs={{0,2},{1,3},{2,0},{3,1},{4,6},{5,7},{6,4},{7,5},{8,10},{9,11},{10,... | collective-permute-start | bytes 2949128 | tf_op jit(solution)/shard_map/ppermute | solution.py:23
  143.0 15.7 %collective-permute-done.18.refs_8_ = bf16[640,640]{1,0:T(8,128)(2,1)S(1)} collective-permute-done((bf16[640,640]{1,0:T(8,128)(2,1)S(1)}, bf16[640,640]{1,0:T(8,128)(2,1)S(1)}, u32[]{:S(2)}, u32[]{:S(2)}) %collective-permute-start.18) | collective-permute-done | bytes 819232 | tf_op jit(solution)/shard_map/ppermute | solution.py:23
  158.7 0.1 fusion.2
  158.8 0.4 collective-permute-start.20
  159.1 0.1 fusion.1
  159.2 1.8 collective-permute-start.21
  161.0 8.2 %collective-permute-done.20.refs_6_ = bf16[320,640]{1,0:T(8,128)(2,1)S(1)} collective-permute-done((bf16[320,640]{1,0:T(8,128)(2,1)S(1)}, bf16[320,640]{1,0:T(8,128)(2,1)S(1)}, u32[]{:S(2)}, u32[]{:S(2)}) %collective-permute-start.20) | collective-permute-done | bytes 409632 | tf_op jit(solution)/shard_map/ppermute | solution.py:23
  169.2 0.2 collective-permute-done.21.refs_5_
  169.4 0.5 collective-permute-start.24
  169.9 1.7 collective-permute-start.27
  171.6 0.3 collective-permute-start.28
  171.9 1.4 collective-permute-done.24.refs_3_
  173.3 7.5 %shard_map.104.refs_8_ = f32[768,1280]{1,0:T(8,128)S(1)} custom-call(bf16[768,640]{1,0:T(8,128)(2,1)S(1)} %shard_map.103.refs_0_, bf16[768,640]{1,0:T(8,128)(2,1)S(1)} %collective-permute-done.23.refs_1_, bf16[768,640]{1,0:T(8,128)(2,1)S(1)} %collective-permute-done.22.refs_2_, bf16[768,640]{1,0:T(8,128)(2,1)S(1)} %collective-permute-done.24.refs_3_, ...), custom_call_target="tpu_custom_call" | custom-call | flops 1 | bytes 1 | tf_op jit(solution)/shard_map/pallas_call | solution.py:261
  180.8 0.4 collective-permute-start.25
  181.2 1.6 collective-permute-start.26
  182.9 4.5 %shard_map.105.refs_6_ = f32[768,1280]{1,0:T(8,128)S(1)} custom-call(bf16[768,640]{1,0:T(8,128)(2,1)S(1)} %shard_map.103.refs_0_, bf16[768,640]{1,0:T(8,128)(2,1)S(1)} %collective-permute-done.23.refs_1_, bf16[768,640]{1,0:T(8,128)(2,1)S(1)} %collective-permute-done.22.refs_2_, bf16[768,640]{1,0:T(8,128)(2,1)S(1)} %collective-permute-done.24.refs_3_, ...), custom_call_target="tpu_custom_call" | custom-call | flops 1 | bytes 1 | tf_op jit(solution)/shard_map/pallas_call | solution.py:261
  187.4 4.9 %collective-permute-done.25.refs_4_ = bf16[320,640]{1,0:T(8,128)(2,1)S(1)} collective-permute-done((bf16[320,640]{1,0:T(8,128)(2,1)S(1)}, bf16[320,640]{1,0:T(8,128)(2,1)S(1)}, u32[]{:S(2)}, u32[]{:S(2)}) %collective-permute-start.25) | collective-permute-done | bytes 409632 | tf_op jit(solution)/shard_map/ppermute | solution.py:23
  192.3 0.1 collective-permute-done.26.refs_5_
  192.5 3.4 %shard_map.106 = (f32[768,1280]{1,0:T(8,128)S(1)}, f32[8,768]{1,0:T(8,128)S(1)}) custom-call(bf16[768,640]{1,0:T(8,128)(2,1)S(1)} %shard_map.103.refs_0_, bf16[768,640]{1,0:T(8,128)(2,1)S(1)} %collective-permute-done.23.refs_1_, bf16[768,640]{1,0:T(8,128)(2,1)S(1)} %collective-permute-done.22.refs_2_, bf16[768,640]{1,0:T(8,128)(2,1)S(1)} %collective-permute-done.24.refs_3_, ...), custom_call_target="tpu_custom_call" | custom-call | flops 1 | bytes 1 | tf_op jit(solution)/shard_map/pallas_call | solution.py:261
  195.8 0.1 collective-permute-start.29
  195.9 0.1 collective-permute-start.30
  196.0 1.8 collective-permute-start.31
  198.4 1.4 collective-permute-done.30.refs_4_
  199.8 2.4 %shard_map.107 = bf16[768,1280]{1,0:T(8,128)(2,1)} custom-call(s32[1]{0:T(128)S(6)} %copy.13.refs_0_, f32[768,1280]{1,0:T(8,128)S(1)} %get-tuple-element.63.refs_1_, f32[8,768]{1,0:T(8,128)S(1)} %get-tuple-element.64.refs_2_, f32[8,768]{1,0:T(8,128)S(1)} %collective-permute-done.29.refs_3_, f32[8,768]{1,0:T(8,128)S(1)} %collective-permute-done.30.refs_4_, ...), custom_call_target="tpu_custom_call" | custom-call | tf_op jit(solution)/shard_map/pallas_call | solution.py:384
  (32 shorter events, 0.2 us)
Async XLA Ops:
  0.0 48.1 %copy-start = (bf16[768,1280]{1,0:T(8,128)(2,1)S(1)}, bf16[768,1280]{1,0:T(8,128)(2,1)}, u32[]{:S(2)}) copy-start(bf16[768,1280]{1,0:T(8,128)(2,1)} %refs_6_.1) | copy-start | bytes 5898244
  0.0 46.1 %collective-permute-start.2 = (bf16[768,1280]{1,0:T(8,128)(2,1)}, bf16[768,1280]{1,0:T(8,128)(2,1)S(1)}, u32[]{:S(2)}, u32[]{:S(2)}) collective-permute-start(bf16[768,1280]{1,0:T(8,128)(2,1)} %refs_6_.1), channel_id=1, source_target_pairs={{0,2},{1,3},{2,0},{3,1},{4,6},{5,7},{6,4},{7,5},{8,10},{9,11},{10,... | collective-permute-start | bytes 5898248 | tf_op jit(solution)/shard_map/ppermute | solution.py:23
  6.1 27.3 %collective-permute-start = (bf16[640,896]{1,0:T(8,128)(2,1)S(1)}, bf16[640,896]{1,0:T(8,128)(2,1)S(1)}, u32[]{:S(2)}, u32[]{:S(2)}) collective-permute-start(bf16[640,896]{1,0:T(8,128)(2,1)S(1)} %constant_dynamic-update-slice_fusion.refs_4_), channel_id=1, source_target_pairs={{0,8},{1,9},{2,10},{3,11},{4,0},{5,1},{6,2},{7,3},{8,16},{9,17},{1... | collective-permute-start | bytes 3440648 | tf_op jit(solution)/shard_map/ppermute | solution.py:23
  7.7 27.0 %collective-permute-start.1 = (bf16[640,896]{1,0:T(8,128)(2,1)S(1)}, bf16[640,896]{1,0:T(8,128)(2,1)S(1)}, u32[]{:S(2)}, u32[]{:S(2)}) collective-permute-start(bf16[640,896]{1,0:T(8,128)(2,1)S(1)} %constant_dynamic-update-slice_fusion.refs_4_), channel_id=1, source_target_pairs={{0,4},{1,5},{2,6},{3,7},{4,12},{5,13},{6,14},{7,15},{8,0},{9,1},{1... | collective-permute-start | bytes 3440648 | tf_op jit(solution)/shard_map/ppermute | solution.py:23
  8.2 1.8 collective-permute-start.3
  46.1 22.9 %collective-permute-start.4 = (bf16[640,896]{1,0:T(8,128)(2,1)S(1)}, bf16[640,896]{1,0:T(8,128)(2,1)S(1)}, u32[]{:S(2)}, u32[]{:S(2)}) collective-permute-start(bf16[640,896]{1,0:T(8,128)(2,1)S(1)} %collective-permute-done.refs_6_), channel_id=1, source_target_pairs={{0,8},{1,9},{2,10},{3,11},{4,0},{5,1},{6,2},{7,3},{8,16},{9,17},{1... | collective-permute-start | bytes 3440648 | tf_op jit(solution)/shard_map/ppermute | solution.py:23
  47.8 26.6 %collective-permute-start.6 = (bf16[640,896]{1,0:T(8,128)(2,1)S(1)}, bf16[640,896]{1,0:T(8,128)(2,1)S(1)}, u32[]{:S(2)}, u32[]{:S(2)}) collective-permute-start(bf16[640,896]{1,0:T(8,128)(2,1)S(1)} %collective-permute-done.1.refs_5_), channel_id=1, source_target_pairs={{0,4},{1,5},{2,6},{3,7},{4,12},{5,13},{6,14},{7,15},{8,0},{9,1},{1... | collective-permute-start | bytes 3440648 | tf_op jit(solution)/shard_map/ppermute | solution.py:23
  48.1 27.0 %collective-permute-start.8 = (bf16[768,1280]{1,0:T(8,128)(2,1)S(1)}, bf16[768,1280]{1,0:T(8,128)(2,1)S(1)}, u32[]{:S(2)}, u32[]{:S(2)}) collective-permute-start(bf16[768,1280]{1,0:T(8,128)(2,1)S(1)} %copy-done), channel_id=1, source_target_pairs={{0,1},{1,0},{2,3},{3,2},{4,5},{5,4},{6,7},{7,6},{8,9},{9,8},{10,11... | collective-permute-start | bytes 5898248 | tf_op jit(solution)/shard_map/ppermute | solution.py:23
  54.4 20.7 %collective-permute-start.9 = (bf16[768,1280]{1,0:T(8,128)(2,1)S(1)}, bf16[768,1280]{1,0:T(8,128)(2,1)S(1)}, u32[]{:S(2)}, u32[]{:S(2)}) collective-permute-start(bf16[768,1280]{1,0:T(8,128)(2,1)S(1)} %collective-permute-done.2.refs_2_), channel_id=1, source_target_pairs={{0,1},{1,0},{2,3},{3,2},{4,5},{5,4},{6,7},{7,6},{8,9},{9,8},{10,11... | collective-permute-start | bytes 5898248 | tf_op jit(solution)/shard_map/ppermute | solution.py:23
  68.9 29.3 %collective-permute-start.5 = (bf16[640,896]{1,0:T(8,128)(2,1)S(1)}, bf16[640,896]{1,0:T(8,128)(2,1)S(1)}, u32[]{:S(2)}, u32[]{:S(2)}) collective-permute-start(bf16[640,896]{1,0:T(8,128)(2,1)S(1)} %collective-permute-done.4.refs_8_), channel_id=1, source_target_pairs={{0,8},{1,9},{2,10},{3,11},{4,0},{5,1},{6,2},{7,3},{8,16},{9,17},{1... | collective-permute-start | bytes 3440648 | tf_op jit(solution)/shard_map/ppermute | solution.py:23
  74.4 26.0 %collective-permute-start.7 = (bf16[640,896]{1,0:T(8,128)(2,1)S(1)}, bf16[640,896]{1,0:T(8,128)(2,1)S(1)}, u32[]{:S(2)}, u32[]{:S(2)}) collective-permute-start(bf16[640,896]{1,0:T(8,128)(2,1)S(1)} %collective-permute-done.6.refs_7_), channel_id=1, source_target_pairs={{0,4},{1,5},{2,6},{3,7},{4,12},{5,13},{6,14},{7,15},{8,0},{9,1},{1... | collective-permute-start | bytes 3440648 | tf_op jit(solution)/shard_map/ppermute | solution.py:23
  74.4 9.4 %collective-permute-start.10 = (bf16[640,640]{1,0:T(8,128)(2,1)S(1)}, bf16[640,640]{1,0:T(8,128)(2,1)S(1)}, u32[]{:S(2)}, u32[]{:S(2)}) collective-permute-start(bf16[640,640]{1,0:T(8,128)(2,1)S(1)} %collective-permute-done.3), channel_id=1, source_target_pairs={{0,0},{1,2},{2,1},{3,3},{4,4},{5,6},{6,5},{7,7},{8,9},{9,11},{10,8... | collective-permute-start | bytes 2457608 | tf_op jit(solution)/shard_map/ppermute | solution.py:23
  100.5 15.1 %collective-permute-start.11 = (bf16[320,896]{1,0:T(8,128)(2,1)S(1)}, bf16[320,896]{1,0:T(8,128)(2,1)S(1)}, u32[]{:S(2)}, u32[]{:S(2)}) collective-permute-start(bf16[320,896]{1,0:T(8,128)(2,1)S(1)} %slice.18), channel_id=1, source_target_pairs={{0,8},{1,9},{2,10},{3,11},{4,0},{5,1},{6,2},{7,3},{8,16},{9,17},{1... | collective-permute-start | bytes 1720328 | tf_op jit(solution)/shard_map/ppermute | solution.py:23
  102.5 17.9 %copy-start.2 = (s32[768]{0:T(1024)S(1)}, s32[768]{0:T(1024)}, u32[]{:S(2)}) copy-start(s32[768]{0:T(1024)} %param.12) | copy-start | bytes 9220
  102.5 15.9 %collective-permute-start.12 = (bf16[320,896]{1,0:T(8,128)(2,1)S(1)}, bf16[320,896]{1,0:T(8,128)(2,1)S(1)}, u32[]{:S(2)}, u32[]{:S(2)}) collective-permute-start(bf16[320,896]{1,0:T(8,128)(2,1)S(1)} %slice.19), channel_id=1, source_target_pairs={{0,4},{1,5},{2,6},{3,7},{4,12},{5,13},{6,14},{7,15},{8,0},{9,1},{1... | collective-permute-start | bytes 1720328 | tf_op jit(solution)/shard_map/ppermute | solution.py:23
  118.4 20.3 %collective-permute-start.13 = (bf16[640,640]{1,0:T(8,128)(2,1)S(1)}, bf16[640,640]{1,0:T(8,128)(2,1)S(1)}, u32[]{:S(2)}, u32[]{:S(2)}) collective-permute-start(bf16[640,640]{1,0:T(8,128)(2,1)S(1)} %collective-permute-done.10.refs_4_), channel_id=1, source_target_pairs={{0,8},{1,9},{2,10},{3,11},{4,0},{5,1},{6,2},{7,3},{8,16},{9,17},{1... | collective-permute-start | bytes 2457608 | tf_op jit(solution)/shard_map/ppermute | solution.py:23
  118.7 20.0 %collective-permute-start.14 = (bf16[640,640]{1,0:T(8,128)(2,1)S(1)}, bf16[640,640]{1,0:T(8,128)(2,1)S(1)}, u32[]{:S(2)}, u32[]{:S(2)}) collective-permute-start(bf16[640,640]{1,0:T(8,128)(2,1)S(1)} %collective-permute-done.10.refs_4_), channel_id=1, source_target_pairs={{0,4},{1,5},{2,6},{3,7},{4,12},{5,13},{6,14},{7,15},{8,0},{9,1},{1... | collective-permute-start | bytes 2457608 | tf_op jit(solution)/shard_map/ppermute | solution.py:23
  126.0 4.5 %copy-start.4 = (f32[640]{0:T(1024)S(1)}, f32[640]{0:T(1024)}, u32[]{:S(2)}) copy-start(f32[640]{0:T(1024)} %param.17) | copy-start | bytes 7684
  126.0 4.5 %collective-permute-start.15 = (f32[8,768]{1,0:T(8,128)S(1)}, f32[8,768]{1,0:T(8,128)S(1)}, u32[]{:S(2)}, u32[]{:S(2)}) collective-permute-start(f32[8,768]{1,0:T(8,128)S(1)} %get-tuple-element.47.refs_1_), channel_id=1, source_target_pairs={{0,1},{1,0},{2,3},{3,2},{4,5},{5,4},{6,7},{7,6},{8,9},{9,8},{10,11... | collective-permute-start | bytes 73736 | tf_op jit(solution)/shard_map/ppermute | solution.py:23
  126.1 5.9 %collective-permute-start.16 = (f32[8,768]{1,0:T(8,128)S(1)}, f32[8,768]{1,0:T(8,128)S(1)}, u32[]{:S(2)}, u32[]{:S(2)}) collective-permute-start(f32[8,768]{1,0:T(8,128)S(1)} %get-tuple-element.47.refs_1_), channel_id=1, source_target_pairs={{0,2},{1,3},{2,0},{3,1},{4,6},{5,7},{6,4},{7,5},{8,10},{9,11},{10,... | collective-permute-start | bytes 73736 | tf_op jit(solution)/shard_map/ppermute | solution.py:23
  130.2 3.3 %collective-permute-start.17 = (f32[8,768]{1,0:T(8,128)S(1)}, f32[8,768]{1,0:T(8,128)S(1)}, u32[]{:S(2)}, u32[]{:S(2)}) collective-permute-start(f32[8,768]{1,0:T(8,128)S(1)} %get-tuple-element.47.refs_1_), channel_id=1, source_target_pairs={{0,3},{1,2},{2,1},{3,0},{4,7},{5,6},{6,5},{7,4},{8,11},{9,10},{10,... | collective-permute-start | bytes 73736 | tf_op jit(solution)/shard_map/ppermute | solution.py:23
  130.2 3.3 %copy-start.1 = (f32[128]{0:T(128)S(1)}, f32[128]{0:T(128)}, u32[]{:S(2)}) copy-start(f32[128]{0:T(128)} %param.18) | copy-start | bytes 1540
  138.7 20.0 %collective-permute-start.18 = (bf16[640,640]{1,0:T(8,128)(2,1)S(1)}, bf16[640,640]{1,0:T(8,128)(2,1)S(1)}, u32[]{:S(2)}, u32[]{:S(2)}) collective-permute-start(bf16[640,640]{1,0:T(8,128)(2,1)S(1)} %collective-permute-done.13.refs_6_), channel_id=1, source_target_pairs={{0,8},{1,9},{2,10},{3,11},{4,0},{5,1},{6,2},{7,3},{8,16},{9,17},{1... | collective-permute-start | bytes 2457608 | tf_op jit(solution)/shard_map/ppermute | solution.py:23
  139.0 20.2 %collective-permute-start.19 = (bf16[640,640]{1,0:T(8,128)(2,1)S(1)}, bf16[640,640]{1,0:T(8,128)(2,1)S(1)}, u32[]{:S(2)}, u32[]{:S(2)}) collective-permute-start(bf16[640,640]{1,0:T(8,128)(2,1)S(1)} %collective-permute-done.14.refs_5_), channel_id=1, source_target_pairs={{0,4},{1,5},{2,6},{3,7},{4,12},{5,13},{6,14},{7,15},{8,0},{9,1},{1... | collective-permute-start | bytes 2457608 | tf_op jit(solution)/shard_map/ppermute | solution.py:23
  140.7 28.6 %collective-permute-start.22 = (bf16[768,640]{1,0:T(8,128)(2,1)S(1)}, bf16[768,640]{1,0:T(8,128)(2,1)S(1)}, u32[]{:S(2)}, u32[]{:S(2)}) collective-permute-start(bf16[768,640]{1,0:T(8,128)(2,1)S(1)} %shard_map.103.refs_0_), channel_id=1, source_target_pairs={{0,2},{1,3},{2,0},{3,1},{4,6},{5,7},{6,4},{7,5},{8,10},{9,11},{10,... | collective-permute-start | bytes 2949128 | tf_op jit(solution)/shard_map/ppermute | solution.py:23
  158.8 10.4 %collective-permute-start.20 = (bf16[320,640]{1,0:T(8,128)(2,1)S(1)}, bf16[320,640]{1,0:T(8,128)(2,1)S(1)}, u32[]{:S(2)}, u32[]{:S(2)}) collective-permute-start(bf16[320,640]{1,0:T(8,128)(2,1)S(1)} %get-tuple-element.67), channel_id=1, source_target_pairs={{0,8},{1,9},{2,10},{3,11},{4,0},{5,1},{6,2},{7,3},{8,16},{9,17},{1... | collective-permute-start | bytes 1228808 | tf_op jit(solution)/shard_map/ppermute | solution.py:23
  159.2 10.1 %collective-permute-start.21 = (bf16[320,640]{1,0:T(8,128)(2,1)S(1)}, bf16[320,640]{1,0:T(8,128)(2,1)S(1)}, u32[]{:S(2)}, u32[]{:S(2)}) collective-permute-start(bf16[320,640]{1,0:T(8,128)(2,1)S(1)} %get-tuple-element.65), channel_id=1, source_target_pairs={{0,4},{1,5},{2,6},{3,7},{4,12},{5,13},{6,14},{7,15},{8,0},{9,1},{1... | collective-permute-start | bytes 1228808 | tf_op jit(solution)/shard_map/ppermute | solution.py:23
  169.4 2.6 %collective-permute-start.23 = (bf16[768,640]{1,0:T(8,128)(2,1)S(1)}, bf16[768,640]{1,0:T(8,128)(2,1)S(1)}, u32[]{:S(2)}, u32[]{:S(2)}) collective-permute-start(bf16[768,640]{1,0:T(8,128)(2,1)S(1)} %shard_map.103.refs_0_), channel_id=1, source_target_pairs={{0,1},{1,0},{2,3},{3,2},{4,5},{5,4},{6,7},{7,6},{8,9},{9,8},{10,11... | collective-permute-start | bytes 2949128 | tf_op jit(solution)/shard_map/ppermute | solution.py:23
  169.4 4.0 %collective-permute-start.24 = (bf16[768,640]{1,0:T(8,128)(2,1)S(1)}, bf16[768,640]{1,0:T(8,128)(2,1)S(1)}, u32[]{:S(2)}, u32[]{:S(2)}) collective-permute-start(bf16[768,640]{1,0:T(8,128)(2,1)S(1)} %collective-permute-done.22.refs_2_), channel_id=1, source_target_pairs={{0,1},{1,0},{2,3},{3,2},{4,5},{5,4},{6,7},{7,6},{8,9},{9,8},{10,11... | collective-permute-start | bytes 2949128 | tf_op jit(solution)/shard_map/ppermute | solution.py:23
  169.9 13.0 %collective-permute-start.27 = (bf16[320,640]{1,0:T(8,128)(2,1)S(1)}, bf16[320,640]{1,0:T(8,128)(2,1)S(1)}, u32[]{:S(2)}, u32[]{:S(2)}) collective-permute-start(bf16[320,640]{1,0:T(8,128)(2,1)S(1)} %get-tuple-element.60), channel_id=1, source_target_pairs={{0,4},{1,5},{2,6},{3,7},{4,12},{5,13},{6,14},{7,15},{8,0},{9,1},{1... | collective-permute-start | bytes 1228808 | tf_op jit(solution)/shard_map/ppermute | solution.py:23
  171.6 11.3 %collective-permute-start.28 = (bf16[320,640]{1,0:T(8,128)(2,1)S(1)}, bf16[320,640]{1,0:T(8,128)(2,1)S(1)}, u32[]{:S(2)}, u32[]{:S(2)}) collective-permute-start(bf16[320,640]{1,0:T(8,128)(2,1)S(1)} %get-tuple-element.61), channel_id=1, source_target_pairs={{0,8},{1,9},{2,10},{3,11},{4,0},{5,1},{6,2},{7,3},{8,16},{9,17},{1... | collective-permute-start | bytes 1228808 | tf_op jit(solution)/shard_map/ppermute | solution.py:23
  180.8 11.5 %collective-permute-start.25 = (bf16[320,640]{1,0:T(8,128)(2,1)S(1)}, bf16[320,640]{1,0:T(8,128)(2,1)S(1)}, u32[]{:S(2)}, u32[]{:S(2)}) collective-permute-start(bf16[320,640]{1,0:T(8,128)(2,1)S(1)} %collective-permute-done.20.refs_6_), channel_id=1, source_target_pairs={{0,8},{1,9},{2,10},{3,11},{4,0},{5,1},{6,2},{7,3},{8,16},{9,17},{1... | collective-permute-start | bytes 1228808 | tf_op jit(solution)/shard_map/ppermute | solution.py:23
  181.2 11.2 %collective-permute-start.26 = (bf16[320,640]{1,0:T(8,128)(2,1)S(1)}, bf16[320,640]{1,0:T(8,128)(2,1)S(1)}, u32[]{:S(2)}, u32[]{:S(2)}) collective-permute-start(bf16[320,640]{1,0:T(8,128)(2,1)S(1)} %collective-permute-done.21.refs_5_), channel_id=1, source_target_pairs={{0,4},{1,5},{2,6},{3,7},{4,12},{5,13},{6,14},{7,15},{8,0},{9,1},{1... | collective-permute-start | bytes 1228808 | tf_op jit(solution)/shard_map/ppermute | solution.py:23
  187.4 10.3 %copy-start.3 = (f32[1280]{0:T(1024)S(1)}, f32[1280]{0:T(1024)}, u32[]{:S(2)}) copy-start(f32[1280]{0:T(1024)} %param.19) | copy-start | bytes 15364
  195.8 2.6 %collective-permute-start.29 = (f32[8,768]{1,0:T(8,128)S(1)}, f32[8,768]{1,0:T(8,128)S(1)}, u32[]{:S(2)}, u32[]{:S(2)}) collective-permute-start(f32[8,768]{1,0:T(8,128)S(1)} %get-tuple-element.64.refs_2_), channel_id=1, source_target_pairs={{0,1},{1,0},{2,3},{3,2},{4,5},{5,4},{6,7},{7,6},{8,9},{9,8},{10,11... | collective-permute-start | bytes 73736 | tf_op jit(solution)/shard_map/ppermute | solution.py:23
  195.9 3.9 %collective-permute-start.30 = (f32[8,768]{1,0:T(8,128)S(1)}, f32[8,768]{1,0:T(8,128)S(1)}, u32[]{:S(2)}, u32[]{:S(2)}) collective-permute-start(f32[8,768]{1,0:T(8,128)S(1)} %get-tuple-element.64.refs_2_), channel_id=1, source_target_pairs={{0,2},{1,3},{2,0},{3,1},{4,6},{5,7},{6,4},{7,5},{8,10},{9,11},{10,... | collective-permute-start | bytes 73736 | tf_op jit(solution)/shard_map/ppermute | solution.py:23
  196.0 3.8 %collective-permute-start.31 = (f32[8,768]{1,0:T(8,128)S(1)}, f32[8,768]{1,0:T(8,128)S(1)}, u32[]{:S(2)}, u32[]{:S(2)}) collective-permute-start(f32[8,768]{1,0:T(8,128)S(1)} %get-tuple-element.64.refs_2_), channel_id=1, source_target_pairs={{0,3},{1,2},{2,1},{3,0},{4,7},{5,6},{6,5},{7,4},{8,11},{9,10},{10,... | collective-permute-start | bytes 73736 | tf_op jit(solution)/shard_map/ppermute | solution.py:23

commit v6 on v5

--- a/solution.py
+++ b/solution.py
@@ -82,20 +82,6 @@
     forward, backward = ring["forward"][-1], ring["backward"][-1]
     half = forward.shape[0] // 2
     ring["middle"] = ring_send((forward[:half], backward[half:]), sizes)
-
-
-def ring_end(ring, sizes, between):
-    forward, backward = ring["forward"][-1], ring["backward"][-1]
-    half = forward.shape[0] // 2
-    ahead = ring_send((forward[:half], backward[half:]), sizes)
-    rest, ahead = lax.optimization_barrier(((forward[half:], backward[:half]), ahead))
-    rest = ring_send(rest, sizes)
-    ring["forward"].append([ahead[0], rest[0]])
-    ring["backward"].append([rest[1], ahead[1]])
-    ahead, result = lax.optimization_barrier((ahead, between(ahead)))
-    halves = ring_send(ahead, sizes)
-    ring["middle"] = halves
-    return result
 
 
 def ring_tie(ring, other):
@@ -153,10 +139,11 @@
         squares += [jnp.zeros_like(squares[0])] * (8 - len(squares))
         return total, jnp.stack(squares)
 
-    tile = 256 if rows % 256 == 0 else rows
-    tiles = rows // tile
     extra = 0 if accumulated is None else 1
     whole = width == columns
+    tile = 384 if whole else 256
+    tile = tile if rows % tile == 0 else rows
+    tiles = rows // tile
 
     def kernel(*refs):
         held = sum(len(source) for source in sources)
@@ -364,7 +351,7 @@
 
 def finish(attn_out, sums, tokens, out_gain, live_rows, features):
     rows, width = tokens.shape
-    tile = 256 if rows % 256 == 0 else rows
+    tile = 384 if rows % 384 == 0 else rows
 
     def kernel(*refs):
         live_ref, attn_ref, sum_refs = refs[0], refs[1], refs[2 : 2 + len(sums)]
@@ -424,8 +411,20 @@
             t,
         ),
     )
+    row_ids = jnp.arange(capacity, dtype=jnp.int32)
+    positions = (row_ids - first_row).astype(jnp.float32)
+    half_dim = HEAD_DIM // 2
+    freqs = jnp.power(
+        ROPE_BASE, -(jnp.arange(half_dim, dtype=jnp.float32) * 2.0 / HEAD_DIM)
+    )
+    angle = positions[:, None] * freqs[None, :]
+    cosine, sine = jnp.cos(angle), jnp.sin(angle)
+    cosine = jnp.concatenate([cosine, cosine], axis=1)
+    sine = jnp.concatenate([-sine, sine], axis=1)
+    starts = jnp.broadcast_to(first_row[:, None], (capacity, HEAD_DIM))
+
+    weights = jnp.concatenate([w_query, w_key, w_value], axis=1)
     token_blocks = gather_first(tokens, sizes)
-    weights = jnp.concatenate([w_query, w_key, w_value], axis=1)
     first_ring = ring_open(weights)
     q_width, k_width = w_query.shape[1], w_key.shape[1]
 
@@ -453,7 +452,9 @@
                 moved, sizes, lambda f, t: (f, (f // per_tensor) ^ reverse_bits(t, tensor_size))
             )
     ring_step(first_ring, sizes)
-    total, moved = ring_tie(first_ring, (qkv_product(0, None), moved))
+    total, moved, cosine, sine, starts = ring_tie(
+        first_ring, (qkv_product(0, None), moved, cosine, sine, starts)
+    )
     ring_middle(first_ring, sizes)
     for number in range(1, len(groups) - 1):
         total = qkv_product(number, total)
@@ -465,20 +466,12 @@
     second_ring = ring_open(moved)
     ring_step(second_ring, sizes)
     square_blocks = swap_small(squares, sizes)
-    row_ids = jnp.arange(capacity, dtype=jnp.int32)
-    positions = (row_ids - first_row).astype(jnp.float32)
-    half_dim = HEAD_DIM // 2
-    freqs = jnp.power(
-        ROPE_BASE, -(jnp.arange(half_dim, dtype=jnp.float32) * 2.0 / HEAD_DIM)
-    )
-    angle = positions[:, None] * freqs[None, :]
-    cosine, sine = jnp.cos(angle), jnp.sin(angle)
     attended = attention(
         total,
         square_blocks,
-        jnp.concatenate([cosine, cosine], axis=1),
-        jnp.concatenate([-sine, sine], axis=1),
-        jnp.broadcast_to(first_row[:, None], (capacity, HEAD_DIM)),
+        cosine,
+        sine,
+        starts,
         query_gain[None, :],
         key_gain[None, :],
         tensor_size,
@@ -493,28 +486,28 @@
         source = traced_reverse((block // per_tensor) ^ t_index, tensor_size)
         return source ^ t_index, 0, lax.rem(block, per_tensor) * w_out.shape[1]
 
-    def out_product(number, sources, attn_out):
+    def out_product(offsets, sources, attn_out):
         return block_product(
             sources,
             choose_attended,
-            {offset: ring_block(second_ring, offset, n) for offset in groups[number]},
+            {offset: ring_block(second_ring, offset, n) for offset in offsets},
             attn_out,
             width,
-            [(0, width)] if number == len(groups) - 1 else None,
+            [(0, width)] if last in offsets else None,
         )
 
     for step in range(2, last - 1):
         ring_step(second_ring, sizes)
 
-    def first_product(ahead):
-        have, _ = lax.optimization_barrier((attended_blocks, ahead))
-        have = gather_rest(have, sizes)
-        return have, out_product(0, have, None)
-
-    attended_blocks, attn_out = ring_end(second_ring, sizes, first_product)
-    for number in range(1, len(groups)):
-        attn_out = out_product(number, attended_blocks, attn_out)
-    attn_out, out_squares = attn_out
+    attended_blocks, _ = lax.optimization_barrier(
+        (attended_blocks, (second_ring["forward"][-1], second_ring["backward"][-1]))
+    )
+    attended_blocks = gather_rest(attended_blocks, sizes)
+    ring_step(second_ring, sizes)
+    attn_out = ring_tie(second_ring, out_product(groups[0], attended_blocks, None))
+    ring_middle(second_ring, sizes)
+    attn_out = out_product(groups[1], attended_blocks, attn_out)
+    attn_out, out_squares = out_product(groups[2], attended_blocks, attn_out)
     return finish(
         attn_out,
         swap_small(out_squares, sizes),

time: 202 us -> 201 us (level)
  waiting for transfers between devices: 115 us -> 121 us
  starting transfers between devices: 41.5 us -> 37.8 us
  Pallas kernels: 39.5 us -> 36.3 us
    ppermute x32 -> x30, waiting for transfers between devices: 115 us -> 121 us  [permute(): return lax.ppermute(array, AXES, pairs)]
    ppermute x32 -> x30, starting transfers between devices: 41.5 us -> 37.8 us  [permute(): return lax.ppermute(array, AXES, pairs)]
    pallas_call x6, Pallas kernels: 32.7 us -> 29.9 us  [block_product(): pl.pallas_call(kernel, out_shape=out_shape, in_specs=[any_space] * len(op...]
  transfers between devices with their start and end apart: 32 -> 30, of which waited for: 19 -> 18; matrix products, arithmetic and copies ran while one was open for 3% -> 2% of each run, Pallas kernels for 17% -> 15%
where the time goes in v6:
time: 201 us
  waiting for transfers between devices  121 us (60%)
  starting transfers between devices  37.8 us (19%)
  Pallas kernels  36.3 us (18%)
  local copies, waits for them, and re-layouts  3.48 us (2%)
    ppermute x30, waiting for transfers between devices, permute(): return lax.ppermute(array, AXES, pairs)  121 us
    ppermute x30, starting transfers between devices, permute(): return lax.ppermute(array, AXES, pairs)  37.8 us
    pallas_call x6, Pallas kernels, block_product(): pl.pallas_call(kernel, out_shape=out_shape, in_specs=[any_space] * len(op...  29.9 us
    pallas_call x1, Pallas kernels, attention(): pl.pallas_call(kernel, grid=(capacity // half_rows,), out_shape=jax.Shape...  4.4 us
  transfers between devices with their start and end apart: 30, of which 18 were waited for; matrix products, arithmetic and copies ran while one was open for 2% of the time, Pallas kernels for 15%

profile of v6, /device:TPU:0, one launch (start us, length us, event | category | flops | bytes accessed | tf_op | source)
XLA Modules:
  0.0 201.2 jit_solution(2372008830344404971)
XLA Ops:
  0.0 3.0 %collective-permute-start.2 = (bf16[768,1280]{1,0:T(8,128)(2,1)}, bf16[768,1280]{1,0:T(8,128)(2,1)S(1)}, u32[]{:S(2)}, u32[]{:S(2)}) collective-permute-start(bf16[768,1280]{1,0:T(8,128)(2,1)} %refs_6_.1), channel_id=1, source_target_pairs={{0,2},{1,3},{2,0},{3,1},{4,6},{5,7},{6,4},{7,5},{8,10},{9,11},{10,... | collective-permute-start | bytes 5898248 | tf_op jit(solution)/shard_map/ppermute | solution.py:23
  3.0 1.2 constant_dynamic-update-slice_fusion.2
  4.2 1.0 constant_dynamic-update-slice_fusion.1
  5.2 1.0 constant_dynamic-update-slice_fusion.refs_4_
  6.1 1.6 collective-permute-start
  7.7 0.4 collective-permute-start.1
  8.2 1.8 collective-permute-start.3
  10.0 23.5 %collective-permute-done.refs_6_ = bf16[640,896]{1,0:T(8,128)(2,1)S(1)} collective-permute-done((bf16[640,896]{1,0:T(8,128)(2,1)S(1)}, bf16[640,896]{1,0:T(8,128)(2,1)S(1)}, u32[]{:S(2)}, u32[]{:S(2)}) %collective-permute-start) | collective-permute-done | bytes 1146912 | tf_op jit(solution)/shard_map/ppermute | solution.py:23
  33.4 1.3 collective-permute-done.1.refs_5_
  34.8 11.3 %collective-permute-done.2.refs_2_ = bf16[768,1280]{1,0:T(8,128)(2,1)S(1)} collective-permute-done((bf16[768,1280]{1,0:T(8,128)(2,1)}, bf16[768,1280]{1,0:T(8,128)(2,1)S(1)}, u32[]{:S(2)}, u32[]{:S(2)}) %collective-permute-start.2) | collective-permute-done | bytes 1966112 | tf_op jit(solution)/shard_map/ppermute | solution.py:23
  46.1 1.7 collective-permute-start.6
  47.8 0.3 collective-permute-start.8
  48.1 6.3 %collective-permute-start.4 = (bf16[768,1280]{1,0:T(8,128)(2,1)S(1)}, bf16[768,1280]{1,0:T(8,128)(2,1)S(1)}, u32[]{:S(2)}, u32[]{:S(2)}) collective-permute-start(bf16[768,1280]{1,0:T(8,128)(2,1)S(1)} %copy-done), channel_id=1, source_target_pairs={{0,1},{1,0},{2,3},{3,2},{4,5},{5,4},{6,7},{7,6},{8,9},{9,8},{10,11... | collective-permute-start | bytes 5898248 | tf_op jit(solution)/shard_map/ppermute | solution.py:23
  54.4 14.5 %collective-permute-done.6.refs_8_ = bf16[640,896]{1,0:T(8,128)(2,1)S(1)} collective-permute-done((bf16[640,896]{1,0:T(8,128)(2,1)S(1)}, bf16[640,896]{1,0:T(8,128)(2,1)S(1)}, u32[]{:S(2)}, u32[]{:S(2)}) %collective-permute-start.6) | collective-permute-done | bytes 1146912 | tf_op jit(solution)/shard_map/ppermute | solution.py:23
  68.9 4.2 %collective-permute-start.7 = (bf16[640,896]{1,0:T(8,128)(2,1)S(1)}, bf16[640,896]{1,0:T(8,128)(2,1)S(1)}, u32[]{:S(2)}, u32[]{:S(2)}) collective-permute-start(bf16[640,896]{1,0:T(8,128)(2,1)S(1)} %collective-permute-done.6.refs_8_), channel_id=1, source_target_pairs={{0,8},{1,9},{2,10},{3,11},{4,0},{5,1},{6,2},{7,3},{8,16},{9,17},{1... | collective-permute-start | bytes 3440648 | tf_op jit(solution)/shard_map/ppermute | solution.py:23
  73.2 1.2 collective-permute-done.8.refs_7_
  74.4 0.7 collective-permute-start.10
  75.2 1.4 fusion
  76.6 0.3 pad_maximum_fusion
  76.9 8.1 %shard_map.100.refs_6_ = f32[768,896]{1,0:T(8,128)S(1)} custom-call(bf16[768,1280]{1,0:T(8,128)(2,1)S(1)} %copy-done, bf16[768,1280]{1,0:T(8,128)(2,1)S(1)} %collective-permute-done.4.refs_1_, bf16[768,1280]{1,0:T(8,128)(2,1)S(1)} %collective-permute-done.2.refs_2_, bf16[768,1280]{1,0:T(8,128)(2,1)S(1)} %collective-permute-done.5.refs_3_, ...), custom_call_target="tpu_custom_call" | custom-call | flops 1 | bytes 1 | tf_op jit(solution)/shard_map/pallas_call | solution.py:248
  85.0 13.2 %collective-permute-done.7.refs_5_ = bf16[640,896]{1,0:T(8,128)(2,1)S(1)} collective-permute-done((bf16[640,896]{1,0:T(8,128)(2,1)S(1)}, bf16[640,896]{1,0:T(8,128)(2,1)S(1)}, u32[]{:S(2)}, u32[]{:S(2)}) %collective-permute-start.7) | collective-permute-done | bytes 1146912 | tf_op jit(solution)/shard_map/ppermute | solution.py:23
  98.2 2.2 %collective-permute-done.9.refs_4_ = bf16[640,896]{1,0:T(8,128)(2,1)S(1)} collective-permute-done((bf16[640,896]{1,0:T(8,128)(2,1)S(1)}, bf16[640,896]{1,0:T(8,128)(2,1)S(1)}, u32[]{:S(2)}, u32[]{:S(2)}) %collective-permute-start.9) | collective-permute-done | bytes 1146912 | tf_op jit(solution)/shard_map/ppermute | solution.py:23
  100.4 0.2 broadcast_in_dim.8.refs_7_
  100.6 2.0 collective-permute-start.11
  102.7 0.1 collective-permute-start.12
  102.8 3.8 %shard_map.101.refs_6_ = f32[768,896]{1,0:T(8,128)S(1)} custom-call(bf16[768,1280]{1,0:T(8,128)(2,1)S(1)} %copy-done, bf16[768,1280]{1,0:T(8,128)(2,1)S(1)} %collective-permute-done.4.refs_1_, bf16[768,1280]{1,0:T(8,128)(2,1)S(1)} %collective-permute-done.2.refs_2_, bf16[768,1280]{1,0:T(8,128)(2,1)S(1)} %collective-permute-done.5.refs_3_, ...), custom_call_target="tpu_custom_call" | custom-call | flops 1 | bytes 1 | tf_op jit(solution)/shard_map/pallas_call | solution.py:248
  106.6 0.0 copy-start.4
  106.6 0.0 copy-start.1
  106.6 9.1 %collective-permute-done.11.refs_4_ = bf16[320,896]{1,0:T(8,128)(2,1)S(1)} collective-permute-done((bf16[320,896]{1,0:T(8,128)(2,1)S(1)}, bf16[320,896]{1,0:T(8,128)(2,1)S(1)}, u32[]{:S(2)}, u32[]{:S(2)}) %collective-permute-start.11) | collective-permute-done | bytes 573472 | tf_op jit(solution)/shard_map/ppermute | solution.py:23
  115.7 2.9 %collective-permute-done.12.refs_5_ = bf16[320,896]{1,0:T(8,128)(2,1)S(1)} collective-permute-done((bf16[320,896]{1,0:T(8,128)(2,1)S(1)}, bf16[320,896]{1,0:T(8,128)(2,1)S(1)}, u32[]{:S(2)}, u32[]{:S(2)}) %collective-permute-start.12) | collective-permute-done | bytes 573472 | tf_op jit(solution)/shard_map/ppermute | solution.py:23
  118.6 0.3 collective-permute-start.17
  118.8 1.8 collective-permute-start.18
  120.6 3.4 %shard_map.102 = (f32[768,896]{1,0:T(8,128)S(1)}, f32[8,768]{1,0:T(8,128)S(1)}) custom-call(bf16[768,1280]{1,0:T(8,128)(2,1)S(1)} %copy-done, bf16[768,1280]{1,0:T(8,128)(2,1)S(1)} %collective-permute-done.4.refs_1_, bf16[768,1280]{1,0:T(8,128)(2,1)S(1)} %collective-permute-done.2.refs_2_, bf16[768,1280]{1,0:T(8,128)(2,1)S(1)} %collective-permute-done.5.refs_3_, ...), custom_call_target="tpu_custom_call" | custom-call | flops 1 | bytes 1 | tf_op jit(solution)/shard_map/pallas_call | solution.py:248
  124.0 0.1 collective-permute-start.13
  124.1 4.1 %collective-permute-start.14 = (f32[8,768]{1,0:T(8,128)S(1)}, f32[8,768]{1,0:T(8,128)S(1)}, u32[]{:S(2)}, u32[]{:S(2)}) collective-permute-start(f32[8,768]{1,0:T(8,128)S(1)} %get-tuple-element.41.refs_1_), channel_id=1, source_target_pairs={{0,2},{1,3},{2,0},{3,1},{4,6},{5,7},{6,4},{7,5},{8,10},{9,11},{10,... | collective-permute-start | bytes 73736 | tf_op jit(solution)/shard_map/ppermute | solution.py:23
  128.1 0.1 collective-permute-start.15
  128.2 1.7 collective-permute-done.14.refs_3_
  129.9 1.4 collective-permute-done.15.refs_4_
  131.4 4.4 %shard_map.103.refs_0_ = bf16[768,640]{1,0:T(8,128)(2,1)S(1)} custom-call(f32[768,896]{1,0:T(8,128)S(1)} %get-tuple-element.40.refs_0_, f32[8,768]{1,0:T(8,128)S(1)} %get-tuple-element.41.refs_1_, f32[8,768]{1,0:T(8,128)S(1)} %collective-permute-done.13.refs_2_, f32[8,768]{1,0:T(8,128)S(1)} %collective-permute-done.14.refs_3_, ...), custom_call_target="tpu_custom_call" | custom-call | flops 1 | bytes 1 | tf_op jit(solution)/shard_map/pallas_call | solution.py:338
  135.8 0.7 collective-permute-start.16
  136.4 2.4 %collective-permute-done.17.refs_6_ = bf16[640,640]{1,0:T(8,128)(2,1)S(1)} collective-permute-done((bf16[640,640]{1,0:T(8,128)(2,1)S(1)}, bf16[640,640]{1,0:T(8,128)(2,1)S(1)}, u32[]{:S(2)}, u32[]{:S(2)}) %collective-permute-start.17) | collective-permute-done | bytes 819232 | tf_op jit(solution)/shard_map/ppermute | solution.py:23
  138.8 0.0 collective-permute-done.18.refs_5_
  138.8 0.3 collective-permute-start.19
  139.1 1.7 collective-permute-start.20
  140.9 19.1 %collective-permute-done.16.refs_2_ = bf16[768,640]{1,0:T(8,128)(2,1)S(1)} collective-permute-done((bf16[768,640]{1,0:T(8,128)(2,1)S(1)}, bf16[768,640]{1,0:T(8,128)(2,1)S(1)}, u32[]{:S(2)}, u32[]{:S(2)}) %collective-permute-start.16) | collective-permute-done | bytes 983072 | tf_op jit(solution)/shard_map/ppermute | solution.py:23
  160.0 0.5 collective-permute-start.22
  160.5 0.3 collective-permute-start.23
  160.8 1.7 collective-permute-start.24
  162.5 0.0 collective-permute-done.21.refs_1_
  162.5 1.4 collective-permute-done.22.refs_3_
  164.0 7.2 %shard_map.104.refs_6_ = f32[768,1280]{1,0:T(8,128)S(1)} custom-call(bf16[768,640]{1,0:T(8,128)(2,1)S(1)} %shard_map.103.refs_0_, bf16[768,640]{1,0:T(8,128)(2,1)S(1)} %collective-permute-done.21.refs_1_, bf16[768,640]{1,0:T(8,128)(2,1)S(1)} %collective-permute-done.16.refs_2_, bf16[768,640]{1,0:T(8,128)(2,1)S(1)} %collective-permute-done.22.refs_3_, ...), custom_call_target="tpu_custom_call" | custom-call | flops 1 | bytes 1 | tf_op jit(solution)/shard_map/pallas_call | solution.py:248
  171.2 9.5 %collective-permute-done.23.refs_5_ = bf16[640,640]{1,0:T(8,128)(2,1)S(1)} collective-permute-done((bf16[640,640]{1,0:T(8,128)(2,1)S(1)}, bf16[640,640]{1,0:T(8,128)(2,1)S(1)}, u32[]{:S(2)}, u32[]{:S(2)}) %collective-permute-start.23) | collective-permute-done | bytes 819232 | tf_op jit(solution)/shard_map/ppermute | solution.py:23
  180.7 0.0 collective-permute-done.24.refs_4_
  180.8 1.1 collective-permute-start.25
  181.9 1.1 collective-permute-start.26
  182.9 4.1 %shard_map.105.refs_6_ = f32[768,1280]{1,0:T(8,128)S(1)} custom-call(bf16[768,640]{1,0:T(8,128)(2,1)S(1)} %shard_map.103.refs_0_, bf16[768,640]{1,0:T(8,128)(2,1)S(1)} %collective-permute-done.21.refs_1_, bf16[768,640]{1,0:T(8,128)(2,1)S(1)} %collective-permute-done.16.refs_2_, bf16[768,640]{1,0:T(8,128)(2,1)S(1)} %collective-permute-done.22.refs_3_, ...), custom_call_target="tpu_custom_call" | custom-call | flops 1 | bytes 1 | tf_op jit(solution)/shard_map/pallas_call | solution.py:248
  187.1 4.3 %collective-permute-done.25.refs_4_ = bf16[320,640]{1,0:T(8,128)(2,1)S(1)} collective-permute-done((bf16[320,640]{1,0:T(8,128)(2,1)S(1)}, bf16[320,640]{1,0:T(8,128)(2,1)S(1)}, u32[]{:S(2)}, u32[]{:S(2)}) %collective-permute-start.25) | collective-permute-done | bytes 409632 | tf_op jit(solution)/shard_map/ppermute | solution.py:23
  191.4 0.5 collective-permute-done.26.refs_5_
  191.9 3.4 %shard_map.106 = (f32[768,1280]{1,0:T(8,128)S(1)}, f32[8,768]{1,0:T(8,128)S(1)}) custom-call(bf16[768,640]{1,0:T(8,128)(2,1)S(1)} %shard_map.103.refs_0_, bf16[768,640]{1,0:T(8,128)(2,1)S(1)} %collective-permute-done.21.refs_1_, bf16[768,640]{1,0:T(8,128)(2,1)S(1)} %collective-permute-done.16.refs_2_, bf16[768,640]{1,0:T(8,128)(2,1)S(1)} %collective-permute-done.22.refs_3_, ...), custom_call_target="tpu_custom_call" | custom-call | flops 1 | bytes 1 | tf_op jit(solution)/shard_map/pallas_call | solution.py:248
  195.2 0.1 collective-permute-start.27
  195.3 0.2 collective-permute-start.28
  195.6 1.6 collective-permute-start.29
  197.8 1.4 collective-permute-done.28.refs_4_
  199.2 2.0 shard_map.107
  (28 shorter events, 0.2 us)
Async XLA Ops:
  0.0 48.1 %copy-start = (bf16[768,1280]{1,0:T(8,128)(2,1)S(1)}, bf16[768,1280]{1,0:T(8,128)(2,1)}, u32[]{:S(2)}) copy-start(bf16[768,1280]{1,0:T(8,128)(2,1)} %refs_6_.1) | copy-start | bytes 5898244
  0.0 75.1 %copy-start.2 = (s32[768]{0:T(1024)S(1)}, s32[768]{0:T(1024)}, u32[]{:S(2)}) copy-start(s32[768]{0:T(1024)} %param.12) | copy-start | bytes 9220
  0.0 46.1 %collective-permute-start.2 = (bf16[768,1280]{1,0:T(8,128)(2,1)}, bf16[768,1280]{1,0:T(8,128)(2,1)S(1)}, u32[]{:S(2)}, u32[]{:S(2)}) collective-permute-start(bf16[768,1280]{1,0:T(8,128)(2,1)} %refs_6_.1), channel_id=1, source_target_pairs={{0,2},{1,3},{2,0},{3,1},{4,6},{5,7},{6,4},{7,5},{8,10},{9,11},{10,... | collective-permute-start | bytes 5898248 | tf_op jit(solution)/shard_map/ppermute | solution.py:23
  6.1 27.3 %collective-permute-start = (bf16[640,896]{1,0:T(8,128)(2,1)S(1)}, bf16[640,896]{1,0:T(8,128)(2,1)S(1)}, u32[]{:S(2)}, u32[]{:S(2)}) collective-permute-start(bf16[640,896]{1,0:T(8,128)(2,1)S(1)} %constant_dynamic-update-slice_fusion.refs_4_), channel_id=1, source_target_pairs={{0,8},{1,9},{2,10},{3,11},{4,0},{5,1},{6,2},{7,3},{8,16},{9,17},{1... | collective-permute-start | bytes 3440648 | tf_op jit(solution)/shard_map/ppermute | solution.py:23
  7.7 27.0 %collective-permute-start.1 = (bf16[640,896]{1,0:T(8,128)(2,1)S(1)}, bf16[640,896]{1,0:T(8,128)(2,1)S(1)}, u32[]{:S(2)}, u32[]{:S(2)}) collective-permute-start(bf16[640,896]{1,0:T(8,128)(2,1)S(1)} %constant_dynamic-update-slice_fusion.refs_4_), channel_id=1, source_target_pairs={{0,4},{1,5},{2,6},{3,7},{4,12},{5,13},{6,14},{7,15},{8,0},{9,1},{1... | collective-permute-start | bytes 3440648 | tf_op jit(solution)/shard_map/ppermute | solution.py:23
  8.2 1.8 collective-permute-start.3
  46.1 22.9 %collective-permute-start.6 = (bf16[640,896]{1,0:T(8,128)(2,1)S(1)}, bf16[640,896]{1,0:T(8,128)(2,1)S(1)}, u32[]{:S(2)}, u32[]{:S(2)}) collective-permute-start(bf16[640,896]{1,0:T(8,128)(2,1)S(1)} %collective-permute-done.refs_6_), channel_id=1, source_target_pairs={{0,8},{1,9},{2,10},{3,11},{4,0},{5,1},{6,2},{7,3},{8,16},{9,17},{1... | collective-permute-start | bytes 3440648 | tf_op jit(solution)/shard_map/ppermute | solution.py:23
  47.8 26.6 %collective-permute-start.8 = (bf16[640,896]{1,0:T(8,128)(2,1)S(1)}, bf16[640,896]{1,0:T(8,128)(2,1)S(1)}, u32[]{:S(2)}, u32[]{:S(2)}) collective-permute-start(bf16[640,896]{1,0:T(8,128)(2,1)S(1)} %collective-permute-done.1.refs_5_), channel_id=1, source_target_pairs={{0,4},{1,5},{2,6},{3,7},{4,12},{5,13},{6,14},{7,15},{8,0},{9,1},{1... | collective-permute-start | bytes 3440648 | tf_op jit(solution)/shard_map/ppermute | solution.py:23
  48.1 28.8 %collective-permute-start.4 = (bf16[768,1280]{1,0:T(8,128)(2,1)S(1)}, bf16[768,1280]{1,0:T(8,128)(2,1)S(1)}, u32[]{:S(2)}, u32[]{:S(2)}) collective-permute-start(bf16[768,1280]{1,0:T(8,128)(2,1)S(1)} %copy-done), channel_id=1, source_target_pairs={{0,1},{1,0},{2,3},{3,2},{4,5},{5,4},{6,7},{7,6},{8,9},{9,8},{10,11... | collective-permute-start | bytes 5898248 | tf_op jit(solution)/shard_map/ppermute | solution.py:23
  54.4 22.5 %collective-permute-start.5 = (bf16[768,1280]{1,0:T(8,128)(2,1)S(1)}, bf16[768,1280]{1,0:T(8,128)(2,1)S(1)}, u32[]{:S(2)}, u32[]{:S(2)}) collective-permute-start(bf16[768,1280]{1,0:T(8,128)(2,1)S(1)} %collective-permute-done.2.refs_2_), channel_id=1, source_target_pairs={{0,1},{1,0},{2,3},{3,2},{4,5},{5,4},{6,7},{7,6},{8,9},{9,8},{10,11... | collective-permute-start | bytes 5898248 | tf_op jit(solution)/shard_map/ppermute | solution.py:23
  68.9 29.3 %collective-permute-start.7 = (bf16[640,896]{1,0:T(8,128)(2,1)S(1)}, bf16[640,896]{1,0:T(8,128)(2,1)S(1)}, u32[]{:S(2)}, u32[]{:S(2)}) collective-permute-start(bf16[640,896]{1,0:T(8,128)(2,1)S(1)} %collective-permute-done.6.refs_8_), channel_id=1, source_target_pairs={{0,8},{1,9},{2,10},{3,11},{4,0},{5,1},{6,2},{7,3},{8,16},{9,17},{1... | collective-permute-start | bytes 3440648 | tf_op jit(solution)/shard_map/ppermute | solution.py:23
  74.4 26.0 %collective-permute-start.9 = (bf16[640,896]{1,0:T(8,128)(2,1)S(1)}, bf16[640,896]{1,0:T(8,128)(2,1)S(1)}, u32[]{:S(2)}, u32[]{:S(2)}) collective-permute-start(bf16[640,896]{1,0:T(8,128)(2,1)S(1)} %collective-permute-done.8.refs_7_), channel_id=1, source_target_pairs={{0,4},{1,5},{2,6},{3,7},{4,12},{5,13},{6,14},{7,15},{8,0},{9,1},{1... | collective-permute-start | bytes 3440648 | tf_op jit(solution)/shard_map/ppermute | solution.py:23
  74.4 10.6 %collective-permute-start.10 = (bf16[640,640]{1,0:T(8,128)(2,1)S(1)}, bf16[640,640]{1,0:T(8,128)(2,1)S(1)}, u32[]{:S(2)}, u32[]{:S(2)}) collective-permute-start(bf16[640,640]{1,0:T(8,128)(2,1)S(1)} %collective-permute-done.3), channel_id=1, source_target_pairs={{0,0},{1,2},{2,1},{3,3},{4,4},{5,6},{6,5},{7,7},{8,9},{9,11},{10,8... | collective-permute-start | bytes 2457608 | tf_op jit(solution)/shard_map/ppermute | solution.py:23
  100.6 15.1 %collective-permute-start.11 = (bf16[320,896]{1,0:T(8,128)(2,1)S(1)}, bf16[320,896]{1,0:T(8,128)(2,1)S(1)}, u32[]{:S(2)}, u32[]{:S(2)}) collective-permute-start(bf16[320,896]{1,0:T(8,128)(2,1)S(1)} %slice.12), channel_id=1, source_target_pairs={{0,8},{1,9},{2,10},{3,11},{4,0},{5,1},{6,2},{7,3},{8,16},{9,17},{1... | collective-permute-start | bytes 1720328 | tf_op jit(solution)/shard_map/ppermute | solution.py:23
  102.7 15.9 %collective-permute-start.12 = (bf16[320,896]{1,0:T(8,128)(2,1)S(1)}, bf16[320,896]{1,0:T(8,128)(2,1)S(1)}, u32[]{:S(2)}, u32[]{:S(2)}) collective-permute-start(bf16[320,896]{1,0:T(8,128)(2,1)S(1)} %slice.13), channel_id=1, source_target_pairs={{0,4},{1,5},{2,6},{3,7},{4,12},{5,13},{6,14},{7,15},{8,0},{9,1},{1... | collective-permute-start | bytes 1720328 | tf_op jit(solution)/shard_map/ppermute | solution.py:23
  106.6 21.6 %copy-start.4 = (f32[640]{0:T(1024)S(1)}, f32[640]{0:T(1024)}, u32[]{:S(2)}) copy-start(f32[640]{0:T(1024)} %param.17) | copy-start | bytes 7684
  106.6 24.8 %copy-start.1 = (f32[128]{0:T(128)S(1)}, f32[128]{0:T(128)}, u32[]{:S(2)}) copy-start(f32[128]{0:T(128)} %param.18) | copy-start | bytes 1540
  118.6 20.3 %collective-permute-start.17 = (bf16[640,640]{1,0:T(8,128)(2,1)S(1)}, bf16[640,640]{1,0:T(8,128)(2,1)S(1)}, u32[]{:S(2)}, u32[]{:S(2)}) collective-permute-start(bf16[640,640]{1,0:T(8,128)(2,1)S(1)} %collective-permute-done.10.refs_4_), channel_id=1, source_target_pairs={{0,8},{1,9},{2,10},{3,11},{4,0},{5,1},{6,2},{7,3},{8,16},{9,17},{1... | collective-permute-start | bytes 2457608 | tf_op jit(solution)/shard_map/ppermute | solution.py:23
  118.8 20.0 %collective-permute-start.18 = (bf16[640,640]{1,0:T(8,128)(2,1)S(1)}, bf16[640,640]{1,0:T(8,128)(2,1)S(1)}, u32[]{:S(2)}, u32[]{:S(2)}) collective-permute-start(bf16[640,640]{1,0:T(8,128)(2,1)S(1)} %collective-permute-done.10.refs_4_), channel_id=1, source_target_pairs={{0,4},{1,5},{2,6},{3,7},{4,12},{5,13},{6,14},{7,15},{8,0},{9,1},{1... | collective-permute-start | bytes 2457608 | tf_op jit(solution)/shard_map/ppermute | solution.py:23
  124.0 4.2 %collective-permute-start.13 = (f32[8,768]{1,0:T(8,128)S(1)}, f32[8,768]{1,0:T(8,128)S(1)}, u32[]{:S(2)}, u32[]{:S(2)}) collective-permute-start(f32[8,768]{1,0:T(8,128)S(1)} %get-tuple-element.41.refs_1_), channel_id=1, source_target_pairs={{0,1},{1,0},{2,3},{3,2},{4,5},{5,4},{6,7},{7,6},{8,9},{9,8},{10,11... | collective-permute-start | bytes 73736 | tf_op jit(solution)/shard_map/ppermute | solution.py:23
  124.1 5.9 %collective-permute-start.14 = (f32[8,768]{1,0:T(8,128)S(1)}, f32[8,768]{1,0:T(8,128)S(1)}, u32[]{:S(2)}, u32[]{:S(2)}) collective-permute-start(f32[8,768]{1,0:T(8,128)S(1)} %get-tuple-element.41.refs_1_), channel_id=1, source_target_pairs={{0,2},{1,3},{2,0},{3,1},{4,6},{5,7},{6,4},{7,5},{8,10},{9,11},{10,... | collective-permute-start | bytes 73736 | tf_op jit(solution)/shard_map/ppermute | solution.py:23
  128.1 3.3 %collective-permute-start.15 = (f32[8,768]{1,0:T(8,128)S(1)}, f32[8,768]{1,0:T(8,128)S(1)}, u32[]{:S(2)}, u32[]{:S(2)}) collective-permute-start(f32[8,768]{1,0:T(8,128)S(1)} %get-tuple-element.41.refs_1_), channel_id=1, source_target_pairs={{0,3},{1,2},{2,1},{3,0},{4,7},{5,6},{6,5},{7,4},{8,11},{9,10},{10,... | collective-permute-start | bytes 73736 | tf_op jit(solution)/shard_map/ppermute | solution.py:23
  135.8 24.2 %collective-permute-start.16 = (bf16[768,640]{1,0:T(8,128)(2,1)S(1)}, bf16[768,640]{1,0:T(8,128)(2,1)S(1)}, u32[]{:S(2)}, u32[]{:S(2)}) collective-permute-start(bf16[768,640]{1,0:T(8,128)(2,1)S(1)} %shard_map.103.refs_0_), channel_id=1, source_target_pairs={{0,2},{1,3},{2,0},{3,1},{4,6},{5,7},{6,4},{7,5},{8,10},{9,11},{10,... | collective-permute-start | bytes 2949128 | tf_op jit(solution)/shard_map/ppermute | solution.py:23
  138.8 21.1 %collective-permute-start.19 = (bf16[640,640]{1,0:T(8,128)(2,1)S(1)}, bf16[640,640]{1,0:T(8,128)(2,1)S(1)}, u32[]{:S(2)}, u32[]{:S(2)}) collective-permute-start(bf16[640,640]{1,0:T(8,128)(2,1)S(1)} %collective-permute-done.17.refs_6_), channel_id=1, source_target_pairs={{0,8},{1,9},{2,10},{3,11},{4,0},{5,1},{6,2},{7,3},{8,16},{9,17},{1... | collective-permute-start | bytes 2457608 | tf_op jit(solution)/shard_map/ppermute | solution.py:23
  139.1 20.8 %collective-permute-start.20 = (bf16[640,640]{1,0:T(8,128)(2,1)S(1)}, bf16[640,640]{1,0:T(8,128)(2,1)S(1)}, u32[]{:S(2)}, u32[]{:S(2)}) collective-permute-start(bf16[640,640]{1,0:T(8,128)(2,1)S(1)} %collective-permute-done.18.refs_5_), channel_id=1, source_target_pairs={{0,4},{1,5},{2,6},{3,7},{4,12},{5,13},{6,14},{7,15},{8,0},{9,1},{1... | collective-permute-start | bytes 2457608 | tf_op jit(solution)/shard_map/ppermute | solution.py:23
  160.0 2.6 %collective-permute-start.21 = (bf16[768,640]{1,0:T(8,128)(2,1)S(1)}, bf16[768,640]{1,0:T(8,128)(2,1)S(1)}, u32[]{:S(2)}, u32[]{:S(2)}) collective-permute-start(bf16[768,640]{1,0:T(8,128)(2,1)S(1)} %shard_map.103.refs_0_), channel_id=1, source_target_pairs={{0,1},{1,0},{2,3},{3,2},{4,5},{5,4},{6,7},{7,6},{8,9},{9,8},{10,11... | collective-permute-start | bytes 2949128 | tf_op jit(solution)/shard_map/ppermute | solution.py:23
  160.0 4.0 %collective-permute-start.22 = (bf16[768,640]{1,0:T(8,128)(2,1)S(1)}, bf16[768,640]{1,0:T(8,128)(2,1)S(1)}, u32[]{:S(2)}, u32[]{:S(2)}) collective-permute-start(bf16[768,640]{1,0:T(8,128)(2,1)S(1)} %collective-permute-done.16.refs_2_), channel_id=1, source_target_pairs={{0,1},{1,0},{2,3},{3,2},{4,5},{5,4},{6,7},{7,6},{8,9},{9,8},{10,11... | collective-permute-start | bytes 2949128 | tf_op jit(solution)/shard_map/ppermute | solution.py:23
  160.5 20.2 %collective-permute-start.23 = (bf16[640,640]{1,0:T(8,128)(2,1)S(1)}, bf16[640,640]{1,0:T(8,128)(2,1)S(1)}, u32[]{:S(2)}, u32[]{:S(2)}) collective-permute-start(bf16[640,640]{1,0:T(8,128)(2,1)S(1)} %collective-permute-done.19.refs_8_), channel_id=1, source_target_pairs={{0,8},{1,9},{2,10},{3,11},{4,0},{5,1},{6,2},{7,3},{8,16},{9,17},{1... | collective-permute-start | bytes 2457608 | tf_op jit(solution)/shard_map/ppermute | solution.py:23
  160.8 19.9 %collective-permute-start.24 = (bf16[640,640]{1,0:T(8,128)(2,1)S(1)}, bf16[640,640]{1,0:T(8,128)(2,1)S(1)}, u32[]{:S(2)}, u32[]{:S(2)}) collective-permute-start(bf16[640,640]{1,0:T(8,128)(2,1)S(1)} %collective-permute-done.20.refs_7_), channel_id=1, source_target_pairs={{0,4},{1,5},{2,6},{3,7},{4,12},{5,13},{6,14},{7,15},{8,0},{9,1},{1... | collective-permute-start | bytes 2457608 | tf_op jit(solution)/shard_map/ppermute | solution.py:23
  180.8 10.6 %collective-permute-start.25 = (bf16[320,640]{1,0:T(8,128)(2,1)S(1)}, bf16[320,640]{1,0:T(8,128)(2,1)S(1)}, u32[]{:S(2)}, u32[]{:S(2)}) collective-permute-start(bf16[320,640]{1,0:T(8,128)(2,1)S(1)} %slice.14), channel_id=1, source_target_pairs={{0,8},{1,9},{2,10},{3,11},{4,0},{5,1},{6,2},{7,3},{8,16},{9,17},{1... | collective-permute-start | bytes 1228808 | tf_op jit(solution)/shard_map/ppermute | solution.py:23
  181.9 10.0 %collective-permute-start.26 = (bf16[320,640]{1,0:T(8,128)(2,1)S(1)}, bf16[320,640]{1,0:T(8,128)(2,1)S(1)}, u32[]{:S(2)}, u32[]{:S(2)}) collective-permute-start(bf16[320,640]{1,0:T(8,128)(2,1)S(1)} %slice.15), channel_id=1, source_target_pairs={{0,4},{1,5},{2,6},{3,7},{4,12},{5,13},{6,14},{7,15},{8,0},{9,1},{1... | collective-permute-start | bytes 1228808 | tf_op jit(solution)/shard_map/ppermute | solution.py:23
  187.1 10.1 %copy-start.3 = (f32[1280]{0:T(1024)S(1)}, f32[1280]{0:T(1024)}, u32[]{:S(2)}) copy-start(f32[1280]{0:T(1024)} %param.19) | copy-start | bytes 15364
  195.2 2.6 %collective-permute-start.27 = (f32[8,768]{1,0:T(8,128)S(1)}, f32[8,768]{1,0:T(8,128)S(1)}, u32[]{:S(2)}, u32[]{:S(2)}) collective-permute-start(f32[8,768]{1,0:T(8,128)S(1)} %get-tuple-element.54.refs_2_), channel_id=1, source_target_pairs={{0,1},{1,0},{2,3},{3,2},{4,5},{5,4},{6,7},{7,6},{8,9},{9,8},{10,11... | collective-permute-start | bytes 73736 | tf_op jit(solution)/shard_map/ppermute | solution.py:23
  195.3 3.9 %collective-permute-start.28 = (f32[8,768]{1,0:T(8,128)S(1)}, f32[8,768]{1,0:T(8,128)S(1)}, u32[]{:S(2)}, u32[]{:S(2)}) collective-permute-start(f32[8,768]{1,0:T(8,128)S(1)} %get-tuple-element.54.refs_2_), channel_id=1, source_target_pairs={{0,2},{1,3},{2,0},{3,1},{4,6},{5,7},{6,4},{7,5},{8,10},{9,11},{10,... | collective-permute-start | bytes 73736 | tf_op jit(solution)/shard_map/ppermute | solution.py:23
  195.6 3.7 %collective-permute-start.29 = (f32[8,768]{1,0:T(8,128)S(1)}, f32[8,768]{1,0:T(8,128)S(1)}, u32[]{:S(2)}, u32[]{:S(2)}) collective-permute-start(f32[8,768]{1,0:T(8,128)S(1)} %get-tuple-element.54.refs_2_), channel_id=1, source_target_pairs={{0,3},{1,2},{2,1},{3,0},{4,7},{5,6},{6,5},{7,4},{8,11},{9,10},{10,... | collective-permute-start | bytes 73736 | tf_op jit(solution)/shard_map/ppermute | solution.py:23

commit v7 on v6

--- a/solution.py
+++ b/solution.py
@@ -141,6 +141,7 @@
 
     extra = 0 if accumulated is None else 1
     whole = width == columns
+    in_place = extra == 1 and not whole and count == 1
     tile = 384 if whole else 256
     tile = tile if rows % tile == 0 else rows
     tiles = rows // tile
@@ -184,6 +185,11 @@
 
         def out_copy(i):
             part = pl.ds(i * tile, tile)
+            if in_place:
+                span = pl.ds(pl.multiple_of(choices[0][2], 128), width)
+                return pltpu.make_async_copy(
+                    total.at[part, span], out.at[part, span], tile_sems.at[i, 1]
+                )
             return pltpu.make_async_copy(total.at[part], out.at[part], tile_sems.at[i, 1])
 
         for j in range(count):
@@ -250,6 +256,7 @@
         out_shape=out_shape,
         in_specs=[any_space] * len(operands),
         out_specs=out_specs,
+        input_output_aliases={len(operands) - 1: 0} if in_place else {},
         scratch_shapes=[
             pltpu.VMEM((rows, count * depth), sources[0][0].dtype),
             pltpu.VMEM((count * depth, width), chunks[0][0].dtype),

time: 201 us -> 201 us (level)
  no operation moved by 1% of the time
where the time goes in v7:
time: 201 us
  waiting for transfers between devices  121 us (60%)
  starting transfers between devices  37.8 us (19%)
  Pallas kernels  36.1 us (18%)
  local copies, waits for them, and re-layouts  3.48 us (2%)
    ppermute x30, waiting for transfers between devices, permute(): return lax.ppermute(array, AXES, pairs)  121 us
    ppermute x30, starting transfers between devices, permute(): return lax.ppermute(array, AXES, pairs)  37.8 us
    pallas_call x6, Pallas kernels, block_product(): pl.pallas_call(kernel, out_shape=out_shape, in_specs=[any_space] * len(op...  29.8 us
    pallas_call x1, Pallas kernels, attention(): pl.pallas_call(kernel, grid=(capacity // half_rows,), out_shape=jax.Shape...  4.4 us
  transfers between devices with their start and end apart: 30, of which 18 were waited for; matrix products, arithmetic and copies ran while one was open for 2% of the time, Pallas kernels for 15%

profile of v7, /device:TPU:0, one launch (start us, length us, event | category | flops | bytes accessed | tf_op | source)
XLA Modules:
  0.0 201.0 jit_solution(10328457554763497440)
XLA Ops:
  0.0 3.0 %collective-permute-start.2 = (bf16[768,1280]{1,0:T(8,128)(2,1)}, bf16[768,1280]{1,0:T(8,128)(2,1)S(1)}, u32[]{:S(2)}, u32[]{:S(2)}) collective-permute-start(bf16[768,1280]{1,0:T(8,128)(2,1)} %refs_6_.1), channel_id=1, source_target_pairs={{0,2},{1,3},{2,0},{3,1},{4,6},{5,7},{6,4},{7,5},{8,10},{9,11},{10,... | collective-permute-start | bytes 5898248 | tf_op jit(solution)/shard_map/ppermute | solution.py:23
  3.0 1.2 constant_dynamic-update-slice_fusion.2
  4.2 1.0 constant_dynamic-update-slice_fusion.1
  5.2 1.0 constant_dynamic-update-slice_fusion.refs_4_
  6.1 1.6 collective-permute-start
  7.7 0.4 collective-permute-start.1
  8.2 1.8 collective-permute-start.3
  10.0 23.5 %collective-permute-done.refs_6_ = bf16[640,896]{1,0:T(8,128)(2,1)S(1)} collective-permute-done((bf16[640,896]{1,0:T(8,128)(2,1)S(1)}, bf16[640,896]{1,0:T(8,128)(2,1)S(1)}, u32[]{:S(2)}, u32[]{:S(2)}) %collective-permute-start) | collective-permute-done | bytes 1146912 | tf_op jit(solution)/shard_map/ppermute | solution.py:23
  33.4 1.3 collective-permute-done.1.refs_5_
  34.8 11.3 %collective-permute-done.2.refs_2_ = bf16[768,1280]{1,0:T(8,128)(2,1)S(1)} collective-permute-done((bf16[768,1280]{1,0:T(8,128)(2,1)}, bf16[768,1280]{1,0:T(8,128)(2,1)S(1)}, u32[]{:S(2)}, u32[]{:S(2)}) %collective-permute-start.2) | collective-permute-done | bytes 1966112 | tf_op jit(solution)/shard_map/ppermute | solution.py:23
  46.1 1.7 collective-permute-start.6
  47.8 0.3 collective-permute-start.8
  48.1 6.3 %collective-permute-start.4 = (bf16[768,1280]{1,0:T(8,128)(2,1)S(1)}, bf16[768,1280]{1,0:T(8,128)(2,1)S(1)}, u32[]{:S(2)}, u32[]{:S(2)}) collective-permute-start(bf16[768,1280]{1,0:T(8,128)(2,1)S(1)} %copy-done), channel_id=1, source_target_pairs={{0,1},{1,0},{2,3},{3,2},{4,5},{5,4},{6,7},{7,6},{8,9},{9,8},{10,11... | collective-permute-start | bytes 5898248 | tf_op jit(solution)/shard_map/ppermute | solution.py:23
  54.4 14.5 %collective-permute-done.6.refs_8_ = bf16[640,896]{1,0:T(8,128)(2,1)S(1)} collective-permute-done((bf16[640,896]{1,0:T(8,128)(2,1)S(1)}, bf16[640,896]{1,0:T(8,128)(2,1)S(1)}, u32[]{:S(2)}, u32[]{:S(2)}) %collective-permute-start.6) | collective-permute-done | bytes 1146912 | tf_op jit(solution)/shard_map/ppermute | solution.py:23
  68.9 4.2 %collective-permute-start.7 = (bf16[640,896]{1,0:T(8,128)(2,1)S(1)}, bf16[640,896]{1,0:T(8,128)(2,1)S(1)}, u32[]{:S(2)}, u32[]{:S(2)}) collective-permute-start(bf16[640,896]{1,0:T(8,128)(2,1)S(1)} %collective-permute-done.6.refs_8_), channel_id=1, source_target_pairs={{0,8},{1,9},{2,10},{3,11},{4,0},{5,1},{6,2},{7,3},{8,16},{9,17},{1... | collective-permute-start | bytes 3440648 | tf_op jit(solution)/shard_map/ppermute | solution.py:23
  73.2 1.2 collective-permute-done.8.refs_7_
  74.4 0.7 collective-permute-start.10
  75.2 1.4 fusion
  76.6 0.3 pad_maximum_fusion
  76.9 8.1 %shard_map.100.refs_6_ = f32[768,896]{1,0:T(8,128)S(1)} custom-call(bf16[768,1280]{1,0:T(8,128)(2,1)S(1)} %copy-done, bf16[768,1280]{1,0:T(8,128)(2,1)S(1)} %collective-permute-done.4.refs_1_, bf16[768,1280]{1,0:T(8,128)(2,1)S(1)} %collective-permute-done.2.refs_2_, bf16[768,1280]{1,0:T(8,128)(2,1)S(1)} %collective-permute-done.5.refs_3_, ...), custom_call_target="tpu_custom_call" | custom-call | flops 1 | bytes 1 | tf_op jit(solution)/shard_map/pallas_call | solution.py:254
  85.0 13.2 %collective-permute-done.7.refs_5_ = bf16[640,896]{1,0:T(8,128)(2,1)S(1)} collective-permute-done((bf16[640,896]{1,0:T(8,128)(2,1)S(1)}, bf16[640,896]{1,0:T(8,128)(2,1)S(1)}, u32[]{:S(2)}, u32[]{:S(2)}) %collective-permute-start.7) | collective-permute-done | bytes 1146912 | tf_op jit(solution)/shard_map/ppermute | solution.py:23
  98.2 2.2 %collective-permute-done.9.refs_4_ = bf16[640,896]{1,0:T(8,128)(2,1)S(1)} collective-permute-done((bf16[640,896]{1,0:T(8,128)(2,1)S(1)}, bf16[640,896]{1,0:T(8,128)(2,1)S(1)}, u32[]{:S(2)}, u32[]{:S(2)}) %collective-permute-start.9) | collective-permute-done | bytes 1146912 | tf_op jit(solution)/shard_map/ppermute | solution.py:23
  100.4 0.2 broadcast_in_dim.8.refs_7_
  100.6 2.0 collective-permute-start.11
  102.7 0.1 collective-permute-start.12
  102.8 3.8 %shard_map.101.refs_6_ = f32[768,896]{1,0:T(8,128)S(1)} custom-call(bf16[768,1280]{1,0:T(8,128)(2,1)S(1)} %copy-done, bf16[768,1280]{1,0:T(8,128)(2,1)S(1)} %collective-permute-done.4.refs_1_, bf16[768,1280]{1,0:T(8,128)(2,1)S(1)} %collective-permute-done.2.refs_2_, bf16[768,1280]{1,0:T(8,128)(2,1)S(1)} %collective-permute-done.5.refs_3_, ...), custom_call_target="tpu_custom_call" | custom-call | flops 1 | bytes 1 | tf_op jit(solution)/shard_map/pallas_call | solution.py:254
  106.6 0.0 copy-start.4
  106.6 0.0 copy-start.1
  106.6 9.1 %collective-permute-done.11.refs_4_ = bf16[320,896]{1,0:T(8,128)(2,1)S(1)} collective-permute-done((bf16[320,896]{1,0:T(8,128)(2,1)S(1)}, bf16[320,896]{1,0:T(8,128)(2,1)S(1)}, u32[]{:S(2)}, u32[]{:S(2)}) %collective-permute-start.11) | collective-permute-done | bytes 573472 | tf_op jit(solution)/shard_map/ppermute | solution.py:23
  115.7 2.9 %collective-permute-done.12.refs_5_ = bf16[320,896]{1,0:T(8,128)(2,1)S(1)} collective-permute-done((bf16[320,896]{1,0:T(8,128)(2,1)S(1)}, bf16[320,896]{1,0:T(8,128)(2,1)S(1)}, u32[]{:S(2)}, u32[]{:S(2)}) %collective-permute-start.12) | collective-permute-done | bytes 573472 | tf_op jit(solution)/shard_map/ppermute | solution.py:23
  118.6 0.3 collective-permute-start.17
  118.8 1.8 collective-permute-start.18
  120.6 3.4 %shard_map.102 = (f32[768,896]{1,0:T(8,128)S(1)}, f32[8,768]{1,0:T(8,128)S(1)}) custom-call(bf16[768,1280]{1,0:T(8,128)(2,1)S(1)} %copy-done, bf16[768,1280]{1,0:T(8,128)(2,1)S(1)} %collective-permute-done.4.refs_1_, bf16[768,1280]{1,0:T(8,128)(2,1)S(1)} %collective-permute-done.2.refs_2_, bf16[768,1280]{1,0:T(8,128)(2,1)S(1)} %collective-permute-done.5.refs_3_, ...), custom_call_target="tpu_custom_call" | custom-call | flops 1 | bytes 1 | tf_op jit(solution)/shard_map/pallas_call | solution.py:254
  124.0 0.1 collective-permute-start.13
  124.1 4.1 %collective-permute-start.14 = (f32[8,768]{1,0:T(8,128)S(1)}, f32[8,768]{1,0:T(8,128)S(1)}, u32[]{:S(2)}, u32[]{:S(2)}) collective-permute-start(f32[8,768]{1,0:T(8,128)S(1)} %get-tuple-element.41.refs_1_), channel_id=1, source_target_pairs={{0,2},{1,3},{2,0},{3,1},{4,6},{5,7},{6,4},{7,5},{8,10},{9,11},{10,... | collective-permute-start | bytes 73736 | tf_op jit(solution)/shard_map/ppermute | solution.py:23
  128.1 0.1 collective-permute-start.15
  128.2 1.7 collective-permute-done.14.refs_3_
  129.9 1.4 collective-permute-done.15.refs_4_
  131.4 4.4 %shard_map.103.refs_0_ = bf16[768,640]{1,0:T(8,128)(2,1)S(1)} custom-call(f32[768,896]{1,0:T(8,128)S(1)} %get-tuple-element.40.refs_0_, f32[8,768]{1,0:T(8,128)S(1)} %get-tuple-element.41.refs_1_, f32[8,768]{1,0:T(8,128)S(1)} %collective-permute-done.13.refs_2_, f32[8,768]{1,0:T(8,128)S(1)} %collective-permute-done.14.refs_3_, ...), custom_call_target="tpu_custom_call" | custom-call | flops 1 | bytes 1 | tf_op jit(solution)/shard_map/pallas_call | solution.py:345
  135.8 0.7 collective-permute-start.16
  136.4 2.4 %collective-permute-done.17.refs_6_ = bf16[640,640]{1,0:T(8,128)(2,1)S(1)} collective-permute-done((bf16[640,640]{1,0:T(8,128)(2,1)S(1)}, bf16[640,640]{1,0:T(8,128)(2,1)S(1)}, u32[]{:S(2)}, u32[]{:S(2)}) %collective-permute-start.17) | collective-permute-done | bytes 819232 | tf_op jit(solution)/shard_map/ppermute | solution.py:23
  138.8 0.0 collective-permute-done.18.refs_5_
  138.8 0.3 collective-permute-start.19
  139.1 1.7 collective-permute-start.20
  140.9 19.1 %collective-permute-done.16.refs_2_ = bf16[768,640]{1,0:T(8,128)(2,1)S(1)} collective-permute-done((bf16[768,640]{1,0:T(8,128)(2,1)S(1)}, bf16[768,640]{1,0:T(8,128)(2,1)S(1)}, u32[]{:S(2)}, u32[]{:S(2)}) %collective-permute-start.16) | collective-permute-done | bytes 983072 | tf_op jit(solution)/shard_map/ppermute | solution.py:23
  160.0 0.5 collective-permute-start.22
  160.5 0.3 collective-permute-start.23
  160.8 1.7 collective-permute-start.24
  162.5 0.0 collective-permute-done.21.refs_1_
  162.5 1.4 collective-permute-done.22.refs_3_
  164.0 7.2 %shard_map.104.refs_6_ = f32[768,1280]{1,0:T(8,128)S(1)} custom-call(bf16[768,640]{1,0:T(8,128)(2,1)S(1)} %shard_map.103.refs_0_, bf16[768,640]{1,0:T(8,128)(2,1)S(1)} %collective-permute-done.21.refs_1_, bf16[768,640]{1,0:T(8,128)(2,1)S(1)} %collective-permute-done.16.refs_2_, bf16[768,640]{1,0:T(8,128)(2,1)S(1)} %collective-permute-done.22.refs_3_, ...), custom_call_target="tpu_custom_call" | custom-call | flops 1 | bytes 1 | tf_op jit(solution)/shard_map/pallas_call | solution.py:254
  171.2 9.5 %collective-permute-done.23.refs_5_ = bf16[640,640]{1,0:T(8,128)(2,1)S(1)} collective-permute-done((bf16[640,640]{1,0:T(8,128)(2,1)S(1)}, bf16[640,640]{1,0:T(8,128)(2,1)S(1)}, u32[]{:S(2)}, u32[]{:S(2)}) %collective-permute-start.23) | collective-permute-done | bytes 819232 | tf_op jit(solution)/shard_map/ppermute | solution.py:23
  180.7 0.0 collective-permute-done.24.refs_4_
  180.8 1.1 collective-permute-start.25
  181.9 1.1 collective-permute-start.26
  182.9 4.1 %shard_map.105.refs_6_ = f32[768,1280]{1,0:T(8,128)S(1)} custom-call(bf16[768,640]{1,0:T(8,128)(2,1)S(1)} %shard_map.103.refs_0_, bf16[768,640]{1,0:T(8,128)(2,1)S(1)} %collective-permute-done.21.refs_1_, bf16[768,640]{1,0:T(8,128)(2,1)S(1)} %collective-permute-done.16.refs_2_, bf16[768,640]{1,0:T(8,128)(2,1)S(1)} %collective-permute-done.22.refs_3_, ...), custom_call_target="tpu_custom_call" | custom-call | flops 1 | bytes 1 | tf_op jit(solution)/shard_map/pallas_call | solution.py:254
  187.1 4.3 %collective-permute-done.25.refs_4_ = bf16[320,640]{1,0:T(8,128)(2,1)S(1)} collective-permute-done((bf16[320,640]{1,0:T(8,128)(2,1)S(1)}, bf16[320,640]{1,0:T(8,128)(2,1)S(1)}, u32[]{:S(2)}, u32[]{:S(2)}) %collective-permute-start.25) | collective-permute-done | bytes 409632 | tf_op jit(solution)/shard_map/ppermute | solution.py:23
  191.4 0.5 collective-permute-done.26.refs_5_
  191.9 3.2 %shard_map.106 = (f32[768,1280]{1,0:T(8,128)S(1)}, f32[8,768]{1,0:T(8,128)S(1)}) custom-call(bf16[768,640]{1,0:T(8,128)(2,1)S(1)} %shard_map.103.refs_0_, bf16[768,640]{1,0:T(8,128)(2,1)S(1)} %collective-permute-done.21.refs_1_, bf16[768,640]{1,0:T(8,128)(2,1)S(1)} %collective-permute-done.16.refs_2_, ...), custom_call_target="tpu_custom_call", output_to_operand_aliasing={{0}: (6, {})} | custom-call | flops 1 | bytes 1 | tf_op jit(solution)/shard_map/pallas_call | solution.py:254
  195.1 0.1 collective-permute-start.27
  195.2 0.2 collective-permute-start.28
  195.4 1.6 collective-permute-start.29
  197.7 1.4 collective-permute-done.28.refs_4_
  199.1 1.9 shard_map.107
  (28 shorter events, 0.2 us)
Async XLA Ops:
  0.0 48.1 %copy-start = (bf16[768,1280]{1,0:T(8,128)(2,1)S(1)}, bf16[768,1280]{1,0:T(8,128)(2,1)}, u32[]{:S(2)}) copy-start(bf16[768,1280]{1,0:T(8,128)(2,1)} %refs_6_.1) | copy-start | bytes 5898244
  0.0 75.1 %copy-start.2 = (s32[768]{0:T(1024)S(1)}, s32[768]{0:T(1024)}, u32[]{:S(2)}) copy-start(s32[768]{0:T(1024)} %param.12) | copy-start | bytes 9220
  0.0 46.1 %collective-permute-start.2 = (bf16[768,1280]{1,0:T(8,128)(2,1)}, bf16[768,1280]{1,0:T(8,128)(2,1)S(1)}, u32[]{:S(2)}, u32[]{:S(2)}) collective-permute-start(bf16[768,1280]{1,0:T(8,128)(2,1)} %refs_6_.1), channel_id=1, source_target_pairs={{0,2},{1,3},{2,0},{3,1},{4,6},{5,7},{6,4},{7,5},{8,10},{9,11},{10,... | collective-permute-start | bytes 5898248 | tf_op jit(solution)/shard_map/ppermute | solution.py:23
  6.1 27.3 %collective-permute-start = (bf16[640,896]{1,0:T(8,128)(2,1)S(1)}, bf16[640,896]{1,0:T(8,128)(2,1)S(1)}, u32[]{:S(2)}, u32[]{:S(2)}) collective-permute-start(bf16[640,896]{1,0:T(8,128)(2,1)S(1)} %constant_dynamic-update-slice_fusion.refs_4_), channel_id=1, source_target_pairs={{0,8},{1,9},{2,10},{3,11},{4,0},{5,1},{6,2},{7,3},{8,16},{9,17},{1... | collective-permute-start | bytes 3440648 | tf_op jit(solution)/shard_map/ppermute | solution.py:23
  7.7 27.0 %collective-permute-start.1 = (bf16[640,896]{1,0:T(8,128)(2,1)S(1)}, bf16[640,896]{1,0:T(8,128)(2,1)S(1)}, u32[]{:S(2)}, u32[]{:S(2)}) collective-permute-start(bf16[640,896]{1,0:T(8,128)(2,1)S(1)} %constant_dynamic-update-slice_fusion.refs_4_), channel_id=1, source_target_pairs={{0,4},{1,5},{2,6},{3,7},{4,12},{5,13},{6,14},{7,15},{8,0},{9,1},{1... | collective-permute-start | bytes 3440648 | tf_op jit(solution)/shard_map/ppermute | solution.py:23
  8.2 1.8 collective-permute-start.3
  46.1 22.9 %collective-permute-start.6 = (bf16[640,896]{1,0:T(8,128)(2,1)S(1)}, bf16[640,896]{1,0:T(8,128)(2,1)S(1)}, u32[]{:S(2)}, u32[]{:S(2)}) collective-permute-start(bf16[640,896]{1,0:T(8,128)(2,1)S(1)} %collective-permute-done.refs_6_), channel_id=1, source_target_pairs={{0,8},{1,9},{2,10},{3,11},{4,0},{5,1},{6,2},{7,3},{8,16},{9,17},{1... | collective-permute-start | bytes 3440648 | tf_op jit(solution)/shard_map/ppermute | solution.py:23
  47.8 26.6 %collective-permute-start.8 = (bf16[640,896]{1,0:T(8,128)(2,1)S(1)}, bf16[640,896]{1,0:T(8,128)(2,1)S(1)}, u32[]{:S(2)}, u32[]{:S(2)}) collective-permute-start(bf16[640,896]{1,0:T(8,128)(2,1)S(1)} %collective-permute-done.1.refs_5_), channel_id=1, source_target_pairs={{0,4},{1,5},{2,6},{3,7},{4,12},{5,13},{6,14},{7,15},{8,0},{9,1},{1... | collective-permute-start | bytes 3440648 | tf_op jit(solution)/shard_map/ppermute | solution.py:23
  48.1 28.8 %collective-permute-start.4 = (bf16[768,1280]{1,0:T(8,128)(2,1)S(1)}, bf16[768,1280]{1,0:T(8,128)(2,1)S(1)}, u32[]{:S(2)}, u32[]{:S(2)}) collective-permute-start(bf16[768,1280]{1,0:T(8,128)(2,1)S(1)} %copy-done), channel_id=1, source_target_pairs={{0,1},{1,0},{2,3},{3,2},{4,5},{5,4},{6,7},{7,6},{8,9},{9,8},{10,11... | collective-permute-start | bytes 5898248 | tf_op jit(solution)/shard_map/ppermute | solution.py:23
  54.4 22.5 %collective-permute-start.5 = (bf16[768,1280]{1,0:T(8,128)(2,1)S(1)}, bf16[768,1280]{1,0:T(8,128)(2,1)S(1)}, u32[]{:S(2)}, u32[]{:S(2)}) collective-permute-start(bf16[768,1280]{1,0:T(8,128)(2,1)S(1)} %collective-permute-done.2.refs_2_), channel_id=1, source_target_pairs={{0,1},{1,0},{2,3},{3,2},{4,5},{5,4},{6,7},{7,6},{8,9},{9,8},{10,11... | collective-permute-start | bytes 5898248 | tf_op jit(solution)/shard_map/ppermute | solution.py:23
  68.9 29.3 %collective-permute-start.7 = (bf16[640,896]{1,0:T(8,128)(2,1)S(1)}, bf16[640,896]{1,0:T(8,128)(2,1)S(1)}, u32[]{:S(2)}, u32[]{:S(2)}) collective-permute-start(bf16[640,896]{1,0:T(8,128)(2,1)S(1)} %collective-permute-done.6.refs_8_), channel_id=1, source_target_pairs={{0,8},{1,9},{2,10},{3,11},{4,0},{5,1},{6,2},{7,3},{8,16},{9,17},{1... | collective-permute-start | bytes 3440648 | tf_op jit(solution)/shard_map/ppermute | solution.py:23
  74.4 26.0 %collective-permute-start.9 = (bf16[640,896]{1,0:T(8,128)(2,1)S(1)}, bf16[640,896]{1,0:T(8,128)(2,1)S(1)}, u32[]{:S(2)}, u32[]{:S(2)}) collective-permute-start(bf16[640,896]{1,0:T(8,128)(2,1)S(1)} %collective-permute-done.8.refs_7_), channel_id=1, source_target_pairs={{0,4},{1,5},{2,6},{3,7},{4,12},{5,13},{6,14},{7,15},{8,0},{9,1},{1... | collective-permute-start | bytes 3440648 | tf_op jit(solution)/shard_map/ppermute | solution.py:23
  74.4 10.6 %collective-permute-start.10 = (bf16[640,640]{1,0:T(8,128)(2,1)S(1)}, bf16[640,640]{1,0:T(8,128)(2,1)S(1)}, u32[]{:S(2)}, u32[]{:S(2)}) collective-permute-start(bf16[640,640]{1,0:T(8,128)(2,1)S(1)} %collective-permute-done.3), channel_id=1, source_target_pairs={{0,0},{1,2},{2,1},{3,3},{4,4},{5,6},{6,5},{7,7},{8,9},{9,11},{10,8... | collective-permute-start | bytes 2457608 | tf_op jit(solution)/shard_map/ppermute | solution.py:23
  100.6 15.1 %collective-permute-start.11 = (bf16[320,896]{1,0:T(8,128)(2,1)S(1)}, bf16[320,896]{1,0:T(8,128)(2,1)S(1)}, u32[]{:S(2)}, u32[]{:S(2)}) collective-permute-start(bf16[320,896]{1,0:T(8,128)(2,1)S(1)} %slice.12), channel_id=1, source_target_pairs={{0,8},{1,9},{2,10},{3,11},{4,0},{5,1},{6,2},{7,3},{8,16},{9,17},{1... | collective-permute-start | bytes 1720328 | tf_op jit(solution)/shard_map/ppermute | solution.py:23
  102.7 15.9 %collective-permute-start.12 = (bf16[320,896]{1,0:T(8,128)(2,1)S(1)}, bf16[320,896]{1,0:T(8,128)(2,1)S(1)}, u32[]{:S(2)}, u32[]{:S(2)}) collective-permute-start(bf16[320,896]{1,0:T(8,128)(2,1)S(1)} %slice.13), channel_id=1, source_target_pairs={{0,4},{1,5},{2,6},{3,7},{4,12},{5,13},{6,14},{7,15},{8,0},{9,1},{1... | collective-permute-start | bytes 1720328 | tf_op jit(solution)/shard_map/ppermute | solution.py:23
  106.6 21.6 %copy-start.4 = (f32[640]{0:T(1024)S(1)}, f32[640]{0:T(1024)}, u32[]{:S(2)}) copy-start(f32[640]{0:T(1024)} %param.17) | copy-start | bytes 7684
  106.6 24.8 %copy-start.1 = (f32[128]{0:T(128)S(1)}, f32[128]{0:T(128)}, u32[]{:S(2)}) copy-start(f32[128]{0:T(128)} %param.18) | copy-start | bytes 1540
  118.6 20.3 %collective-permute-start.17 = (bf16[640,640]{1,0:T(8,128)(2,1)S(1)}, bf16[640,640]{1,0:T(8,128)(2,1)S(1)}, u32[]{:S(2)}, u32[]{:S(2)}) collective-permute-start(bf16[640,640]{1,0:T(8,128)(2,1)S(1)} %collective-permute-done.10.refs_4_), channel_id=1, source_target_pairs={{0,8},{1,9},{2,10},{3,11},{4,0},{5,1},{6,2},{7,3},{8,16},{9,17},{1... | collective-permute-start | bytes 2457608 | tf_op jit(solution)/shard_map/ppermute | solution.py:23
  118.8 20.0 %collective-permute-start.18 = (bf16[640,640]{1,0:T(8,128)(2,1)S(1)}, bf16[640,640]{1,0:T(8,128)(2,1)S(1)}, u32[]{:S(2)}, u32[]{:S(2)}) collective-permute-start(bf16[640,640]{1,0:T(8,128)(2,1)S(1)} %collective-permute-done.10.refs_4_), channel_id=1, source_target_pairs={{0,4},{1,5},{2,6},{3,7},{4,12},{5,13},{6,14},{7,15},{8,0},{9,1},{1... | collective-permute-start | bytes 2457608 | tf_op jit(solution)/shard_map/ppermute | solution.py:23
  124.0 4.2 %collective-permute-start.13 = (f32[8,768]{1,0:T(8,128)S(1)}, f32[8,768]{1,0:T(8,128)S(1)}, u32[]{:S(2)}, u32[]{:S(2)}) collective-permute-start(f32[8,768]{1,0:T(8,128)S(1)} %get-tuple-element.41.refs_1_), channel_id=1, source_target_pairs={{0,1},{1,0},{2,3},{3,2},{4,5},{5,4},{6,7},{7,6},{8,9},{9,8},{10,11... | collective-permute-start | bytes 73736 | tf_op jit(solution)/shard_map/ppermute | solution.py:23
  124.1 5.9 %collective-permute-start.14 = (f32[8,768]{1,0:T(8,128)S(1)}, f32[8,768]{1,0:T(8,128)S(1)}, u32[]{:S(2)}, u32[]{:S(2)}) collective-permute-start(f32[8,768]{1,0:T(8,128)S(1)} %get-tuple-element.41.refs_1_), channel_id=1, source_target_pairs={{0,2},{1,3},{2,0},{3,1},{4,6},{5,7},{6,4},{7,5},{8,10},{9,11},{10,... | collective-permute-start | bytes 73736 | tf_op jit(solution)/shard_map/ppermute | solution.py:23
  128.1 3.3 %collective-permute-start.15 = (f32[8,768]{1,0:T(8,128)S(1)}, f32[8,768]{1,0:T(8,128)S(1)}, u32[]{:S(2)}, u32[]{:S(2)}) collective-permute-start(f32[8,768]{1,0:T(8,128)S(1)} %get-tuple-element.41.refs_1_), channel_id=1, source_target_pairs={{0,3},{1,2},{2,1},{3,0},{4,7},{5,6},{6,5},{7,4},{8,11},{9,10},{10,... | collective-permute-start | bytes 73736 | tf_op jit(solution)/shard_map/ppermute | solution.py:23
  135.8 24.2 %collective-permute-start.16 = (bf16[768,640]{1,0:T(8,128)(2,1)S(1)}, bf16[768,640]{1,0:T(8,128)(2,1)S(1)}, u32[]{:S(2)}, u32[]{:S(2)}) collective-permute-start(bf16[768,640]{1,0:T(8,128)(2,1)S(1)} %shard_map.103.refs_0_), channel_id=1, source_target_pairs={{0,2},{1,3},{2,0},{3,1},{4,6},{5,7},{6,4},{7,5},{8,10},{9,11},{10,... | collective-permute-start | bytes 2949128 | tf_op jit(solution)/shard_map/ppermute | solution.py:23
  138.8 21.1 %collective-permute-start.19 = (bf16[640,640]{1,0:T(8,128)(2,1)S(1)}, bf16[640,640]{1,0:T(8,128)(2,1)S(1)}, u32[]{:S(2)}, u32[]{:S(2)}) collective-permute-start(bf16[640,640]{1,0:T(8,128)(2,1)S(1)} %collective-permute-done.17.refs_6_), channel_id=1, source_target_pairs={{0,8},{1,9},{2,10},{3,11},{4,0},{5,1},{6,2},{7,3},{8,16},{9,17},{1... | collective-permute-start | bytes 2457608 | tf_op jit(solution)/shard_map/ppermute | solution.py:23
  139.1 20.8 %collective-permute-start.20 = (bf16[640,640]{1,0:T(8,128)(2,1)S(1)}, bf16[640,640]{1,0:T(8,128)(2,1)S(1)}, u32[]{:S(2)}, u32[]{:S(2)}) collective-permute-start(bf16[640,640]{1,0:T(8,128)(2,1)S(1)} %collective-permute-done.18.refs_5_), channel_id=1, source_target_pairs={{0,4},{1,5},{2,6},{3,7},{4,12},{5,13},{6,14},{7,15},{8,0},{9,1},{1... | collective-permute-start | bytes 2457608 | tf_op jit(solution)/shard_map/ppermute | solution.py:23
  160.0 2.6 %collective-permute-start.21 = (bf16[768,640]{1,0:T(8,128)(2,1)S(1)}, bf16[768,640]{1,0:T(8,128)(2,1)S(1)}, u32[]{:S(2)}, u32[]{:S(2)}) collective-permute-start(bf16[768,640]{1,0:T(8,128)(2,1)S(1)} %shard_map.103.refs_0_), channel_id=1, source_target_pairs={{0,1},{1,0},{2,3},{3,2},{4,5},{5,4},{6,7},{7,6},{8,9},{9,8},{10,11... | collective-permute-start | bytes 2949128 | tf_op jit(solution)/shard_map/ppermute | solution.py:23
  160.0 4.0 %collective-permute-start.22 = (bf16[768,640]{1,0:T(8,128)(2,1)S(1)}, bf16[768,640]{1,0:T(8,128)(2,1)S(1)}, u32[]{:S(2)}, u32[]{:S(2)}) collective-permute-start(bf16[768,640]{1,0:T(8,128)(2,1)S(1)} %collective-permute-done.16.refs_2_), channel_id=1, source_target_pairs={{0,1},{1,0},{2,3},{3,2},{4,5},{5,4},{6,7},{7,6},{8,9},{9,8},{10,11... | collective-permute-start | bytes 2949128 | tf_op jit(solution)/shard_map/ppermute | solution.py:23
  160.5 20.2 %collective-permute-start.23 = (bf16[640,640]{1,0:T(8,128)(2,1)S(1)}, bf16[640,640]{1,0:T(8,128)(2,1)S(1)}, u32[]{:S(2)}, u32[]{:S(2)}) collective-permute-start(bf16[640,640]{1,0:T(8,128)(2,1)S(1)} %collective-permute-done.19.refs_8_), channel_id=1, source_target_pairs={{0,8},{1,9},{2,10},{3,11},{4,0},{5,1},{6,2},{7,3},{8,16},{9,17},{1... | collective-permute-start | bytes 2457608 | tf_op jit(solution)/shard_map/ppermute | solution.py:23
  160.8 19.9 %collective-permute-start.24 = (bf16[640,640]{1,0:T(8,128)(2,1)S(1)}, bf16[640,640]{1,0:T(8,128)(2,1)S(1)}, u32[]{:S(2)}, u32[]{:S(2)}) collective-permute-start(bf16[640,640]{1,0:T(8,128)(2,1)S(1)} %collective-permute-done.20.refs_7_), channel_id=1, source_target_pairs={{0,4},{1,5},{2,6},{3,7},{4,12},{5,13},{6,14},{7,15},{8,0},{9,1},{1... | collective-permute-start | bytes 2457608 | tf_op jit(solution)/shard_map/ppermute | solution.py:23
  180.8 10.6 %collective-permute-start.25 = (bf16[320,640]{1,0:T(8,128)(2,1)S(1)}, bf16[320,640]{1,0:T(8,128)(2,1)S(1)}, u32[]{:S(2)}, u32[]{:S(2)}) collective-permute-start(bf16[320,640]{1,0:T(8,128)(2,1)S(1)} %slice.14), channel_id=1, source_target_pairs={{0,8},{1,9},{2,10},{3,11},{4,0},{5,1},{6,2},{7,3},{8,16},{9,17},{1... | collective-permute-start | bytes 1228808 | tf_op jit(solution)/shard_map/ppermute | solution.py:23
  181.9 10.0 %collective-permute-start.26 = (bf16[320,640]{1,0:T(8,128)(2,1)S(1)}, bf16[320,640]{1,0:T(8,128)(2,1)S(1)}, u32[]{:S(2)}, u32[]{:S(2)}) collective-permute-start(bf16[320,640]{1,0:T(8,128)(2,1)S(1)} %slice.15), channel_id=1, source_target_pairs={{0,4},{1,5},{2,6},{3,7},{4,12},{5,13},{6,14},{7,15},{8,0},{9,1},{1... | collective-permute-start | bytes 1228808 | tf_op jit(solution)/shard_map/ppermute | solution.py:23
  187.1 10.0 %copy-start.3 = (f32[1280]{0:T(1024)S(1)}, f32[1280]{0:T(1024)}, u32[]{:S(2)}) copy-start(f32[1280]{0:T(1024)} %param.19) | copy-start | bytes 15364
  195.1 2.6 %collective-permute-start.27 = (f32[8,768]{1,0:T(8,128)S(1)}, f32[8,768]{1,0:T(8,128)S(1)}, u32[]{:S(2)}, u32[]{:S(2)}) collective-permute-start(f32[8,768]{1,0:T(8,128)S(1)} %get-tuple-element.54.refs_2_), channel_id=1, source_target_pairs={{0,1},{1,0},{2,3},{3,2},{4,5},{5,4},{6,7},{7,6},{8,9},{9,8},{10,11... | collective-permute-start | bytes 73736 | tf_op jit(solution)/shard_map/ppermute | solution.py:23
  195.2 3.9 %collective-permute-start.28 = (f32[8,768]{1,0:T(8,128)S(1)}, f32[8,768]{1,0:T(8,128)S(1)}, u32[]{:S(2)}, u32[]{:S(2)}) collective-permute-start(f32[8,768]{1,0:T(8,128)S(1)} %get-tuple-element.54.refs_2_), channel_id=1, source_target_pairs={{0,2},{1,3},{2,0},{3,1},{4,6},{5,7},{6,4},{7,5},{8,10},{9,11},{10,... | collective-permute-start | bytes 73736 | tf_op jit(solution)/shard_map/ppermute | solution.py:23
  195.4 3.7 %collective-permute-start.29 = (f32[8,768]{1,0:T(8,128)S(1)}, f32[8,768]{1,0:T(8,128)S(1)}, u32[]{:S(2)}, u32[]{:S(2)}) collective-permute-start(f32[8,768]{1,0:T(8,128)S(1)} %get-tuple-element.54.refs_2_), channel_id=1, source_target_pairs={{0,3},{1,2},{2,1},{3,0},{4,7},{5,6},{6,5},{7,4},{8,11},{9,10},{10,... | collective-permute-start | bytes 73736 | tf_op jit(solution)/shard_map/ppermute | solution.py:23
